TPU v7x, 32 devices: a whole 2x2x4 slice. The times are simulated.
32 devices in a mesh: section: 4 (over y, core), seq: 8 (over z, x).
Axes of the slice: x: 2, y: 2, z: 4, core: 2. Of those that a mesh axis runs over, the one named last changes fastest.
Arguments:
- resident_microbatch: bfloat16 [4, 1024, 1024], P('section', 'seq'), may hold values from -36 to 36
- upcoming_amino_ids: int32 [1024], P('seq'), may hold values from 0 to 31
- upcoming_polymer_sizes: int32 [8], replicated, may hold values from 1 to 256, 1024 in all
- amino_acid_vectors: bfloat16 [32, 1024], replicated, may hold values from -36 to 36
- polymer_vectors: bfloat16 [8, 1024], replicated, may hold values from -3 to 3
- normalizer_scaling: float32 [4, 1024], P('section'), may hold values from 0.25 to 1.75
- entry_projection_matrix: bfloat16 [4, 1024, 3072], P('section'), may hold values from -0.1875 to 0.1875
- convolution_kernels_long: float32 [4, 2, 1024, 1024], P('section', None, 'seq'), may hold values from -4 to 4
- convolution_skip_coefficients: float32 [4, 2, 1024], P('section', None, 'seq'), may hold values from -1 to 1
- exit_projection_matrix: bfloat16 [4, 1024, 1024], P('section'), may hold values from -0.1875 to 0.1875
- adjoint_seeds: bfloat16 [4, 2, 1024, 1024], P('section', None, 'seq'), may hold values from -0.0625 to 0.0625
Outputs:
- passed: bfloat16 [4, 1024, 1024], P('section', 'seq')
- out_grad: float32 [4, 1024, 1024], P('section', 'seq')
All inputs are finite; a program needn't handle non-finite values.
Results may differ from a plain program's by a relative error of at most 0.025.
Values may be sent and summed in bfloat16 or wider, within the bound.
No kernel may reach another device: no remote copies, remote signals or barrier semaphores. Data moves between devices by JAX's collectives and lax.ppermute only.
A program may use at most 128 MiB of HBM per device.

v0:
```python
import functools
import math

import jax
import jax.numpy as jnp
import ml_dtypes
import numpy as np
from jax import lax
from jax.experimental import pallas as pl
from jax.experimental.pallas import tpu as pltpu
from jax.sharding import PartitionSpec as P

epsilon = 1e-06
lanes = 128
parts = 4
f32 = jnp.float32
bf16 = jnp.bfloat16


def dot(a, b, contract=(1, 0)):
    return lax.dot_general(
        a, b, (((contract[0],), (contract[1],)), ((), ())), preferred_element_type=f32
    )


def params(mib):
    return pltpu.CompilerParams(vmem_limit_bytes=mib << 20)


def whole():
    return pl.BlockSpec(memory_space=pltpu.VMEM)


def scalars():
    return pl.BlockSpec(memory_space=pltpu.SMEM)


def cost(flops, bytes_accessed):
    return pl.CostEstimate(flops=flops, bytes_accessed=bytes_accessed, transcendentals=0)


def exchange(value, distance):
    peers = lax.axis_size("seq")
    return lax.ppermute(value, "seq", [(i, i ^ distance) for i in range(peers)])


def odd_transform(size):
    bins = 2 * np.arange(size)[:, None] + 1
    angle = (bins * np.arange(size)[None, :] % (4 * size)) * (math.pi / (2 * size))
    rows = np.concatenate([np.cos(angle), -np.sin(angle)], axis=0)
    forward = rows.astype(ml_dtypes.bfloat16)
    backward = (rows.T / size).astype(ml_dtypes.bfloat16)
    return jnp.asarray(forward), jnp.asarray(backward)


def prepare_kernel(
    base_ref, sizes_ref, ids_ref, amino_ref, polymer_ref, filters_ref, forward_ref, spectra_ref, embedded_ref
):
    size = forward_ref.shape[1]
    chunks = filters_ref.shape[2] // size
    sign = 1.0 - 2.0 * (lax.broadcasted_iota(jnp.int32, (size, 1), 0) & 1).astype(f32)
    for which in range(2):
        earlier = None
        for chunk in range(chunks):
            block = filters_ref[which, :, chunk * size : (chunk + 1) * size].astype(bf16)
            found = dot(forward_ref[...], block, (1, 1))
            real, imag = found[:size], found[size:]
            if earlier is None:
                spectra_ref[which, chunk, :size] = real
                spectra_ref[which, chunk, size:] = imag
            else:
                spectra_ref[which, chunk, :size] = real - sign * earlier[1]
                spectra_ref[which, chunk, size:] = imag + sign * earlier[0]
            earlier = (real, imag)
    count = ids_ref.shape[1]
    position = base_ref[0] + lax.broadcasted_iota(jnp.int32, (1, count), 1)
    chain = jnp.zeros((1, count), jnp.int32)
    end = jnp.int32(0)
    for j in range(sizes_ref.shape[0] - 1):
        end = end + sizes_ref[j]
        chain = chain + (position >= end).astype(jnp.int32)

    def rows_of(table_ref, index):
        entries = table_ref.shape[0]
        chosen = lax.broadcasted_iota(jnp.int32, (entries, count), 0) == index
        return dot(chosen.astype(f32).astype(bf16), table_ref[...], (0, 0))

    embedded_ref[...] = (rows_of(amino_ref, ids_ref[...]) + rows_of(polymer_ref, chain)).astype(bf16)


def prepare(base, sizes, ids, amino, polymer, filters, forward):
    size = forward.shape[1]
    channels, length = filters.shape[1:]
    chunks = length // size
    return pl.pallas_call(
        prepare_kernel,
        out_shape=(
            jax.ShapeDtypeStruct((2, chunks, 2 * size, channels), f32),
            jax.ShapeDtypeStruct((ids.shape[0], amino.shape[1]), bf16),
        ),
        in_specs=[scalars(), scalars()] + [whole()] * 5,
        out_specs=(whole(), whole()),
        compiler_params=params(32),
        cost_estimate=cost(8 * size * length * channels, 16 * length * channels),
        name="prepare",
    )(base, sizes, ids[None], amino, polymer, filters, forward)


def normalized(values, gain):
    values = values.astype(f32)
    inverse_rms = lax.rsqrt(jnp.mean(values * values, axis=1, keepdims=True) + epsilon)
    return (values * inverse_rms * gain).astype(bf16)


def project_kernel(table_ref, x_ref, other_ref, gain_ref, left_ref, right_ref, *rest):
    *pieces, normed_ref = rest
    step = pl.program_id(0)

    @pl.when(step == 0)
    def _():
        values = x_ref[...]
        if other_ref is not x_ref:
            values = jnp.where(table_ref[len(pieces)] == 1, other_ref[...], values)
        normed_ref[...] = normalized(values, gain_ref[...])

    normed = normed_ref[...]
    found = jnp.concatenate([dot(normed, left_ref[...]), dot(normed, right_ref[...])], axis=1).astype(bf16)
    for k, piece in enumerate(pieces):

        @pl.when(step == k)
        def _(piece=piece):
            piece[...] = found


def second_project_kernel(table_ref, normed_ref, left_ref, right_ref, *pieces):
    step = pl.program_id(0)
    normed = normed_ref[...]
    found = jnp.concatenate([dot(normed, left_ref[...]), dot(normed, right_ref[...])], axis=1).astype(bf16)
    for k, piece in enumerate(pieces):

        @pl.when(step == k)
        def _(piece=piece):
            piece[...] = found


def project(x, other, use_other, gain, weight, me, order, group_order):
    rows, width = x.shape
    peers = len(order)
    half = peers // 2
    block = width // peers
    near = me ^ jnp.asarray(order, jnp.int32)
    close = me ^ jnp.asarray(group_order, jnp.int32)
    if block % lanes:
        normed = normalized(jnp.where(use_other, other, x), gain)
        cut = dot(normed, weight).astype(bf16).reshape(rows, 3, peers, block)

        def pick(kind, index):
            return lax.dynamic_index_in_dim(cut[:, kind], index, axis=1, keepdims=False)

        first = [jnp.concatenate([pick(0, near[i]), pick(1, near[i])], axis=1) for i in range(peers)]
        second = [jnp.concatenate([pick(2, close[i]), pick(2, close[i] ^ half)], axis=1) for i in range(half)]
        return first, second

    def fixed(i, table):
        return (0, 0)

    piece = jax.ShapeDtypeStruct((rows, 2 * block), bf16)
    table = jnp.concatenate([near, use_other.astype(jnp.int32)[None]])
    *first, normed = pl.pallas_call(
        project_kernel,
        out_shape=(piece,) * peers + (jax.ShapeDtypeStruct((rows, width), bf16),),
        grid_spec=pltpu.PrefetchScalarGridSpec(
            num_scalar_prefetch=1,
            grid=(peers,),
            in_specs=[
                pl.BlockSpec((rows, width), fixed),
                pl.BlockSpec((rows, width), fixed),
                pl.BlockSpec((1, width), fixed),
                pl.BlockSpec((width, block), lambda i, table: (0, table[i])),
                pl.BlockSpec((width, block), lambda i, table: (0, peers + table[i])),
            ],
            out_specs=[pl.BlockSpec((rows, 2 * block), fixed)] * peers + [pl.BlockSpec((rows, width), fixed)],
        ),
        compiler_params=params(16),
        cost_estimate=cost(4 * rows * width * width, 4 * width * width),
        name="value_and_gate_one",
    )(table, x, other, gain[None], weight, weight)
    second = pl.pallas_call(
        second_project_kernel,
        out_shape=(piece,) * half,
        grid_spec=pltpu.PrefetchScalarGridSpec(
            num_scalar_prefetch=1,
            grid=(half,),
            in_specs=[
                pl.BlockSpec((rows, width), fixed),
                pl.BlockSpec((width, block), lambda i, table: (0, 2 * peers + table[i])),
                pl.BlockSpec((width, block), lambda i, table: (0, 2 * peers + (table[i] ^ half))),
            ],
            out_specs=[pl.BlockSpec((rows, 2 * block), fixed)] * half,
        ),
        compiler_params=params(16),
        cost_estimate=cost(2 * rows * width * width, 2 * width * width),
        name="gate_two",
    )(close, normed, weight, weight)
    return first, list(second)


def filter_kernel(order, where_ref, skips_ref, spectra_ref, forward_ref, backward_ref, *rest):
    pieces = rest[: len(order)]
    keep_ref, send_ref, value_ref, gate_ref, gated_ref, found_ref, mixed_ref = rest[len(order) :]
    me = where_ref[0]
    half = where_ref[1]
    channels = spectra_ref.shape[3]
    chunks = spectra_ref.shape[1]
    size = forward_ref.shape[1]
    rows = pieces[0].shape[0]
    for distance, piece in zip(order, pieces):
        place = pl.ds(pl.multiple_of((me ^ distance) * rows, rows), rows)
        value_ref[place, :] = piece[:, :channels]
        gate_ref[place, :] = piece[:, channels:]

    def chunk_rows(j):
        return slice(j * size, (j + 1) * size)

    def chunk_lanes(j):
        return slice(j * channels, (j + 1) * channels)

    step = 16

    def convolve(signal, which):
        found_ref[...] = dot(forward_ref[...], signal)

        def multiply(at, _):
            real_rows = pl.ds(pl.multiple_of(at * step, step), step)
            imag_rows = pl.ds(pl.multiple_of(size + at * step, step), step)
            signal_real = [found_ref[real_rows, chunk_lanes(j)] for j in range(chunks)]
            signal_imag = [found_ref[imag_rows, chunk_lanes(j)] for j in range(chunks)]
            kernel_real = [spectra_ref[which, j, real_rows, :] for j in range(chunks)]
            kernel_imag = [spectra_ref[which, j, imag_rows, :] for j in range(chunks)]
            for i in range(chunks):
                real = sum(
                    signal_real[j] * kernel_real[i - j] - signal_imag[j] * kernel_imag[i - j] for j in range(i + 1)
                )
                imag = sum(
                    signal_real[j] * kernel_imag[i - j] + signal_imag[j] * kernel_real[i - j] for j in range(i + 1)
                )
                mixed_ref[real_rows, chunk_lanes(i)] = real.astype(bf16)
                mixed_ref[imag_rows, chunk_lanes(i)] = imag.astype(bf16)
            return 0

        lax.fori_loop(0, size // step, multiply, 0)
        return dot(backward_ref[...], mixed_ref[...])

    result = convolve(jnp.concatenate([value_ref[chunk_rows(j), :] for j in range(chunks)], axis=1), 0)
    for j in range(chunks):
        value = value_ref[chunk_rows(j), :].astype(f32)
        gate = gate_ref[chunk_rows(j), :].astype(f32)
        gated_ref[:, chunk_lanes(j)] = gate * (result[:, chunk_lanes(j)] + skips_ref[0:1, :] * value)
    result = convolve(gated_ref[...].astype(bf16), 1)
    final = [
        (result[:, chunk_lanes(j)] + skips_ref[1:2, :] * gated_ref[:, chunk_lanes(j)]).astype(bf16)
        for j in range(chunks)
    ]
    for j in range(chunks // 2):
        low, high = final[j], final[j + chunks // 2]
        keep_ref[chunk_rows(j), :] = jnp.where(half == 0, low, high)
        send_ref[chunk_rows(j), :] = jnp.where(half == 0, high, low)


def filtered(received, order, where, skips, spectra, forward, backward):
    chunks, _, channels = spectra.shape[1:]
    size = forward.shape[1]
    length = chunks * size
    out = jax.ShapeDtypeStruct((length // 2, channels), bf16)
    return pl.pallas_call(
        functools.partial(filter_kernel, order),
        out_shape=(out, out),
        in_specs=[scalars()] + [whole()] * (4 + len(order)),
        out_specs=(whole(), whole()),
        scratch_shapes=[
            pltpu.VMEM((length, channels), bf16),
            pltpu.VMEM((length, channels), bf16),
            pltpu.VMEM((size, chunks * channels), f32),
            pltpu.VMEM((2 * size, chunks * channels), f32),
            pltpu.VMEM((2 * size, chunks * channels), bf16),
        ],
        compiler_params=params(40),
        cost_estimate=cost(16 * size * length * channels, 8 * length * channels),
        name="two_filters",
    )(where, skips, spectra, forward, backward, *received)


def gate_kernel(order, where_ref, keep_ref, come_ref, *rest):
    gates, outs = rest[: len(order)], rest[len(order) :]
    mine = where_ref[2]
    rows = gates[0].shape[0]
    for distance, gate, out in zip(order, gates, outs):
        place = pl.ds(pl.multiple_of((mine ^ distance) * rows, rows), rows)
        mixed = jnp.concatenate([keep_ref[place, :], come_ref[place, :]], axis=1)
        out[...] = (gate[...].astype(f32) * mixed.astype(f32)).astype(bf16)


def gate_two(where, keep, come, gates, order):
    return pl.pallas_call(
        functools.partial(gate_kernel, order),
        out_shape=tuple(jax.ShapeDtypeStruct(g.shape, bf16) for g in gates),
        in_specs=[scalars()] + [whole()] * (2 + len(gates)),
        out_specs=(whole(),) * len(gates),
        compiler_params=params(8),
        cost_estimate=cost(keep.size * 2, keep.size * 8),
        name="second_gate",
    )(where, keep, come, *gates)


def exit_kernel(order, where_ref, x_ref, other_ref, weight_ref, *rest):
    hyenas, out_ref = rest[: len(order)], rest[len(order)]
    me = where_ref[0]
    peers = 2 * len(order)
    block = weight_ref.shape[0] // peers
    values = x_ref[...]
    if other_ref is not x_ref:
        values = jnp.where(where_ref[3] == 1, other_ref[...], values)
    total = values.astype(f32)
    for distance, hyena in zip(order, hyenas):
        near = pl.ds(pl.multiple_of((me ^ distance) * block, block), block)
        far = pl.ds(pl.multiple_of((me ^ distance ^ len(order)) * block, block), block)
        total += dot(hyena[...], jnp.concatenate([weight_ref[near, :], weight_ref[far, :]], axis=0))
    out_ref[...] = total.astype(bf16)


def exit_projection(where, x, other, weight, hyenas, order):
    return pl.pallas_call(
        functools.partial(exit_kernel, order),
        out_shape=jax.ShapeDtypeStruct(x.shape, bf16),
        in_specs=[scalars()] + [whole()] * (3 + len(hyenas)),
        out_specs=whole(),
        compiler_params=params(12),
        cost_estimate=cost(2 * x.size * weight.shape[0], 2 * weight.size),
        name="exit_projection",
    )(where, x, other, weight, *hyenas)


def gradient_kernel(side, count, *refs):
    firsts, seconds, seeds = refs[:count], refs[count : 2 * count], refs[2 * count : 3 * count]
    out_ref = refs[3 * count]
    block = out_ref.shape[0]
    columns = slice(side * block, (side + 1) * block)
    total = jnp.zeros(out_ref.shape, f32)
    for first, second, seed in zip(firsts, seconds, seeds):
        hyenas = jnp.concatenate([first[:, columns], second[:, columns]], axis=0)
        rows = hyenas.shape[0] // 2
        total += dot(hyenas, seed[...].reshape(2 * rows, -1), (0, 0))
    out_ref[...] = total.astype(out_ref.dtype)


def gradient(firsts, seconds, seeds, side, dtype, name):
    count = len(firsts)
    block = firsts[0].shape[1] // 2
    width = seeds[0].shape[2]
    return pl.pallas_call(
        functools.partial(gradient_kernel, side, count),
        out_shape=jax.ShapeDtypeStruct((block, width), dtype),
        in_specs=[whole()] * (3 * count),
        out_specs=whole(),
        compiler_params=params(16),
        cost_estimate=cost(4 * count * firsts[0].size * width, 4 * count * width * firsts[0].shape[0]),
        name=name,
    )(*firsts, *seconds, *seeds)


def local(
    resident_microbatch,
    upcoming_amino_ids,
    upcoming_polymer_sizes,
    amino_acid_vectors,
    polymer_vectors,
    normalizer_scaling,
    entry_projection_matrix,
    convolution_kernels_long,
    convolution_skip_coefficients,
    exit_projection_matrix,
    adjoint_seeds,
):
    peers = lax.axis_size("seq")
    sections = lax.axis_size("section")
    group = peers // 2
    me = lax.axis_index("seq")
    first_section = (lax.axis_index("section") == 0).astype(jnp.int32)
    order = tuple(range(group, peers)) + tuple(range(group - 1, -1, -1))
    group_order = tuple(range(group - 1, -1, -1))
    where = jnp.stack([me, me // group, me % group, first_section])

    filters = convolution_kernels_long[0]
    size = filters.shape[2] // parts
    forward, backward = odd_transform(size)
    rows = upcoming_amino_ids.shape[0]
    spectra, embedded = prepare(
        (me * rows)[None],
        upcoming_polymer_sizes,
        upcoming_amino_ids,
        amino_acid_vectors,
        polymer_vectors,
        filters,
        forward,
    )
    gain, weight_in, weight_out = normalizer_scaling[0], entry_projection_matrix[0], exit_projection_matrix[0]
    skips = convolution_skip_coefficients[0]

    def layer(x, other, use_other):
        first, second = project(x, other, use_other, gain, weight_in, me, order, group_order)
        come = [exchange(v, d) if d else v for v, d in zip(first, order)]
        gates = [exchange(v, d) if d else v for v, d in zip(second, group_order)]
        keep, send = filtered(come, order, where, skips, spectra, forward, backward)
        hyenas = gate_two(where, keep, exchange(send, group), gates, group_order)
        home = [exchange(v, d) if d else v for v, d in zip(hyenas, group_order)]
        return home, hyenas

    resident = resident_microbatch[0]
    home, first_hyenas = layer(resident, resident, jnp.int32(0))
    first_out = exit_projection(where, resident, resident, weight_out, home, group_order)
    handed = lax.ppermute(first_out, "section", [(i, i + 1) for i in range(sections - 1)])
    seeds = [exchange(adjoint_seeds[0], d) if d else adjoint_seeds[0] for d in group_order]
    home, second_hyenas = layer(handed, embedded, first_section)
    away = gradient(first_hyenas, second_hyenas, seeds, 1, bf16, "gradient_away")
    mine = gradient(first_hyenas, second_hyenas, seeds, 0, f32, "gradient_mine")
    passed = exit_projection(where, handed, embedded, weight_out, home, group_order)
    out_grad = mine + exchange(away, group).astype(f32)
    return (passed[None], out_grad[None])


def solution(mesh):
    placed = (
        P("section", "seq", None),
        P("seq"),
        P(),
        P(),
        P(),
        P("section", None),
        P("section", None, None),
        P("section", None, "seq", None),
        P("section", None, "seq"),
        P("section", None, None),
        P("section", None, "seq", None),
    )
    return jax.shard_map(
        local,
        mesh=mesh,
        in_specs=placed,
        out_specs=(P("section", "seq", None), P("section", "seq", None)),
        check_vma=False,
    )
```

profile of v0, /device:TPU:0, one launch (start us, length us, event | category | flops | bytes accessed | tf_op | source)
XLA Modules:
  0.0 126.9 jit_solution(2975955379775389045)
XLA Ops:
  0.6 0.7 broadcast_xor_fusion.1
  1.4 2.8 %copy-done = bf16[1,1024,3072]{2,1,0:T(8,128)(2,1)S(1)} copy-done((bf16[1,1024,3072]{2,1,0:T(8,128)(2,1)S(1)}, bf16[1,1024,3072]{2,1,0:T(8,128)(2,1)}, u32[]{:S(2)}) %copy-start) | copy-done | bytes 6291480
  4.2 0.9 copy-done.3
  5.1 0.7 copy-done.11
  5.9 4.7 %value_and_gate_one.2 = (bf16[128,256]{1,0:T(8,128)(2,1)S(1)}, bf16[128,256]{1,0:T(8,128)(2,1)S(1)}, bf16[128,256]{1,0:T(8,128)(2,1)S(1)}, bf16[128,256]{1,0:T(8...) custom-call(s32[9]{0:T(128)S(1)} %get-tuple-element.83.table_ref, ...), custom_call_target="tpu_custom_call" | custom-call | flops 536870912 | bytes 4194304 | tf_op jit(solution)/shard_map/value_and_gate_one/pallas_call | solution.py:169
  10.5 4.1 %collective-permute-start = (bf16[128,256]{1,0:T(8,128)(2,1)S(1)}, bf16[128,256]{1,0:T(8,128)(2,1)S(1)}, u32[]{:S(2)}, u32[]{:S(2)}) collective-permute-start(bf16[128,256]{1,0:T(8,128)(2,1)S(1)} %get-tuple-element.43), channel_id=1, source_target_pairs={{0,4},{1,5},{2,6},{3,7},{4,0},{5,1},{6,2},{7,3},{8,12},{9,13},{10,... | collective-permute-start | bytes 196616 | tf_op jit(solution)/shard_map/ppermute | solution.py:44
  14.6 1.3 collective-permute-start.1
  15.9 3.6 %collective-permute-start.2 = (bf16[128,256]{1,0:T(8,128)(2,1)S(1)}, bf16[128,256]{1,0:T(8,128)(2,1)S(1)}, u32[]{:S(2)}, u32[]{:S(2)}) collective-permute-start(bf16[128,256]{1,0:T(8,128)(2,1)S(1)} %get-tuple-element.45), channel_id=1, source_target_pairs={{0,6},{1,7},{2,4},{3,5},{4,2},{5,3},{6,0},{7,1},{8,14},{9,15},{10,... | collective-permute-start | bytes 196616 | tf_op jit(solution)/shard_map/ppermute | solution.py:44
  19.5 0.9 collective-permute-start.4
  20.4 2.2 %collective-permute-start.5 = (bf16[128,256]{1,0:T(8,128)(2,1)S(1)}, bf16[128,256]{1,0:T(8,128)(2,1)S(1)}, u32[]{:S(2)}, u32[]{:S(2)}) collective-permute-start(bf16[128,256]{1,0:T(8,128)(2,1)S(1)} %get-tuple-element.48), channel_id=1, source_target_pairs={{0,2},{1,3},{2,0},{3,1},{4,6},{5,7},{6,4},{7,5},{8,10},{9,11},{10,... | collective-permute-start | bytes 196616 | tf_op jit(solution)/shard_map/ppermute | solution.py:44
  22.7 1.2 collective-permute-done.1.rest_1_
  23.9 2.3 %collective-permute-start.6 = (bf16[128,256]{1,0:T(8,128)(2,1)S(1)}, bf16[128,256]{1,0:T(8,128)(2,1)S(1)}, u32[]{:S(2)}, u32[]{:S(2)}) collective-permute-start(bf16[128,256]{1,0:T(8,128)(2,1)S(1)} %get-tuple-element.49), channel_id=1, source_target_pairs={{0,1},{1,0},{2,3},{3,2},{4,5},{5,4},{6,7},{7,6},{8,9},{9,8},{10,11... | collective-permute-start | bytes 196616 | tf_op jit(solution)/shard_map/ppermute | solution.py:44
  26.3 1.4 %prepare.1 = (f32[2,4,512,128]{3,2,1,0:T(8,128)S(1)}, bf16[128,1024]{1,0:T(8,128)(2,1)S(1)}) custom-call(s32[1]{0:T(128)} %bitcast.7.base_ref, s32[8]{0:T(128)S(1)} %copy-done.14, s32[1,128]{1,0:T(1,128)S(1)} %bitcast.39, bf16[32,1024]{1,0:T(8,128)(2,1)S(1)} %copy-done.9, bf16[8,1024]{1,0:T(8,128)(2,1)S(1)} %copy-done.10, f32[2,128,1024]{2,1,0:T(8,128)S(1)} %bitcast.36, ...), custom_call_target="tpu_custom_call" | custom-call | flops 268435456 | bytes 2097152 | tf_op jit(solution)/shard_map/prepare/pallas_call | solution.py:95
  27.7 0.7 collective-permute-done.6.rest_6_
  28.4 2.7 %two_filters.2 = (bf16[512,128]{1,0:T(8,128)(2,1)S(1)}, bf16[512,128]{1,0:T(8,128)(2,1)S(1)}) custom-call(s32[4]{0:T(128)S(1)} %pad_add_fusion.where_ref, f32[2,128]{1,0:T(2,128)S(1)} %bitcast.37, f32[2,4,512,128]{3,2,1,0:T(8,128)S(1)} %get-tuple-element.42.spectra_ref, bf16[512,256]{1,0:T(8,128)(2,1)S(1)} %copy-done.5, bf16[256,512]{1,0:T(8,128)(2,1)S(1)} %copy-done.7, ...), custom_call_target="tpu_custom_call" | custom-call | flops 536870912 | bytes 1048576 | tf_op jit(solution)/shard_map/two_filters/pallas_call | solution.py:275
  31.1 2.5 %collective-permute-start.7 = (bf16[512,128]{1,0:T(8,128)(2,1)S(1)}, bf16[512,128]{1,0:T(8,128)(2,1)S(1)}, u32[]{:S(2)}, u32[]{:S(2)}) collective-permute-start(bf16[512,128]{1,0:T(8,128)(2,1)S(1)} %get-tuple-element.52), channel_id=1, source_target_pairs={{0,4},{1,5},{2,6},{3,7},{4,0},{5,1},{6,2},{7,3},{8,12},{9,13},{10,... | collective-permute-start | bytes 393224 | tf_op jit(solution)/shard_map/ppermute | solution.py:44
  33.7 2.8 %copy-done.1 = bf16[1,1024,3072]{2,1,0:T(8,128)(2,1)S(1)} copy-done((bf16[1,1024,3072]{2,1,0:T(8,128)(2,1)S(1)}, bf16[1,1024,3072]{2,1,0:T(8,128)(2,1)}, u32[]{:S(2)}) %copy-start.1) | copy-done | bytes 6291480
  36.5 2.4 %gate_two.2 = (bf16[128,256]{1,0:T(8,128)(2,1)S(1)}, bf16[128,256]{1,0:T(8,128)(2,1)S(1)}, bf16[128,256]{1,0:T(8,128)(2,1)S(1)}, bf16[128,256]{1,0:T(8,128)(2,1)S(1)}) custom-call(s32[4]{0:T(128)S(1)} %broadcast_xor_fusion.table_ref, bf16[128,1024]{1,0:T(8,128)(2,1)S(1)} %get-tuple-element.53.normed_ref, bf16[1024,3072]{1,0:T(8,128)(2,1)S(1)} %bitcast.17, ...), custom_call_target="tpu_custom_call" | custom-call | flops 268435456 | bytes 2097152 | tf_op jit(solution)/shard_map/gate_two/pallas_call | solution.py:188
  38.9 1.6 %collective-permute-start.10 = (bf16[128,256]{1,0:T(8,128)(2,1)S(1)}, bf16[128,256]{1,0:T(8,128)(2,1)S(1)}, u32[]{:S(2)}, u32[]{:S(2)}) collective-permute-start(bf16[128,256]{1,0:T(8,128)(2,1)S(1)} %get-tuple-element.56), channel_id=1, source_target_pairs={{0,1},{1,0},{2,3},{3,2},{4,5},{5,4},{6,7},{7,6},{8,9},{9,8},{10,11... | collective-permute-start | bytes 196616 | tf_op jit(solution)/shard_map/ppermute | solution.py:44
  40.5 2.2 %collective-permute-start.8 = (bf16[128,256]{1,0:T(8,128)(2,1)S(1)}, bf16[128,256]{1,0:T(8,128)(2,1)S(1)}, u32[]{:S(2)}, u32[]{:S(2)}) collective-permute-start(bf16[128,256]{1,0:T(8,128)(2,1)S(1)} %get-tuple-element.54), channel_id=1, source_target_pairs={{0,3},{1,2},{2,1},{3,0},{4,7},{5,6},{6,5},{7,4},{8,11},{9,10},{10,... | collective-permute-start | bytes 196616 | tf_op jit(solution)/shard_map/ppermute | solution.py:44
  42.8 0.8 collective-permute-done.10.rest_2_
  43.6 2.2 %collective-permute-done.8.rest_0_ = bf16[128,256]{1,0:T(8,128)(2,1)S(1)} collective-permute-done((bf16[128,256]{1,0:T(8,128)(2,1)S(1)}, bf16[128,256]{1,0:T(8,128)(2,1)S(1)}, u32[]{:S(2)}, u32[]{:S(2)}) %collective-permute-start.8) | collective-permute-done | bytes 65568 | tf_op jit(solution)/shard_map/ppermute | solution.py:44
  45.7 1.3 %collective-permute-done.9.rest_1_ = bf16[128,256]{1,0:T(8,128)(2,1)S(1)} collective-permute-done((bf16[128,256]{1,0:T(8,128)(2,1)S(1)}, bf16[128,256]{1,0:T(8,128)(2,1)S(1)}, u32[]{:S(2)}, u32[]{:S(2)}) %collective-permute-start.9) | collective-permute-done | bytes 65568 | tf_op jit(solution)/shard_map/ppermute | solution.py:44
  47.0 0.6 second_gate.2
  47.7 1.0 collective-permute-start.11
  48.6 1.3 %collective-permute-start.12 = (bf16[128,256]{1,0:T(8,128)(2,1)S(1)}, bf16[128,256]{1,0:T(8,128)(2,1)S(1)}, u32[]{:S(2)}, u32[]{:S(2)}) collective-permute-start(bf16[128,256]{1,0:T(8,128)(2,1)S(1)} %get-tuple-element.59.refs_1_), channel_id=1, source_target_pairs={{0,2},{1,3},{2,0},{3,1},{4,6},{5,7},{6,4},{7,5},{8,10},{9,11},{10,... | collective-permute-start | bytes 196616 | tf_op jit(solution)/shard_map/ppermute | solution.py:44
  49.9 1.3 %collective-permute-start.13 = (bf16[128,256]{1,0:T(8,128)(2,1)S(1)}, bf16[128,256]{1,0:T(8,128)(2,1)S(1)}, u32[]{:S(2)}, u32[]{:S(2)}) collective-permute-start(bf16[128,256]{1,0:T(8,128)(2,1)S(1)} %get-tuple-element.60.refs_2_), channel_id=1, source_target_pairs={{0,1},{1,0},{2,3},{3,2},{4,5},{5,4},{6,7},{7,6},{8,9},{9,8},{10,11... | collective-permute-start | bytes 196616 | tf_op jit(solution)/shard_map/ppermute | solution.py:44
  51.2 1.7 %collective-permute-done.11.rest_0_ = bf16[128,256]{1,0:T(8,128)(2,1)S(1)} collective-permute-done((bf16[128,256]{1,0:T(8,128)(2,1)S(1)}, bf16[128,256]{1,0:T(8,128)(2,1)S(1)}, u32[]{:S(2)}, u32[]{:S(2)}) %collective-permute-start.11) | collective-permute-done | bytes 65568 | tf_op jit(solution)/shard_map/ppermute | solution.py:44
  52.9 1.3 %collective-permute-done.13.rest_2_ = bf16[128,256]{1,0:T(8,128)(2,1)S(1)} collective-permute-done((bf16[128,256]{1,0:T(8,128)(2,1)S(1)}, bf16[128,256]{1,0:T(8,128)(2,1)S(1)}, u32[]{:S(2)}, u32[]{:S(2)}) %collective-permute-start.13) | collective-permute-done | bytes 65568 | tf_op jit(solution)/shard_map/ppermute | solution.py:44
  54.2 1.0 exit_projection.2
  55.2 1.3 %collective-permute-start.14 = (bf16[128,1024]{1,0:T(8,128)(2,1)S(1)}, bf16[128,1024]{1,0:T(8,128)(2,1)S(1)}, u32[]{:S(2)}, u32[]{:S(2)}) collective-permute-start(bf16[128,1024]{1,0:T(8,128)(2,1)S(1)} %exit_projection.2), channel_id=1, source_target_pairs={{0,8},{8,16},{16,24},{1,9},{9,17},{17,25},{2,10},{10,18},{18,26},{... | collective-permute-start | bytes 786440 | tf_op jit(solution)/shard_map/ppermute | solution.py:421
  56.5 1.5 %collective-permute-start.29 = (bf16[2,128,1024]{2,1,0:T(8,128)(2,1)S(1)}, bf16[2,128,1024]{2,1,0:T(8,128)(2,1)S(1)}, u32[]{:S(2)}, u32[]{:S(2)}) collective-permute-start(bf16[2,128,1024]{2,1,0:T(8,128)(2,1)S(1)} %bitcast.31), channel_id=1, source_target_pairs={{0,3},{1,2},{2,1},{3,0},{4,7},{5,6},{6,5},{7,4},{8,11},{9,10},{10,... | collective-permute-start | bytes 1572872 | tf_op jit(solution)/shard_map/ppermute | solution.py:44
  58.0 1.3 %collective-permute-start.30 = (bf16[2,128,1024]{2,1,0:T(8,128)(2,1)S(1)}, bf16[2,128,1024]{2,1,0:T(8,128)(2,1)S(1)}, u32[]{:S(2)}, u32[]{:S(2)}) collective-permute-start(bf16[2,128,1024]{2,1,0:T(8,128)(2,1)S(1)} %bitcast.32), channel_id=1, source_target_pairs={{0,2},{1,3},{2,0},{3,1},{4,6},{5,7},{6,4},{7,5},{8,10},{9,11},{10,... | collective-permute-start | bytes 1572872 | tf_op jit(solution)/shard_map/ppermute | solution.py:44
  59.3 0.7 collective-permute-start.31
  60.1 4.7 %value_and_gate_one.3 = (bf16[128,256]{1,0:T(8,128)(2,1)S(1)}, bf16[128,256]{1,0:T(8,128)(2,1)S(1)}, bf16[128,256]{1,0:T(8,128)(2,1)S(1)}, bf16[128,256]{1,0:T(8...) custom-call(s32[9]{0:T(128)S(1)} %get-tuple-element.82.table_ref, ...), custom_call_target="tpu_custom_call" | custom-call | flops 536870912 | bytes 4194304 | tf_op jit(solution)/shard_map/value_and_gate_one/pallas_call | solution.py:169
  65.0 3.5 %collective-permute-start.16 = (bf16[128,256]{1,0:T(8,128)(2,1)S(1)}, bf16[128,256]{1,0:T(8,128)(2,1)S(1)}, u32[]{:S(2)}, u32[]{:S(2)}) collective-permute-start(bf16[128,256]{1,0:T(8,128)(2,1)S(1)} %get-tuple-element.64), channel_id=1, source_target_pairs={{0,5},{1,4},{2,7},{3,6},{4,1},{5,0},{6,3},{7,2},{8,13},{9,12},{10,... | collective-permute-start | bytes 196616 | tf_op jit(solution)/shard_map/ppermute | solution.py:44
  68.5 13.2 %collective-permute-done.15.rest_0_ = bf16[128,256]{1,0:T(8,128)(2,1)S(1)} collective-permute-done((bf16[128,256]{1,0:T(8,128)(2,1)S(1)}, bf16[128,256]{1,0:T(8,128)(2,1)S(1)}, u32[]{:S(2)}, u32[]{:S(2)}) %collective-permute-start.15) | collective-permute-done | bytes 65568 | tf_op jit(solution)/shard_map/ppermute | solution.py:44
  81.7 0.8 collective-permute-start.17
  82.5 0.6 collective-permute-done.16.rest_1_
  83.1 2.6 %collective-permute-start.18 = (bf16[128,256]{1,0:T(8,128)(2,1)S(1)}, bf16[128,256]{1,0:T(8,128)(2,1)S(1)}, u32[]{:S(2)}, u32[]{:S(2)}) collective-permute-start(bf16[128,256]{1,0:T(8,128)(2,1)S(1)} %get-tuple-element.66), channel_id=1, source_target_pairs={{0,7},{1,6},{2,5},{3,4},{4,3},{5,2},{6,1},{7,0},{8,15},{9,14},{10,... | collective-permute-start | bytes 196616 | tf_op jit(solution)/shard_map/ppermute | solution.py:44
  85.7 2.1 %collective-permute-done.17.rest_2_ = bf16[128,256]{1,0:T(8,128)(2,1)S(1)} collective-permute-done((bf16[128,256]{1,0:T(8,128)(2,1)S(1)}, bf16[128,256]{1,0:T(8,128)(2,1)S(1)}, u32[]{:S(2)}, u32[]{:S(2)}) %collective-permute-start.17) | collective-permute-done | bytes 65568 | tf_op jit(solution)/shard_map/ppermute | solution.py:44
  87.9 0.9 collective-permute-start.19
  88.8 1.3 %collective-permute-done.18.rest_3_ = bf16[128,256]{1,0:T(8,128)(2,1)S(1)} collective-permute-done((bf16[128,256]{1,0:T(8,128)(2,1)S(1)}, bf16[128,256]{1,0:T(8,128)(2,1)S(1)}, u32[]{:S(2)}, u32[]{:S(2)}) %collective-permute-start.18) | collective-permute-done | bytes 65568 | tf_op jit(solution)/shard_map/ppermute | solution.py:44
  90.1 2.7 %collective-permute-start.20 = (bf16[128,256]{1,0:T(8,128)(2,1)S(1)}, bf16[128,256]{1,0:T(8,128)(2,1)S(1)}, u32[]{:S(2)}, u32[]{:S(2)}) collective-permute-start(bf16[128,256]{1,0:T(8,128)(2,1)S(1)} %get-tuple-element.68), channel_id=1, source_target_pairs={{0,2},{1,3},{2,0},{3,1},{4,6},{5,7},{6,4},{7,5},{8,10},{9,11},{10,... | collective-permute-start | bytes 196616 | tf_op jit(solution)/shard_map/ppermute | solution.py:44
  92.8 0.7 collective-permute-done.19.rest_4_
  93.5 0.3 collective-permute-start.21
  93.8 2.4 %gate_two.3 = (bf16[128,256]{1,0:T(8,128)(2,1)S(1)}, bf16[128,256]{1,0:T(8,128)(2,1)S(1)}, bf16[128,256]{1,0:T(8,128)(2,1)S(1)}, bf16[128,256]{1,0:T(8,128)(2,1)S(1)}) custom-call(s32[4]{0:T(128)S(1)} %broadcast_xor_fusion.table_ref, bf16[128,1024]{1,0:T(8,128)(2,1)S(1)} %get-tuple-element.73.normed_ref, bf16[1024,3072]{1,0:T(8,128)(2,1)S(1)} %bitcast.23, ...), custom_call_target="tpu_custom_call" | custom-call | flops 268435456 | bytes 2097152 | tf_op jit(solution)/shard_map/gate_two/pallas_call | solution.py:188
  96.3 1.7 %collective-permute-start.23 = (bf16[128,256]{1,0:T(8,128)(2,1)S(1)}, bf16[128,256]{1,0:T(8,128)(2,1)S(1)}, u32[]{:S(2)}, u32[]{:S(2)}) collective-permute-start(bf16[128,256]{1,0:T(8,128)(2,1)S(1)} %get-tuple-element.74), channel_id=1, source_target_pairs={{0,3},{1,2},{2,1},{3,0},{4,7},{5,6},{6,5},{7,4},{8,11},{9,10},{10,... | collective-permute-start | bytes 196616 | tf_op jit(solution)/shard_map/ppermute | solution.py:44
  98.0 1.5 %collective-permute-start.24 = (bf16[128,256]{1,0:T(8,128)(2,1)S(1)}, bf16[128,256]{1,0:T(8,128)(2,1)S(1)}, u32[]{:S(2)}, u32[]{:S(2)}) collective-permute-start(bf16[128,256]{1,0:T(8,128)(2,1)S(1)} %get-tuple-element.75), channel_id=1, source_target_pairs={{0,2},{1,3},{2,0},{3,1},{4,6},{5,7},{6,4},{7,5},{8,10},{9,11},{10,... | collective-permute-start | bytes 196616 | tf_op jit(solution)/shard_map/ppermute | solution.py:44
  99.5 2.7 %two_filters.3 = (bf16[512,128]{1,0:T(8,128)(2,1)S(1)}, bf16[512,128]{1,0:T(8,128)(2,1)S(1)}) custom-call(s32[4]{0:T(128)S(1)} %pad_add_fusion.where_ref, f32[2,128]{1,0:T(2,128)S(1)} %bitcast.38, f32[2,4,512,128]{3,2,1,0:T(8,128)S(1)} %get-tuple-element.42.spectra_ref, bf16[512,256]{1,0:T(8,128)(2,1)S(1)} %copy-done.5, bf16[256,512]{1,0:T(8,128)(2,1)S(1)} %copy-done.7, ...), custom_call_target="tpu_custom_call" | custom-call | flops 536870912 | bytes 1048576 | tf_op jit(solution)/shard_map/two_filters/pallas_call | solution.py:275
  102.3 2.3 %collective-permute-start.22 = (bf16[512,128]{1,0:T(8,128)(2,1)S(1)}, bf16[512,128]{1,0:T(8,128)(2,1)S(1)}, u32[]{:S(2)}, u32[]{:S(2)}) collective-permute-start(bf16[512,128]{1,0:T(8,128)(2,1)S(1)} %get-tuple-element.72), channel_id=1, source_target_pairs={{0,4},{1,5},{2,6},{3,7},{4,0},{5,1},{6,2},{7,3},{8,12},{9,13},{10,... | collective-permute-start | bytes 393224 | tf_op jit(solution)/shard_map/ppermute | solution.py:44
  104.5 1.3 %collective-permute-start.25 = (bf16[128,256]{1,0:T(8,128)(2,1)S(1)}, bf16[128,256]{1,0:T(8,128)(2,1)S(1)}, u32[]{:S(2)}, u32[]{:S(2)}) collective-permute-start(bf16[128,256]{1,0:T(8,128)(2,1)S(1)} %get-tuple-element.76), channel_id=1, source_target_pairs={{0,1},{1,0},{2,3},{3,2},{4,5},{5,4},{6,7},{7,6},{8,9},{9,8},{10,11... | collective-permute-start | bytes 196616 | tf_op jit(solution)/shard_map/ppermute | solution.py:44
  105.9 2.9 %collective-permute-done.25.rest_2_ = bf16[128,256]{1,0:T(8,128)(2,1)S(1)} collective-permute-done((bf16[128,256]{1,0:T(8,128)(2,1)S(1)}, bf16[128,256]{1,0:T(8,128)(2,1)S(1)}, u32[]{:S(2)}, u32[]{:S(2)}) %collective-permute-start.25) | collective-permute-done | bytes 65568 | tf_op jit(solution)/shard_map/ppermute | solution.py:44
  108.8 2.6 %collective-permute-done.22.come_ref = bf16[512,128]{1,0:T(8,128)(2,1)S(1)} collective-permute-done((bf16[512,128]{1,0:T(8,128)(2,1)S(1)}, bf16[512,128]{1,0:T(8,128)(2,1)S(1)}, u32[]{:S(2)}, u32[]{:S(2)}) %collective-permute-start.22) | collective-permute-done | bytes 131104 | tf_op jit(solution)/shard_map/ppermute | solution.py:44
  111.4 0.6 second_gate.3
  112.0 0.5 gradient_away.1
  112.6 2.4 %collective-permute-start.26 = (bf16[128,256]{1,0:T(8,128)(2,1)S(1)}, bf16[128,256]{1,0:T(8,128)(2,1)S(1)}, u32[]{:S(2)}, u32[]{:S(2)}) collective-permute-start(bf16[128,256]{1,0:T(8,128)(2,1)S(1)} %get-tuple-element.78.refs_4_), channel_id=1, source_target_pairs={{0,3},{1,2},{2,1},{3,0},{4,7},{5,6},{6,5},{7,4},{8,11},{9,10},{10,... | collective-permute-start | bytes 196616 | tf_op jit(solution)/shard_map/ppermute | solution.py:44
  115.3 1.5 %collective-permute-start.28 = (bf16[128,256]{1,0:T(8,128)(2,1)S(1)}, bf16[128,256]{1,0:T(8,128)(2,1)S(1)}, u32[]{:S(2)}, u32[]{:S(2)}) collective-permute-start(bf16[128,256]{1,0:T(8,128)(2,1)S(1)} %get-tuple-element.80.refs_6_), channel_id=1, source_target_pairs={{0,1},{1,0},{2,3},{3,2},{4,5},{5,4},{6,7},{7,6},{8,9},{9,8},{10,11... | collective-permute-start | bytes 196616 | tf_op jit(solution)/shard_map/ppermute | solution.py:44
  116.8 0.5 gradient_mine.1
  117.3 2.5 %collective-permute-done.26.rest_0_ = bf16[128,256]{1,0:T(8,128)(2,1)S(1)} collective-permute-done((bf16[128,256]{1,0:T(8,128)(2,1)S(1)}, bf16[128,256]{1,0:T(8,128)(2,1)S(1)}, u32[]{:S(2)}, u32[]{:S(2)}) %collective-permute-start.26) | collective-permute-done | bytes 65568 | tf_op jit(solution)/shard_map/ppermute | solution.py:44
  119.8 0.7 collective-permute-done.27.rest_1_
  120.5 1.7 %exit_projection.3 = bf16[128,1024]{1,0:T(8,128)(2,1)} custom-call(s32[4]{0:T(128)S(1)} %pad_add_fusion.where_ref, bf16[128,1024]{1,0:T(8,128)(2,1)S(1)} %collective-permute-done.14.x_ref, bf16[128,1024]{1,0:T(8,128)(2,1)S(1)} %get-tuple-element.62.other_ref, bf16[1024,1024]{1,0:T(8,128)(2,1)S(1)} %bitcast.26, ...), custom_call_target="tpu_custom_call" | custom-call | flops 268435456 | bytes 2097152 | tf_op jit(solution)/shard_map/exit_projection/pallas_call | solution.py:332
  122.3 3.8 %collective-permute-done.32 = bf16[128,1024]{1,0:T(8,128)(2,1)S(1)} collective-permute-done((bf16[128,1024]{1,0:T(8,128)(2,1)S(1)}, bf16[128,1024]{1,0:T(8,128)(2,1)S(1)}, u32[]{:S(2)}, u32[]{:S(2)}) %collective-permute-start.32) | collective-permute-done | bytes 262176 | tf_op jit(solution)/shard_map/ppermute | solution.py:44
  126.0 0.9 add_bitcast_fusion
  (59 shorter events, 0.9 us)
Async XLA Ops:
  1.4 2.8 %copy-start = (bf16[1,1024,3072]{2,1,0:T(8,128)(2,1)S(1)}, bf16[1,1024,3072]{2,1,0:T(8,128)(2,1)}, u32[]{:S(2)}) copy-start(bf16[1,1024,3072]{2,1,0:T(8,128)(2,1)} %param.23) | copy-start | bytes 18874372
  4.2 0.9 copy-start.3
  5.1 0.7 copy-start.11
  5.8 20.4 %copy-start.5 = (bf16[512,256]{1,0:T(8,128)(2,1)S(1)}, bf16[512,256]{1,0:T(8,128)(2,1)}, u32[]{:S(2)}) copy-start(bf16[512,256]{1,0:T(8,128)(2,1)} %constant.47.clone.forward_ref) | copy-start | bytes 786436
  5.8 20.4 %copy-start.8 = (f32[1,2,128,1024]{3,2,1,0:T(8,128)S(1)}, f32[1,2,128,1024]{3,2,1,0:T(8,128)}, u32[]{:S(2)}) copy-start(f32[1,2,128,1024]{3,2,1,0:T(8,128)} %param.24) | copy-start | bytes 3145732
  5.8 20.4 %copy-start.9 = (bf16[32,1024]{1,0:T(8,128)(2,1)S(1)}, bf16[32,1024]{1,0:T(8,128)(2,1)}, u32[]{:S(2)}) copy-start(bf16[32,1024]{1,0:T(8,128)(2,1)} %amino_ref.1) | copy-start | bytes 196612
  5.8 20.4 %copy-start.10 = (bf16[8,1024]{1,0:T(8,128)(2,1)S(1)}, bf16[8,1024]{1,0:T(8,128)(2,1)}, u32[]{:S(2)}) copy-start(bf16[8,1024]{1,0:T(8,128)(2,1)} %polymer_ref.1) | copy-start | bytes 49156
  5.8 20.4 %copy-start.14 = (s32[8]{0:T(128)S(1)}, s32[8]{0:T(128)}, u32[]{:S(2)}) copy-start(s32[8]{0:T(128)} %sizes_ref.1) | copy-start | bytes 100
  5.8 20.4 %copy-start.15 = (s32[128]{0:T(128)S(1)}, s32[128]{0:T(128)}, u32[]{:S(2)}) copy-start(s32[128]{0:T(128)} %param.18) | copy-start | bytes 1540
  5.8 22.6 %copy-start.7 = (bf16[256,512]{1,0:T(8,128)(2,1)S(1)}, bf16[256,512]{1,0:T(8,128)(2,1)}, u32[]{:S(2)}) copy-start(bf16[256,512]{1,0:T(8,128)(2,1)} %constant.48.clone.backward_ref) | copy-start | bytes 786436
  5.9 22.6 %copy-start.13 = (f32[1,2,128]{2,1,0:T(2,128)S(1)}, f32[1,2,128]{2,1,0:T(2,128)}, u32[]{:S(2)}) copy-start(f32[1,2,128]{2,1,0:T(2,128)} %param.25) | copy-start | bytes 3076
  10.5 9.9 %collective-permute-start = (bf16[128,256]{1,0:T(8,128)(2,1)S(1)}, bf16[128,256]{1,0:T(8,128)(2,1)S(1)}, u32[]{:S(2)}, u32[]{:S(2)}) collective-permute-start(bf16[128,256]{1,0:T(8,128)(2,1)S(1)} %get-tuple-element.43), channel_id=1, source_target_pairs={{0,4},{1,5},{2,6},{3,7},{4,0},{5,1},{6,2},{7,3},{8,12},{9,13},{10,... | collective-permute-start | bytes 196616 | tf_op jit(solution)/shard_map/ppermute | solution.py:44
  14.6 9.3 %collective-permute-start.1 = (bf16[128,256]{1,0:T(8,128)(2,1)S(1)}, bf16[128,256]{1,0:T(8,128)(2,1)S(1)}, u32[]{:S(2)}, u32[]{:S(2)}) collective-permute-start(bf16[128,256]{1,0:T(8,128)(2,1)S(1)} %get-tuple-element.44), channel_id=1, source_target_pairs={{0,5},{1,4},{2,7},{3,6},{4,1},{5,0},{6,3},{7,2},{8,13},{9,12},{10,... | collective-permute-start | bytes 196616 | tf_op jit(solution)/shard_map/ppermute | solution.py:44
  15.9 11.8 %collective-permute-start.2 = (bf16[128,256]{1,0:T(8,128)(2,1)S(1)}, bf16[128,256]{1,0:T(8,128)(2,1)S(1)}, u32[]{:S(2)}, u32[]{:S(2)}) collective-permute-start(bf16[128,256]{1,0:T(8,128)(2,1)S(1)} %get-tuple-element.45), channel_id=1, source_target_pairs={{0,6},{1,7},{2,4},{3,5},{4,2},{5,3},{6,0},{7,1},{8,14},{9,15},{10,... | collective-permute-start | bytes 196616 | tf_op jit(solution)/shard_map/ppermute | solution.py:44
  19.5 8.2 %collective-permute-start.3 = (bf16[128,256]{1,0:T(8,128)(2,1)S(1)}, bf16[128,256]{1,0:T(8,128)(2,1)S(1)}, u32[]{:S(2)}, u32[]{:S(2)}) collective-permute-start(bf16[128,256]{1,0:T(8,128)(2,1)S(1)} %get-tuple-element.46), channel_id=1, source_target_pairs={{0,7},{1,6},{2,5},{3,4},{4,3},{5,2},{6,1},{7,0},{8,15},{9,14},{10,... | collective-permute-start | bytes 196616 | tf_op jit(solution)/shard_map/ppermute | solution.py:44
  19.5 8.2 %collective-permute-start.4 = (bf16[128,256]{1,0:T(8,128)(2,1)S(1)}, bf16[128,256]{1,0:T(8,128)(2,1)S(1)}, u32[]{:S(2)}, u32[]{:S(2)}) collective-permute-start(bf16[128,256]{1,0:T(8,128)(2,1)S(1)} %get-tuple-element.47), channel_id=1, source_target_pairs={{0,3},{1,2},{2,1},{3,0},{4,7},{5,6},{6,5},{7,4},{8,11},{9,10},{10,... | collective-permute-start | bytes 196616 | tf_op jit(solution)/shard_map/ppermute | solution.py:44
  20.4 7.3 %collective-permute-start.5 = (bf16[128,256]{1,0:T(8,128)(2,1)S(1)}, bf16[128,256]{1,0:T(8,128)(2,1)S(1)}, u32[]{:S(2)}, u32[]{:S(2)}) collective-permute-start(bf16[128,256]{1,0:T(8,128)(2,1)S(1)} %get-tuple-element.48), channel_id=1, source_target_pairs={{0,2},{1,3},{2,0},{3,1},{4,6},{5,7},{6,4},{7,5},{8,10},{9,11},{10,... | collective-permute-start | bytes 196616 | tf_op jit(solution)/shard_map/ppermute | solution.py:44
  23.9 4.5 %collective-permute-start.6 = (bf16[128,256]{1,0:T(8,128)(2,1)S(1)}, bf16[128,256]{1,0:T(8,128)(2,1)S(1)}, u32[]{:S(2)}, u32[]{:S(2)}) collective-permute-start(bf16[128,256]{1,0:T(8,128)(2,1)S(1)} %get-tuple-element.49), channel_id=1, source_target_pairs={{0,1},{1,0},{2,3},{3,2},{4,5},{5,4},{6,7},{7,6},{8,9},{9,8},{10,11... | collective-permute-start | bytes 196616 | tf_op jit(solution)/shard_map/ppermute | solution.py:44
  26.3 7.4 %copy-start.16 = (s32[4]{0:T(128)S(1)}, s32[4]{0:T(128)}, u32[]{:S(2)}) copy-start(s32[4]{0:T(128)} %constant.50.clone) | copy-start | bytes 52
  26.3 33.8 %slice-start = ((s8[6291456]{0:T(1024)(128)(4,1)}), s8[2097152]{0:T(1024)(128)(4,1)S(1)}, s32[]{:S(2)}) async-start(s8[6291456]{0:T(1024)(128)(4,1)} %bitcast.19), calls=%async_computation | async-start | bytes 4194304
  31.1 15.9 %collective-permute-start.7 = (bf16[512,128]{1,0:T(8,128)(2,1)S(1)}, bf16[512,128]{1,0:T(8,128)(2,1)S(1)}, u32[]{:S(2)}, u32[]{:S(2)}) collective-permute-start(bf16[512,128]{1,0:T(8,128)(2,1)S(1)} %get-tuple-element.52), channel_id=1, source_target_pairs={{0,4},{1,5},{2,6},{3,7},{4,0},{5,1},{6,2},{7,3},{8,12},{9,13},{10,... | collective-permute-start | bytes 393224 | tf_op jit(solution)/shard_map/ppermute | solution.py:44
  33.7 2.8 %copy-start.1 = (bf16[1,1024,3072]{2,1,0:T(8,128)(2,1)S(1)}, bf16[1,1024,3072]{2,1,0:T(8,128)(2,1)}, u32[]{:S(2)}) copy-start(bf16[1,1024,3072]{2,1,0:T(8,128)(2,1)} %param.23) | copy-start | bytes 18874372
  36.5 17.7 %copy-start.2 = (bf16[1,1024,1024]{2,1,0:T(8,128)(2,1)S(1)}, bf16[1,1024,1024]{2,1,0:T(8,128)(2,1)}, u32[]{:S(2)}) copy-start(bf16[1,1024,1024]{2,1,0:T(8,128)(2,1)} %param.26) | copy-start | bytes 6291460
  36.5 17.7 %copy-start.4 = (bf16[1,128,1024]{2,1,0:T(8,128)(2,1)S(1)}, bf16[1,128,1024]{2,1,0:T(8,128)(2,1)}, u32[]{:S(2)}) copy-start(bf16[1,128,1024]{2,1,0:T(8,128)(2,1)} %param.17) | copy-start | bytes 786436
  36.5 23.6 %slice-start.1 = ((s8[6291456]{0:T(1024)(128)(4,1)}), s8[4194304]{0:T(1024)(128)(4,1)S(1)}, s32[]{:S(2)}) async-start(s8[6291456]{0:T(1024)(128)(4,1)} %bitcast.19), calls=%async_computation.1 | async-start | bytes 8388608
  38.9 17.6 %copy-start.6 = (bf16[1,2,128,1024]{3,2,1,0:T(8,128)(2,1)S(1)}, bf16[1,2,128,1024]{3,2,1,0:T(8,128)(2,1)}, u32[]{:S(2)}) copy-start(bf16[1,2,128,1024]{3,2,1,0:T(8,128)(2,1)} %param.27) | copy-start | bytes 1572868
  38.9 21.1 %copy-start.12 = (f32[1,1024]{1,0:T(1,128)S(1)}, f32[1,1024]{1,0:T(1,128)}, u32[]{:S(2)}) copy-start(f32[1,1024]{1,0:T(1,128)} %gain_ref.3) | copy-start | bytes 12292
  38.9 4.6 %collective-permute-start.10 = (bf16[128,256]{1,0:T(8,128)(2,1)S(1)}, bf16[128,256]{1,0:T(8,128)(2,1)S(1)}, u32[]{:S(2)}, u32[]{:S(2)}) collective-permute-start(bf16[128,256]{1,0:T(8,128)(2,1)S(1)} %get-tuple-element.56), channel_id=1, source_target_pairs={{0,1},{1,0},{2,3},{3,2},{4,5},{5,4},{6,7},{7,6},{8,9},{9,8},{10,11... | collective-permute-start | bytes 196616 | tf_op jit(solution)/shard_map/ppermute | solution.py:44
  40.5 5.2 %collective-permute-start.8 = (bf16[128,256]{1,0:T(8,128)(2,1)S(1)}, bf16[128,256]{1,0:T(8,128)(2,1)S(1)}, u32[]{:S(2)}, u32[]{:S(2)}) collective-permute-start(bf16[128,256]{1,0:T(8,128)(2,1)S(1)} %get-tuple-element.54), channel_id=1, source_target_pairs={{0,3},{1,2},{2,1},{3,0},{4,7},{5,6},{6,5},{7,4},{8,11},{9,10},{10,... | collective-permute-start | bytes 196616 | tf_op jit(solution)/shard_map/ppermute | solution.py:44
  42.8 4.3 %collective-permute-start.9 = (bf16[128,256]{1,0:T(8,128)(2,1)S(1)}, bf16[128,256]{1,0:T(8,128)(2,1)S(1)}, u32[]{:S(2)}, u32[]{:S(2)}) collective-permute-start(bf16[128,256]{1,0:T(8,128)(2,1)S(1)} %get-tuple-element.55), channel_id=1, source_target_pairs={{0,2},{1,3},{2,0},{3,1},{4,6},{5,7},{6,4},{7,5},{8,10},{9,11},{10,... | collective-permute-start | bytes 196616 | tf_op jit(solution)/shard_map/ppermute | solution.py:44
  47.7 5.2 %collective-permute-start.11 = (bf16[128,256]{1,0:T(8,128)(2,1)S(1)}, bf16[128,256]{1,0:T(8,128)(2,1)S(1)}, u32[]{:S(2)}, u32[]{:S(2)}) collective-permute-start(bf16[128,256]{1,0:T(8,128)(2,1)S(1)} %get-tuple-element.58.refs_0_), channel_id=1, source_target_pairs={{0,3},{1,2},{2,1},{3,0},{4,7},{5,6},{6,5},{7,4},{8,11},{9,10},{10,... | collective-permute-start | bytes 196616 | tf_op jit(solution)/shard_map/ppermute | solution.py:44
  48.6 4.3 %collective-permute-start.12 = (bf16[128,256]{1,0:T(8,128)(2,1)S(1)}, bf16[128,256]{1,0:T(8,128)(2,1)S(1)}, u32[]{:S(2)}, u32[]{:S(2)}) collective-permute-start(bf16[128,256]{1,0:T(8,128)(2,1)S(1)} %get-tuple-element.59.refs_1_), channel_id=1, source_target_pairs={{0,2},{1,3},{2,0},{3,1},{4,6},{5,7},{6,4},{7,5},{8,10},{9,11},{10,... | collective-permute-start | bytes 196616 | tf_op jit(solution)/shard_map/ppermute | solution.py:44
  49.9 4.3 %collective-permute-start.13 = (bf16[128,256]{1,0:T(8,128)(2,1)S(1)}, bf16[128,256]{1,0:T(8,128)(2,1)S(1)}, u32[]{:S(2)}, u32[]{:S(2)}) collective-permute-start(bf16[128,256]{1,0:T(8,128)(2,1)S(1)} %get-tuple-element.60.refs_2_), channel_id=1, source_target_pairs={{0,1},{1,0},{2,3},{3,2},{4,5},{5,4},{6,7},{7,6},{8,9},{9,8},{10,11... | collective-permute-start | bytes 196616 | tf_op jit(solution)/shard_map/ppermute | solution.py:44
  55.2 4.9 %collective-permute-start.14 = (bf16[128,1024]{1,0:T(8,128)(2,1)S(1)}, bf16[128,1024]{1,0:T(8,128)(2,1)S(1)}, u32[]{:S(2)}, u32[]{:S(2)}) collective-permute-start(bf16[128,1024]{1,0:T(8,128)(2,1)S(1)} %exit_projection.2), channel_id=1, source_target_pairs={{0,8},{8,16},{16,24},{1,9},{9,17},{17,25},{2,10},{10,18},{18,26},{... | collective-permute-start | bytes 786440 | tf_op jit(solution)/shard_map/ppermute | solution.py:421
  56.5 55.5 %collective-permute-start.29 = (bf16[2,128,1024]{2,1,0:T(8,128)(2,1)S(1)}, bf16[2,128,1024]{2,1,0:T(8,128)(2,1)S(1)}, u32[]{:S(2)}, u32[]{:S(2)}) collective-permute-start(bf16[2,128,1024]{2,1,0:T(8,128)(2,1)S(1)} %bitcast.31), channel_id=1, source_target_pairs={{0,3},{1,2},{2,1},{3,0},{4,7},{5,6},{6,5},{7,4},{8,11},{9,10},{10,... | collective-permute-start | bytes 1572872 | tf_op jit(solution)/shard_map/ppermute | solution.py:44
  58.0 54.0 %collective-permute-start.30 = (bf16[2,128,1024]{2,1,0:T(8,128)(2,1)S(1)}, bf16[2,128,1024]{2,1,0:T(8,128)(2,1)S(1)}, u32[]{:S(2)}, u32[]{:S(2)}) collective-permute-start(bf16[2,128,1024]{2,1,0:T(8,128)(2,1)S(1)} %bitcast.32), channel_id=1, source_target_pairs={{0,2},{1,3},{2,0},{3,1},{4,6},{5,7},{6,4},{7,5},{8,10},{9,11},{10,... | collective-permute-start | bytes 1572872 | tf_op jit(solution)/shard_map/ppermute | solution.py:44
  59.3 52.7 %collective-permute-start.31 = (bf16[2,128,1024]{2,1,0:T(8,128)(2,1)S(1)}, bf16[2,128,1024]{2,1,0:T(8,128)(2,1)S(1)}, u32[]{:S(2)}, u32[]{:S(2)}) collective-permute-start(bf16[2,128,1024]{2,1,0:T(8,128)(2,1)S(1)} %bitcast.33), channel_id=1, source_target_pairs={{0,1},{1,0},{2,3},{3,2},{4,5},{5,4},{6,7},{7,6},{8,9},{9,8},{10,11... | collective-permute-start | bytes 1572872 | tf_op jit(solution)/shard_map/ppermute | solution.py:44
  64.8 17.0 %collective-permute-start.15 = (bf16[128,256]{1,0:T(8,128)(2,1)S(1)}, bf16[128,256]{1,0:T(8,128)(2,1)S(1)}, u32[]{:S(2)}, u32[]{:S(2)}) collective-permute-start(bf16[128,256]{1,0:T(8,128)(2,1)S(1)} %get-tuple-element.63), channel_id=1, source_target_pairs={{0,4},{1,5},{2,6},{3,7},{4,0},{5,1},{6,2},{7,3},{8,12},{9,13},{10,... | collective-permute-start | bytes 196616 | tf_op jit(solution)/shard_map/ppermute | solution.py:44
  65.0 18.1 %collective-permute-start.16 = (bf16[128,256]{1,0:T(8,128)(2,1)S(1)}, bf16[128,256]{1,0:T(8,128)(2,1)S(1)}, u32[]{:S(2)}, u32[]{:S(2)}) collective-permute-start(bf16[128,256]{1,0:T(8,128)(2,1)S(1)} %get-tuple-element.64), channel_id=1, source_target_pairs={{0,5},{1,4},{2,7},{3,6},{4,1},{5,0},{6,3},{7,2},{8,13},{9,12},{10,... | collective-permute-start | bytes 196616 | tf_op jit(solution)/shard_map/ppermute | solution.py:44
  81.7 6.2 %collective-permute-start.17 = (bf16[128,256]{1,0:T(8,128)(2,1)S(1)}, bf16[128,256]{1,0:T(8,128)(2,1)S(1)}, u32[]{:S(2)}, u32[]{:S(2)}) collective-permute-start(bf16[128,256]{1,0:T(8,128)(2,1)S(1)} %get-tuple-element.65), channel_id=1, source_target_pairs={{0,6},{1,7},{2,4},{3,5},{4,2},{5,3},{6,0},{7,1},{8,14},{9,15},{10,... | collective-permute-start | bytes 196616 | tf_op jit(solution)/shard_map/ppermute | solution.py:44
  83.1 7.0 %collective-permute-start.18 = (bf16[128,256]{1,0:T(8,128)(2,1)S(1)}, bf16[128,256]{1,0:T(8,128)(2,1)S(1)}, u32[]{:S(2)}, u32[]{:S(2)}) collective-permute-start(bf16[128,256]{1,0:T(8,128)(2,1)S(1)} %get-tuple-element.66), channel_id=1, source_target_pairs={{0,7},{1,6},{2,5},{3,4},{4,3},{5,2},{6,1},{7,0},{8,15},{9,14},{10,... | collective-permute-start | bytes 196616 | tf_op jit(solution)/shard_map/ppermute | solution.py:44
  87.9 5.6 %collective-permute-start.19 = (bf16[128,256]{1,0:T(8,128)(2,1)S(1)}, bf16[128,256]{1,0:T(8,128)(2,1)S(1)}, u32[]{:S(2)}, u32[]{:S(2)}) collective-permute-start(bf16[128,256]{1,0:T(8,128)(2,1)S(1)} %get-tuple-element.67), channel_id=1, source_target_pairs={{0,3},{1,2},{2,1},{3,0},{4,7},{5,6},{6,5},{7,4},{8,11},{9,10},{10,... | collective-permute-start | bytes 196616 | tf_op jit(solution)/shard_map/ppermute | solution.py:44
  90.1 6.2 %collective-permute-start.20 = (bf16[128,256]{1,0:T(8,128)(2,1)S(1)}, bf16[128,256]{1,0:T(8,128)(2,1)S(1)}, u32[]{:S(2)}, u32[]{:S(2)}) collective-permute-start(bf16[128,256]{1,0:T(8,128)(2,1)S(1)} %get-tuple-element.68), channel_id=1, source_target_pairs={{0,2},{1,3},{2,0},{3,1},{4,6},{5,7},{6,4},{7,5},{8,10},{9,11},{10,... | collective-permute-start | bytes 196616 | tf_op jit(solution)/shard_map/ppermute | solution.py:44
  93.5 4.5 %collective-permute-start.21 = (bf16[128,256]{1,0:T(8,128)(2,1)S(1)}, bf16[128,256]{1,0:T(8,128)(2,1)S(1)}, u32[]{:S(2)}, u32[]{:S(2)}) collective-permute-start(bf16[128,256]{1,0:T(8,128)(2,1)S(1)} %get-tuple-element.69), channel_id=1, source_target_pairs={{0,1},{1,0},{2,3},{3,2},{4,5},{5,4},{6,7},{7,6},{8,9},{9,8},{10,11... | collective-permute-start | bytes 196616 | tf_op jit(solution)/shard_map/ppermute | solution.py:44
  96.3 6.0 %collective-permute-start.23 = (bf16[128,256]{1,0:T(8,128)(2,1)S(1)}, bf16[128,256]{1,0:T(8,128)(2,1)S(1)}, u32[]{:S(2)}, u32[]{:S(2)}) collective-permute-start(bf16[128,256]{1,0:T(8,128)(2,1)S(1)} %get-tuple-element.74), channel_id=1, source_target_pairs={{0,3},{1,2},{2,1},{3,0},{4,7},{5,6},{6,5},{7,4},{8,11},{9,10},{10,... | collective-permute-start | bytes 196616 | tf_op jit(solution)/shard_map/ppermute | solution.py:44
  98.0 6.5 %collective-permute-start.24 = (bf16[128,256]{1,0:T(8,128)(2,1)S(1)}, bf16[128,256]{1,0:T(8,128)(2,1)S(1)}, u32[]{:S(2)}, u32[]{:S(2)}) collective-permute-start(bf16[128,256]{1,0:T(8,128)(2,1)S(1)} %get-tuple-element.75), channel_id=1, source_target_pairs={{0,2},{1,3},{2,0},{3,1},{4,6},{5,7},{6,4},{7,5},{8,10},{9,11},{10,... | collective-permute-start | bytes 196616 | tf_op jit(solution)/shard_map/ppermute | solution.py:44
  102.3 9.1 %collective-permute-start.22 = (bf16[512,128]{1,0:T(8,128)(2,1)S(1)}, bf16[512,128]{1,0:T(8,128)(2,1)S(1)}, u32[]{:S(2)}, u32[]{:S(2)}) collective-permute-start(bf16[512,128]{1,0:T(8,128)(2,1)S(1)} %get-tuple-element.72), channel_id=1, source_target_pairs={{0,4},{1,5},{2,6},{3,7},{4,0},{5,1},{6,2},{7,3},{8,12},{9,13},{10,... | collective-permute-start | bytes 393224 | tf_op jit(solution)/shard_map/ppermute | solution.py:44
  104.5 4.3 %collective-permute-start.25 = (bf16[128,256]{1,0:T(8,128)(2,1)S(1)}, bf16[128,256]{1,0:T(8,128)(2,1)S(1)}, u32[]{:S(2)}, u32[]{:S(2)}) collective-permute-start(bf16[128,256]{1,0:T(8,128)(2,1)S(1)} %get-tuple-element.76), channel_id=1, source_target_pairs={{0,1},{1,0},{2,3},{3,2},{4,5},{5,4},{6,7},{7,6},{8,9},{9,8},{10,11... | collective-permute-start | bytes 196616 | tf_op jit(solution)/shard_map/ppermute | solution.py:44
  112.5 13.5 %collective-permute-start.32 = (bf16[128,1024]{1,0:T(8,128)(2,1)S(1)}, bf16[128,1024]{1,0:T(8,128)(2,1)S(1)}, u32[]{:S(2)}, u32[]{:S(2)}) collective-permute-start(bf16[128,1024]{1,0:T(8,128)(2,1)S(1)} %gradient_away.1), channel_id=1, source_target_pairs={{0,4},{1,5},{2,6},{3,7},{4,0},{5,1},{6,2},{7,3},{8,12},{9,13},{10,... | collective-permute-start | bytes 786440 | tf_op jit(solution)/shard_map/ppermute | solution.py:44
  112.6 7.2 %collective-permute-start.26 = (bf16[128,256]{1,0:T(8,128)(2,1)S(1)}, bf16[128,256]{1,0:T(8,128)(2,1)S(1)}, u32[]{:S(2)}, u32[]{:S(2)}) collective-permute-start(bf16[128,256]{1,0:T(8,128)(2,1)S(1)} %get-tuple-element.78.refs_4_), channel_id=1, source_target_pairs={{0,3},{1,2},{2,1},{3,0},{4,7},{5,6},{6,5},{7,4},{8,11},{9,10},{10,... | collective-permute-start | bytes 196616 | tf_op jit(solution)/shard_map/ppermute | solution.py:44
  115.0 5.5 %collective-permute-start.27 = (bf16[128,256]{1,0:T(8,128)(2,1)S(1)}, bf16[128,256]{1,0:T(8,128)(2,1)S(1)}, u32[]{:S(2)}, u32[]{:S(2)}) collective-permute-start(bf16[128,256]{1,0:T(8,128)(2,1)S(1)} %get-tuple-element.79.refs_5_), channel_id=1, source_target_pairs={{0,2},{1,3},{2,0},{3,1},{4,6},{5,7},{6,4},{7,5},{8,10},{9,11},{10,... | collective-permute-start | bytes 196616 | tf_op jit(solution)/shard_map/ppermute | solution.py:44
  115.3 5.2 %collective-permute-start.28 = (bf16[128,256]{1,0:T(8,128)(2,1)S(1)}, bf16[128,256]{1,0:T(8,128)(2,1)S(1)}, u32[]{:S(2)}, u32[]{:S(2)}) collective-permute-start(bf16[128,256]{1,0:T(8,128)(2,1)S(1)} %get-tuple-element.80.refs_6_), channel_id=1, source_target_pairs={{0,1},{1,0},{2,3},{3,2},{4,5},{5,4},{6,7},{7,6},{8,9},{9,8},{10,11... | collective-permute-start | bytes 196616 | tf_op jit(solution)/shard_map/ppermute | solution.py:44
where the time goes:
time: 127 us
  starting transfers between devices  51.4 us (40%)
  waiting for transfers between devices  39.6 us (31%)
  Pallas kernels  26 us (20%)
  local copies, waits for them, and re-layouts  7.29 us (6%)
  other arithmetic  1.67 us (1%)
    ppermute x32, starting transfers between devices, exchange(): return lax.ppermute(value, 'seq', [(i, i ^ distance) for i in range(peers)])  50.1 us
    ppermute x32, waiting for transfers between devices, exchange(): return lax.ppermute(value, 'seq', [(i, i ^ distance) for i in range(peers)])  39.6 us
    pallas_call x2, Pallas kernels, project(): pl.pallas_call(project_kernel, out_shape=(piece,) * peers + (jax.ShapeDty...  9.33 us
    unnamed x38, local copies, waits for them, and re-layouts  7.29 us
    pallas_call x2, Pallas kernels, filtered(): pl.pallas_call(functools.partial(filter_kernel, order), out_shape=(out, o...  5.44 us
    pallas_call x2, Pallas kernels, project(): pl.pallas_call(second_project_kernel, out_shape=(piece,) * half, grid_spe...  4.89 us
    pallas_call x2, Pallas kernels, exit_projection(): pl.pallas_call(functools.partial(exit_kernel, order), out_shape=jax.Shape...  2.75 us
  transfers between devices with their start and end apart: 33, of which 17 were waited for; matrix products, arithmetic and copies ran while one was open for 0% of the time, Pallas kernels for 13%

commit v1 on v0

v1 whole, which is shorter than its diff:
```python
import functools
import math

import jax
import jax.numpy as jnp
import ml_dtypes
import numpy as np
from jax import lax
from jax.experimental import pallas as pl
from jax.experimental.pallas import tpu as pltpu
from jax.sharding import PartitionSpec as P

epsilon = 1e-06
lanes = 128
parts = 4
f32 = jnp.float32
bf16 = jnp.bfloat16


def dot(a, b, contract=(1, 0)):
    return lax.dot_general(
        a, b, (((contract[0],), (contract[1],)), ((), ())), preferred_element_type=f32
    )


def params(mib):
    return pltpu.CompilerParams(vmem_limit_bytes=mib << 20)


def whole():
    return pl.BlockSpec(memory_space=pltpu.VMEM)


def scalars():
    return pl.BlockSpec(memory_space=pltpu.SMEM)


def cost(flops, bytes_accessed):
    return pl.CostEstimate(flops=flops, bytes_accessed=bytes_accessed, transcendentals=0)


def exchange(value, distance):
    peers = lax.axis_size("seq")
    return lax.ppermute(value, "seq", [(i, i ^ distance) for i in range(peers)])


def odd_transform(size):
    bins = 2 * np.arange(size)[:, None] + 1
    angle = (bins * np.arange(size)[None, :] % (4 * size)) * (math.pi / (2 * size))
    rows = np.concatenate([np.cos(angle), -np.sin(angle)], axis=0)
    forward = rows.astype(ml_dtypes.bfloat16)
    backward = (rows.T / size).astype(ml_dtypes.bfloat16)
    return jnp.asarray(forward), jnp.asarray(backward)


def prepare_kernel(
    sizes_ref, ids_ref, amino_ref, polymer_ref, filters_ref, forward_ref, seeds_ref, spectra_ref, embedded_ref, *split_refs
):
    for step, split_ref in enumerate(split_refs):
        split_ref[...] = seeds_ref[step]
    size = forward_ref.shape[1]
    chunks = filters_ref.shape[2] // size
    sign = 1.0 - 2.0 * (lax.broadcasted_iota(jnp.int32, (size, 1), 0) & 1).astype(f32)
    for which in range(2):
        earlier = None
        for chunk in range(chunks):
            block = filters_ref[which, :, chunk * size : (chunk + 1) * size].astype(bf16)
            found = dot(forward_ref[...], block, (1, 1))
            real, imag = found[:size], found[size:]
            if earlier is None:
                spectra_ref[which, chunk, :size] = real
                spectra_ref[which, chunk, size:] = imag
            else:
                spectra_ref[which, chunk, :size] = real - sign * earlier[1]
                spectra_ref[which, chunk, size:] = imag + sign * earlier[0]
            earlier = (real, imag)
    count = ids_ref.shape[1]
    position = lax.axis_index("seq") * count + lax.broadcasted_iota(jnp.int32, (1, count), 1)
    chain = jnp.zeros((1, count), jnp.int32)
    end = jnp.int32(0)
    for j in range(sizes_ref.shape[0] - 1):
        end = end + sizes_ref[j]
        chain = chain + (position >= end).astype(jnp.int32)

    def rows_of(table_ref, index):
        entries = table_ref.shape[0]
        chosen = lax.broadcasted_iota(jnp.int32, (entries, count), 0) == index
        return dot(chosen.astype(f32).astype(bf16), table_ref[...], (0, 0))

    embedded_ref[...] = (rows_of(amino_ref, ids_ref[...]) + rows_of(polymer_ref, chain)).astype(bf16)


def prepare(sizes, ids, amino, polymer, filters, forward, seeds):
    size = forward.shape[1]
    channels, length = filters.shape[1:]
    chunks = length // size
    return pl.pallas_call(
        prepare_kernel,
        out_shape=(
            jax.ShapeDtypeStruct((2, chunks, 2 * size, channels), f32),
            jax.ShapeDtypeStruct((ids.shape[0], amino.shape[1]), bf16),
        )
        + (pltpu.HBM(seeds.shape[1:], bf16),) * seeds.shape[0],
        in_specs=[scalars()] + [whole()] * 6,
        out_specs=(whole(),) * (2 + seeds.shape[0]),
        compiler_params=params(12 if channels % lanes == 0 else 32),
        cost_estimate=cost(8 * size * length * channels, 16 * length * channels),
        name="prepare",
    )(sizes, ids[None], amino, polymer, filters, forward, seeds)


def normalized(values, gain):
    values = values.astype(f32)
    inverse_rms = lax.rsqrt(jnp.mean(values * values, axis=1, keepdims=True) + epsilon)
    return (values * inverse_rms * gain).astype(bf16)


def half_columns(kind, half, width):
    return pl.ds(pl.multiple_of((2 * kind + half) * width, width), width)


def block_columns(base, index, block):
    return pl.ds(pl.multiple_of(base + index * block, block), block)


def write_far(far, me, normed, columns, pieces, found_ref):
    group = len(far)
    block = pieces[0].shape[1] // 2
    for kind in range(2):
        found_ref[kind] = dot(normed, columns[kind]).astype(bf16)
    for distance, piece in zip(far, pieces):
        place = block_columns(0, (me ^ distance) & (group - 1), block)
        for kind in range(2):
            piece[:, kind * block : (kind + 1) * block] = found_ref[kind, :, place]


def far_stream_kernel(far, x_ref, gain_ref, weight_ref, *rest):
    pieces, rest = rest[: len(far)], rest[len(far) :]
    normed_ref, near_ref, values_ref, scale_ref, held_ref, found_ref, arrived = rest
    me = lax.axis_index("seq")
    width = held_ref.shape[2]
    half = me // len(far)
    moves = [(x_ref, values_ref), (gain_ref, scale_ref)]
    moves += [(weight_ref.at[:, half_columns(kind, 1 - half, width)], held_ref.at[kind]) for kind in range(2)]
    moves += [
        (weight_ref.at[:, half_columns(kind, half, width)], near_ref.at[:, pl.ds(kind * width, width)])
        for kind in range(2)
    ]
    moves += [(weight_ref.at[:, pl.ds(4 * width, 2 * width)], near_ref.at[:, pl.ds(2 * width, 2 * width)])]
    copies = [pltpu.make_async_copy(source, target, arrived.at[i]) for i, (source, target) in enumerate(moves)]
    for copy in copies:
        copy.start()
    copies[0].wait()
    copies[1].wait()
    normed_ref[...] = normalized(values_ref[...], scale_ref[...])
    copies[2].wait()
    copies[3].wait()
    write_far(far, me, normed_ref[...], [held_ref[0], held_ref[1]], pieces, found_ref)
    for copy in copies[4:]:
        copy.wait()


def far_kernel(far, choice_ref, x_ref, other_ref, gain_ref, weight_ref, *rest):
    *pieces, normed_ref, found_ref = rest
    me = lax.axis_index("seq")
    width = found_ref.shape[2]
    values = jnp.where(choice_ref[0] == 1, other_ref[...], x_ref[...])
    normed_ref[...] = normalized(values, gain_ref[...])
    columns = [weight_ref[:, half_columns(kind, 1 - me // len(far), width)] for kind in range(2)]
    write_far(far, me, normed_ref[...], columns, pieces, found_ref)


def near_kernel(near, compact, normed_ref, weight_ref, *rest):
    *pieces, found_ref = rest
    me = lax.axis_index("seq")
    group = len(near)
    block = pieces[0].shape[1] // 4
    width = group * block
    half = me // group
    for kind in range(2):
        columns = pl.ds(kind * width, width) if compact else half_columns(kind, half, width)
        found_ref[:, kind * width : (kind + 1) * width] = dot(normed_ref[...], weight_ref[:, columns]).astype(bf16)
    last = weight_ref.shape[1] - 2 * width
    found_ref[:, 2 * width :] = dot(normed_ref[...], weight_ref[:, last:]).astype(bf16)
    for distance, piece in zip(near, pieces):
        peer = me ^ distance
        places = [block_columns(kind * width, peer & (group - 1), block) for kind in range(2)]
        places += [block_columns(2 * width, index, block) for index in (peer, peer ^ group)]
        for k, place in enumerate(places):
            piece[:, k * block : (k + 1) * block] = found_ref[:, place]


def hold_kernel(count, *refs):
    sources, held, arrived = refs[:count], refs[count : 2 * count], refs[2 * count]
    copies = [pltpu.make_async_copy(sources[i], held[i], arrived.at[i]) for i in range(count)]
    for copy in copies:
        copy.start()
    for copy in copies:
        copy.wait()


def hold(arrays, name):
    count = len(arrays)
    return pl.pallas_call(
        functools.partial(hold_kernel, count),
        out_shape=tuple(pltpu.VMEM(array.shape, array.dtype) for array in arrays),
        in_specs=[pl.BlockSpec(memory_space=pl.ANY)] * count,
        out_specs=(whole(),) * count,
        scratch_shapes=[pltpu.SemaphoreType.DMA((count,))],
        compiler_params=params(48),
        cost_estimate=cost(0, 2 * sum(array.size for array in arrays)),
        name=name,
    )(*arrays)


def project(x, other, choice, gain, weight, far, near):
    rows, width = x.shape
    group = len(near)
    peers = 2 * group
    block = width // peers
    if block % lanes:
        me = lax.axis_index("seq")
        values = x if other is None else jnp.where(choice[0] == 1, other, x)
        cut = dot(normalized(values, gain), weight).astype(bf16).reshape(rows, 3, peers, block)

        def pick(distance, *kinds):
            return jnp.concatenate(
                [
                    lax.dynamic_index_in_dim(cut[:, kind], me ^ distance ^ flip, axis=1, keepdims=False)
                    for kind, flip in kinds
                ],
                axis=1,
            )

        first = [pick(d, (0, 0), (1, 0)) for d in far]
        return first, [pick(d, (0, 0), (1, 0), (2, 0), (2, group)) for d in near]
    work = cost(2 * rows * width * width, 2 * width * width)
    found = pltpu.VMEM((2, rows, width // 2), bf16)
    if other is None:
        outs = (pltpu.VMEM((rows, 2 * block), bf16),) * group
        outs += (pltpu.VMEM((rows, width), bf16), pltpu.VMEM((width, 2 * width), bf16))
        *first, normed, weight = pl.pallas_call(
            functools.partial(far_stream_kernel, far),
            out_shape=outs,
            in_specs=[pl.BlockSpec(memory_space=pl.ANY)] * 3,
            out_specs=(whole(),) * (group + 2),
            scratch_shapes=[
                pltpu.VMEM((rows, width), bf16),
                pltpu.VMEM((1, width), f32),
                pltpu.VMEM((2, width, width // 2), bf16),
                found,
                pltpu.SemaphoreType.DMA((7,)),
            ],
            compiler_params=params(56),
            cost_estimate=work,
            name="far_pieces_streamed",
        )(x, gain[None], weight)
    else:
        outs = (jax.ShapeDtypeStruct((rows, 2 * block), bf16),) * group
        outs += (jax.ShapeDtypeStruct((rows, width), bf16),)
        *first, normed = pl.pallas_call(
            functools.partial(far_kernel, far),
            out_shape=outs,
            in_specs=[scalars()] + [whole()] * 4,
            out_specs=(whole(),) * (group + 1),
            scratch_shapes=[found],
            compiler_params=params(10),
            cost_estimate=work,
            name="far_pieces",
        )(choice, x, other, gain[None], weight)
    second = pl.pallas_call(
        functools.partial(near_kernel, near, other is None),
        out_shape=(jax.ShapeDtypeStruct((rows, 4 * block), bf16),) * group,
        in_specs=[whole()] * 2,
        out_specs=(whole(),) * group,
        scratch_shapes=[pltpu.VMEM((rows, 2 * width), bf16)],
        compiler_params=params(10),
        cost_estimate=cost(4 * rows * width * width, 4 * width * width),
        name="near_pieces",
    )(normed, weight)
    return first, list(second)


def filter_kernel(order, skips_ref, spectra_ref, forward_ref, backward_ref, *rest):
    pieces = rest[: len(order)]
    keep_ref, send_ref, value_ref, gate_ref, gated_ref, found_ref, mixed_ref = rest[len(order) :]
    me = lax.axis_index("seq")
    half = me // (len(order) // 2)
    channels = spectra_ref.shape[3]
    chunks = spectra_ref.shape[1]
    size = forward_ref.shape[1]
    rows = pieces[0].shape[0]
    for distance, piece in zip(order, pieces):
        place = pl.ds(pl.multiple_of((me ^ distance) * rows, rows), rows)
        value_ref[place, :] = piece[:, :channels]
        gate_ref[place, :] = piece[:, channels : 2 * channels]

    def chunk_rows(j):
        return slice(j * size, (j + 1) * size)

    def chunk_lanes(j):
        return slice(j * channels, (j + 1) * channels)

    step = 16

    def convolve(signal, which):
        found_ref[...] = dot(forward_ref[...], signal)

        def multiply(at, _):
            real_rows = pl.ds(pl.multiple_of(at * step, step), step)
            imag_rows = pl.ds(pl.multiple_of(size + at * step, step), step)
            signal_real = [found_ref[real_rows, chunk_lanes(j)] for j in range(chunks)]
            signal_imag = [found_ref[imag_rows, chunk_lanes(j)] for j in range(chunks)]
            kernel_real = [spectra_ref[which, j, real_rows, :] for j in range(chunks)]
            kernel_imag = [spectra_ref[which, j, imag_rows, :] for j in range(chunks)]
            for i in range(chunks):
                real = sum(
                    signal_real[j] * kernel_real[i - j] - signal_imag[j] * kernel_imag[i - j] for j in range(i + 1)
                )
                imag = sum(
                    signal_real[j] * kernel_imag[i - j] + signal_imag[j] * kernel_real[i - j] for j in range(i + 1)
                )
                mixed_ref[real_rows, chunk_lanes(i)] = real.astype(bf16)
                mixed_ref[imag_rows, chunk_lanes(i)] = imag.astype(bf16)
            return 0

        lax.fori_loop(0, size // step, multiply, 0)
        return dot(backward_ref[...], mixed_ref[...])

    result = convolve(jnp.concatenate([value_ref[chunk_rows(j), :] for j in range(chunks)], axis=1), 0)
    for j in range(chunks):
        value = value_ref[chunk_rows(j), :].astype(f32)
        gate = gate_ref[chunk_rows(j), :].astype(f32)
        gated_ref[:, chunk_lanes(j)] = gate * (result[:, chunk_lanes(j)] + skips_ref[0:1, :] * value)
    result = convolve(gated_ref[...].astype(bf16), 1)
    final = [
        (result[:, chunk_lanes(j)] + skips_ref[1:2, :] * gated_ref[:, chunk_lanes(j)]).astype(bf16)
        for j in range(chunks)
    ]
    for j in range(chunks // 2):
        low, high = final[j], final[j + chunks // 2]
        keep_ref[chunk_rows(j), :] = jnp.where(half == 0, low, high)
        send_ref[chunk_rows(j), :] = jnp.where(half == 0, high, low)


def filtered(received, order, skips, spectra, forward, backward):
    chunks, _, channels = spectra.shape[1:]
    size = forward.shape[1]
    length = chunks * size
    out = jax.ShapeDtypeStruct((length // 2, channels), bf16)
    return pl.pallas_call(
        functools.partial(filter_kernel, order),
        out_shape=(out, out),
        in_specs=[whole()] * (4 + len(order)),
        out_specs=(whole(), whole()),
        scratch_shapes=[
            pltpu.VMEM((length, channels), bf16),
            pltpu.VMEM((length, channels), bf16),
            pltpu.VMEM((size, chunks * channels), f32),
            pltpu.VMEM((2 * size, chunks * channels), f32),
            pltpu.VMEM((2 * size, chunks * channels), bf16),
        ],
        compiler_params=params(12 if channels % lanes == 0 else 48),
        cost_estimate=cost(16 * size * length * channels, 8 * length * channels),
        name="two_filters",
    )(skips, spectra, forward, backward, *received)


def gate_kernel(order, keep_ref, come_ref, *rest):
    gates, (*outs, kept_ref) = rest[: len(order)], rest[len(order) :]
    mine = lax.rem(lax.axis_index("seq"), len(order))
    rows = gates[0].shape[0]
    channels = keep_ref.shape[1]
    for k, (distance, gate, out) in enumerate(zip(order, gates, outs)):
        place = pl.ds(pl.multiple_of((mine ^ distance) * rows, rows), rows)
        mixed = jnp.concatenate([keep_ref[place, :], come_ref[place, :]], axis=1)
        hyena = (gate[:, 2 * channels :].astype(f32) * mixed.astype(f32)).astype(bf16)
        out[...] = hyena
        kept_ref[k] = hyena


def gate_two(keep, come, gates, order, later):
    rows, width = gates[0].shape
    out = jax.ShapeDtypeStruct((rows, width // 2), bf16)
    kept = (len(gates), rows, width // 2)
    kept = pltpu.HBM(kept, bf16) if later else jax.ShapeDtypeStruct(kept, bf16)
    return pl.pallas_call(
        functools.partial(gate_kernel, order),
        out_shape=(out,) * len(gates) + (kept,),
        in_specs=[whole()] * (2 + len(gates)),
        out_specs=(whole(),) * (len(gates) + 1),
        compiler_params=params(8),
        cost_estimate=cost(keep.size * 2, keep.size * 8),
        name="second_gate",
    )(keep, come, *gates)


def exit_kernel(order, choice_ref, x_ref, other_ref, weight_ref, *rest):
    hyenas, out_ref = rest[: len(order)], rest[len(order)]
    me = lax.axis_index("seq")
    peers = 2 * len(order)
    block = weight_ref.shape[0] // peers
    values = jnp.where(choice_ref[0] == 1, other_ref[...], x_ref[...])
    total = values.astype(f32)
    for distance, hyena in zip(order, hyenas):
        near = pl.ds(pl.multiple_of((me ^ distance) * block, block), block)
        far = pl.ds(pl.multiple_of((me ^ distance ^ len(order)) * block, block), block)
        total += dot(hyena[...], jnp.concatenate([weight_ref[near, :], weight_ref[far, :]], axis=0))
    out_ref[...] = total.astype(bf16)


def exit_projection(choice, x, other, weight, hyenas, order):
    return pl.pallas_call(
        functools.partial(exit_kernel, order),
        out_shape=jax.ShapeDtypeStruct(x.shape, bf16),
        in_specs=[scalars()] + [whole()] * (3 + len(hyenas)),
        out_specs=whole(),
        compiler_params=params(12),
        cost_estimate=cost(2 * x.size * weight.shape[0], 2 * weight.size),
        name="exit_projection",
    )(choice, x, other, weight, *hyenas)


def gradient_kernel(side, first_ref, second_ref, *refs):
    *seeds, out_ref = refs
    block = out_ref.shape[0]
    columns = slice(side * block, (side + 1) * block)
    total = jnp.zeros(out_ref.shape, f32)
    count = len(seeds) // 2
    for k in range(count):
        hyenas = jnp.concatenate([first_ref[k, :, columns], second_ref[k, :, columns]], axis=0)
        total += dot(hyenas, jnp.concatenate([seeds[k][...], seeds[count + k][...]], axis=0), (0, 0))
    out_ref[...] = total.astype(out_ref.dtype)


def gradient(first, second, seeds, side, dtype, name):
    count, rows, both = first.shape
    width = seeds[0].shape[1]
    return pl.pallas_call(
        functools.partial(gradient_kernel, side),
        out_shape=jax.ShapeDtypeStruct((both // 2, width), dtype),
        in_specs=[whole()] * (2 + 2 * count),
        out_specs=whole(),
        compiler_params=params(10),
        cost_estimate=cost(2 * count * rows * both * width, 4 * count * width * rows),
        name=name,
    )(first, second, *seeds)


def local(
    resident_microbatch,
    upcoming_amino_ids,
    upcoming_polymer_sizes,
    amino_acid_vectors,
    polymer_vectors,
    normalizer_scaling,
    entry_projection_matrix,
    convolution_kernels_long,
    convolution_skip_coefficients,
    exit_projection_matrix,
    adjoint_seeds,
):
    peers = lax.axis_size("seq")
    sections = lax.axis_size("section")
    group = peers // 2
    far = tuple(range(group, peers))
    near = tuple(range(group - 1, -1, -1))
    never = jnp.zeros((1,), jnp.int32)
    first_section = (lax.axis_index("section") == 0).astype(jnp.int32)[None]

    filters = convolution_kernels_long[0]
    size = filters.shape[2] // parts
    forward, backward = odd_transform(size)
    spectra, embedded, *own_seeds = prepare(
        upcoming_polymer_sizes,
        upcoming_amino_ids,
        amino_acid_vectors,
        polymer_vectors,
        filters,
        forward,
        adjoint_seeds[0],
    )
    gain, weight_in, weight_out = normalizer_scaling[0], entry_projection_matrix[0], exit_projection_matrix[0]
    skips = convolution_skip_coefficients[0]

    width_of_block = exit_projection_matrix.shape[1] // peers

    aligned = width_of_block % lanes == 0

    def tie(values, *others):
        return lax.optimization_barrier((values, others))[0]

    def layer(x, other, choice, weight, beside):
        far_pieces, near_pieces = project(x, other, choice, gain, weight, far, near)
        come = [exchange(v, d) for v, d in zip(far_pieces, far)]
        come += [exchange(v, d) if d else v for v, d in zip(near_pieces, near)]
        beside = beside(come)
        keep, send = filtered(come, far + near, skips, spectra, forward, backward)
        kept = beside(send)
        swapped, kept = lax.optimization_barrier((exchange(send, group), kept))
        *hyenas, stacked = gate_two(keep, swapped, come[group:], near, choice is never)
        home = [exchange(v, d) if d else v for v, d in zip(hyenas, near)]
        return send, home, stacked, kept

    seeds = {(step, 0): own for step, own in enumerate(own_seeds)}

    def spread(wanted, *earlier):
        for step, d in wanted:
            seeds[step, d] = exchange(tie(seeds[step, d & (d - 1)], *earlier), d & -d)

    resident = resident_microbatch[0]
    send, home, first_hyenas, _ = layer(resident, None, never, weight_in, lambda come: lambda send: send)
    spread([(0, 1)], send)
    home, seeds[0, 1] = lax.optimization_barrier((home, seeds[0, 1]))
    spread([(1, 1)], first_hyenas)
    first_out = exit_projection(never, resident, resident, weight_out, home, near)
    handed = lax.ppermute(first_out, "section", [(i, i + 1) for i in range(sections - 1)])
    weight_again = tie(weight_in, first_out)
    if aligned:
        weight_again = hold([weight_again], "hold_entry")[0]
    handed, seeds[1, 1], weight_again = lax.optimization_barrier((handed, seeds[1, 1], weight_again))
    spread([(step, d) for step in range(2) for d in range(2, group, 2)], home)

    def second_beside(come):
        spread([(step, d) for step in range(2) for d in range(3, group, 2)], come)

        def held(send):
            early = [weight_out, first_hyenas] + [seeds[step, d] for step in range(2) for d in near if d % 2 == 0 or d == 1]
            return hold(tie(early, send), "hold_exit") if aligned else early

        return held

    send, home, second_hyenas, kept = layer(handed, embedded, first_section, weight_again, second_beside)
    weight_again, first_hyenas, *early = kept
    seeds = [early.pop(0) if d % 2 == 0 or d == 1 else seeds[step, d] for step in range(2) for d in near]
    away = gradient(first_hyenas, second_hyenas, seeds, 1, bf16, "gradient_away")
    mine = gradient(first_hyenas, second_hyenas, seeds, 0, f32, "gradient_mine")
    passed = exit_projection(first_section, handed, embedded, weight_again, home, near)
    out_grad = mine + exchange(away, group).astype(f32)
    return (passed[None], out_grad[None])


def solution(mesh):
    placed = (
        P("section", "seq", None),
        P("seq"),
        P(),
        P(),
        P(),
        P("section", None),
        P("section", None, None),
        P("section", None, "seq", None),
        P("section", None, "seq"),
        P("section", None, None),
        P("section", None, "seq", None),
    )
    return jax.shard_map(
        local,
        mesh=mesh,
        in_specs=placed,
        out_specs=(P("section", "seq", None), P("section", "seq", None)),
        check_vma=False,
    )
```

time: 127 us -> 102 us (0.80)
  starting transfers between devices: 51.4 us -> 42.6 us
  local copies, waits for them, and re-layouts: 7.29 us -> 0.07 us
  Pallas kernels: 26 us -> 20.3 us
  waiting for transfers between devices: 39.6 us -> 36.8 us
    ppermute x32 -> x29, starting transfers between devices: 50.1 us -> 41.3 us  [exchange(): return lax.ppermute(value, 'seq', [(i, i ^ distance) for i in range(peers)])]
    unnamed x38 -> x30, local copies, waits for them, and re-layouts: 7.29 us -> 0.07 us
    pallas_call x8 -> x10, Pallas kernels: 16.4 us -> 12.1 us  [the longest x2 4.77 us: hold(): pl.pallas_call(functools.partial(hold_kernel, count), out_shape=tuple((pl...]
    ppermute x32 -> x29, waiting for transfers between devices: 39.6 us -> 36.8 us  [exchange(): return lax.ppermute(value, 'seq', [(i, i ^ distance) for i in range(peers)])]
  transfers between devices with their start and end apart: 33 -> 30, of which waited for: 17 -> 12; matrix products, arithmetic and copies ran while one was open for 0% -> 0% of each run, Pallas kernels for 13% -> 14%
where the time goes in v1:
time: 102 us
  starting transfers between devices  42.6 us (42%)
  waiting for transfers between devices  36.8 us (36%)
  Pallas kernels  20.3 us (20%)
    ppermute x29, starting transfers between devices, exchange(): return lax.ppermute(value, 'seq', [(i, i ^ distance) for i in range(peers)])  41.3 us
    ppermute x29, waiting for transfers between devices, exchange(): return lax.ppermute(value, 'seq', [(i, i ^ distance) for i in range(peers)])  36.8 us
    pallas_call x2, Pallas kernels, hold(): pl.pallas_call(functools.partial(hold_kernel, count), out_shape=tuple((pl...  4.77 us
    pallas_call x2, Pallas kernels, filtered(): pl.pallas_call(functools.partial(filter_kernel, order), out_shape=(out, o...  4.35 us
    pallas_call x1, Pallas kernels, project(): pl.pallas_call(functools.partial(far_stream_kernel, far), out_shape=outs,...  3.13 us
    pallas_call x1, Pallas kernels, prepare(): pl.pallas_call(prepare_kernel, out_shape=(jax.ShapeDtypeStruct((2, chunks...  2.12 us
  transfers between devices with their start and end apart: 30, of which 12 were waited for; matrix products, arithmetic and copies ran while one was open for 0% of the time, Pallas kernels for 14%

profile of v1, /device:TPU:0, one launch (start us, length us, event | category | flops | bytes accessed | tf_op | source)
XLA Modules:
  0.0 101.6 jit_solution(11731010914289657337)
XLA Ops:
  0.6 0.0 copy-start.1
  0.7 3.1 %far_pieces_streamed.1 = (bf16[128,256]{1,0:T(8,128)(2,1)S(1)}, bf16[128,256]{1,0:T(8,128)(2,1)S(1)}, bf16[128,256]{1,0:T(8,128)(2,1)S(1)}, bf16[128,256]{1,0:T(...) custom-call(bf16[128,1024]{1,0:T(8,128)(2,1)} %bitcast.13, f32[1,1024]{1,0:T(1,128)} %gain_ref.3, ...), custom_call_target="tpu_custom_call" | custom-call | flops 268435456 | bytes 2097152 | tf_op jit(solution)/shard_map/far_pieces_streamed/pallas_call | solution.py:242
  3.8 0.0 copy-start.4
  3.8 0.0 copy-start.3
  3.9 0.0 copy-start.12
  3.9 4.1 %collective-permute-start = (bf16[128,256]{1,0:T(8,128)(2,1)S(1)}, bf16[128,256]{1,0:T(8,128)(2,1)S(1)}, u32[]{:S(2)}, u32[]{:S(2)}) collective-permute-start(bf16[128,256]{1,0:T(8,128)(2,1)S(1)} %get-tuple-element.81), channel_id=1, source_target_pairs={{0,4},{1,5},{2,6},{3,7},{4,0},{5,1},{6,2},{7,3},{8,12},{9,13},{10,... | collective-permute-start | bytes 196616 | tf_op jit(solution)/shard_map/ppermute | solution.py:44
  8.0 1.3 %collective-permute-start.1 = (bf16[128,256]{1,0:T(8,128)(2,1)S(1)}, bf16[128,256]{1,0:T(8,128)(2,1)S(1)}, u32[]{:S(2)}, u32[]{:S(2)}) collective-permute-start(bf16[128,256]{1,0:T(8,128)(2,1)S(1)} %get-tuple-element.82), channel_id=1, source_target_pairs={{0,5},{1,4},{2,7},{3,6},{4,1},{5,0},{6,3},{7,2},{8,13},{9,12},{10,... | collective-permute-start | bytes 196616 | tf_op jit(solution)/shard_map/ppermute | solution.py:44
  9.2 0.9 near_pieces.2
  10.2 1.6 %collective-permute-start.4 = (bf16[128,512]{1,0:T(8,128)(2,1)S(1)}, bf16[128,512]{1,0:T(8,128)(2,1)S(1)}, u32[]{:S(2)}, u32[]{:S(2)}) collective-permute-start(bf16[128,512]{1,0:T(8,128)(2,1)S(1)} %get-tuple-element.87), channel_id=1, source_target_pairs={{0,3},{1,2},{2,1},{3,0},{4,7},{5,6},{6,5},{7,4},{8,11},{9,10},{10,... | collective-permute-start | bytes 393224 | tf_op jit(solution)/shard_map/ppermute | solution.py:44
  11.8 0.2 collective-permute-start.5
  12.0 1.7 %collective-permute-start.6 = (bf16[128,512]{1,0:T(8,128)(2,1)S(1)}, bf16[128,512]{1,0:T(8,128)(2,1)S(1)}, u32[]{:S(2)}, u32[]{:S(2)}) collective-permute-start(bf16[128,512]{1,0:T(8,128)(2,1)S(1)} %get-tuple-element.89), channel_id=1, source_target_pairs={{0,1},{1,0},{2,3},{3,2},{4,5},{5,4},{6,7},{7,6},{8,9},{9,8},{10,11... | collective-permute-start | bytes 393224 | tf_op jit(solution)/shard_map/ppermute | solution.py:44
  13.7 0.0 collective-permute-done.rest_0_
  13.7 3.6 %collective-permute-start.2 = (bf16[128,256]{1,0:T(8,128)(2,1)S(1)}, bf16[128,256]{1,0:T(8,128)(2,1)S(1)}, u32[]{:S(2)}, u32[]{:S(2)}) collective-permute-start(bf16[128,256]{1,0:T(8,128)(2,1)S(1)} %get-tuple-element.83), channel_id=1, source_target_pairs={{0,6},{1,7},{2,4},{3,5},{4,2},{5,3},{6,0},{7,1},{8,14},{9,15},{10,... | collective-permute-start | bytes 196616 | tf_op jit(solution)/shard_map/ppermute | solution.py:44
  17.3 1.5 %collective-permute-start.3 = (bf16[128,256]{1,0:T(8,128)(2,1)S(1)}, bf16[128,256]{1,0:T(8,128)(2,1)S(1)}, u32[]{:S(2)}, u32[]{:S(2)}) collective-permute-start(bf16[128,256]{1,0:T(8,128)(2,1)S(1)} %get-tuple-element.84), channel_id=1, source_target_pairs={{0,7},{1,6},{2,5},{3,4},{4,3},{5,2},{6,1},{7,0},{8,15},{9,14},{10,... | collective-permute-start | bytes 196616 | tf_op jit(solution)/shard_map/ppermute | solution.py:44
  18.9 2.1 %prepare.1 = (f32[2,4,512,128]{3,2,1,0:T(8,128)S(1)}, bf16[128,1024]{1,0:T(8,128)(2,1)S(1)}, bf16[128,1024]{1,0:T(8,128)(2,1)}, bf16[128,1024]{1,0:T(8,128)(2,1)}) custom-call(s32[8]{0:T(128)S(1)} %copy-done.13, s32[1,128]{1,0:T(1,128)S(1)} %bitcast.20, bf16[32,1024]{1,0:T(8,128)(2,1)S(1)} %copy-done.9, bf16[8,1024]{1,0:T(8,128)(2,1)S(1)} %copy-done.10, ...), custom_call_target="tpu_custom_call" | custom-call | flops 268435456 | bytes 2097152 | tf_op jit(solution)/shard_map/prepare/pallas_call | solution.py:97
  21.1 1.2 %collective-permute-done.2.rest_2_ = bf16[128,256]{1,0:T(8,128)(2,1)S(1)} collective-permute-done((bf16[128,256]{1,0:T(8,128)(2,1)S(1)}, bf16[128,256]{1,0:T(8,128)(2,1)S(1)}, u32[]{:S(2)}, u32[]{:S(2)}) %collective-permute-start.2) | collective-permute-done | bytes 65568 | tf_op jit(solution)/shard_map/ppermute | solution.py:44
  22.2 2.1 %collective-permute-done.3.rest_3_ = bf16[128,256]{1,0:T(8,128)(2,1)S(1)} collective-permute-done((bf16[128,256]{1,0:T(8,128)(2,1)S(1)}, bf16[128,256]{1,0:T(8,128)(2,1)S(1)}, u32[]{:S(2)}, u32[]{:S(2)}) %collective-permute-start.3) | collective-permute-done | bytes 65568 | tf_op jit(solution)/shard_map/ppermute | solution.py:44
  24.3 2.2 %two_filters.2 = (bf16[512,128]{1,0:T(8,128)(2,1)S(1)}, bf16[512,128]{1,0:T(8,128)(2,1)S(1)}) custom-call(f32[2,128]{1,0:T(2,128)S(1)} %bitcast.18, f32[2,4,512,128]{3,2,1,0:T(8,128)S(1)} %get-tuple-element.80.spectra_ref, bf16[512,256]{1,0:T(8,128)(2,1)S(1)} %copy-done.1, bf16[256,512]{1,0:T(8,128)(2,1)S(1)} %copy-done.3, ...), custom_call_target="tpu_custom_call" | custom-call | flops 536870912 | bytes 1048576 | tf_op jit(solution)/shard_map/two_filters/pallas_call | solution.py:351
  26.5 0.8 collective-permute-start.11
  27.3 0.7 collective-permute-start.7
  28.1 7.0 %collective-permute-done.7.come_ref = bf16[512,128]{1,0:T(8,128)(2,1)S(1)} collective-permute-done((bf16[512,128]{1,0:T(8,128)(2,1)S(1)}, bf16[512,128]{1,0:T(8,128)(2,1)S(1)}, u32[]{:S(2)}, u32[]{:S(2)}) %collective-permute-start.7) | collective-permute-done | bytes 131104 | tf_op jit(solution)/shard_map/ppermute | solution.py:44
  35.0 0.8 second_gate.2
  35.8 2.2 %collective-permute-start.9 = (bf16[128,256]{1,0:T(8,128)(2,1)S(1)}, bf16[128,256]{1,0:T(8,128)(2,1)S(1)}, u32[]{:S(2)}, u32[]{:S(2)}) collective-permute-start(bf16[128,256]{1,0:T(8,128)(2,1)S(1)} %get-tuple-element.95), channel_id=1, source_target_pairs={{0,2},{1,3},{2,0},{3,1},{4,6},{5,7},{6,4},{7,5},{8,10},{9,11},{10,... | collective-permute-start | bytes 196616 | tf_op jit(solution)/shard_map/ppermute | solution.py:44
  38.0 1.3 %collective-permute-start.10 = (bf16[128,256]{1,0:T(8,128)(2,1)S(1)}, bf16[128,256]{1,0:T(8,128)(2,1)S(1)}, u32[]{:S(2)}, u32[]{:S(2)}) collective-permute-start(bf16[128,256]{1,0:T(8,128)(2,1)S(1)} %get-tuple-element.96), channel_id=1, source_target_pairs={{0,1},{1,0},{2,3},{3,2},{4,5},{5,4},{6,7},{7,6},{8,9},{9,8},{10,11... | collective-permute-start | bytes 196616 | tf_op jit(solution)/shard_map/ppermute | solution.py:44
  39.3 0.7 collective-permute-start.13
  40.0 1.1 %collective-permute-done.8.rest_0_ = bf16[128,256]{1,0:T(8,128)(2,1)S(1)} collective-permute-done((bf16[128,256]{1,0:T(8,128)(2,1)S(1)}, bf16[128,256]{1,0:T(8,128)(2,1)S(1)}, u32[]{:S(2)}, u32[]{:S(2)}) %collective-permute-start.8) | collective-permute-done | bytes 65568 | tf_op jit(solution)/shard_map/ppermute | solution.py:44
  41.1 1.9 %collective-permute-done.10.rest_2_ = bf16[128,256]{1,0:T(8,128)(2,1)S(1)} collective-permute-done((bf16[128,256]{1,0:T(8,128)(2,1)S(1)}, bf16[128,256]{1,0:T(8,128)(2,1)S(1)}, u32[]{:S(2)}, u32[]{:S(2)}) %collective-permute-start.10) | collective-permute-done | bytes 65568 | tf_op jit(solution)/shard_map/ppermute | solution.py:44
  43.0 0.0 collective-permute-done.11.refs_3_
  43.1 0.5 exit_projection.2
  43.6 1.3 %collective-permute-start.12 = (bf16[128,1024]{1,0:T(8,128)(2,1)S(1)}, bf16[128,1024]{1,0:T(8,128)(2,1)S(1)}, u32[]{:S(2)}, u32[]{:S(2)}) collective-permute-start(bf16[128,1024]{1,0:T(8,128)(2,1)S(1)} %exit_projection.2), channel_id=1, source_target_pairs={{0,8},{8,16},{16,24},{1,9},{9,17},{17,25},{2,10},{10,18},{18,26},{... | collective-permute-start | bytes 786440 | tf_op jit(solution)/shard_map/ppermute | solution.py:517
  44.9 0.1 collective-permute-start.22
  45.0 2.0 %collective-permute-start.23 = (bf16[128,1024]{1,0:T(8,128)(2,1)}, bf16[128,1024]{1,0:T(8,128)(2,1)}, u32[]{:S(2)}, u32[]{:S(2)}) collective-permute-start(bf16[128,1024]{1,0:T(8,128)(2,1)} %get-tuple-element.132.refs_7_), channel_id=1, source_target_pairs={{0,2},{1,3},{2,0},{3,1},{4,6},{5,7},{6,4},{7,5},{8,10},{9,11},{10,... | collective-permute-start | bytes 786440 | tf_op jit(solution)/shard_map/ppermute | solution.py:44
  47.0 2.8 %hold_entry.1.weight_ref = bf16[1024,3072]{1,0:T(8,128)(2,1)S(1)} custom-call(bf16[1024,3072]{1,0:T(8,128)(2,1)} %bitcast.22), custom_call_target="tpu_custom_call" | custom-call | bytes 6291456 | tf_op jit(solution)/shard_map/hold_entry/pallas_call | solution.py:204
  49.8 0.0 collective-permute-done.13.refs_6_
  49.8 0.6 far_pieces.1
  50.4 1.3 %collective-permute-start.14 = (bf16[128,256]{1,0:T(8,128)(2,1)S(1)}, bf16[128,256]{1,0:T(8,128)(2,1)S(1)}, u32[]{:S(2)}, u32[]{:S(2)}) collective-permute-start(bf16[128,256]{1,0:T(8,128)(2,1)S(1)} %get-tuple-element.111), channel_id=1, source_target_pairs={{0,4},{1,5},{2,6},{3,7},{4,0},{5,1},{6,2},{7,3},{8,12},{9,13},{10,... | collective-permute-start | bytes 196616 | tf_op jit(solution)/shard_map/ppermute | solution.py:44
  51.7 2.4 %collective-permute-start.15 = (bf16[128,256]{1,0:T(8,128)(2,1)S(1)}, bf16[128,256]{1,0:T(8,128)(2,1)S(1)}, u32[]{:S(2)}, u32[]{:S(2)}) collective-permute-start(bf16[128,256]{1,0:T(8,128)(2,1)S(1)} %get-tuple-element.112), channel_id=1, source_target_pairs={{0,5},{1,4},{2,7},{3,6},{4,1},{5,0},{6,3},{7,2},{8,13},{9,12},{10,... | collective-permute-start | bytes 196616 | tf_op jit(solution)/shard_map/ppermute | solution.py:44
  54.1 2.8 %collective-permute-start.16 = (bf16[128,256]{1,0:T(8,128)(2,1)S(1)}, bf16[128,256]{1,0:T(8,128)(2,1)S(1)}, u32[]{:S(2)}, u32[]{:S(2)}) collective-permute-start(bf16[128,256]{1,0:T(8,128)(2,1)S(1)} %get-tuple-element.113), channel_id=1, source_target_pairs={{0,6},{1,7},{2,4},{3,5},{4,2},{5,3},{6,0},{7,1},{8,14},{9,15},{10,... | collective-permute-start | bytes 196616 | tf_op jit(solution)/shard_map/ppermute | solution.py:44
  56.9 0.9 near_pieces.3
  57.9 0.1 collective-permute-start.18
  58.0 3.0 %collective-permute-start.19 = (bf16[128,512]{1,0:T(8,128)(2,1)S(1)}, bf16[128,512]{1,0:T(8,128)(2,1)S(1)}, u32[]{:S(2)}, u32[]{:S(2)}) collective-permute-start(bf16[128,512]{1,0:T(8,128)(2,1)S(1)} %get-tuple-element.117), channel_id=1, source_target_pairs={{0,2},{1,3},{2,0},{3,1},{4,6},{5,7},{6,4},{7,5},{8,10},{9,11},{10,... | collective-permute-start | bytes 393224 | tf_op jit(solution)/shard_map/ppermute | solution.py:44
  60.9 1.4 %collective-permute-start.20 = (bf16[128,512]{1,0:T(8,128)(2,1)S(1)}, bf16[128,512]{1,0:T(8,128)(2,1)S(1)}, u32[]{:S(2)}, u32[]{:S(2)}) collective-permute-start(bf16[128,512]{1,0:T(8,128)(2,1)S(1)} %get-tuple-element.118), channel_id=1, source_target_pairs={{0,1},{1,0},{2,3},{3,2},{4,5},{5,4},{6,7},{7,6},{8,9},{9,8},{10,11... | collective-permute-start | bytes 393224 | tf_op jit(solution)/shard_map/ppermute | solution.py:44
  62.4 0.8 collective-permute-done.16.rest_2_
  63.2 2.1 %collective-permute-start.17 = (bf16[128,256]{1,0:T(8,128)(2,1)S(1)}, bf16[128,256]{1,0:T(8,128)(2,1)S(1)}, u32[]{:S(2)}, u32[]{:S(2)}) collective-permute-start(bf16[128,256]{1,0:T(8,128)(2,1)S(1)} %get-tuple-element.114), channel_id=1, source_target_pairs={{0,7},{1,6},{2,5},{3,4},{4,3},{5,2},{6,1},{7,0},{8,15},{9,14},{10,... | collective-permute-start | bytes 196616 | tf_op jit(solution)/shard_map/ppermute | solution.py:44
  65.2 5.8 %collective-permute-done.17.rest_3_ = bf16[128,256]{1,0:T(8,128)(2,1)S(1)} collective-permute-done((bf16[128,256]{1,0:T(8,128)(2,1)S(1)}, bf16[128,256]{1,0:T(8,128)(2,1)S(1)}, u32[]{:S(2)}, u32[]{:S(2)}) %collective-permute-start.17) | collective-permute-done | bytes 65568 | tf_op jit(solution)/shard_map/ppermute | solution.py:44
  71.1 1.3 %collective-permute-start.27 = (bf16[128,1024]{1,0:T(8,128)(2,1)}, bf16[128,1024]{1,0:T(8,128)(2,1)S(1)}, u32[]{:S(2)}, u32[]{:S(2)}) collective-permute-start(bf16[128,1024]{1,0:T(8,128)(2,1)} %collective-permute-done.22.refs_2_), channel_id=1, source_target_pairs={{0,1},{1,0},{2,3},{3,2},{4,5},{5,4},{6,7},{7,6},{8,9},{9,8},{10,11... | collective-permute-start | bytes 786440 | tf_op jit(solution)/shard_map/ppermute | solution.py:44
  72.4 0.8 collective-permute-start.28
  73.2 2.2 %two_filters.3 = (bf16[512,128]{1,0:T(8,128)(2,1)S(1)}, bf16[512,128]{1,0:T(8,128)(2,1)S(1)}) custom-call(f32[2,128]{1,0:T(2,128)S(1)} %bitcast.19, f32[2,4,512,128]{3,2,1,0:T(8,128)S(1)} %get-tuple-element.80.spectra_ref, bf16[512,256]{1,0:T(8,128)(2,1)S(1)} %copy-done.1, bf16[256,512]{1,0:T(8,128)(2,1)S(1)} %copy-done.3, ...), custom_call_target="tpu_custom_call" | custom-call | flops 536870912 | bytes 1048576 | tf_op jit(solution)/shard_map/two_filters/pallas_call | solution.py:351
  75.4 0.2 collective-permute-start.21
  75.6 2.0 %hold_exit.1 = (bf16[1024,1024]{1,0:T(8,128)(2,1)S(1)}, bf16[4,128,256]{2,1,0:T(8,128)(2,1)S(1)}, bf16[128,1024]{1,0:T(8,128)(2,1)S(1)}, bf16[128,1024]{1,0:T(8,...) custom-call(bf16[1024,1024]{1,0:T(8,128)(2,1)} %bitcast.11, ...), custom_call_target="tpu_custom_call" | custom-call | bytes 3932160 | tf_op jit(solution)/shard_map/hold_exit/pallas_call | solution.py:204
  77.6 6.8 %collective-permute-done.21.come_ref = bf16[512,128]{1,0:T(8,128)(2,1)S(1)} collective-permute-done((bf16[512,128]{1,0:T(8,128)(2,1)S(1)}, bf16[512,128]{1,0:T(8,128)(2,1)S(1)}, u32[]{:S(2)}, u32[]{:S(2)}) %collective-permute-start.21) | collective-permute-done | bytes 131104 | tf_op jit(solution)/shard_map/ppermute | solution.py:44
  84.4 0.1 second_gate.3
  84.5 1.3 %collective-permute-done.28.refs_4_ = bf16[128,1024]{1,0:T(8,128)(2,1)S(1)} collective-permute-done((bf16[128,1024]{1,0:T(8,128)(2,1)}, bf16[128,1024]{1,0:T(8,128)(2,1)S(1)}, u32[]{:S(2)}, u32[]{:S(2)}) %collective-permute-start.28) | collective-permute-done | bytes 262176 | tf_op jit(solution)/shard_map/ppermute | solution.py:44
  85.7 0.5 gradient_away.1
  86.2 0.6 collective-permute-start.29
  86.8 1.9 %collective-permute-start.24 = (bf16[128,256]{1,0:T(8,128)(2,1)S(1)}, bf16[128,256]{1,0:T(8,128)(2,1)S(1)}, u32[]{:S(2)}, u32[]{:S(2)}) collective-permute-start(bf16[128,256]{1,0:T(8,128)(2,1)S(1)} %get-tuple-element.144), channel_id=1, source_target_pairs={{0,3},{1,2},{2,1},{3,0},{4,7},{5,6},{6,5},{7,4},{8,11},{9,10},{10,... | collective-permute-start | bytes 196616 | tf_op jit(solution)/shard_map/ppermute | solution.py:44
  88.7 0.6 collective-permute-start.25
  89.3 1.0 collective-permute-start.26
  90.3 4.5 %collective-permute-done.24.rest_0_ = bf16[128,256]{1,0:T(8,128)(2,1)S(1)} collective-permute-done((bf16[128,256]{1,0:T(8,128)(2,1)S(1)}, bf16[128,256]{1,0:T(8,128)(2,1)S(1)}, u32[]{:S(2)}, u32[]{:S(2)}) %collective-permute-start.24) | collective-permute-done | bytes 65568 | tf_op jit(solution)/shard_map/ppermute | solution.py:44
  94.8 0.7 collective-permute-done.25.rest_1_
  95.5 1.2 %exit_projection.3 = bf16[128,1024]{1,0:T(8,128)(2,1)} custom-call(s32[1]{0:T(128)} %bitcast.choice_ref, bf16[128,1024]{1,0:T(8,128)(2,1)S(1)} %collective-permute-done.12.x_ref, bf16[128,1024]{1,0:T(8,128)(2,1)S(1)} %get-tuple-element.109.other_ref, bf16[1024,1024]{1,0:T(8,128)(2,1)S(1)} %get-tuple-element.141.weight_ref, ...), custom_call_target="tpu_custom_call" | custom-call | flops 268435456 | bytes 2097152 | tf_op jit(solution)/shard_map/exit_projection/pallas_call | solution.py:413
  96.7 0.5 gradient_mine.1
  97.2 3.6 %collective-permute-done.29 = bf16[128,1024]{1,0:T(8,128)(2,1)S(1)} collective-permute-done((bf16[128,1024]{1,0:T(8,128)(2,1)S(1)}, bf16[128,1024]{1,0:T(8,128)(2,1)S(1)}, u32[]{:S(2)}, u32[]{:S(2)}) %collective-permute-start.29) | collective-permute-done | bytes 262176 | tf_op jit(solution)/shard_map/ppermute | solution.py:44
  100.7 0.9 add_bitcast_fusion
  (42 shorter events, 0.1 us)
Async XLA Ops:
  0.6 18.3 %copy-start.1 = (bf16[512,256]{1,0:T(8,128)(2,1)S(1)}, bf16[512,256]{1,0:T(8,128)(2,1)}, u32[]{:S(2)}) copy-start(bf16[512,256]{1,0:T(8,128)(2,1)} %constant.13.clone.forward_ref) | copy-start | bytes 786436
  0.6 18.2 %copy-start.5 = (bf16[1,2,128,1024]{3,2,1,0:T(8,128)(2,1)S(1)}, bf16[1,2,128,1024]{3,2,1,0:T(8,128)(2,1)}, u32[]{:S(2)}) copy-start(bf16[1,2,128,1024]{3,2,1,0:T(8,128)(2,1)} %param.23) | copy-start | bytes 1572868
  0.7 18.2 %copy-start.9 = (bf16[32,1024]{1,0:T(8,128)(2,1)S(1)}, bf16[32,1024]{1,0:T(8,128)(2,1)}, u32[]{:S(2)}) copy-start(bf16[32,1024]{1,0:T(8,128)(2,1)} %amino_ref.1) | copy-start | bytes 196612
  0.7 18.2 %copy-start.10 = (bf16[8,1024]{1,0:T(8,128)(2,1)S(1)}, bf16[8,1024]{1,0:T(8,128)(2,1)}, u32[]{:S(2)}) copy-start(bf16[8,1024]{1,0:T(8,128)(2,1)} %polymer_ref.1) | copy-start | bytes 49156
  0.7 18.2 %copy-start.13 = (s32[8]{0:T(128)S(1)}, s32[8]{0:T(128)}, u32[]{:S(2)}) copy-start(s32[8]{0:T(128)} %sizes_ref.1) | copy-start | bytes 100
  0.7 18.2 %copy-start.14 = (s32[128]{0:T(128)S(1)}, s32[128]{0:T(128)}, u32[]{:S(2)}) copy-start(s32[128]{0:T(128)} %param.14) | copy-start | bytes 1540
  3.8 15.1 %copy-start.4 = (f32[1,2,128,1024]{3,2,1,0:T(8,128)S(1)}, f32[1,2,128,1024]{3,2,1,0:T(8,128)}, u32[]{:S(2)}) copy-start(f32[1,2,128,1024]{3,2,1,0:T(8,128)} %param.20) | copy-start | bytes 3145732
  3.8 20.5 %copy-start.3 = (bf16[256,512]{1,0:T(8,128)(2,1)S(1)}, bf16[256,512]{1,0:T(8,128)(2,1)}, u32[]{:S(2)}) copy-start(bf16[256,512]{1,0:T(8,128)(2,1)} %constant.14.clone.backward_ref) | copy-start | bytes 786436
  3.9 20.5 %copy-start.12 = (f32[1,2,128]{2,1,0:T(2,128)S(1)}, f32[1,2,128]{2,1,0:T(2,128)}, u32[]{:S(2)}) copy-start(f32[1,2,128]{2,1,0:T(2,128)} %param.21) | copy-start | bytes 3076
  3.9 9.9 %collective-permute-start = (bf16[128,256]{1,0:T(8,128)(2,1)S(1)}, bf16[128,256]{1,0:T(8,128)(2,1)S(1)}, u32[]{:S(2)}, u32[]{:S(2)}) collective-permute-start(bf16[128,256]{1,0:T(8,128)(2,1)S(1)} %get-tuple-element.81), channel_id=1, source_target_pairs={{0,4},{1,5},{2,6},{3,7},{4,0},{5,1},{6,2},{7,3},{8,12},{9,13},{10,... | collective-permute-start | bytes 196616 | tf_op jit(solution)/shard_map/ppermute | solution.py:44
  8.0 9.4 %collective-permute-start.1 = (bf16[128,256]{1,0:T(8,128)(2,1)S(1)}, bf16[128,256]{1,0:T(8,128)(2,1)S(1)}, u32[]{:S(2)}, u32[]{:S(2)}) collective-permute-start(bf16[128,256]{1,0:T(8,128)(2,1)S(1)} %get-tuple-element.82), channel_id=1, source_target_pairs={{0,5},{1,4},{2,7},{3,6},{4,1},{5,0},{6,3},{7,2},{8,13},{9,12},{10,... | collective-permute-start | bytes 196616 | tf_op jit(solution)/shard_map/ppermute | solution.py:44
  9.2 33.8 %copy-start = (bf16[1,1024,1024]{2,1,0:T(8,128)(2,1)S(1)}, bf16[1,1024,1024]{2,1,0:T(8,128)(2,1)}, u32[]{:S(2)}) copy-start(bf16[1,1024,1024]{2,1,0:T(8,128)(2,1)} %param.22) | copy-start | bytes 6291460
  9.2 33.8 %copy-start.2 = (bf16[1,128,1024]{2,1,0:T(8,128)(2,1)S(1)}, bf16[1,128,1024]{2,1,0:T(8,128)(2,1)}, u32[]{:S(2)}) copy-start(bf16[1,128,1024]{2,1,0:T(8,128)(2,1)} %param.13) | copy-start | bytes 786436
  10.2 14.1 %collective-permute-start.4 = (bf16[128,512]{1,0:T(8,128)(2,1)S(1)}, bf16[128,512]{1,0:T(8,128)(2,1)S(1)}, u32[]{:S(2)}, u32[]{:S(2)}) collective-permute-start(bf16[128,512]{1,0:T(8,128)(2,1)S(1)} %get-tuple-element.87), channel_id=1, source_target_pairs={{0,3},{1,2},{2,1},{3,0},{4,7},{5,6},{6,5},{7,4},{8,11},{9,10},{10,... | collective-permute-start | bytes 393224 | tf_op jit(solution)/shard_map/ppermute | solution.py:44
  11.8 12.5 %collective-permute-start.5 = (bf16[128,512]{1,0:T(8,128)(2,1)S(1)}, bf16[128,512]{1,0:T(8,128)(2,1)S(1)}, u32[]{:S(2)}, u32[]{:S(2)}) collective-permute-start(bf16[128,512]{1,0:T(8,128)(2,1)S(1)} %get-tuple-element.88), channel_id=1, source_target_pairs={{0,2},{1,3},{2,0},{3,1},{4,6},{5,7},{6,4},{7,5},{8,10},{9,11},{10,... | collective-permute-start | bytes 393224 | tf_op jit(solution)/shard_map/ppermute | solution.py:44
  12.0 12.3 %collective-permute-start.6 = (bf16[128,512]{1,0:T(8,128)(2,1)S(1)}, bf16[128,512]{1,0:T(8,128)(2,1)S(1)}, u32[]{:S(2)}, u32[]{:S(2)}) collective-permute-start(bf16[128,512]{1,0:T(8,128)(2,1)S(1)} %get-tuple-element.89), channel_id=1, source_target_pairs={{0,1},{1,0},{2,3},{3,2},{4,5},{5,4},{6,7},{7,6},{8,9},{9,8},{10,11... | collective-permute-start | bytes 393224 | tf_op jit(solution)/shard_map/ppermute | solution.py:44
  13.7 8.5 %collective-permute-start.2 = (bf16[128,256]{1,0:T(8,128)(2,1)S(1)}, bf16[128,256]{1,0:T(8,128)(2,1)S(1)}, u32[]{:S(2)}, u32[]{:S(2)}) collective-permute-start(bf16[128,256]{1,0:T(8,128)(2,1)S(1)} %get-tuple-element.83), channel_id=1, source_target_pairs={{0,6},{1,7},{2,4},{3,5},{4,2},{5,3},{6,0},{7,1},{8,14},{9,15},{10,... | collective-permute-start | bytes 196616 | tf_op jit(solution)/shard_map/ppermute | solution.py:44
  17.3 7.0 %collective-permute-start.3 = (bf16[128,256]{1,0:T(8,128)(2,1)S(1)}, bf16[128,256]{1,0:T(8,128)(2,1)S(1)}, u32[]{:S(2)}, u32[]{:S(2)}) collective-permute-start(bf16[128,256]{1,0:T(8,128)(2,1)S(1)} %get-tuple-element.84), channel_id=1, source_target_pairs={{0,7},{1,6},{2,5},{3,4},{4,3},{5,2},{6,1},{7,0},{8,15},{9,14},{10,... | collective-permute-start | bytes 196616 | tf_op jit(solution)/shard_map/ppermute | solution.py:44
  26.5 16.5 %collective-permute-start.11 = (bf16[128,1024]{1,0:T(8,128)(2,1)}, bf16[128,1024]{1,0:T(8,128)(2,1)S(1)}, u32[]{:S(2)}, u32[]{:S(2)}) collective-permute-start(bf16[128,1024]{1,0:T(8,128)(2,1)} %get-tuple-element.129.refs_4_), channel_id=1, source_target_pairs={{0,1},{1,0},{2,3},{3,2},{4,5},{5,4},{6,7},{7,6},{8,9},{9,8},{10,11... | collective-permute-start | bytes 786440 | tf_op jit(solution)/shard_map/ppermute | solution.py:44
  27.3 7.7 %collective-permute-start.7 = (bf16[512,128]{1,0:T(8,128)(2,1)S(1)}, bf16[512,128]{1,0:T(8,128)(2,1)S(1)}, u32[]{:S(2)}, u32[]{:S(2)}) collective-permute-start(bf16[512,128]{1,0:T(8,128)(2,1)S(1)} %get-tuple-element.92), channel_id=1, source_target_pairs={{0,4},{1,5},{2,6},{3,7},{4,0},{5,1},{6,2},{7,3},{8,12},{9,13},{10,... | collective-permute-start | bytes 393224 | tf_op jit(solution)/shard_map/ppermute | solution.py:44
  35.8 5.3 %collective-permute-start.8 = (bf16[128,256]{1,0:T(8,128)(2,1)S(1)}, bf16[128,256]{1,0:T(8,128)(2,1)S(1)}, u32[]{:S(2)}, u32[]{:S(2)}) collective-permute-start(bf16[128,256]{1,0:T(8,128)(2,1)S(1)} %get-tuple-element.94), channel_id=1, source_target_pairs={{0,3},{1,2},{2,1},{3,0},{4,7},{5,6},{6,5},{7,4},{8,11},{9,10},{10,... | collective-permute-start | bytes 196616 | tf_op jit(solution)/shard_map/ppermute | solution.py:44
  35.8 5.3 %collective-permute-start.9 = (bf16[128,256]{1,0:T(8,128)(2,1)S(1)}, bf16[128,256]{1,0:T(8,128)(2,1)S(1)}, u32[]{:S(2)}, u32[]{:S(2)}) collective-permute-start(bf16[128,256]{1,0:T(8,128)(2,1)S(1)} %get-tuple-element.95), channel_id=1, source_target_pairs={{0,2},{1,3},{2,0},{3,1},{4,6},{5,7},{6,4},{7,5},{8,10},{9,11},{10,... | collective-permute-start | bytes 196616 | tf_op jit(solution)/shard_map/ppermute | solution.py:44
  38.0 5.0 %collective-permute-start.10 = (bf16[128,256]{1,0:T(8,128)(2,1)S(1)}, bf16[128,256]{1,0:T(8,128)(2,1)S(1)}, u32[]{:S(2)}, u32[]{:S(2)}) collective-permute-start(bf16[128,256]{1,0:T(8,128)(2,1)S(1)} %get-tuple-element.96), channel_id=1, source_target_pairs={{0,1},{1,0},{2,3},{3,2},{4,5},{5,4},{6,7},{7,6},{8,9},{9,8},{10,11... | collective-permute-start | bytes 196616 | tf_op jit(solution)/shard_map/ppermute | solution.py:44
  39.3 10.5 %collective-permute-start.13 = (bf16[128,1024]{1,0:T(8,128)(2,1)}, bf16[128,1024]{1,0:T(8,128)(2,1)}, u32[]{:S(2)}, u32[]{:S(2)}) collective-permute-start(bf16[128,1024]{1,0:T(8,128)(2,1)} %get-tuple-element.132.refs_7_), channel_id=1, source_target_pairs={{0,1},{1,0},{2,3},{3,2},{4,5},{5,4},{6,7},{7,6},{8,9},{9,8},{10,11... | collective-permute-start | bytes 786440 | tf_op jit(solution)/shard_map/ppermute | solution.py:44
  43.0 1.9 %copy-start.6 = (bf16[128,1024]{1,0:T(8,128)(2,1)}, bf16[128,1024]{1,0:T(8,128)(2,1)S(1)}, u32[]{:S(2)}) copy-start(bf16[128,1024]{1,0:T(8,128)(2,1)S(1)} %collective-permute-done.11.refs_3_) | copy-start | bytes 786436
  43.6 6.2 %collective-permute-start.12 = (bf16[128,1024]{1,0:T(8,128)(2,1)S(1)}, bf16[128,1024]{1,0:T(8,128)(2,1)S(1)}, u32[]{:S(2)}, u32[]{:S(2)}) collective-permute-start(bf16[128,1024]{1,0:T(8,128)(2,1)S(1)} %exit_projection.2), channel_id=1, source_target_pairs={{0,8},{8,16},{16,24},{1,9},{9,17},{17,25},{2,10},{10,18},{18,26},{... | collective-permute-start | bytes 786440 | tf_op jit(solution)/shard_map/ppermute | solution.py:517
  44.9 13.0 %collective-permute-start.22 = (bf16[128,1024]{1,0:T(8,128)(2,1)}, bf16[128,1024]{1,0:T(8,128)(2,1)}, u32[]{:S(2)}, u32[]{:S(2)}) collective-permute-start(bf16[128,1024]{1,0:T(8,128)(2,1)} %get-tuple-element.129.refs_4_), channel_id=1, source_target_pairs={{0,2},{1,3},{2,0},{3,1},{4,6},{5,7},{6,4},{7,5},{8,10},{9,11},{10,... | collective-permute-start | bytes 786440 | tf_op jit(solution)/shard_map/ppermute | solution.py:44
  45.0 27.4 %collective-permute-start.23 = (bf16[128,1024]{1,0:T(8,128)(2,1)}, bf16[128,1024]{1,0:T(8,128)(2,1)}, u32[]{:S(2)}, u32[]{:S(2)}) collective-permute-start(bf16[128,1024]{1,0:T(8,128)(2,1)} %get-tuple-element.132.refs_7_), channel_id=1, source_target_pairs={{0,2},{1,3},{2,0},{3,1},{4,6},{5,7},{6,4},{7,5},{8,10},{9,11},{10,... | collective-permute-start | bytes 786440 | tf_op jit(solution)/shard_map/ppermute | solution.py:44
  47.0 2.8 %copy-start.11 = (f32[1,1024]{1,0:T(1,128)S(1)}, f32[1,1024]{1,0:T(1,128)}, u32[]{:S(2)}) copy-start(f32[1,1024]{1,0:T(1,128)} %gain_ref.3) | copy-start | bytes 12292
  50.4 7.5 %collective-permute-start.14 = (bf16[128,256]{1,0:T(8,128)(2,1)S(1)}, bf16[128,256]{1,0:T(8,128)(2,1)S(1)}, u32[]{:S(2)}, u32[]{:S(2)}) collective-permute-start(bf16[128,256]{1,0:T(8,128)(2,1)S(1)} %get-tuple-element.111), channel_id=1, source_target_pairs={{0,4},{1,5},{2,6},{3,7},{4,0},{5,1},{6,2},{7,3},{8,12},{9,13},{10,... | collective-permute-start | bytes 196616 | tf_op jit(solution)/shard_map/ppermute | solution.py:44
  51.7 9.2 %collective-permute-start.15 = (bf16[128,256]{1,0:T(8,128)(2,1)S(1)}, bf16[128,256]{1,0:T(8,128)(2,1)S(1)}, u32[]{:S(2)}, u32[]{:S(2)}) collective-permute-start(bf16[128,256]{1,0:T(8,128)(2,1)S(1)} %get-tuple-element.112), channel_id=1, source_target_pairs={{0,5},{1,4},{2,7},{3,6},{4,1},{5,0},{6,3},{7,2},{8,13},{9,12},{10,... | collective-permute-start | bytes 196616 | tf_op jit(solution)/shard_map/ppermute | solution.py:44
  54.1 9.0 %collective-permute-start.16 = (bf16[128,256]{1,0:T(8,128)(2,1)S(1)}, bf16[128,256]{1,0:T(8,128)(2,1)S(1)}, u32[]{:S(2)}, u32[]{:S(2)}) collective-permute-start(bf16[128,256]{1,0:T(8,128)(2,1)S(1)} %get-tuple-element.113), channel_id=1, source_target_pairs={{0,6},{1,7},{2,4},{3,5},{4,2},{5,3},{6,0},{7,1},{8,14},{9,15},{10,... | collective-permute-start | bytes 196616 | tf_op jit(solution)/shard_map/ppermute | solution.py:44
  56.9 18.7 %copy-start.7 = (bf16[128,1024]{1,0:T(8,128)(2,1)S(1)}, bf16[128,1024]{1,0:T(8,128)(2,1)}, u32[]{:S(2)}) copy-start(bf16[128,1024]{1,0:T(8,128)(2,1)} %copy-done.6) | copy-start | bytes 786436
  56.9 18.7 %copy-start.8 = (bf16[4,128,256]{2,1,0:T(8,128)(2,1)S(1)}, bf16[4,128,256]{2,1,0:T(8,128)(2,1)}, u32[]{:S(2)}) copy-start(bf16[4,128,256]{2,1,0:T(8,128)(2,1)} %get-tuple-element.126.refs_1_) | copy-start | bytes 786436
  57.9 13.2 %collective-permute-start.18 = (bf16[128,512]{1,0:T(8,128)(2,1)S(1)}, bf16[128,512]{1,0:T(8,128)(2,1)S(1)}, u32[]{:S(2)}, u32[]{:S(2)}) collective-permute-start(bf16[128,512]{1,0:T(8,128)(2,1)S(1)} %get-tuple-element.116), channel_id=1, source_target_pairs={{0,3},{1,2},{2,1},{3,0},{4,7},{5,6},{6,5},{7,4},{8,11},{9,10},{10,... | collective-permute-start | bytes 393224 | tf_op jit(solution)/shard_map/ppermute | solution.py:44
  58.0 13.1 %collective-permute-start.19 = (bf16[128,512]{1,0:T(8,128)(2,1)S(1)}, bf16[128,512]{1,0:T(8,128)(2,1)S(1)}, u32[]{:S(2)}, u32[]{:S(2)}) collective-permute-start(bf16[128,512]{1,0:T(8,128)(2,1)S(1)} %get-tuple-element.117), channel_id=1, source_target_pairs={{0,2},{1,3},{2,0},{3,1},{4,6},{5,7},{6,4},{7,5},{8,10},{9,11},{10,... | collective-permute-start | bytes 393224 | tf_op jit(solution)/shard_map/ppermute | solution.py:44
  60.9 10.2 %collective-permute-start.20 = (bf16[128,512]{1,0:T(8,128)(2,1)S(1)}, bf16[128,512]{1,0:T(8,128)(2,1)S(1)}, u32[]{:S(2)}, u32[]{:S(2)}) collective-permute-start(bf16[128,512]{1,0:T(8,128)(2,1)S(1)} %get-tuple-element.118), channel_id=1, source_target_pairs={{0,1},{1,0},{2,3},{3,2},{4,5},{5,4},{6,7},{7,6},{8,9},{9,8},{10,11... | collective-permute-start | bytes 393224 | tf_op jit(solution)/shard_map/ppermute | solution.py:44
  63.2 7.9 %collective-permute-start.17 = (bf16[128,256]{1,0:T(8,128)(2,1)S(1)}, bf16[128,256]{1,0:T(8,128)(2,1)S(1)}, u32[]{:S(2)}, u32[]{:S(2)}) collective-permute-start(bf16[128,256]{1,0:T(8,128)(2,1)S(1)} %get-tuple-element.114), channel_id=1, source_target_pairs={{0,7},{1,6},{2,5},{3,4},{4,3},{5,2},{6,1},{7,0},{8,15},{9,14},{10,... | collective-permute-start | bytes 196616 | tf_op jit(solution)/shard_map/ppermute | solution.py:44
  71.1 13.4 %collective-permute-start.27 = (bf16[128,1024]{1,0:T(8,128)(2,1)}, bf16[128,1024]{1,0:T(8,128)(2,1)S(1)}, u32[]{:S(2)}, u32[]{:S(2)}) collective-permute-start(bf16[128,1024]{1,0:T(8,128)(2,1)} %collective-permute-done.22.refs_2_), channel_id=1, source_target_pairs={{0,1},{1,0},{2,3},{3,2},{4,5},{5,4},{6,7},{7,6},{8,9},{9,8},{10,11... | collective-permute-start | bytes 786440 | tf_op jit(solution)/shard_map/ppermute | solution.py:44
  72.4 13.3 %collective-permute-start.28 = (bf16[128,1024]{1,0:T(8,128)(2,1)}, bf16[128,1024]{1,0:T(8,128)(2,1)S(1)}, u32[]{:S(2)}, u32[]{:S(2)}) collective-permute-start(bf16[128,1024]{1,0:T(8,128)(2,1)} %collective-permute-done.23.refs_5_), channel_id=1, source_target_pairs={{0,1},{1,0},{2,3},{3,2},{4,5},{5,4},{6,7},{7,6},{8,9},{9,8},{10,11... | collective-permute-start | bytes 786440 | tf_op jit(solution)/shard_map/ppermute | solution.py:44
  75.4 9.0 %collective-permute-start.21 = (bf16[512,128]{1,0:T(8,128)(2,1)S(1)}, bf16[512,128]{1,0:T(8,128)(2,1)S(1)}, u32[]{:S(2)}, u32[]{:S(2)}) collective-permute-start(bf16[512,128]{1,0:T(8,128)(2,1)S(1)} %get-tuple-element.120), channel_id=1, source_target_pairs={{0,4},{1,5},{2,6},{3,7},{4,0},{5,1},{6,2},{7,3},{8,12},{9,13},{10,... | collective-permute-start | bytes 393224 | tf_op jit(solution)/shard_map/ppermute | solution.py:44
  86.2 14.5 %collective-permute-start.29 = (bf16[128,1024]{1,0:T(8,128)(2,1)S(1)}, bf16[128,1024]{1,0:T(8,128)(2,1)S(1)}, u32[]{:S(2)}, u32[]{:S(2)}) collective-permute-start(bf16[128,1024]{1,0:T(8,128)(2,1)S(1)} %gradient_away.1), channel_id=1, source_target_pairs={{0,4},{1,5},{2,6},{3,7},{4,0},{5,1},{6,2},{7,3},{8,12},{9,13},{10,... | collective-permute-start | bytes 786440 | tf_op jit(solution)/shard_map/ppermute | solution.py:44
  86.8 8.0 %collective-permute-start.24 = (bf16[128,256]{1,0:T(8,128)(2,1)S(1)}, bf16[128,256]{1,0:T(8,128)(2,1)S(1)}, u32[]{:S(2)}, u32[]{:S(2)}) collective-permute-start(bf16[128,256]{1,0:T(8,128)(2,1)S(1)} %get-tuple-element.144), channel_id=1, source_target_pairs={{0,3},{1,2},{2,1},{3,0},{4,7},{5,6},{6,5},{7,4},{8,11},{9,10},{10,... | collective-permute-start | bytes 196616 | tf_op jit(solution)/shard_map/ppermute | solution.py:44
  88.7 6.8 %collective-permute-start.25 = (bf16[128,256]{1,0:T(8,128)(2,1)S(1)}, bf16[128,256]{1,0:T(8,128)(2,1)S(1)}, u32[]{:S(2)}, u32[]{:S(2)}) collective-permute-start(bf16[128,256]{1,0:T(8,128)(2,1)S(1)} %get-tuple-element.145), channel_id=1, source_target_pairs={{0,2},{1,3},{2,0},{3,1},{4,6},{5,7},{6,4},{7,5},{8,10},{9,11},{10,... | collective-permute-start | bytes 196616 | tf_op jit(solution)/shard_map/ppermute | solution.py:44
  89.3 6.2 %collective-permute-start.26 = (bf16[128,256]{1,0:T(8,128)(2,1)S(1)}, bf16[128,256]{1,0:T(8,128)(2,1)S(1)}, u32[]{:S(2)}, u32[]{:S(2)}) collective-permute-start(bf16[128,256]{1,0:T(8,128)(2,1)S(1)} %get-tuple-element.146), channel_id=1, source_target_pairs={{0,1},{1,0},{2,3},{3,2},{4,5},{5,4},{6,7},{7,6},{8,9},{9,8},{10,11... | collective-permute-start | bytes 196616 | tf_op jit(solution)/shard_map/ppermute | solution.py:44

commit v2 on v1

--- a/solution.py
+++ b/solution.py
@@ -283,7 +283,7 @@
 
 def filter_kernel(order, skips_ref, spectra_ref, forward_ref, backward_ref, *rest):
     pieces = rest[: len(order)]
-    keep_ref, send_ref, value_ref, gate_ref, gated_ref, found_ref, mixed_ref = rest[len(order) :]
+    send_ref, rest_mixed_ref, rest_gated_ref, value_ref, gate_ref, gated_ref, found_ref, mixed_ref = rest[len(order) :]
     me = lax.axis_index("seq")
     half = me // (len(order) // 2)
     channels = spectra_ref.shape[3]
@@ -325,22 +325,35 @@
             return 0
 
         lax.fori_loop(0, size // step, multiply, 0)
-        return dot(backward_ref[...], mixed_ref[...])
-
-    result = convolve(jnp.concatenate([value_ref[chunk_rows(j), :] for j in range(chunks)], axis=1), 0)
+
+    convolve(jnp.concatenate([value_ref[chunk_rows(j), :] for j in range(chunks)], axis=1), 0)
+    result = dot(backward_ref[...], mixed_ref[...])
     for j in range(chunks):
         value = value_ref[chunk_rows(j), :].astype(f32)
         gate = gate_ref[chunk_rows(j), :].astype(f32)
         gated_ref[:, chunk_lanes(j)] = gate * (result[:, chunk_lanes(j)] + skips_ref[0:1, :] * value)
-    result = convolve(gated_ref[...].astype(bf16), 1)
-    final = [
-        (result[:, chunk_lanes(j)] + skips_ref[1:2, :] * gated_ref[:, chunk_lanes(j)]).astype(bf16)
-        for j in range(chunks)
-    ]
-    for j in range(chunks // 2):
-        low, high = final[j], final[j + chunks // 2]
-        keep_ref[chunk_rows(j), :] = jnp.where(half == 0, low, high)
-        send_ref[chunk_rows(j), :] = jnp.where(half == 0, high, low)
+    convolve(gated_ref[...].astype(bf16), 1)
+
+    def chosen(ref, first):
+        middle = ref.shape[1] // 2
+        return jnp.where(half == first, ref[:, :middle], ref[:, middle:])
+
+    rest_mixed_ref[...] = chosen(mixed_ref, 0)
+    rest_gated_ref[...] = chosen(gated_ref, 0)
+    finish(backward_ref, skips_ref, chosen(mixed_ref, 1), chosen(gated_ref, 1), send_ref)
+
+
+def finish(backward_ref, skips_ref, mixed, gated, out_ref):
+    channels = out_ref.shape[1]
+    size = backward_ref.shape[0]
+    result = dot(backward_ref[...], mixed)
+    for j in range(out_ref.shape[0] // size):
+        place = slice(j * channels, (j + 1) * channels)
+        out_ref[j * size : (j + 1) * size, :] = (result[:, place] + skips_ref[1:2, :] * gated[:, place]).astype(bf16)
+
+
+def finish_kernel(skips_ref, backward_ref, mixed_ref, gated_ref, out_ref):
+    finish(backward_ref, skips_ref, mixed_ref[...], gated_ref[...], out_ref)
 
 
 def filtered(received, order, skips, spectra, forward, backward):
@@ -348,11 +361,14 @@
     size = forward.shape[1]
     length = chunks * size
     out = jax.ShapeDtypeStruct((length // 2, channels), bf16)
-    return pl.pallas_call(
+    kept = jax.ShapeDtypeStruct((2 * size, chunks // 2 * channels), bf16)
+    gated = jax.ShapeDtypeStruct((size, chunks // 2 * channels), f32)
+    limit = 12 if channels % lanes == 0 else 48
+    send, kept, gated = pl.pallas_call(
         functools.partial(filter_kernel, order),
-        out_shape=(out, out),
+        out_shape=(out, kept, gated),
         in_specs=[whole()] * (4 + len(order)),
-        out_specs=(whole(), whole()),
+        out_specs=(whole(),) * 3,
         scratch_shapes=[
             pltpu.VMEM((length, channels), bf16),
             pltpu.VMEM((length, channels), bf16),
@@ -360,10 +376,20 @@
             pltpu.VMEM((2 * size, chunks * channels), f32),
             pltpu.VMEM((2 * size, chunks * channels), bf16),
         ],
-        compiler_params=params(12 if channels % lanes == 0 else 48),
+        compiler_params=params(limit),
         cost_estimate=cost(16 * size * length * channels, 8 * length * channels),
         name="two_filters",
     )(skips, spectra, forward, backward, *received)
+    keep = pl.pallas_call(
+        finish_kernel,
+        out_shape=out,
+        in_specs=[whole()] * 4,
+        out_specs=whole(),
+        compiler_params=params(limit),
+        cost_estimate=cost(2 * size * length * channels, 4 * length * channels),
+        name="own_half",
+    )(skips, backward, kept, gated)
+    return keep, send
 
 
 def gate_kernel(order, keep_ref, come_ref, *rest):
@@ -390,7 +416,7 @@
         in_specs=[whole()] * (2 + len(gates)),
         out_specs=(whole(),) * (len(gates) + 1),
         compiler_params=params(8),
-        cost_estimate=cost(keep.size * 2, keep.size * 8),
+        cost_estimate=cost(10**9, keep.size * 8),
         name="second_gate",
     )(keep, come, *gates)
 
@@ -496,11 +522,11 @@
         come += [exchange(v, d) if d else v for v, d in zip(near_pieces, near)]
         beside = beside(come)
         keep, send = filtered(come, far + near, skips, spectra, forward, backward)
-        kept = beside(send)
+        kept = beside(keep)
         swapped, kept = lax.optimization_barrier((exchange(send, group), kept))
         *hyenas, stacked = gate_two(keep, swapped, come[group:], near, choice is never)
         home = [exchange(v, d) if d else v for v, d in zip(hyenas, near)]
-        return send, home, stacked, kept
+        return keep, home, stacked, kept
 
     seeds = {(step, 0): own for step, own in enumerate(own_seeds)}
 
@@ -509,28 +535,31 @@
             seeds[step, d] = exchange(tie(seeds[step, d & (d - 1)], *earlier), d & -d)
 
     resident = resident_microbatch[0]
-    send, home, first_hyenas, _ = layer(resident, None, never, weight_in, lambda come: lambda send: send)
-    spread([(0, 1)], send)
-    home, seeds[0, 1] = lax.optimization_barrier((home, seeds[0, 1]))
+    keep, home, first_hyenas, _ = layer(resident, None, never, weight_in, lambda come: lambda keep: keep)
+    lines = range(2, group, 2)
+    spread([(0, 1)] + [(1, d) for d in lines], keep)
+    early = {place: seeds[place] for place in seeds if place[1]}
     spread([(1, 1)], first_hyenas)
+    home, early = lax.optimization_barrier((home, early))
+    seeds |= early
     first_out = exit_projection(never, resident, resident, weight_out, home, near)
     handed = lax.ppermute(first_out, "section", [(i, i + 1) for i in range(sections - 1)])
     weight_again = tie(weight_in, first_out)
     if aligned:
         weight_again = hold([weight_again], "hold_entry")[0]
     handed, seeds[1, 1], weight_again = lax.optimization_barrier((handed, seeds[1, 1], weight_again))
-    spread([(step, d) for step in range(2) for d in range(2, group, 2)], home)
+    spread([(0, d) for d in lines], home)
 
     def second_beside(come):
         spread([(step, d) for step in range(2) for d in range(3, group, 2)], come)
 
-        def held(send):
+        def held(keep):
             early = [weight_out, first_hyenas] + [seeds[step, d] for step in range(2) for d in near if d % 2 == 0 or d == 1]
-            return hold(tie(early, send), "hold_exit") if aligned else early
+            return hold(tie(early, keep), "hold_exit") if aligned else early
 
         return held
 
-    send, home, second_hyenas, kept = layer(handed, embedded, first_section, weight_again, second_beside)
+    _, home, second_hyenas, kept = layer(handed, embedded, first_section, weight_again, second_beside)
     weight_again, first_hyenas, *early = kept
     seeds = [early.pop(0) if d % 2 == 0 or d == 1 else seeds[step, d] for step in range(2) for d in near]
     away = gradient(first_hyenas, second_hyenas, seeds, 1, bf16, "gradient_away")

time: 102 us -> 95.9 us (0.940)
  waiting for transfers between devices: 36.8 us -> 27 us
  starting transfers between devices: 42.6 us -> 45.9 us
    ppermute x29, waiting for transfers between devices: 36.8 us -> 27 us  [exchange(): return lax.ppermute(value, 'seq', [(i, i ^ distance) for i in range(peers)])]
    ppermute x29, starting transfers between devices: 41.3 us -> 44.6 us  [exchange(): return lax.ppermute(value, 'seq', [(i, i ^ distance) for i in range(peers)])]
    pallas_call x2 -> x4, Pallas kernels: 4.35 us -> 5.01 us  [the longest x2 4.56 us: filtered(): pl.pallas_call(functools.partial(filter_kernel, order), out_shape=(out, k...]
  transfers between devices with their start and end apart: 30 -> 30, of which waited for: 12 -> 12; matrix products, arithmetic and copies ran while one was open for 0% -> 0% of each run, Pallas kernels for 14% -> 16%
where the time goes in v2:
time: 95.9 us; the launch traced here: 95.7 us
  starting transfers between devices  45.9 us (48%)
  waiting for transfers between devices  27 us (28%)
  Pallas kernels  20.9 us (22%)
  between operations  1.01 us (1%)
    ppermute x29, starting transfers between devices, exchange(): return lax.ppermute(value, 'seq', [(i, i ^ distance) for i in range(peers)])  44.6 us
    ppermute x29, waiting for transfers between devices, exchange(): return lax.ppermute(value, 'seq', [(i, i ^ distance) for i in range(peers)])  27 us
    pallas_call x2, Pallas kernels, hold(): pl.pallas_call(functools.partial(hold_kernel, count), out_shape=tuple((pl...  4.69 us
    pallas_call x2, Pallas kernels, filtered(): pl.pallas_call(functools.partial(filter_kernel, order), out_shape=(out, k...  4.56 us
    pallas_call x1, Pallas kernels, project(): pl.pallas_call(functools.partial(far_stream_kernel, far), out_shape=outs,...  3.13 us
    pallas_call x1, Pallas kernels, prepare(): pl.pallas_call(prepare_kernel, out_shape=(jax.ShapeDtypeStruct((2, chunks...  2.12 us
  transfers between devices with their start and end apart: 30, of which 12 were waited for; matrix products, arithmetic and copies ran while one was open for 0% of the time, Pallas kernels for 16%

profile of v2, /device:TPU:0, one launch (start us, length us, event | category | flops | bytes accessed | tf_op | source)
XLA Modules:
  0.0 95.7 jit_solution(7211772200215555713)
XLA Ops:
  0.6 0.0 copy-start.2
  0.7 3.1 %far_pieces_streamed.1 = (bf16[128,256]{1,0:T(8,128)(2,1)S(1)}, bf16[128,256]{1,0:T(8,128)(2,1)S(1)}, bf16[128,256]{1,0:T(8,128)(2,1)S(1)}, bf16[128,256]{1,0:T(...) custom-call(bf16[128,1024]{1,0:T(8,128)(2,1)} %bitcast.13, f32[1,1024]{1,0:T(1,128)} %gain_ref.3, ...), custom_call_target="tpu_custom_call" | custom-call | flops 268435456 | bytes 2097152 | tf_op jit(solution)/shard_map/far_pieces_streamed/pallas_call | solution.py:242
  3.8 0.0 copy-start.4
  3.8 0.0 copy-start.1
  3.9 0.0 copy-start.12
  3.9 4.1 %collective-permute-start = (bf16[128,256]{1,0:T(8,128)(2,1)S(1)}, bf16[128,256]{1,0:T(8,128)(2,1)S(1)}, u32[]{:S(2)}, u32[]{:S(2)}) collective-permute-start(bf16[128,256]{1,0:T(8,128)(2,1)S(1)} %get-tuple-element.84), channel_id=1, source_target_pairs={{0,4},{1,5},{2,6},{3,7},{4,0},{5,1},{6,2},{7,3},{8,12},{9,13},{10,... | collective-permute-start | bytes 196616 | tf_op jit(solution)/shard_map/ppermute | solution.py:44
  8.0 1.3 %collective-permute-start.1 = (bf16[128,256]{1,0:T(8,128)(2,1)S(1)}, bf16[128,256]{1,0:T(8,128)(2,1)S(1)}, u32[]{:S(2)}, u32[]{:S(2)}) collective-permute-start(bf16[128,256]{1,0:T(8,128)(2,1)S(1)} %get-tuple-element.85), channel_id=1, source_target_pairs={{0,5},{1,4},{2,7},{3,6},{4,1},{5,0},{6,3},{7,2},{8,13},{9,12},{10,... | collective-permute-start | bytes 196616 | tf_op jit(solution)/shard_map/ppermute | solution.py:44
  9.2 0.9 near_pieces.2
  10.2 1.6 %collective-permute-start.4 = (bf16[128,512]{1,0:T(8,128)(2,1)S(1)}, bf16[128,512]{1,0:T(8,128)(2,1)S(1)}, u32[]{:S(2)}, u32[]{:S(2)}) collective-permute-start(bf16[128,512]{1,0:T(8,128)(2,1)S(1)} %get-tuple-element.90), channel_id=1, source_target_pairs={{0,3},{1,2},{2,1},{3,0},{4,7},{5,6},{6,5},{7,4},{8,11},{9,10},{10,... | collective-permute-start | bytes 393224 | tf_op jit(solution)/shard_map/ppermute | solution.py:44
  11.8 0.2 collective-permute-start.5
  12.0 1.7 %collective-permute-start.6 = (bf16[128,512]{1,0:T(8,128)(2,1)S(1)}, bf16[128,512]{1,0:T(8,128)(2,1)S(1)}, u32[]{:S(2)}, u32[]{:S(2)}) collective-permute-start(bf16[128,512]{1,0:T(8,128)(2,1)S(1)} %get-tuple-element.92), channel_id=1, source_target_pairs={{0,1},{1,0},{2,3},{3,2},{4,5},{5,4},{6,7},{7,6},{8,9},{9,8},{10,11... | collective-permute-start | bytes 393224 | tf_op jit(solution)/shard_map/ppermute | solution.py:44
  13.7 3.6 %collective-permute-start.2 = (bf16[128,256]{1,0:T(8,128)(2,1)S(1)}, bf16[128,256]{1,0:T(8,128)(2,1)S(1)}, u32[]{:S(2)}, u32[]{:S(2)}) collective-permute-start(bf16[128,256]{1,0:T(8,128)(2,1)S(1)} %get-tuple-element.86), channel_id=1, source_target_pairs={{0,6},{1,7},{2,4},{3,5},{4,2},{5,3},{6,0},{7,1},{8,14},{9,15},{10,... | collective-permute-start | bytes 196616 | tf_op jit(solution)/shard_map/ppermute | solution.py:44
  17.3 1.6 %collective-permute-start.3 = (bf16[128,256]{1,0:T(8,128)(2,1)S(1)}, bf16[128,256]{1,0:T(8,128)(2,1)S(1)}, u32[]{:S(2)}, u32[]{:S(2)}) collective-permute-start(bf16[128,256]{1,0:T(8,128)(2,1)S(1)} %get-tuple-element.87), channel_id=1, source_target_pairs={{0,7},{1,6},{2,5},{3,4},{4,3},{5,2},{6,1},{7,0},{8,15},{9,14},{10,... | collective-permute-start | bytes 196616 | tf_op jit(solution)/shard_map/ppermute | solution.py:44
  18.9 2.1 %prepare.1 = (f32[2,4,512,128]{3,2,1,0:T(8,128)S(1)}, bf16[128,1024]{1,0:T(8,128)(2,1)S(1)}, bf16[128,1024]{1,0:T(8,128)(2,1)}, bf16[128,1024]{1,0:T(8,128)(2,1)}) custom-call(s32[8]{0:T(128)S(1)} %copy-done.15, s32[1,128]{1,0:T(1,128)S(1)} %bitcast.22, bf16[32,1024]{1,0:T(8,128)(2,1)S(1)} %copy-done.11, bf16[8,1024]{1,0:T(8,128)(2,1)S(1)} %copy-done.13, ...), custom_call_target="tpu_custom_call" | custom-call | flops 268435456 | bytes 2097152 | tf_op jit(solution)/shard_map/prepare/pallas_call | solution.py:97
  21.1 1.2 %collective-permute-done.2.rest_2_ = bf16[128,256]{1,0:T(8,128)(2,1)S(1)} collective-permute-done((bf16[128,256]{1,0:T(8,128)(2,1)S(1)}, bf16[128,256]{1,0:T(8,128)(2,1)S(1)}, u32[]{:S(2)}, u32[]{:S(2)}) %collective-permute-start.2) | collective-permute-done | bytes 65568 | tf_op jit(solution)/shard_map/ppermute | solution.py:44
  22.2 2.1 %collective-permute-done.3.rest_3_ = bf16[128,256]{1,0:T(8,128)(2,1)S(1)} collective-permute-done((bf16[128,256]{1,0:T(8,128)(2,1)S(1)}, bf16[128,256]{1,0:T(8,128)(2,1)S(1)}, u32[]{:S(2)}, u32[]{:S(2)}) %collective-permute-start.3) | collective-permute-done | bytes 65568 | tf_op jit(solution)/shard_map/ppermute | solution.py:44
  24.3 2.3 %two_filters.2 = (bf16[512,128]{1,0:T(8,128)(2,1)S(1)}, bf16[512,256]{1,0:T(8,128)(2,1)S(1)}, f32[256,256]{1,0:T(8,128)S(1)}) custom-call(f32[2,128]{1,0:T(2,128)S(1)} %bitcast.18, f32[2,4,512,128]{3,2,1,0:T(8,128)S(1)} %get-tuple-element.83.spectra_ref, bf16[512,256]{1,0:T(8,128)(2,1)S(1)} %copy-done.2, bf16[256,512]{1,0:T(8,128)(2,1)S(1)} %copy-done.1, ...), custom_call_target="tpu_custom_call" | custom-call | flops 536870912 | bytes 1048576 | tf_op jit(solution)/shard_map/two_filters/pallas_call | solution.py:367
  26.6 0.1 collective-permute-start.7
  26.7 0.2 own_half.2.keep_ref
  27.0 1.5 %collective-permute-start.11 = (bf16[128,1024]{1,0:T(8,128)(2,1)}, bf16[128,1024]{1,0:T(8,128)(2,1)S(1)}, u32[]{:S(2)}, u32[]{:S(2)}) collective-permute-start(bf16[128,1024]{1,0:T(8,128)(2,1)} %get-tuple-element.136.refs_4_), channel_id=1, source_target_pairs={{0,1},{1,0},{2,3},{3,2},{4,5},{5,4},{6,7},{7,6},{8,9},{9,8},{10,11... | collective-permute-start | bytes 786440 | tf_op jit(solution)/shard_map/ppermute | solution.py:44
  28.5 2.5 %collective-permute-start.12 = (bf16[128,1024]{1,0:T(8,128)(2,1)}, bf16[128,1024]{1,0:T(8,128)(2,1)S(1)}, u32[]{:S(2)}, u32[]{:S(2)}) collective-permute-start(bf16[128,1024]{1,0:T(8,128)(2,1)} %get-tuple-element.139.refs_7_), channel_id=1, source_target_pairs={{0,2},{1,3},{2,0},{3,1},{4,6},{5,7},{6,4},{7,5},{8,10},{9,11},{10,... | collective-permute-start | bytes 786440 | tf_op jit(solution)/shard_map/ppermute | solution.py:44
  31.0 3.3 %collective-permute-done.7.come_ref = bf16[512,128]{1,0:T(8,128)(2,1)S(1)} collective-permute-done((bf16[512,128]{1,0:T(8,128)(2,1)S(1)}, bf16[512,128]{1,0:T(8,128)(2,1)S(1)}, u32[]{:S(2)}, u32[]{:S(2)}) %collective-permute-start.7) | collective-permute-done | bytes 131104 | tf_op jit(solution)/shard_map/ppermute | solution.py:44
  34.2 0.8 second_gate.2
  35.0 0.6 collective-permute-start.8
  35.6 2.1 %collective-permute-start.9 = (bf16[128,256]{1,0:T(8,128)(2,1)S(1)}, bf16[128,256]{1,0:T(8,128)(2,1)S(1)}, u32[]{:S(2)}, u32[]{:S(2)}) collective-permute-start(bf16[128,256]{1,0:T(8,128)(2,1)S(1)} %get-tuple-element.99), channel_id=1, source_target_pairs={{0,2},{1,3},{2,0},{3,1},{4,6},{5,7},{6,4},{7,5},{8,10},{9,11},{10,... | collective-permute-start | bytes 196616 | tf_op jit(solution)/shard_map/ppermute | solution.py:44
  37.8 0.7 collective-permute-start.10
  38.5 2.3 %collective-permute-done.8.rest_0_ = bf16[128,256]{1,0:T(8,128)(2,1)S(1)} collective-permute-done((bf16[128,256]{1,0:T(8,128)(2,1)S(1)}, bf16[128,256]{1,0:T(8,128)(2,1)S(1)}, u32[]{:S(2)}, u32[]{:S(2)}) %collective-permute-start.8) | collective-permute-done | bytes 65568 | tf_op jit(solution)/shard_map/ppermute | solution.py:44
  40.8 1.7 %collective-permute-start.14 = (bf16[128,1024]{1,0:T(8,128)(2,1)}, bf16[128,1024]{1,0:T(8,128)(2,1)}, u32[]{:S(2)}, u32[]{:S(2)}) collective-permute-start(bf16[128,1024]{1,0:T(8,128)(2,1)} %get-tuple-element.139.refs_7_), channel_id=1, source_target_pairs={{0,1},{1,0},{2,3},{3,2},{4,5},{5,4},{6,7},{7,6},{8,9},{9,8},{10,11... | collective-permute-start | bytes 786440 | tf_op jit(solution)/shard_map/ppermute | solution.py:44
  42.5 0.5 exit_projection.2
  43.0 1.3 %collective-permute-start.13 = (bf16[128,1024]{1,0:T(8,128)(2,1)S(1)}, bf16[128,1024]{1,0:T(8,128)(2,1)S(1)}, u32[]{:S(2)}, u32[]{:S(2)}) collective-permute-start(bf16[128,1024]{1,0:T(8,128)(2,1)S(1)} %exit_projection.2), channel_id=1, source_target_pairs={{0,8},{8,16},{16,24},{1,9},{9,17},{17,25},{2,10},{10,18},{18,26},{... | collective-permute-start | bytes 786440 | tf_op jit(solution)/shard_map/ppermute | solution.py:546
  44.4 0.1 collective-permute-start.23
  44.5 2.8 %hold_entry.1.weight_ref = bf16[1024,3072]{1,0:T(8,128)(2,1)S(1)} custom-call(bf16[1024,3072]{1,0:T(8,128)(2,1)} %bitcast.24), custom_call_target="tpu_custom_call" | custom-call | bytes 6291456 | tf_op jit(solution)/shard_map/hold_entry/pallas_call | solution.py:204
  47.3 0.5 collective-permute-done.14.refs_6_
  47.8 0.6 far_pieces.1
  48.4 2.6 %collective-permute-start.15 = (bf16[128,256]{1,0:T(8,128)(2,1)S(1)}, bf16[128,256]{1,0:T(8,128)(2,1)S(1)}, u32[]{:S(2)}, u32[]{:S(2)}) collective-permute-start(bf16[128,256]{1,0:T(8,128)(2,1)S(1)} %get-tuple-element.116), channel_id=1, source_target_pairs={{0,4},{1,5},{2,6},{3,7},{4,0},{5,1},{6,2},{7,3},{8,12},{9,13},{10,... | collective-permute-start | bytes 196616 | tf_op jit(solution)/shard_map/ppermute | solution.py:44
  51.0 1.2 %collective-permute-start.16 = (bf16[128,256]{1,0:T(8,128)(2,1)S(1)}, bf16[128,256]{1,0:T(8,128)(2,1)S(1)}, u32[]{:S(2)}, u32[]{:S(2)}) collective-permute-start(bf16[128,256]{1,0:T(8,128)(2,1)S(1)} %get-tuple-element.117), channel_id=1, source_target_pairs={{0,5},{1,4},{2,7},{3,6},{4,1},{5,0},{6,3},{7,2},{8,13},{9,12},{10,... | collective-permute-start | bytes 196616 | tf_op jit(solution)/shard_map/ppermute | solution.py:44
  52.2 2.7 %collective-permute-start.17 = (bf16[128,256]{1,0:T(8,128)(2,1)S(1)}, bf16[128,256]{1,0:T(8,128)(2,1)S(1)}, u32[]{:S(2)}, u32[]{:S(2)}) collective-permute-start(bf16[128,256]{1,0:T(8,128)(2,1)S(1)} %get-tuple-element.118), channel_id=1, source_target_pairs={{0,6},{1,7},{2,4},{3,5},{4,2},{5,3},{6,0},{7,1},{8,14},{9,15},{10,... | collective-permute-start | bytes 196616 | tf_op jit(solution)/shard_map/ppermute | solution.py:44
  54.9 0.9 near_pieces.3
  55.8 0.6 collective-permute-start.19
  56.4 1.7 %collective-permute-start.20 = (bf16[128,512]{1,0:T(8,128)(2,1)S(1)}, bf16[128,512]{1,0:T(8,128)(2,1)S(1)}, u32[]{:S(2)}, u32[]{:S(2)}) collective-permute-start(bf16[128,512]{1,0:T(8,128)(2,1)S(1)} %get-tuple-element.122), channel_id=1, source_target_pairs={{0,2},{1,3},{2,0},{3,1},{4,6},{5,7},{6,4},{7,5},{8,10},{9,11},{10,... | collective-permute-start | bytes 393224 | tf_op jit(solution)/shard_map/ppermute | solution.py:44
  58.1 2.6 %collective-permute-done.16.rest_1_ = bf16[128,256]{1,0:T(8,128)(2,1)S(1)} collective-permute-done((bf16[128,256]{1,0:T(8,128)(2,1)S(1)}, bf16[128,256]{1,0:T(8,128)(2,1)S(1)}, u32[]{:S(2)}, u32[]{:S(2)}) %collective-permute-start.16) | collective-permute-done | bytes 65568 | tf_op jit(solution)/shard_map/ppermute | solution.py:44
  60.6 1.0 %collective-permute-start.21 = (bf16[128,512]{1,0:T(8,128)(2,1)S(1)}, bf16[128,512]{1,0:T(8,128)(2,1)S(1)}, u32[]{:S(2)}, u32[]{:S(2)}) collective-permute-start(bf16[128,512]{1,0:T(8,128)(2,1)S(1)} %get-tuple-element.123), channel_id=1, source_target_pairs={{0,1},{1,0},{2,3},{3,2},{4,5},{5,4},{6,7},{7,6},{8,9},{9,8},{10,11... | collective-permute-start | bytes 393224 | tf_op jit(solution)/shard_map/ppermute | solution.py:44
  61.6 3.4 %collective-permute-start.18 = (bf16[128,256]{1,0:T(8,128)(2,1)S(1)}, bf16[128,256]{1,0:T(8,128)(2,1)S(1)}, u32[]{:S(2)}, u32[]{:S(2)}) collective-permute-start(bf16[128,256]{1,0:T(8,128)(2,1)S(1)} %get-tuple-element.119), channel_id=1, source_target_pairs={{0,7},{1,6},{2,5},{3,4},{4,3},{5,2},{6,1},{7,0},{8,15},{9,14},{10,... | collective-permute-start | bytes 196616 | tf_op jit(solution)/shard_map/ppermute | solution.py:44
  65.0 3.6 %collective-permute-done.18.rest_3_ = bf16[128,256]{1,0:T(8,128)(2,1)S(1)} collective-permute-done((bf16[128,256]{1,0:T(8,128)(2,1)S(1)}, bf16[128,256]{1,0:T(8,128)(2,1)S(1)}, u32[]{:S(2)}, u32[]{:S(2)}) %collective-permute-start.18) | collective-permute-done | bytes 65568 | tf_op jit(solution)/shard_map/ppermute | solution.py:44
  68.6 1.1 %collective-permute-start.27 = (bf16[128,1024]{1,0:T(8,128)(2,1)}, bf16[128,1024]{1,0:T(8,128)(2,1)S(1)}, u32[]{:S(2)}, u32[]{:S(2)}) collective-permute-start(bf16[128,1024]{1,0:T(8,128)(2,1)} %collective-permute-done.23.refs_2_), channel_id=1, source_target_pairs={{0,1},{1,0},{2,3},{3,2},{4,5},{5,4},{6,7},{7,6},{8,9},{9,8},{10,11... | collective-permute-start | bytes 786440 | tf_op jit(solution)/shard_map/ppermute | solution.py:44
  69.7 1.0 %collective-permute-start.28 = (bf16[128,1024]{1,0:T(8,128)(2,1)S(1)}, bf16[128,1024]{1,0:T(8,128)(2,1)S(1)}, u32[]{:S(2)}, u32[]{:S(2)}) collective-permute-start(bf16[128,1024]{1,0:T(8,128)(2,1)S(1)} %copy-done.7), channel_id=1, source_target_pairs={{0,1},{1,0},{2,3},{3,2},{4,5},{5,4},{6,7},{7,6},{8,9},{9,8},{10,11... | collective-permute-start | bytes 786440 | tf_op jit(solution)/shard_map/ppermute | solution.py:44
  70.7 2.3 %two_filters.3 = (bf16[512,128]{1,0:T(8,128)(2,1)S(1)}, bf16[512,256]{1,0:T(8,128)(2,1)S(1)}, f32[256,256]{1,0:T(8,128)S(1)}) custom-call(f32[2,128]{1,0:T(2,128)S(1)} %bitcast.20, f32[2,4,512,128]{3,2,1,0:T(8,128)S(1)} %get-tuple-element.83.spectra_ref, bf16[512,256]{1,0:T(8,128)(2,1)S(1)} %copy-done.2, bf16[256,512]{1,0:T(8,128)(2,1)S(1)} %copy-done.1, ...), custom_call_target="tpu_custom_call" | custom-call | flops 536870912 | bytes 1048576 | tf_op jit(solution)/shard_map/two_filters/pallas_call | solution.py:367
  73.0 0.2 collective-permute-start.22
  73.2 0.2 own_half.3.keep_ref
  73.4 1.9 %hold_exit.1 = (bf16[1024,1024]{1,0:T(8,128)(2,1)S(1)}, bf16[4,128,256]{2,1,0:T(8,128)(2,1)S(1)}, bf16[128,1024]{1,0:T(8,128)(2,1)S(1)}, bf16[128,1024]{1,0:T(8,...) custom-call(bf16[1024,1024]{1,0:T(8,128)(2,1)} %bitcast.11, ...), custom_call_target="tpu_custom_call" | custom-call | bytes 3932160 | tf_op jit(solution)/shard_map/hold_exit/pallas_call | solution.py:204
  75.3 5.0 %collective-permute-done.22.come_ref = bf16[512,128]{1,0:T(8,128)(2,1)S(1)} collective-permute-done((bf16[512,128]{1,0:T(8,128)(2,1)S(1)}, bf16[512,128]{1,0:T(8,128)(2,1)S(1)}, u32[]{:S(2)}, u32[]{:S(2)}) %collective-permute-start.22) | collective-permute-done | bytes 131104 | tf_op jit(solution)/shard_map/ppermute | solution.py:44
  80.3 0.1 second_gate.3
  80.4 1.0 %collective-permute-done.28.refs_4_ = bf16[128,1024]{1,0:T(8,128)(2,1)S(1)} collective-permute-done((bf16[128,1024]{1,0:T(8,128)(2,1)S(1)}, bf16[128,1024]{1,0:T(8,128)(2,1)S(1)}, u32[]{:S(2)}, u32[]{:S(2)}) %collective-permute-start.28) | collective-permute-done | bytes 262176 | tf_op jit(solution)/shard_map/ppermute | solution.py:44
  81.4 0.5 gradient_away.1
  81.9 1.6 %collective-permute-start.29 = (bf16[128,1024]{1,0:T(8,128)(2,1)S(1)}, bf16[128,1024]{1,0:T(8,128)(2,1)S(1)}, u32[]{:S(2)}, u32[]{:S(2)}) collective-permute-start(bf16[128,1024]{1,0:T(8,128)(2,1)S(1)} %gradient_away.1), channel_id=1, source_target_pairs={{0,4},{1,5},{2,6},{3,7},{4,0},{5,1},{6,2},{7,3},{8,12},{9,13},{10,... | collective-permute-start | bytes 786440 | tf_op jit(solution)/shard_map/ppermute | solution.py:44
  83.5 2.4 %collective-permute-start.24 = (bf16[128,256]{1,0:T(8,128)(2,1)S(1)}, bf16[128,256]{1,0:T(8,128)(2,1)S(1)}, u32[]{:S(2)}, u32[]{:S(2)}) collective-permute-start(bf16[128,256]{1,0:T(8,128)(2,1)S(1)} %get-tuple-element.150), channel_id=1, source_target_pairs={{0,3},{1,2},{2,1},{3,0},{4,7},{5,6},{6,5},{7,4},{8,11},{9,10},{10,... | collective-permute-start | bytes 196616 | tf_op jit(solution)/shard_map/ppermute | solution.py:44
  86.0 0.3 collective-permute-start.25
  86.2 1.5 %collective-permute-start.26 = (bf16[128,256]{1,0:T(8,128)(2,1)S(1)}, bf16[128,256]{1,0:T(8,128)(2,1)S(1)}, u32[]{:S(2)}, u32[]{:S(2)}) collective-permute-start(bf16[128,256]{1,0:T(8,128)(2,1)S(1)} %get-tuple-element.152), channel_id=1, source_target_pairs={{0,1},{1,0},{2,3},{3,2},{4,5},{5,4},{6,7},{7,6},{8,9},{9,8},{10,11... | collective-permute-start | bytes 196616 | tf_op jit(solution)/shard_map/ppermute | solution.py:44
  87.7 3.0 %collective-permute-done.24.rest_0_ = bf16[128,256]{1,0:T(8,128)(2,1)S(1)} collective-permute-done((bf16[128,256]{1,0:T(8,128)(2,1)S(1)}, bf16[128,256]{1,0:T(8,128)(2,1)S(1)}, u32[]{:S(2)}, u32[]{:S(2)}) %collective-permute-start.24) | collective-permute-done | bytes 65568 | tf_op jit(solution)/shard_map/ppermute | solution.py:44
  90.7 0.7 collective-permute-done.25.rest_1_
  91.4 1.2 %exit_projection.3 = bf16[128,1024]{1,0:T(8,128)(2,1)} custom-call(s32[1]{0:T(128)} %bitcast.choice_ref, bf16[128,1024]{1,0:T(8,128)(2,1)S(1)} %collective-permute-done.13.x_ref, bf16[128,1024]{1,0:T(8,128)(2,1)S(1)} %get-tuple-element.114.other_ref, bf16[1024,1024]{1,0:T(8,128)(2,1)S(1)} %get-tuple-element.148.weight_ref, ...), custom_call_target="tpu_custom_call" | custom-call | flops 268435456 | bytes 2097152 | tf_op jit(solution)/shard_map/exit_projection/pallas_call | solution.py:439
  92.6 0.5 gradient_mine.1
  93.0 1.8 %collective-permute-done.29 = bf16[128,1024]{1,0:T(8,128)(2,1)S(1)} collective-permute-done((bf16[128,1024]{1,0:T(8,128)(2,1)S(1)}, bf16[128,1024]{1,0:T(8,128)(2,1)S(1)}, u32[]{:S(2)}, u32[]{:S(2)}) %collective-permute-start.29) | collective-permute-done | bytes 262176 | tf_op jit(solution)/shard_map/ppermute | solution.py:44
  94.9 0.9 add_bitcast_fusion
  (48 shorter events, 0.1 us)
Async XLA Ops:
  0.6 18.3 %copy-start.2 = (bf16[512,256]{1,0:T(8,128)(2,1)S(1)}, bf16[512,256]{1,0:T(8,128)(2,1)}, u32[]{:S(2)}) copy-start(bf16[512,256]{1,0:T(8,128)(2,1)} %constant.13.clone.forward_ref) | copy-start | bytes 786436
  0.6 18.2 %copy-start.5 = (bf16[1,2,128,1024]{3,2,1,0:T(8,128)(2,1)S(1)}, bf16[1,2,128,1024]{3,2,1,0:T(8,128)(2,1)}, u32[]{:S(2)}) copy-start(bf16[1,2,128,1024]{3,2,1,0:T(8,128)(2,1)} %param.23) | copy-start | bytes 1572868
  0.7 18.2 %copy-start.11 = (bf16[32,1024]{1,0:T(8,128)(2,1)S(1)}, bf16[32,1024]{1,0:T(8,128)(2,1)}, u32[]{:S(2)}) copy-start(bf16[32,1024]{1,0:T(8,128)(2,1)} %amino_ref.1) | copy-start | bytes 196612
  0.7 18.2 %copy-start.13 = (bf16[8,1024]{1,0:T(8,128)(2,1)S(1)}, bf16[8,1024]{1,0:T(8,128)(2,1)}, u32[]{:S(2)}) copy-start(bf16[8,1024]{1,0:T(8,128)(2,1)} %polymer_ref.1) | copy-start | bytes 49156
  0.7 18.2 %copy-start.15 = (s32[8]{0:T(128)S(1)}, s32[8]{0:T(128)}, u32[]{:S(2)}) copy-start(s32[8]{0:T(128)} %sizes_ref.1) | copy-start | bytes 100
  0.7 18.2 %copy-start.16 = (s32[128]{0:T(128)S(1)}, s32[128]{0:T(128)}, u32[]{:S(2)}) copy-start(s32[128]{0:T(128)} %param.14) | copy-start | bytes 1540
  3.8 15.1 %copy-start.4 = (f32[1,2,128,1024]{3,2,1,0:T(8,128)S(1)}, f32[1,2,128,1024]{3,2,1,0:T(8,128)}, u32[]{:S(2)}) copy-start(f32[1,2,128,1024]{3,2,1,0:T(8,128)} %param.20) | copy-start | bytes 3145732
  3.8 20.5 %copy-start.1 = (bf16[256,512]{1,0:T(8,128)(2,1)S(1)}, bf16[256,512]{1,0:T(8,128)(2,1)}, u32[]{:S(2)}) copy-start(bf16[256,512]{1,0:T(8,128)(2,1)} %constant.14.clone.backward_ref) | copy-start | bytes 786436
  3.9 20.5 %copy-start.12 = (f32[1,2,128]{2,1,0:T(2,128)S(1)}, f32[1,2,128]{2,1,0:T(2,128)}, u32[]{:S(2)}) copy-start(f32[1,2,128]{2,1,0:T(2,128)} %param.21) | copy-start | bytes 3076
  3.9 9.9 %collective-permute-start = (bf16[128,256]{1,0:T(8,128)(2,1)S(1)}, bf16[128,256]{1,0:T(8,128)(2,1)S(1)}, u32[]{:S(2)}, u32[]{:S(2)}) collective-permute-start(bf16[128,256]{1,0:T(8,128)(2,1)S(1)} %get-tuple-element.84), channel_id=1, source_target_pairs={{0,4},{1,5},{2,6},{3,7},{4,0},{5,1},{6,2},{7,3},{8,12},{9,13},{10,... | collective-permute-start | bytes 196616 | tf_op jit(solution)/shard_map/ppermute | solution.py:44
  8.0 9.4 %collective-permute-start.1 = (bf16[128,256]{1,0:T(8,128)(2,1)S(1)}, bf16[128,256]{1,0:T(8,128)(2,1)S(1)}, u32[]{:S(2)}, u32[]{:S(2)}) collective-permute-start(bf16[128,256]{1,0:T(8,128)(2,1)S(1)} %get-tuple-element.85), channel_id=1, source_target_pairs={{0,5},{1,4},{2,7},{3,6},{4,1},{5,0},{6,3},{7,2},{8,13},{9,12},{10,... | collective-permute-start | bytes 196616 | tf_op jit(solution)/shard_map/ppermute | solution.py:44
  10.2 14.1 %collective-permute-start.4 = (bf16[128,512]{1,0:T(8,128)(2,1)S(1)}, bf16[128,512]{1,0:T(8,128)(2,1)S(1)}, u32[]{:S(2)}, u32[]{:S(2)}) collective-permute-start(bf16[128,512]{1,0:T(8,128)(2,1)S(1)} %get-tuple-element.90), channel_id=1, source_target_pairs={{0,3},{1,2},{2,1},{3,0},{4,7},{5,6},{6,5},{7,4},{8,11},{9,10},{10,... | collective-permute-start | bytes 393224 | tf_op jit(solution)/shard_map/ppermute | solution.py:44
  11.8 12.5 %collective-permute-start.5 = (bf16[128,512]{1,0:T(8,128)(2,1)S(1)}, bf16[128,512]{1,0:T(8,128)(2,1)S(1)}, u32[]{:S(2)}, u32[]{:S(2)}) collective-permute-start(bf16[128,512]{1,0:T(8,128)(2,1)S(1)} %get-tuple-element.91), channel_id=1, source_target_pairs={{0,2},{1,3},{2,0},{3,1},{4,6},{5,7},{6,4},{7,5},{8,10},{9,11},{10,... | collective-permute-start | bytes 393224 | tf_op jit(solution)/shard_map/ppermute | solution.py:44
  12.0 12.3 %collective-permute-start.6 = (bf16[128,512]{1,0:T(8,128)(2,1)S(1)}, bf16[128,512]{1,0:T(8,128)(2,1)S(1)}, u32[]{:S(2)}, u32[]{:S(2)}) collective-permute-start(bf16[128,512]{1,0:T(8,128)(2,1)S(1)} %get-tuple-element.92), channel_id=1, source_target_pairs={{0,1},{1,0},{2,3},{3,2},{4,5},{5,4},{6,7},{7,6},{8,9},{9,8},{10,11... | collective-permute-start | bytes 393224 | tf_op jit(solution)/shard_map/ppermute | solution.py:44
  13.7 8.5 %collective-permute-start.2 = (bf16[128,256]{1,0:T(8,128)(2,1)S(1)}, bf16[128,256]{1,0:T(8,128)(2,1)S(1)}, u32[]{:S(2)}, u32[]{:S(2)}) collective-permute-start(bf16[128,256]{1,0:T(8,128)(2,1)S(1)} %get-tuple-element.86), channel_id=1, source_target_pairs={{0,6},{1,7},{2,4},{3,5},{4,2},{5,3},{6,0},{7,1},{8,14},{9,15},{10,... | collective-permute-start | bytes 196616 | tf_op jit(solution)/shard_map/ppermute | solution.py:44
  17.3 7.0 %collective-permute-start.3 = (bf16[128,256]{1,0:T(8,128)(2,1)S(1)}, bf16[128,256]{1,0:T(8,128)(2,1)S(1)}, u32[]{:S(2)}, u32[]{:S(2)}) collective-permute-start(bf16[128,256]{1,0:T(8,128)(2,1)S(1)} %get-tuple-element.87), channel_id=1, source_target_pairs={{0,7},{1,6},{2,5},{3,4},{4,3},{5,2},{6,1},{7,0},{8,15},{9,14},{10,... | collective-permute-start | bytes 196616 | tf_op jit(solution)/shard_map/ppermute | solution.py:44
  21.1 21.5 %copy-start = (bf16[1,1024,1024]{2,1,0:T(8,128)(2,1)S(1)}, bf16[1,1024,1024]{2,1,0:T(8,128)(2,1)}, u32[]{:S(2)}) copy-start(bf16[1,1024,1024]{2,1,0:T(8,128)(2,1)} %param.22) | copy-start | bytes 6291460
  21.1 21.5 %copy-start.3 = (bf16[1,128,1024]{2,1,0:T(8,128)(2,1)S(1)}, bf16[1,128,1024]{2,1,0:T(8,128)(2,1)}, u32[]{:S(2)}) copy-start(bf16[1,128,1024]{2,1,0:T(8,128)(2,1)} %param.13) | copy-start | bytes 786436
  26.6 7.6 %collective-permute-start.7 = (bf16[512,128]{1,0:T(8,128)(2,1)S(1)}, bf16[512,128]{1,0:T(8,128)(2,1)S(1)}, u32[]{:S(2)}, u32[]{:S(2)}) collective-permute-start(bf16[512,128]{1,0:T(8,128)(2,1)S(1)} %get-tuple-element.96), channel_id=1, source_target_pairs={{0,4},{1,5},{2,6},{3,7},{4,0},{5,1},{6,2},{7,3},{8,12},{9,13},{10,... | collective-permute-start | bytes 393224 | tf_op jit(solution)/shard_map/ppermute | solution.py:44
  27.0 15.5 %collective-permute-start.11 = (bf16[128,1024]{1,0:T(8,128)(2,1)}, bf16[128,1024]{1,0:T(8,128)(2,1)S(1)}, u32[]{:S(2)}, u32[]{:S(2)}) collective-permute-start(bf16[128,1024]{1,0:T(8,128)(2,1)} %get-tuple-element.136.refs_4_), channel_id=1, source_target_pairs={{0,1},{1,0},{2,3},{3,2},{4,5},{5,4},{6,7},{7,6},{8,9},{9,8},{10,11... | collective-permute-start | bytes 786440 | tf_op jit(solution)/shard_map/ppermute | solution.py:44
  28.5 14.0 %collective-permute-start.12 = (bf16[128,1024]{1,0:T(8,128)(2,1)}, bf16[128,1024]{1,0:T(8,128)(2,1)S(1)}, u32[]{:S(2)}, u32[]{:S(2)}) collective-permute-start(bf16[128,1024]{1,0:T(8,128)(2,1)} %get-tuple-element.139.refs_7_), channel_id=1, source_target_pairs={{0,2},{1,3},{2,0},{3,1},{4,6},{5,7},{6,4},{7,5},{8,10},{9,11},{10,... | collective-permute-start | bytes 786440 | tf_op jit(solution)/shard_map/ppermute | solution.py:44
  35.0 5.7 %collective-permute-start.8 = (bf16[128,256]{1,0:T(8,128)(2,1)S(1)}, bf16[128,256]{1,0:T(8,128)(2,1)S(1)}, u32[]{:S(2)}, u32[]{:S(2)}) collective-permute-start(bf16[128,256]{1,0:T(8,128)(2,1)S(1)} %get-tuple-element.98), channel_id=1, source_target_pairs={{0,3},{1,2},{2,1},{3,0},{4,7},{5,6},{6,5},{7,4},{8,11},{9,10},{10,... | collective-permute-start | bytes 196616 | tf_op jit(solution)/shard_map/ppermute | solution.py:44
  35.6 6.8 %collective-permute-start.9 = (bf16[128,256]{1,0:T(8,128)(2,1)S(1)}, bf16[128,256]{1,0:T(8,128)(2,1)S(1)}, u32[]{:S(2)}, u32[]{:S(2)}) collective-permute-start(bf16[128,256]{1,0:T(8,128)(2,1)S(1)} %get-tuple-element.99), channel_id=1, source_target_pairs={{0,2},{1,3},{2,0},{3,1},{4,6},{5,7},{6,4},{7,5},{8,10},{9,11},{10,... | collective-permute-start | bytes 196616 | tf_op jit(solution)/shard_map/ppermute | solution.py:44
  37.8 4.7 %collective-permute-start.10 = (bf16[128,256]{1,0:T(8,128)(2,1)S(1)}, bf16[128,256]{1,0:T(8,128)(2,1)S(1)}, u32[]{:S(2)}, u32[]{:S(2)}) collective-permute-start(bf16[128,256]{1,0:T(8,128)(2,1)S(1)} %get-tuple-element.100), channel_id=1, source_target_pairs={{0,1},{1,0},{2,3},{3,2},{4,5},{5,4},{6,7},{7,6},{8,9},{9,8},{10,11... | collective-permute-start | bytes 196616 | tf_op jit(solution)/shard_map/ppermute | solution.py:44
  40.8 7.0 %collective-permute-start.14 = (bf16[128,1024]{1,0:T(8,128)(2,1)}, bf16[128,1024]{1,0:T(8,128)(2,1)}, u32[]{:S(2)}, u32[]{:S(2)}) collective-permute-start(bf16[128,1024]{1,0:T(8,128)(2,1)} %get-tuple-element.139.refs_7_), channel_id=1, source_target_pairs={{0,1},{1,0},{2,3},{3,2},{4,5},{5,4},{6,7},{7,6},{8,9},{9,8},{10,11... | collective-permute-start | bytes 786440 | tf_op jit(solution)/shard_map/ppermute | solution.py:44
  42.5 2.0 %copy-start.8 = (bf16[128,1024]{1,0:T(8,128)(2,1)}, bf16[128,1024]{1,0:T(8,128)(2,1)S(1)}, u32[]{:S(2)}) copy-start(bf16[128,1024]{1,0:T(8,128)(2,1)S(1)} %collective-permute-done.11.refs_3_) | copy-start | bytes 786436
  42.5 1.8 %copy-start.6 = (bf16[128,1024]{1,0:T(8,128)(2,1)}, bf16[128,1024]{1,0:T(8,128)(2,1)S(1)}, u32[]{:S(2)}) copy-start(bf16[128,1024]{1,0:T(8,128)(2,1)S(1)} %collective-permute-done.12.refs_5_) | copy-start | bytes 786436
  43.0 4.7 %collective-permute-start.13 = (bf16[128,1024]{1,0:T(8,128)(2,1)S(1)}, bf16[128,1024]{1,0:T(8,128)(2,1)S(1)}, u32[]{:S(2)}, u32[]{:S(2)}) collective-permute-start(bf16[128,1024]{1,0:T(8,128)(2,1)S(1)} %exit_projection.2), channel_id=1, source_target_pairs={{0,8},{8,16},{16,24},{1,9},{9,17},{17,25},{2,10},{10,18},{18,26},{... | collective-permute-start | bytes 786440 | tf_op jit(solution)/shard_map/ppermute | solution.py:546
  44.4 24.2 %collective-permute-start.23 = (bf16[128,1024]{1,0:T(8,128)(2,1)}, bf16[128,1024]{1,0:T(8,128)(2,1)}, u32[]{:S(2)}, u32[]{:S(2)}) collective-permute-start(bf16[128,1024]{1,0:T(8,128)(2,1)} %get-tuple-element.136.refs_4_), channel_id=1, source_target_pairs={{0,2},{1,3},{2,0},{3,1},{4,6},{5,7},{6,4},{7,5},{8,10},{9,11},{10,... | collective-permute-start | bytes 786440 | tf_op jit(solution)/shard_map/ppermute | solution.py:44
  44.5 3.3 %copy-start.14 = (f32[1,1024]{1,0:T(1,128)S(1)}, f32[1,1024]{1,0:T(1,128)}, u32[]{:S(2)}) copy-start(f32[1,1024]{1,0:T(1,128)} %gain_ref.3) | copy-start | bytes 12292
  48.3 21.4 %copy-start.7 = (bf16[128,1024]{1,0:T(8,128)(2,1)S(1)}, bf16[128,1024]{1,0:T(8,128)(2,1)}, u32[]{:S(2)}) copy-start(bf16[128,1024]{1,0:T(8,128)(2,1)} %copy-done.6) | copy-start | bytes 786436
  48.4 8.0 %collective-permute-start.15 = (bf16[128,256]{1,0:T(8,128)(2,1)S(1)}, bf16[128,256]{1,0:T(8,128)(2,1)S(1)}, u32[]{:S(2)}, u32[]{:S(2)}) collective-permute-start(bf16[128,256]{1,0:T(8,128)(2,1)S(1)} %get-tuple-element.116), channel_id=1, source_target_pairs={{0,4},{1,5},{2,6},{3,7},{4,0},{5,1},{6,2},{7,3},{8,12},{9,13},{10,... | collective-permute-start | bytes 196616 | tf_op jit(solution)/shard_map/ppermute | solution.py:44
  51.0 9.7 %collective-permute-start.16 = (bf16[128,256]{1,0:T(8,128)(2,1)S(1)}, bf16[128,256]{1,0:T(8,128)(2,1)S(1)}, u32[]{:S(2)}, u32[]{:S(2)}) collective-permute-start(bf16[128,256]{1,0:T(8,128)(2,1)S(1)} %get-tuple-element.117), channel_id=1, source_target_pairs={{0,5},{1,4},{2,7},{3,6},{4,1},{5,0},{6,3},{7,2},{8,13},{9,12},{10,... | collective-permute-start | bytes 196616 | tf_op jit(solution)/shard_map/ppermute | solution.py:44
  52.2 9.4 %collective-permute-start.17 = (bf16[128,256]{1,0:T(8,128)(2,1)S(1)}, bf16[128,256]{1,0:T(8,128)(2,1)S(1)}, u32[]{:S(2)}, u32[]{:S(2)}) collective-permute-start(bf16[128,256]{1,0:T(8,128)(2,1)S(1)} %get-tuple-element.118), channel_id=1, source_target_pairs={{0,6},{1,7},{2,4},{3,5},{4,2},{5,3},{6,0},{7,1},{8,14},{9,15},{10,... | collective-permute-start | bytes 196616 | tf_op jit(solution)/shard_map/ppermute | solution.py:44
  54.9 18.6 %copy-start.9 = (bf16[128,1024]{1,0:T(8,128)(2,1)S(1)}, bf16[128,1024]{1,0:T(8,128)(2,1)}, u32[]{:S(2)}) copy-start(bf16[128,1024]{1,0:T(8,128)(2,1)} %copy-done.8) | copy-start | bytes 786436
  54.9 18.6 %copy-start.10 = (bf16[4,128,256]{2,1,0:T(8,128)(2,1)S(1)}, bf16[4,128,256]{2,1,0:T(8,128)(2,1)}, u32[]{:S(2)}) copy-start(bf16[4,128,256]{2,1,0:T(8,128)(2,1)} %get-tuple-element.133.refs_1_) | copy-start | bytes 786436
  55.8 12.8 %collective-permute-start.19 = (bf16[128,512]{1,0:T(8,128)(2,1)S(1)}, bf16[128,512]{1,0:T(8,128)(2,1)S(1)}, u32[]{:S(2)}, u32[]{:S(2)}) collective-permute-start(bf16[128,512]{1,0:T(8,128)(2,1)S(1)} %get-tuple-element.121), channel_id=1, source_target_pairs={{0,3},{1,2},{2,1},{3,0},{4,7},{5,6},{6,5},{7,4},{8,11},{9,10},{10,... | collective-permute-start | bytes 393224 | tf_op jit(solution)/shard_map/ppermute | solution.py:44
  56.4 12.2 %collective-permute-start.20 = (bf16[128,512]{1,0:T(8,128)(2,1)S(1)}, bf16[128,512]{1,0:T(8,128)(2,1)S(1)}, u32[]{:S(2)}, u32[]{:S(2)}) collective-permute-start(bf16[128,512]{1,0:T(8,128)(2,1)S(1)} %get-tuple-element.122), channel_id=1, source_target_pairs={{0,2},{1,3},{2,0},{3,1},{4,6},{5,7},{6,4},{7,5},{8,10},{9,11},{10,... | collective-permute-start | bytes 393224 | tf_op jit(solution)/shard_map/ppermute | solution.py:44
  60.6 7.9 %collective-permute-start.21 = (bf16[128,512]{1,0:T(8,128)(2,1)S(1)}, bf16[128,512]{1,0:T(8,128)(2,1)S(1)}, u32[]{:S(2)}, u32[]{:S(2)}) collective-permute-start(bf16[128,512]{1,0:T(8,128)(2,1)S(1)} %get-tuple-element.123), channel_id=1, source_target_pairs={{0,1},{1,0},{2,3},{3,2},{4,5},{5,4},{6,7},{7,6},{8,9},{9,8},{10,11... | collective-permute-start | bytes 393224 | tf_op jit(solution)/shard_map/ppermute | solution.py:44
  61.6 7.0 %collective-permute-start.18 = (bf16[128,256]{1,0:T(8,128)(2,1)S(1)}, bf16[128,256]{1,0:T(8,128)(2,1)S(1)}, u32[]{:S(2)}, u32[]{:S(2)}) collective-permute-start(bf16[128,256]{1,0:T(8,128)(2,1)S(1)} %get-tuple-element.119), channel_id=1, source_target_pairs={{0,7},{1,6},{2,5},{3,4},{4,3},{5,2},{6,1},{7,0},{8,15},{9,14},{10,... | collective-permute-start | bytes 196616 | tf_op jit(solution)/shard_map/ppermute | solution.py:44
  68.6 11.8 %collective-permute-start.27 = (bf16[128,1024]{1,0:T(8,128)(2,1)}, bf16[128,1024]{1,0:T(8,128)(2,1)S(1)}, u32[]{:S(2)}, u32[]{:S(2)}) collective-permute-start(bf16[128,1024]{1,0:T(8,128)(2,1)} %collective-permute-done.23.refs_2_), channel_id=1, source_target_pairs={{0,1},{1,0},{2,3},{3,2},{4,5},{5,4},{6,7},{7,6},{8,9},{9,8},{10,11... | collective-permute-start | bytes 786440 | tf_op jit(solution)/shard_map/ppermute | solution.py:44
  69.7 11.7 %collective-permute-start.28 = (bf16[128,1024]{1,0:T(8,128)(2,1)S(1)}, bf16[128,1024]{1,0:T(8,128)(2,1)S(1)}, u32[]{:S(2)}, u32[]{:S(2)}) collective-permute-start(bf16[128,1024]{1,0:T(8,128)(2,1)S(1)} %copy-done.7), channel_id=1, source_target_pairs={{0,1},{1,0},{2,3},{3,2},{4,5},{5,4},{6,7},{7,6},{8,9},{9,8},{10,11... | collective-permute-start | bytes 786440 | tf_op jit(solution)/shard_map/ppermute | solution.py:44
  73.0 7.4 %collective-permute-start.22 = (bf16[512,128]{1,0:T(8,128)(2,1)S(1)}, bf16[512,128]{1,0:T(8,128)(2,1)S(1)}, u32[]{:S(2)}, u32[]{:S(2)}) collective-permute-start(bf16[512,128]{1,0:T(8,128)(2,1)S(1)} %get-tuple-element.125), channel_id=1, source_target_pairs={{0,4},{1,5},{2,6},{3,7},{4,0},{5,1},{6,2},{7,3},{8,12},{9,13},{10,... | collective-permute-start | bytes 393224 | tf_op jit(solution)/shard_map/ppermute | solution.py:44
  81.9 12.9 %collective-permute-start.29 = (bf16[128,1024]{1,0:T(8,128)(2,1)S(1)}, bf16[128,1024]{1,0:T(8,128)(2,1)S(1)}, u32[]{:S(2)}, u32[]{:S(2)}) collective-permute-start(bf16[128,1024]{1,0:T(8,128)(2,1)S(1)} %gradient_away.1), channel_id=1, source_target_pairs={{0,4},{1,5},{2,6},{3,7},{4,0},{5,1},{6,2},{7,3},{8,12},{9,13},{10,... | collective-permute-start | bytes 786440 | tf_op jit(solution)/shard_map/ppermute | solution.py:44
  83.5 7.2 %collective-permute-start.24 = (bf16[128,256]{1,0:T(8,128)(2,1)S(1)}, bf16[128,256]{1,0:T(8,128)(2,1)S(1)}, u32[]{:S(2)}, u32[]{:S(2)}) collective-permute-start(bf16[128,256]{1,0:T(8,128)(2,1)S(1)} %get-tuple-element.150), channel_id=1, source_target_pairs={{0,3},{1,2},{2,1},{3,0},{4,7},{5,6},{6,5},{7,4},{8,11},{9,10},{10,... | collective-permute-start | bytes 196616 | tf_op jit(solution)/shard_map/ppermute | solution.py:44
  86.0 5.4 %collective-permute-start.25 = (bf16[128,256]{1,0:T(8,128)(2,1)S(1)}, bf16[128,256]{1,0:T(8,128)(2,1)S(1)}, u32[]{:S(2)}, u32[]{:S(2)}) collective-permute-start(bf16[128,256]{1,0:T(8,128)(2,1)S(1)} %get-tuple-element.151), channel_id=1, source_target_pairs={{0,2},{1,3},{2,0},{3,1},{4,6},{5,7},{6,4},{7,5},{8,10},{9,11},{10,... | collective-permute-start | bytes 196616 | tf_op jit(solution)/shard_map/ppermute | solution.py:44
  86.2 5.1 %collective-permute-start.26 = (bf16[128,256]{1,0:T(8,128)(2,1)S(1)}, bf16[128,256]{1,0:T(8,128)(2,1)S(1)}, u32[]{:S(2)}, u32[]{:S(2)}) collective-permute-start(bf16[128,256]{1,0:T(8,128)(2,1)S(1)} %get-tuple-element.152), channel_id=1, source_target_pairs={{0,1},{1,0},{2,3},{3,2},{4,5},{5,4},{6,7},{7,6},{8,9},{9,8},{10,11... | collective-permute-start | bytes 196616 | tf_op jit(solution)/shard_map/ppermute | solution.py:44

commit v3 on v2

--- a/solution.py
+++ b/solution.py
@@ -544,14 +544,14 @@
     seeds |= early
     first_out = exit_projection(never, resident, resident, weight_out, home, near)
     handed = lax.ppermute(first_out, "section", [(i, i + 1) for i in range(sections - 1)])
-    weight_again = tie(weight_in, first_out)
+    weight_again = tie(weight_in, first_hyenas)
     if aligned:
         weight_again = hold([weight_again], "hold_entry")[0]
     handed, seeds[1, 1], weight_again = lax.optimization_barrier((handed, seeds[1, 1], weight_again))
-    spread([(0, d) for d in lines], home)
+    spread([(0, d) for d in lines] + [(1, d) for d in range(3, group, 2)], home)
 
     def second_beside(come):
-        spread([(step, d) for step in range(2) for d in range(3, group, 2)], come)
+        spread([(0, d) for d in range(3, group, 2)], come)
 
         def held(keep):
             early = [weight_out, first_hyenas] + [seeds[step, d] for step in range(2) for d in near if d % 2 == 0 or d == 1]

time: 95.9 us -> 95.1 us (level)
  starting transfers between devices: 45.9 us -> 43.5 us
  waiting for transfers between devices: 27 us -> 28.6 us
    ppermute x29, starting transfers between devices: 44.6 us -> 42.2 us  [exchange(): return lax.ppermute(value, 'seq', [(i, i ^ distance) for i in range(peers)])]
    ppermute x29, waiting for transfers between devices: 27 us -> 28.6 us  [exchange(): return lax.ppermute(value, 'seq', [(i, i ^ distance) for i in range(peers)])]
  transfers between devices with their start and end apart: 30 -> 30, of which waited for: 12 -> 11; matrix products, arithmetic and copies ran while one was open for 0% -> 0% of each run, Pallas kernels for 16% -> 16%
where the time goes in v3:
time: 95.1 us; the launch traced here: 94.9 us
  starting transfers between devices  43.5 us (46%)
  waiting for transfers between devices  28.6 us (30%)
  Pallas kernels  20.9 us (22%)
  between operations  1.01 us (1%)
    ppermute x29, starting transfers between devices, exchange(): return lax.ppermute(value, 'seq', [(i, i ^ distance) for i in range(peers)])  42.2 us
    ppermute x29, waiting for transfers between devices, exchange(): return lax.ppermute(value, 'seq', [(i, i ^ distance) for i in range(peers)])  28.6 us
    pallas_call x2, Pallas kernels, hold(): pl.pallas_call(functools.partial(hold_kernel, count), out_shape=tuple((pl...  4.69 us
    pallas_call x2, Pallas kernels, filtered(): pl.pallas_call(functools.partial(filter_kernel, order), out_shape=(out, k...  4.55 us
    pallas_call x1, Pallas kernels, project(): pl.pallas_call(functools.partial(far_stream_kernel, far), out_shape=outs,...  3.13 us
    pallas_call x1, Pallas kernels, prepare(): pl.pallas_call(prepare_kernel, out_shape=(jax.ShapeDtypeStruct((2, chunks...  2.12 us
  transfers between devices with their start and end apart: 30, of which 11 were waited for; matrix products, arithmetic and copies ran while one was open for 0% of the time, Pallas kernels for 16%

profile of v3, /device:TPU:0, one launch (start us, length us, event | category | flops | bytes accessed | tf_op | source)
XLA Modules:
  0.0 94.9 jit_solution(420541944804897628)
XLA Ops:
  0.6 0.0 copy-start.2
  0.7 3.1 %far_pieces_streamed.1 = (bf16[128,256]{1,0:T(8,128)(2,1)S(1)}, bf16[128,256]{1,0:T(8,128)(2,1)S(1)}, bf16[128,256]{1,0:T(8,128)(2,1)S(1)}, bf16[128,256]{1,0:T(...) custom-call(bf16[128,1024]{1,0:T(8,128)(2,1)} %bitcast.13, f32[1,1024]{1,0:T(1,128)} %gain_ref.3, ...), custom_call_target="tpu_custom_call" | custom-call | flops 268435456 | bytes 2097152 | tf_op jit(solution)/shard_map/far_pieces_streamed/pallas_call | solution.py:242
  3.8 0.0 copy-start.4
  3.8 0.0 copy-start.1
  3.9 0.0 copy-start.12
  3.9 4.1 %collective-permute-start = (bf16[128,256]{1,0:T(8,128)(2,1)S(1)}, bf16[128,256]{1,0:T(8,128)(2,1)S(1)}, u32[]{:S(2)}, u32[]{:S(2)}) collective-permute-start(bf16[128,256]{1,0:T(8,128)(2,1)S(1)} %get-tuple-element.84), channel_id=1, source_target_pairs={{0,4},{1,5},{2,6},{3,7},{4,0},{5,1},{6,2},{7,3},{8,12},{9,13},{10,... | collective-permute-start | bytes 196616 | tf_op jit(solution)/shard_map/ppermute | solution.py:44
  8.0 1.3 %collective-permute-start.1 = (bf16[128,256]{1,0:T(8,128)(2,1)S(1)}, bf16[128,256]{1,0:T(8,128)(2,1)S(1)}, u32[]{:S(2)}, u32[]{:S(2)}) collective-permute-start(bf16[128,256]{1,0:T(8,128)(2,1)S(1)} %get-tuple-element.85), channel_id=1, source_target_pairs={{0,5},{1,4},{2,7},{3,6},{4,1},{5,0},{6,3},{7,2},{8,13},{9,12},{10,... | collective-permute-start | bytes 196616 | tf_op jit(solution)/shard_map/ppermute | solution.py:44
  9.2 0.9 near_pieces.2
  10.2 1.6 %collective-permute-start.4 = (bf16[128,512]{1,0:T(8,128)(2,1)S(1)}, bf16[128,512]{1,0:T(8,128)(2,1)S(1)}, u32[]{:S(2)}, u32[]{:S(2)}) collective-permute-start(bf16[128,512]{1,0:T(8,128)(2,1)S(1)} %get-tuple-element.90), channel_id=1, source_target_pairs={{0,3},{1,2},{2,1},{3,0},{4,7},{5,6},{6,5},{7,4},{8,11},{9,10},{10,... | collective-permute-start | bytes 393224 | tf_op jit(solution)/shard_map/ppermute | solution.py:44
  11.8 0.2 collective-permute-start.5
  12.0 1.7 %collective-permute-start.6 = (bf16[128,512]{1,0:T(8,128)(2,1)S(1)}, bf16[128,512]{1,0:T(8,128)(2,1)S(1)}, u32[]{:S(2)}, u32[]{:S(2)}) collective-permute-start(bf16[128,512]{1,0:T(8,128)(2,1)S(1)} %get-tuple-element.92), channel_id=1, source_target_pairs={{0,1},{1,0},{2,3},{3,2},{4,5},{5,4},{6,7},{7,6},{8,9},{9,8},{10,11... | collective-permute-start | bytes 393224 | tf_op jit(solution)/shard_map/ppermute | solution.py:44
  13.7 3.6 %collective-permute-start.2 = (bf16[128,256]{1,0:T(8,128)(2,1)S(1)}, bf16[128,256]{1,0:T(8,128)(2,1)S(1)}, u32[]{:S(2)}, u32[]{:S(2)}) collective-permute-start(bf16[128,256]{1,0:T(8,128)(2,1)S(1)} %get-tuple-element.86), channel_id=1, source_target_pairs={{0,6},{1,7},{2,4},{3,5},{4,2},{5,3},{6,0},{7,1},{8,14},{9,15},{10,... | collective-permute-start | bytes 196616 | tf_op jit(solution)/shard_map/ppermute | solution.py:44
  17.3 1.6 %collective-permute-start.3 = (bf16[128,256]{1,0:T(8,128)(2,1)S(1)}, bf16[128,256]{1,0:T(8,128)(2,1)S(1)}, u32[]{:S(2)}, u32[]{:S(2)}) collective-permute-start(bf16[128,256]{1,0:T(8,128)(2,1)S(1)} %get-tuple-element.87), channel_id=1, source_target_pairs={{0,7},{1,6},{2,5},{3,4},{4,3},{5,2},{6,1},{7,0},{8,15},{9,14},{10,... | collective-permute-start | bytes 196616 | tf_op jit(solution)/shard_map/ppermute | solution.py:44
  18.9 2.1 %prepare.1 = (f32[2,4,512,128]{3,2,1,0:T(8,128)S(1)}, bf16[128,1024]{1,0:T(8,128)(2,1)S(1)}, bf16[128,1024]{1,0:T(8,128)(2,1)}, bf16[128,1024]{1,0:T(8,128)(2,1)}) custom-call(s32[8]{0:T(128)S(1)} %copy-done.15, s32[1,128]{1,0:T(1,128)S(1)} %bitcast.22, bf16[32,1024]{1,0:T(8,128)(2,1)S(1)} %copy-done.11, bf16[8,1024]{1,0:T(8,128)(2,1)S(1)} %copy-done.13, ...), custom_call_target="tpu_custom_call" | custom-call | flops 268435456 | bytes 2097152 | tf_op jit(solution)/shard_map/prepare/pallas_call | solution.py:97
  21.1 1.2 %collective-permute-done.2.rest_2_ = bf16[128,256]{1,0:T(8,128)(2,1)S(1)} collective-permute-done((bf16[128,256]{1,0:T(8,128)(2,1)S(1)}, bf16[128,256]{1,0:T(8,128)(2,1)S(1)}, u32[]{:S(2)}, u32[]{:S(2)}) %collective-permute-start.2) | collective-permute-done | bytes 65568 | tf_op jit(solution)/shard_map/ppermute | solution.py:44
  22.2 2.1 %collective-permute-done.3.rest_3_ = bf16[128,256]{1,0:T(8,128)(2,1)S(1)} collective-permute-done((bf16[128,256]{1,0:T(8,128)(2,1)S(1)}, bf16[128,256]{1,0:T(8,128)(2,1)S(1)}, u32[]{:S(2)}, u32[]{:S(2)}) %collective-permute-start.3) | collective-permute-done | bytes 65568 | tf_op jit(solution)/shard_map/ppermute | solution.py:44
  24.3 2.3 %two_filters.2 = (bf16[512,128]{1,0:T(8,128)(2,1)S(1)}, bf16[512,256]{1,0:T(8,128)(2,1)S(1)}, f32[256,256]{1,0:T(8,128)S(1)}) custom-call(f32[2,128]{1,0:T(2,128)S(1)} %bitcast.18, f32[2,4,512,128]{3,2,1,0:T(8,128)S(1)} %get-tuple-element.83.spectra_ref, bf16[512,256]{1,0:T(8,128)(2,1)S(1)} %copy-done.2, bf16[256,512]{1,0:T(8,128)(2,1)S(1)} %copy-done.1, ...), custom_call_target="tpu_custom_call" | custom-call | flops 536870912 | bytes 1048576 | tf_op jit(solution)/shard_map/two_filters/pallas_call | solution.py:367
  26.6 0.1 collective-permute-start.7
  26.7 0.2 own_half.2.keep_ref
  27.0 1.5 %collective-permute-start.11 = (bf16[128,1024]{1,0:T(8,128)(2,1)}, bf16[128,1024]{1,0:T(8,128)(2,1)S(1)}, u32[]{:S(2)}, u32[]{:S(2)}) collective-permute-start(bf16[128,1024]{1,0:T(8,128)(2,1)} %get-tuple-element.136.refs_4_), channel_id=1, source_target_pairs={{0,1},{1,0},{2,3},{3,2},{4,5},{5,4},{6,7},{7,6},{8,9},{9,8},{10,11... | collective-permute-start | bytes 786440 | tf_op jit(solution)/shard_map/ppermute | solution.py:44
  28.5 2.5 %collective-permute-start.12 = (bf16[128,1024]{1,0:T(8,128)(2,1)}, bf16[128,1024]{1,0:T(8,128)(2,1)S(1)}, u32[]{:S(2)}, u32[]{:S(2)}) collective-permute-start(bf16[128,1024]{1,0:T(8,128)(2,1)} %get-tuple-element.139.refs_7_), channel_id=1, source_target_pairs={{0,2},{1,3},{2,0},{3,1},{4,6},{5,7},{6,4},{7,5},{8,10},{9,11},{10,... | collective-permute-start | bytes 786440 | tf_op jit(solution)/shard_map/ppermute | solution.py:44
  31.0 3.3 %collective-permute-done.7.come_ref = bf16[512,128]{1,0:T(8,128)(2,1)S(1)} collective-permute-done((bf16[512,128]{1,0:T(8,128)(2,1)S(1)}, bf16[512,128]{1,0:T(8,128)(2,1)S(1)}, u32[]{:S(2)}, u32[]{:S(2)}) %collective-permute-start.7) | collective-permute-done | bytes 131104 | tf_op jit(solution)/shard_map/ppermute | solution.py:44
  34.2 0.8 second_gate.2
  35.0 0.6 collective-permute-start.8
  35.6 2.1 %collective-permute-start.9 = (bf16[128,256]{1,0:T(8,128)(2,1)S(1)}, bf16[128,256]{1,0:T(8,128)(2,1)S(1)}, u32[]{:S(2)}, u32[]{:S(2)}) collective-permute-start(bf16[128,256]{1,0:T(8,128)(2,1)S(1)} %get-tuple-element.99), channel_id=1, source_target_pairs={{0,2},{1,3},{2,0},{3,1},{4,6},{5,7},{6,4},{7,5},{8,10},{9,11},{10,... | collective-permute-start | bytes 196616 | tf_op jit(solution)/shard_map/ppermute | solution.py:44
  37.8 0.7 collective-permute-start.10
  38.5 2.3 %collective-permute-done.8.rest_0_ = bf16[128,256]{1,0:T(8,128)(2,1)S(1)} collective-permute-done((bf16[128,256]{1,0:T(8,128)(2,1)S(1)}, bf16[128,256]{1,0:T(8,128)(2,1)S(1)}, u32[]{:S(2)}, u32[]{:S(2)}) %collective-permute-start.8) | collective-permute-done | bytes 65568 | tf_op jit(solution)/shard_map/ppermute | solution.py:44
  40.8 1.7 %collective-permute-start.14 = (bf16[128,1024]{1,0:T(8,128)(2,1)}, bf16[128,1024]{1,0:T(8,128)(2,1)}, u32[]{:S(2)}, u32[]{:S(2)}) collective-permute-start(bf16[128,1024]{1,0:T(8,128)(2,1)} %get-tuple-element.139.refs_7_), channel_id=1, source_target_pairs={{0,1},{1,0},{2,3},{3,2},{4,5},{5,4},{6,7},{7,6},{8,9},{9,8},{10,11... | collective-permute-start | bytes 786440 | tf_op jit(solution)/shard_map/ppermute | solution.py:44
  42.5 0.5 exit_projection.2
  43.0 1.3 %collective-permute-start.13 = (bf16[128,1024]{1,0:T(8,128)(2,1)S(1)}, bf16[128,1024]{1,0:T(8,128)(2,1)S(1)}, u32[]{:S(2)}, u32[]{:S(2)}) collective-permute-start(bf16[128,1024]{1,0:T(8,128)(2,1)S(1)} %exit_projection.2), channel_id=1, source_target_pairs={{0,8},{8,16},{16,24},{1,9},{9,17},{17,25},{2,10},{10,18},{18,26},{... | collective-permute-start | bytes 786440 | tf_op jit(solution)/shard_map/ppermute | solution.py:546
  44.4 0.1 collective-permute-start.23
  44.5 0.0 copy-start.14
  44.5 2.8 %hold_entry.1.weight_ref = bf16[1024,3072]{1,0:T(8,128)(2,1)S(1)} custom-call(bf16[1024,3072]{1,0:T(8,128)(2,1)} %bitcast.24), custom_call_target="tpu_custom_call" | custom-call | bytes 6291456 | tf_op jit(solution)/shard_map/hold_entry/pallas_call | solution.py:204
  47.3 0.5 collective-permute-done.14.refs_6_
  47.8 0.6 far_pieces.1
  48.4 2.6 %collective-permute-start.15 = (bf16[128,256]{1,0:T(8,128)(2,1)S(1)}, bf16[128,256]{1,0:T(8,128)(2,1)S(1)}, u32[]{:S(2)}, u32[]{:S(2)}) collective-permute-start(bf16[128,256]{1,0:T(8,128)(2,1)S(1)} %get-tuple-element.116), channel_id=1, source_target_pairs={{0,4},{1,5},{2,6},{3,7},{4,0},{5,1},{6,2},{7,3},{8,12},{9,13},{10,... | collective-permute-start | bytes 196616 | tf_op jit(solution)/shard_map/ppermute | solution.py:44
  51.0 1.2 %collective-permute-start.16 = (bf16[128,256]{1,0:T(8,128)(2,1)S(1)}, bf16[128,256]{1,0:T(8,128)(2,1)S(1)}, u32[]{:S(2)}, u32[]{:S(2)}) collective-permute-start(bf16[128,256]{1,0:T(8,128)(2,1)S(1)} %get-tuple-element.117), channel_id=1, source_target_pairs={{0,5},{1,4},{2,7},{3,6},{4,1},{5,0},{6,3},{7,2},{8,13},{9,12},{10,... | collective-permute-start | bytes 196616 | tf_op jit(solution)/shard_map/ppermute | solution.py:44
  52.2 0.9 near_pieces.3
  53.1 1.7 %collective-permute-start.19 = (bf16[128,512]{1,0:T(8,128)(2,1)S(1)}, bf16[128,512]{1,0:T(8,128)(2,1)S(1)}, u32[]{:S(2)}, u32[]{:S(2)}) collective-permute-start(bf16[128,512]{1,0:T(8,128)(2,1)S(1)} %get-tuple-element.121), channel_id=1, source_target_pairs={{0,3},{1,2},{2,1},{3,0},{4,7},{5,6},{6,5},{7,4},{8,11},{9,10},{10,... | collective-permute-start | bytes 393224 | tf_op jit(solution)/shard_map/ppermute | solution.py:44
  54.8 0.5 collective-permute-start.20
  55.3 1.4 %collective-permute-start.21 = (bf16[128,512]{1,0:T(8,128)(2,1)S(1)}, bf16[128,512]{1,0:T(8,128)(2,1)S(1)}, u32[]{:S(2)}, u32[]{:S(2)}) collective-permute-start(bf16[128,512]{1,0:T(8,128)(2,1)S(1)} %get-tuple-element.123), channel_id=1, source_target_pairs={{0,1},{1,0},{2,3},{3,2},{4,5},{5,4},{6,7},{7,6},{8,9},{9,8},{10,11... | collective-permute-start | bytes 393224 | tf_op jit(solution)/shard_map/ppermute | solution.py:44
  56.7 2.7 %collective-permute-start.17 = (bf16[128,256]{1,0:T(8,128)(2,1)S(1)}, bf16[128,256]{1,0:T(8,128)(2,1)S(1)}, u32[]{:S(2)}, u32[]{:S(2)}) collective-permute-start(bf16[128,256]{1,0:T(8,128)(2,1)S(1)} %get-tuple-element.118), channel_id=1, source_target_pairs={{0,6},{1,7},{2,4},{3,5},{4,2},{5,3},{6,0},{7,1},{8,14},{9,15},{10,... | collective-permute-start | bytes 196616 | tf_op jit(solution)/shard_map/ppermute | solution.py:44
  59.4 2.3 %collective-permute-start.18 = (bf16[128,256]{1,0:T(8,128)(2,1)S(1)}, bf16[128,256]{1,0:T(8,128)(2,1)S(1)}, u32[]{:S(2)}, u32[]{:S(2)}) collective-permute-start(bf16[128,256]{1,0:T(8,128)(2,1)S(1)} %get-tuple-element.119), channel_id=1, source_target_pairs={{0,7},{1,6},{2,5},{3,4},{4,3},{5,2},{6,1},{7,0},{8,15},{9,14},{10,... | collective-permute-start | bytes 196616 | tf_op jit(solution)/shard_map/ppermute | solution.py:44
  61.6 3.8 %collective-permute-done.17.rest_2_ = bf16[128,256]{1,0:T(8,128)(2,1)S(1)} collective-permute-done((bf16[128,256]{1,0:T(8,128)(2,1)S(1)}, bf16[128,256]{1,0:T(8,128)(2,1)S(1)}, u32[]{:S(2)}, u32[]{:S(2)}) %collective-permute-start.17) | collective-permute-done | bytes 65568 | tf_op jit(solution)/shard_map/ppermute | solution.py:44
  65.5 0.6 collective-permute-start.28
  66.1 1.0 %collective-permute-done.18.rest_3_ = bf16[128,256]{1,0:T(8,128)(2,1)S(1)} collective-permute-done((bf16[128,256]{1,0:T(8,128)(2,1)S(1)}, bf16[128,256]{1,0:T(8,128)(2,1)S(1)}, u32[]{:S(2)}, u32[]{:S(2)}) %collective-permute-start.18) | collective-permute-done | bytes 65568 | tf_op jit(solution)/shard_map/ppermute | solution.py:44
  67.1 1.6 %collective-permute-start.27 = (bf16[128,1024]{1,0:T(8,128)(2,1)}, bf16[128,1024]{1,0:T(8,128)(2,1)S(1)}, u32[]{:S(2)}, u32[]{:S(2)}) collective-permute-start(bf16[128,1024]{1,0:T(8,128)(2,1)} %collective-permute-done.23.refs_2_), channel_id=1, source_target_pairs={{0,1},{1,0},{2,3},{3,2},{4,5},{5,4},{6,7},{7,6},{8,9},{9,8},{10,11... | collective-permute-start | bytes 786440 | tf_op jit(solution)/shard_map/ppermute | solution.py:44
  68.8 2.3 %two_filters.3 = (bf16[512,128]{1,0:T(8,128)(2,1)S(1)}, bf16[512,256]{1,0:T(8,128)(2,1)S(1)}, f32[256,256]{1,0:T(8,128)S(1)}) custom-call(f32[2,128]{1,0:T(2,128)S(1)} %bitcast.20, f32[2,4,512,128]{3,2,1,0:T(8,128)S(1)} %get-tuple-element.83.spectra_ref, bf16[512,256]{1,0:T(8,128)(2,1)S(1)} %copy-done.2, bf16[256,512]{1,0:T(8,128)(2,1)S(1)} %copy-done.1, ...), custom_call_target="tpu_custom_call" | custom-call | flops 536870912 | bytes 1048576 | tf_op jit(solution)/shard_map/two_filters/pallas_call | solution.py:367
  71.0 0.5 collective-permute-start.22
  71.5 0.2 own_half.3.keep_ref
  71.8 1.9 %hold_exit.1 = (bf16[1024,1024]{1,0:T(8,128)(2,1)S(1)}, bf16[4,128,256]{2,1,0:T(8,128)(2,1)S(1)}, bf16[128,1024]{1,0:T(8,128)(2,1)S(1)}, bf16[128,1024]{1,0:T(8,...) custom-call(bf16[1024,1024]{1,0:T(8,128)(2,1)} %bitcast.11, ...), custom_call_target="tpu_custom_call" | custom-call | bytes 3932160 | tf_op jit(solution)/shard_map/hold_exit/pallas_call | solution.py:204
  73.7 6.0 %collective-permute-done.22.come_ref = bf16[512,128]{1,0:T(8,128)(2,1)S(1)} collective-permute-done((bf16[512,128]{1,0:T(8,128)(2,1)S(1)}, bf16[512,128]{1,0:T(8,128)(2,1)S(1)}, u32[]{:S(2)}, u32[]{:S(2)}) %collective-permute-start.22) | collective-permute-done | bytes 131104 | tf_op jit(solution)/shard_map/ppermute | solution.py:44
  79.7 0.1 second_gate.3
  79.8 0.0 collective-permute-done.27.refs_0_
  79.8 0.5 gradient_away.1
  80.3 0.1 collective-permute-start.29
  80.3 2.3 %collective-permute-start.24 = (bf16[128,256]{1,0:T(8,128)(2,1)S(1)}, bf16[128,256]{1,0:T(8,128)(2,1)S(1)}, u32[]{:S(2)}, u32[]{:S(2)}) collective-permute-start(bf16[128,256]{1,0:T(8,128)(2,1)S(1)} %get-tuple-element.150), channel_id=1, source_target_pairs={{0,3},{1,2},{2,1},{3,0},{4,7},{5,6},{6,5},{7,4},{8,11},{9,10},{10,... | collective-permute-start | bytes 196616 | tf_op jit(solution)/shard_map/ppermute | solution.py:44
  82.7 1.3 %collective-permute-start.26 = (bf16[128,256]{1,0:T(8,128)(2,1)S(1)}, bf16[128,256]{1,0:T(8,128)(2,1)S(1)}, u32[]{:S(2)}, u32[]{:S(2)}) collective-permute-start(bf16[128,256]{1,0:T(8,128)(2,1)S(1)} %get-tuple-element.152), channel_id=1, source_target_pairs={{0,1},{1,0},{2,3},{3,2},{4,5},{5,4},{6,7},{7,6},{8,9},{9,8},{10,11... | collective-permute-start | bytes 196616 | tf_op jit(solution)/shard_map/ppermute | solution.py:44
  84.0 4.5 %collective-permute-done.24.rest_0_ = bf16[128,256]{1,0:T(8,128)(2,1)S(1)} collective-permute-done((bf16[128,256]{1,0:T(8,128)(2,1)S(1)}, bf16[128,256]{1,0:T(8,128)(2,1)S(1)}, u32[]{:S(2)}, u32[]{:S(2)}) %collective-permute-start.24) | collective-permute-done | bytes 65568 | tf_op jit(solution)/shard_map/ppermute | solution.py:44
  88.4 0.8 collective-permute-done.25.rest_1_
  89.2 1.2 %exit_projection.3 = bf16[128,1024]{1,0:T(8,128)(2,1)} custom-call(s32[1]{0:T(128)} %bitcast.choice_ref, bf16[128,1024]{1,0:T(8,128)(2,1)S(1)} %collective-permute-done.13.x_ref, bf16[128,1024]{1,0:T(8,128)(2,1)S(1)} %get-tuple-element.114.other_ref, bf16[1024,1024]{1,0:T(8,128)(2,1)S(1)} %get-tuple-element.148.weight_ref, ...), custom_call_target="tpu_custom_call" | custom-call | flops 268435456 | bytes 2097152 | tf_op jit(solution)/shard_map/exit_projection/pallas_call | solution.py:439
  90.4 0.5 gradient_mine.1
  90.9 3.2 %collective-permute-done.29 = bf16[128,1024]{1,0:T(8,128)(2,1)S(1)} collective-permute-done((bf16[128,1024]{1,0:T(8,128)(2,1)S(1)}, bf16[128,1024]{1,0:T(8,128)(2,1)S(1)}, u32[]{:S(2)}, u32[]{:S(2)}) %collective-permute-start.29) | collective-permute-done | bytes 262176 | tf_op jit(solution)/shard_map/ppermute | solution.py:44
  94.1 0.9 add_bitcast_fusion
  (48 shorter events, 0.1 us)
Async XLA Ops:
  0.6 18.3 %copy-start.2 = (bf16[512,256]{1,0:T(8,128)(2,1)S(1)}, bf16[512,256]{1,0:T(8,128)(2,1)}, u32[]{:S(2)}) copy-start(bf16[512,256]{1,0:T(8,128)(2,1)} %constant.13.clone.forward_ref) | copy-start | bytes 786436
  0.6 18.2 %copy-start.5 = (bf16[1,2,128,1024]{3,2,1,0:T(8,128)(2,1)S(1)}, bf16[1,2,128,1024]{3,2,1,0:T(8,128)(2,1)}, u32[]{:S(2)}) copy-start(bf16[1,2,128,1024]{3,2,1,0:T(8,128)(2,1)} %param.23) | copy-start | bytes 1572868
  0.7 18.2 %copy-start.11 = (bf16[32,1024]{1,0:T(8,128)(2,1)S(1)}, bf16[32,1024]{1,0:T(8,128)(2,1)}, u32[]{:S(2)}) copy-start(bf16[32,1024]{1,0:T(8,128)(2,1)} %amino_ref.1) | copy-start | bytes 196612
  0.7 18.2 %copy-start.13 = (bf16[8,1024]{1,0:T(8,128)(2,1)S(1)}, bf16[8,1024]{1,0:T(8,128)(2,1)}, u32[]{:S(2)}) copy-start(bf16[8,1024]{1,0:T(8,128)(2,1)} %polymer_ref.1) | copy-start | bytes 49156
  0.7 18.2 %copy-start.15 = (s32[8]{0:T(128)S(1)}, s32[8]{0:T(128)}, u32[]{:S(2)}) copy-start(s32[8]{0:T(128)} %sizes_ref.1) | copy-start | bytes 100
  0.7 18.2 %copy-start.16 = (s32[128]{0:T(128)S(1)}, s32[128]{0:T(128)}, u32[]{:S(2)}) copy-start(s32[128]{0:T(128)} %param.14) | copy-start | bytes 1540
  3.8 15.1 %copy-start.4 = (f32[1,2,128,1024]{3,2,1,0:T(8,128)S(1)}, f32[1,2,128,1024]{3,2,1,0:T(8,128)}, u32[]{:S(2)}) copy-start(f32[1,2,128,1024]{3,2,1,0:T(8,128)} %param.20) | copy-start | bytes 3145732
  3.8 20.5 %copy-start.1 = (bf16[256,512]{1,0:T(8,128)(2,1)S(1)}, bf16[256,512]{1,0:T(8,128)(2,1)}, u32[]{:S(2)}) copy-start(bf16[256,512]{1,0:T(8,128)(2,1)} %constant.14.clone.backward_ref) | copy-start | bytes 786436
  3.9 20.5 %copy-start.12 = (f32[1,2,128]{2,1,0:T(2,128)S(1)}, f32[1,2,128]{2,1,0:T(2,128)}, u32[]{:S(2)}) copy-start(f32[1,2,128]{2,1,0:T(2,128)} %param.21) | copy-start | bytes 3076
  3.9 9.9 %collective-permute-start = (bf16[128,256]{1,0:T(8,128)(2,1)S(1)}, bf16[128,256]{1,0:T(8,128)(2,1)S(1)}, u32[]{:S(2)}, u32[]{:S(2)}) collective-permute-start(bf16[128,256]{1,0:T(8,128)(2,1)S(1)} %get-tuple-element.84), channel_id=1, source_target_pairs={{0,4},{1,5},{2,6},{3,7},{4,0},{5,1},{6,2},{7,3},{8,12},{9,13},{10,... | collective-permute-start | bytes 196616 | tf_op jit(solution)/shard_map/ppermute | solution.py:44
  8.0 9.4 %collective-permute-start.1 = (bf16[128,256]{1,0:T(8,128)(2,1)S(1)}, bf16[128,256]{1,0:T(8,128)(2,1)S(1)}, u32[]{:S(2)}, u32[]{:S(2)}) collective-permute-start(bf16[128,256]{1,0:T(8,128)(2,1)S(1)} %get-tuple-element.85), channel_id=1, source_target_pairs={{0,5},{1,4},{2,7},{3,6},{4,1},{5,0},{6,3},{7,2},{8,13},{9,12},{10,... | collective-permute-start | bytes 196616 | tf_op jit(solution)/shard_map/ppermute | solution.py:44
  10.2 14.1 %collective-permute-start.4 = (bf16[128,512]{1,0:T(8,128)(2,1)S(1)}, bf16[128,512]{1,0:T(8,128)(2,1)S(1)}, u32[]{:S(2)}, u32[]{:S(2)}) collective-permute-start(bf16[128,512]{1,0:T(8,128)(2,1)S(1)} %get-tuple-element.90), channel_id=1, source_target_pairs={{0,3},{1,2},{2,1},{3,0},{4,7},{5,6},{6,5},{7,4},{8,11},{9,10},{10,... | collective-permute-start | bytes 393224 | tf_op jit(solution)/shard_map/ppermute | solution.py:44
  11.8 12.5 %collective-permute-start.5 = (bf16[128,512]{1,0:T(8,128)(2,1)S(1)}, bf16[128,512]{1,0:T(8,128)(2,1)S(1)}, u32[]{:S(2)}, u32[]{:S(2)}) collective-permute-start(bf16[128,512]{1,0:T(8,128)(2,1)S(1)} %get-tuple-element.91), channel_id=1, source_target_pairs={{0,2},{1,3},{2,0},{3,1},{4,6},{5,7},{6,4},{7,5},{8,10},{9,11},{10,... | collective-permute-start | bytes 393224 | tf_op jit(solution)/shard_map/ppermute | solution.py:44
  12.0 12.3 %collective-permute-start.6 = (bf16[128,512]{1,0:T(8,128)(2,1)S(1)}, bf16[128,512]{1,0:T(8,128)(2,1)S(1)}, u32[]{:S(2)}, u32[]{:S(2)}) collective-permute-start(bf16[128,512]{1,0:T(8,128)(2,1)S(1)} %get-tuple-element.92), channel_id=1, source_target_pairs={{0,1},{1,0},{2,3},{3,2},{4,5},{5,4},{6,7},{7,6},{8,9},{9,8},{10,11... | collective-permute-start | bytes 393224 | tf_op jit(solution)/shard_map/ppermute | solution.py:44
  13.7 8.5 %collective-permute-start.2 = (bf16[128,256]{1,0:T(8,128)(2,1)S(1)}, bf16[128,256]{1,0:T(8,128)(2,1)S(1)}, u32[]{:S(2)}, u32[]{:S(2)}) collective-permute-start(bf16[128,256]{1,0:T(8,128)(2,1)S(1)} %get-tuple-element.86), channel_id=1, source_target_pairs={{0,6},{1,7},{2,4},{3,5},{4,2},{5,3},{6,0},{7,1},{8,14},{9,15},{10,... | collective-permute-start | bytes 196616 | tf_op jit(solution)/shard_map/ppermute | solution.py:44
  17.3 7.0 %collective-permute-start.3 = (bf16[128,256]{1,0:T(8,128)(2,1)S(1)}, bf16[128,256]{1,0:T(8,128)(2,1)S(1)}, u32[]{:S(2)}, u32[]{:S(2)}) collective-permute-start(bf16[128,256]{1,0:T(8,128)(2,1)S(1)} %get-tuple-element.87), channel_id=1, source_target_pairs={{0,7},{1,6},{2,5},{3,4},{4,3},{5,2},{6,1},{7,0},{8,15},{9,14},{10,... | collective-permute-start | bytes 196616 | tf_op jit(solution)/shard_map/ppermute | solution.py:44
  21.1 21.5 %copy-start = (bf16[1,1024,1024]{2,1,0:T(8,128)(2,1)S(1)}, bf16[1,1024,1024]{2,1,0:T(8,128)(2,1)}, u32[]{:S(2)}) copy-start(bf16[1,1024,1024]{2,1,0:T(8,128)(2,1)} %param.22) | copy-start | bytes 6291460
  21.1 21.5 %copy-start.3 = (bf16[1,128,1024]{2,1,0:T(8,128)(2,1)S(1)}, bf16[1,128,1024]{2,1,0:T(8,128)(2,1)}, u32[]{:S(2)}) copy-start(bf16[1,128,1024]{2,1,0:T(8,128)(2,1)} %param.13) | copy-start | bytes 786436
  26.6 7.6 %collective-permute-start.7 = (bf16[512,128]{1,0:T(8,128)(2,1)S(1)}, bf16[512,128]{1,0:T(8,128)(2,1)S(1)}, u32[]{:S(2)}, u32[]{:S(2)}) collective-permute-start(bf16[512,128]{1,0:T(8,128)(2,1)S(1)} %get-tuple-element.96), channel_id=1, source_target_pairs={{0,4},{1,5},{2,6},{3,7},{4,0},{5,1},{6,2},{7,3},{8,12},{9,13},{10,... | collective-permute-start | bytes 393224 | tf_op jit(solution)/shard_map/ppermute | solution.py:44
  27.0 15.5 %collective-permute-start.11 = (bf16[128,1024]{1,0:T(8,128)(2,1)}, bf16[128,1024]{1,0:T(8,128)(2,1)S(1)}, u32[]{:S(2)}, u32[]{:S(2)}) collective-permute-start(bf16[128,1024]{1,0:T(8,128)(2,1)} %get-tuple-element.136.refs_4_), channel_id=1, source_target_pairs={{0,1},{1,0},{2,3},{3,2},{4,5},{5,4},{6,7},{7,6},{8,9},{9,8},{10,11... | collective-permute-start | bytes 786440 | tf_op jit(solution)/shard_map/ppermute | solution.py:44
  28.5 14.0 %collective-permute-start.12 = (bf16[128,1024]{1,0:T(8,128)(2,1)}, bf16[128,1024]{1,0:T(8,128)(2,1)S(1)}, u32[]{:S(2)}, u32[]{:S(2)}) collective-permute-start(bf16[128,1024]{1,0:T(8,128)(2,1)} %get-tuple-element.139.refs_7_), channel_id=1, source_target_pairs={{0,2},{1,3},{2,0},{3,1},{4,6},{5,7},{6,4},{7,5},{8,10},{9,11},{10,... | collective-permute-start | bytes 786440 | tf_op jit(solution)/shard_map/ppermute | solution.py:44
  35.0 5.7 %collective-permute-start.8 = (bf16[128,256]{1,0:T(8,128)(2,1)S(1)}, bf16[128,256]{1,0:T(8,128)(2,1)S(1)}, u32[]{:S(2)}, u32[]{:S(2)}) collective-permute-start(bf16[128,256]{1,0:T(8,128)(2,1)S(1)} %get-tuple-element.98), channel_id=1, source_target_pairs={{0,3},{1,2},{2,1},{3,0},{4,7},{5,6},{6,5},{7,4},{8,11},{9,10},{10,... | collective-permute-start | bytes 196616 | tf_op jit(solution)/shard_map/ppermute | solution.py:44
  35.6 6.8 %collective-permute-start.9 = (bf16[128,256]{1,0:T(8,128)(2,1)S(1)}, bf16[128,256]{1,0:T(8,128)(2,1)S(1)}, u32[]{:S(2)}, u32[]{:S(2)}) collective-permute-start(bf16[128,256]{1,0:T(8,128)(2,1)S(1)} %get-tuple-element.99), channel_id=1, source_target_pairs={{0,2},{1,3},{2,0},{3,1},{4,6},{5,7},{6,4},{7,5},{8,10},{9,11},{10,... | collective-permute-start | bytes 196616 | tf_op jit(solution)/shard_map/ppermute | solution.py:44
  37.8 4.7 %collective-permute-start.10 = (bf16[128,256]{1,0:T(8,128)(2,1)S(1)}, bf16[128,256]{1,0:T(8,128)(2,1)S(1)}, u32[]{:S(2)}, u32[]{:S(2)}) collective-permute-start(bf16[128,256]{1,0:T(8,128)(2,1)S(1)} %get-tuple-element.100), channel_id=1, source_target_pairs={{0,1},{1,0},{2,3},{3,2},{4,5},{5,4},{6,7},{7,6},{8,9},{9,8},{10,11... | collective-permute-start | bytes 196616 | tf_op jit(solution)/shard_map/ppermute | solution.py:44
  40.8 7.0 %collective-permute-start.14 = (bf16[128,1024]{1,0:T(8,128)(2,1)}, bf16[128,1024]{1,0:T(8,128)(2,1)}, u32[]{:S(2)}, u32[]{:S(2)}) collective-permute-start(bf16[128,1024]{1,0:T(8,128)(2,1)} %get-tuple-element.139.refs_7_), channel_id=1, source_target_pairs={{0,1},{1,0},{2,3},{3,2},{4,5},{5,4},{6,7},{7,6},{8,9},{9,8},{10,11... | collective-permute-start | bytes 786440 | tf_op jit(solution)/shard_map/ppermute | solution.py:44
  42.5 2.0 %copy-start.8 = (bf16[128,1024]{1,0:T(8,128)(2,1)}, bf16[128,1024]{1,0:T(8,128)(2,1)S(1)}, u32[]{:S(2)}) copy-start(bf16[128,1024]{1,0:T(8,128)(2,1)S(1)} %collective-permute-done.11.refs_3_) | copy-start | bytes 786436
  42.5 1.8 %copy-start.6 = (bf16[128,1024]{1,0:T(8,128)(2,1)}, bf16[128,1024]{1,0:T(8,128)(2,1)S(1)}, u32[]{:S(2)}) copy-start(bf16[128,1024]{1,0:T(8,128)(2,1)S(1)} %collective-permute-done.12.refs_5_) | copy-start | bytes 786436
  43.0 4.7 %collective-permute-start.13 = (bf16[128,1024]{1,0:T(8,128)(2,1)S(1)}, bf16[128,1024]{1,0:T(8,128)(2,1)S(1)}, u32[]{:S(2)}, u32[]{:S(2)}) collective-permute-start(bf16[128,1024]{1,0:T(8,128)(2,1)S(1)} %exit_projection.2), channel_id=1, source_target_pairs={{0,8},{8,16},{16,24},{1,9},{9,17},{17,25},{2,10},{10,18},{18,26},{... | collective-permute-start | bytes 786440 | tf_op jit(solution)/shard_map/ppermute | solution.py:546
  44.4 10.9 %collective-permute-start.23 = (bf16[128,1024]{1,0:T(8,128)(2,1)}, bf16[128,1024]{1,0:T(8,128)(2,1)}, u32[]{:S(2)}, u32[]{:S(2)}) collective-permute-start(bf16[128,1024]{1,0:T(8,128)(2,1)} %get-tuple-element.136.refs_4_), channel_id=1, source_target_pairs={{0,2},{1,3},{2,0},{3,1},{4,6},{5,7},{6,4},{7,5},{8,10},{9,11},{10,... | collective-permute-start | bytes 786440 | tf_op jit(solution)/shard_map/ppermute | solution.py:44
  44.5 3.3 %copy-start.14 = (f32[1,1024]{1,0:T(1,128)S(1)}, f32[1,1024]{1,0:T(1,128)}, u32[]{:S(2)}) copy-start(f32[1,1024]{1,0:T(1,128)} %gain_ref.3) | copy-start | bytes 12292
  48.3 17.1 %copy-start.7 = (bf16[128,1024]{1,0:T(8,128)(2,1)S(1)}, bf16[128,1024]{1,0:T(8,128)(2,1)}, u32[]{:S(2)}) copy-start(bf16[128,1024]{1,0:T(8,128)(2,1)} %copy-done.6) | copy-start | bytes 786436
  48.4 8.4 %collective-permute-start.15 = (bf16[128,256]{1,0:T(8,128)(2,1)S(1)}, bf16[128,256]{1,0:T(8,128)(2,1)S(1)}, u32[]{:S(2)}, u32[]{:S(2)}) collective-permute-start(bf16[128,256]{1,0:T(8,128)(2,1)S(1)} %get-tuple-element.116), channel_id=1, source_target_pairs={{0,4},{1,5},{2,6},{3,7},{4,0},{5,1},{6,2},{7,3},{8,12},{9,13},{10,... | collective-permute-start | bytes 196616 | tf_op jit(solution)/shard_map/ppermute | solution.py:44
  51.0 8.4 %collective-permute-start.16 = (bf16[128,256]{1,0:T(8,128)(2,1)S(1)}, bf16[128,256]{1,0:T(8,128)(2,1)S(1)}, u32[]{:S(2)}, u32[]{:S(2)}) collective-permute-start(bf16[128,256]{1,0:T(8,128)(2,1)S(1)} %get-tuple-element.117), channel_id=1, source_target_pairs={{0,5},{1,4},{2,7},{3,6},{4,1},{5,0},{6,3},{7,2},{8,13},{9,12},{10,... | collective-permute-start | bytes 196616 | tf_op jit(solution)/shard_map/ppermute | solution.py:44
  52.2 19.5 %copy-start.9 = (bf16[128,1024]{1,0:T(8,128)(2,1)S(1)}, bf16[128,1024]{1,0:T(8,128)(2,1)}, u32[]{:S(2)}) copy-start(bf16[128,1024]{1,0:T(8,128)(2,1)} %copy-done.8) | copy-start | bytes 786436
  52.2 19.6 %copy-start.10 = (bf16[4,128,256]{2,1,0:T(8,128)(2,1)S(1)}, bf16[4,128,256]{2,1,0:T(8,128)(2,1)}, u32[]{:S(2)}) copy-start(bf16[4,128,256]{2,1,0:T(8,128)(2,1)} %get-tuple-element.133.refs_1_) | copy-start | bytes 786436
  53.1 14.0 %collective-permute-start.19 = (bf16[128,512]{1,0:T(8,128)(2,1)S(1)}, bf16[128,512]{1,0:T(8,128)(2,1)S(1)}, u32[]{:S(2)}, u32[]{:S(2)}) collective-permute-start(bf16[128,512]{1,0:T(8,128)(2,1)S(1)} %get-tuple-element.121), channel_id=1, source_target_pairs={{0,3},{1,2},{2,1},{3,0},{4,7},{5,6},{6,5},{7,4},{8,11},{9,10},{10,... | collective-permute-start | bytes 393224 | tf_op jit(solution)/shard_map/ppermute | solution.py:44
  54.8 12.3 %collective-permute-start.20 = (bf16[128,512]{1,0:T(8,128)(2,1)S(1)}, bf16[128,512]{1,0:T(8,128)(2,1)S(1)}, u32[]{:S(2)}, u32[]{:S(2)}) collective-permute-start(bf16[128,512]{1,0:T(8,128)(2,1)S(1)} %get-tuple-element.122), channel_id=1, source_target_pairs={{0,2},{1,3},{2,0},{3,1},{4,6},{5,7},{6,4},{7,5},{8,10},{9,11},{10,... | collective-permute-start | bytes 393224 | tf_op jit(solution)/shard_map/ppermute | solution.py:44
  55.3 11.9 %collective-permute-start.21 = (bf16[128,512]{1,0:T(8,128)(2,1)S(1)}, bf16[128,512]{1,0:T(8,128)(2,1)S(1)}, u32[]{:S(2)}, u32[]{:S(2)}) collective-permute-start(bf16[128,512]{1,0:T(8,128)(2,1)S(1)} %get-tuple-element.123), channel_id=1, source_target_pairs={{0,1},{1,0},{2,3},{3,2},{4,5},{5,4},{6,7},{7,6},{8,9},{9,8},{10,11... | collective-permute-start | bytes 393224 | tf_op jit(solution)/shard_map/ppermute | solution.py:44
  56.7 8.8 %collective-permute-start.17 = (bf16[128,256]{1,0:T(8,128)(2,1)S(1)}, bf16[128,256]{1,0:T(8,128)(2,1)S(1)}, u32[]{:S(2)}, u32[]{:S(2)}) collective-permute-start(bf16[128,256]{1,0:T(8,128)(2,1)S(1)} %get-tuple-element.118), channel_id=1, source_target_pairs={{0,6},{1,7},{2,4},{3,5},{4,2},{5,3},{6,0},{7,1},{8,14},{9,15},{10,... | collective-permute-start | bytes 196616 | tf_op jit(solution)/shard_map/ppermute | solution.py:44
  59.4 7.7 %collective-permute-start.18 = (bf16[128,256]{1,0:T(8,128)(2,1)S(1)}, bf16[128,256]{1,0:T(8,128)(2,1)S(1)}, u32[]{:S(2)}, u32[]{:S(2)}) collective-permute-start(bf16[128,256]{1,0:T(8,128)(2,1)S(1)} %get-tuple-element.119), channel_id=1, source_target_pairs={{0,7},{1,6},{2,5},{3,4},{4,3},{5,2},{6,1},{7,0},{8,15},{9,14},{10,... | collective-permute-start | bytes 196616 | tf_op jit(solution)/shard_map/ppermute | solution.py:44
  65.5 14.3 %collective-permute-start.28 = (bf16[128,1024]{1,0:T(8,128)(2,1)S(1)}, bf16[128,1024]{1,0:T(8,128)(2,1)S(1)}, u32[]{:S(2)}, u32[]{:S(2)}) collective-permute-start(bf16[128,1024]{1,0:T(8,128)(2,1)S(1)} %copy-done.7), channel_id=1, source_target_pairs={{0,1},{1,0},{2,3},{3,2},{4,5},{5,4},{6,7},{7,6},{8,9},{9,8},{10,11... | collective-permute-start | bytes 786440 | tf_op jit(solution)/shard_map/ppermute | solution.py:44
  67.1 12.6 %collective-permute-start.27 = (bf16[128,1024]{1,0:T(8,128)(2,1)}, bf16[128,1024]{1,0:T(8,128)(2,1)S(1)}, u32[]{:S(2)}, u32[]{:S(2)}) collective-permute-start(bf16[128,1024]{1,0:T(8,128)(2,1)} %collective-permute-done.23.refs_2_), channel_id=1, source_target_pairs={{0,1},{1,0},{2,3},{3,2},{4,5},{5,4},{6,7},{7,6},{8,9},{9,8},{10,11... | collective-permute-start | bytes 786440 | tf_op jit(solution)/shard_map/ppermute | solution.py:44
  71.0 8.6 %collective-permute-start.22 = (bf16[512,128]{1,0:T(8,128)(2,1)S(1)}, bf16[512,128]{1,0:T(8,128)(2,1)S(1)}, u32[]{:S(2)}, u32[]{:S(2)}) collective-permute-start(bf16[512,128]{1,0:T(8,128)(2,1)S(1)} %get-tuple-element.125), channel_id=1, source_target_pairs={{0,4},{1,5},{2,6},{3,7},{4,0},{5,1},{6,2},{7,3},{8,12},{9,13},{10,... | collective-permute-start | bytes 393224 | tf_op jit(solution)/shard_map/ppermute | solution.py:44
  80.3 13.8 %collective-permute-start.29 = (bf16[128,1024]{1,0:T(8,128)(2,1)S(1)}, bf16[128,1024]{1,0:T(8,128)(2,1)S(1)}, u32[]{:S(2)}, u32[]{:S(2)}) collective-permute-start(bf16[128,1024]{1,0:T(8,128)(2,1)S(1)} %gradient_away.1), channel_id=1, source_target_pairs={{0,4},{1,5},{2,6},{3,7},{4,0},{5,1},{6,2},{7,3},{8,12},{9,13},{10,... | collective-permute-start | bytes 786440 | tf_op jit(solution)/shard_map/ppermute | solution.py:44
  80.3 8.1 %collective-permute-start.24 = (bf16[128,256]{1,0:T(8,128)(2,1)S(1)}, bf16[128,256]{1,0:T(8,128)(2,1)S(1)}, u32[]{:S(2)}, u32[]{:S(2)}) collective-permute-start(bf16[128,256]{1,0:T(8,128)(2,1)S(1)} %get-tuple-element.150), channel_id=1, source_target_pairs={{0,3},{1,2},{2,1},{3,0},{4,7},{5,6},{6,5},{7,4},{8,11},{9,10},{10,... | collective-permute-start | bytes 196616 | tf_op jit(solution)/shard_map/ppermute | solution.py:44
  82.7 6.5 %collective-permute-start.25 = (bf16[128,256]{1,0:T(8,128)(2,1)S(1)}, bf16[128,256]{1,0:T(8,128)(2,1)S(1)}, u32[]{:S(2)}, u32[]{:S(2)}) collective-permute-start(bf16[128,256]{1,0:T(8,128)(2,1)S(1)} %get-tuple-element.151), channel_id=1, source_target_pairs={{0,2},{1,3},{2,0},{3,1},{4,6},{5,7},{6,4},{7,5},{8,10},{9,11},{10,... | collective-permute-start | bytes 196616 | tf_op jit(solution)/shard_map/ppermute | solution.py:44
  82.7 6.5 %collective-permute-start.26 = (bf16[128,256]{1,0:T(8,128)(2,1)S(1)}, bf16[128,256]{1,0:T(8,128)(2,1)S(1)}, u32[]{:S(2)}, u32[]{:S(2)}) collective-permute-start(bf16[128,256]{1,0:T(8,128)(2,1)S(1)} %get-tuple-element.152), channel_id=1, source_target_pairs={{0,1},{1,0},{2,3},{3,2},{4,5},{5,4},{6,7},{7,6},{8,9},{9,8},{10,11... | collective-permute-start | bytes 196616 | tf_op jit(solution)/shard_map/ppermute | solution.py:44

commit v4 on v3

--- a/solution.py
+++ b/solution.py
@@ -324,7 +324,7 @@
                 mixed_ref[imag_rows, chunk_lanes(i)] = imag.astype(bf16)
             return 0
 
-        lax.fori_loop(0, size // step, multiply, 0)
+        lax.fori_loop(0, size // step, multiply, 0, unroll=min(16, size // step))
 
     convolve(jnp.concatenate([value_ref[chunk_rows(j), :] for j in range(chunks)], axis=1), 0)
     result = dot(backward_ref[...], mixed_ref[...])
@@ -489,7 +489,7 @@
     peers = lax.axis_size("seq")
     sections = lax.axis_size("section")
     group = peers // 2
-    far = tuple(range(group, peers))
+    far = tuple(range(group, peers, 2)) + tuple(range(group + 1, peers, 2))
     near = tuple(range(group - 1, -1, -1))
     never = jnp.zeros((1,), jnp.int32)
     first_section = (lax.axis_index("section") == 0).astype(jnp.int32)[None]

time: 95.1 us -> 92.9 us (0.977)
  waiting for transfers between devices: 28.6 us -> 26.7 us
  Pallas kernels: 20.9 us -> 19.6 us
  starting transfers between devices: 43.5 us -> 44.5 us
    ppermute x29, waiting for transfers between devices: 28.6 us -> 26.7 us  [exchange(): return lax.ppermute(value, 'seq', [(i, i ^ distance) for i in range(peers)])]
    pallas_call x2, Pallas kernels: 4.55 us -> 3.3 us  [filtered(): pl.pallas_call(functools.partial(filter_kernel, order), out_shape=(out, k...]
    ppermute x29, starting transfers between devices: 42.2 us -> 43.2 us  [exchange(): return lax.ppermute(value, 'seq', [(i, i ^ distance) for i in range(peers)])]
where the time goes in v4:
time: 92.9 us; the launch traced here: 92.7 us
  starting transfers between devices  44.5 us (48%)
  waiting for transfers between devices  26.7 us (29%)
  Pallas kernels  19.6 us (21%)
  between operations  1 us (1%)
    ppermute x29, starting transfers between devices, exchange(): return lax.ppermute(value, 'seq', [(i, i ^ distance) for i in range(peers)])  43.2 us
    ppermute x29, waiting for transfers between devices, exchange(): return lax.ppermute(value, 'seq', [(i, i ^ distance) for i in range(peers)])  26.7 us
    pallas_call x2, Pallas kernels, hold(): pl.pallas_call(functools.partial(hold_kernel, count), out_shape=tuple((pl...  4.7 us
    pallas_call x2, Pallas kernels, filtered(): pl.pallas_call(functools.partial(filter_kernel, order), out_shape=(out, k...  3.3 us
    pallas_call x1, Pallas kernels, project(): pl.pallas_call(functools.partial(far_stream_kernel, far), out_shape=outs,...  3.13 us
    pallas_call x1, Pallas kernels, prepare(): pl.pallas_call(prepare_kernel, out_shape=(jax.ShapeDtypeStruct((2, chunks...  2.12 us
  transfers between devices with their start and end apart: 30, of which 11 were waited for; matrix products, arithmetic and copies ran while one was open for 0% of the time, Pallas kernels for 16%

profile of v4, /device:TPU:0, one launch (start us, length us, event | category | flops | bytes accessed | tf_op | source)
XLA Modules:
  0.0 92.7 jit_solution(14824800474760141356)
XLA Ops:
  0.6 0.0 copy-start.2
  0.7 3.1 %far_pieces_streamed.1 = (bf16[128,256]{1,0:T(8,128)(2,1)S(1)}, bf16[128,256]{1,0:T(8,128)(2,1)S(1)}, bf16[128,256]{1,0:T(8,128)(2,1)S(1)}, bf16[128,256]{1,0:T(...) custom-call(bf16[128,1024]{1,0:T(8,128)(2,1)} %bitcast.13, f32[1,1024]{1,0:T(1,128)} %gain_ref.3, ...), custom_call_target="tpu_custom_call" | custom-call | flops 268435456 | bytes 2097152 | tf_op jit(solution)/shard_map/far_pieces_streamed/pallas_call | solution.py:242
  3.8 0.0 copy-start.4
  3.8 0.0 copy-start.1
  3.9 0.0 copy-start.12
  3.9 4.1 %collective-permute-start = (bf16[128,256]{1,0:T(8,128)(2,1)S(1)}, bf16[128,256]{1,0:T(8,128)(2,1)S(1)}, u32[]{:S(2)}, u32[]{:S(2)}) collective-permute-start(bf16[128,256]{1,0:T(8,128)(2,1)S(1)} %get-tuple-element.84), channel_id=1, source_target_pairs={{0,4},{1,5},{2,6},{3,7},{4,0},{5,1},{6,2},{7,3},{8,12},{9,13},{10,... | collective-permute-start | bytes 196616 | tf_op jit(solution)/shard_map/ppermute | solution.py:44
  8.0 1.3 %collective-permute-start.1 = (bf16[128,256]{1,0:T(8,128)(2,1)S(1)}, bf16[128,256]{1,0:T(8,128)(2,1)S(1)}, u32[]{:S(2)}, u32[]{:S(2)}) collective-permute-start(bf16[128,256]{1,0:T(8,128)(2,1)S(1)} %get-tuple-element.85), channel_id=1, source_target_pairs={{0,6},{1,7},{2,4},{3,5},{4,2},{5,3},{6,0},{7,1},{8,14},{9,15},{10,... | collective-permute-start | bytes 196616 | tf_op jit(solution)/shard_map/ppermute | solution.py:44
  9.3 0.9 near_pieces.2
  10.3 1.2 %collective-permute-start.4 = (bf16[128,512]{1,0:T(8,128)(2,1)S(1)}, bf16[128,512]{1,0:T(8,128)(2,1)S(1)}, u32[]{:S(2)}, u32[]{:S(2)}) collective-permute-start(bf16[128,512]{1,0:T(8,128)(2,1)S(1)} %get-tuple-element.90), channel_id=1, source_target_pairs={{0,3},{1,2},{2,1},{3,0},{4,7},{5,6},{6,5},{7,4},{8,11},{9,10},{10,... | collective-permute-start | bytes 393224 | tf_op jit(solution)/shard_map/ppermute | solution.py:44
  11.5 1.8 %collective-permute-start.5 = (bf16[128,512]{1,0:T(8,128)(2,1)S(1)}, bf16[128,512]{1,0:T(8,128)(2,1)S(1)}, u32[]{:S(2)}, u32[]{:S(2)}) collective-permute-start(bf16[128,512]{1,0:T(8,128)(2,1)S(1)} %get-tuple-element.91), channel_id=1, source_target_pairs={{0,2},{1,3},{2,0},{3,1},{4,6},{5,7},{6,4},{7,5},{8,10},{9,11},{10,... | collective-permute-start | bytes 393224 | tf_op jit(solution)/shard_map/ppermute | solution.py:44
  13.3 0.5 collective-permute-start.6
  13.8 2.6 %collective-permute-start.2 = (bf16[128,256]{1,0:T(8,128)(2,1)S(1)}, bf16[128,256]{1,0:T(8,128)(2,1)S(1)}, u32[]{:S(2)}, u32[]{:S(2)}) collective-permute-start(bf16[128,256]{1,0:T(8,128)(2,1)S(1)} %get-tuple-element.86), channel_id=1, source_target_pairs={{0,5},{1,4},{2,7},{3,6},{4,1},{5,0},{6,3},{7,2},{8,13},{9,12},{10,... | collective-permute-start | bytes 196616 | tf_op jit(solution)/shard_map/ppermute | solution.py:44
  16.4 0.0 collective-permute-done.1.rest_1_
  16.4 1.4 %collective-permute-start.3 = (bf16[128,256]{1,0:T(8,128)(2,1)S(1)}, bf16[128,256]{1,0:T(8,128)(2,1)S(1)}, u32[]{:S(2)}, u32[]{:S(2)}) collective-permute-start(bf16[128,256]{1,0:T(8,128)(2,1)S(1)} %get-tuple-element.87), channel_id=1, source_target_pairs={{0,7},{1,6},{2,5},{3,4},{4,3},{5,2},{6,1},{7,0},{8,15},{9,14},{10,... | collective-permute-start | bytes 196616 | tf_op jit(solution)/shard_map/ppermute | solution.py:44
  17.8 2.1 %prepare.1 = (f32[2,4,512,128]{3,2,1,0:T(8,128)S(1)}, bf16[128,1024]{1,0:T(8,128)(2,1)S(1)}, bf16[128,1024]{1,0:T(8,128)(2,1)}, bf16[128,1024]{1,0:T(8,128)(2,1)}) custom-call(s32[8]{0:T(128)S(1)} %copy-done.15, s32[1,128]{1,0:T(1,128)S(1)} %bitcast.22, bf16[32,1024]{1,0:T(8,128)(2,1)S(1)} %copy-done.11, bf16[8,1024]{1,0:T(8,128)(2,1)S(1)} %copy-done.13, ...), custom_call_target="tpu_custom_call" | custom-call | flops 268435456 | bytes 2097152 | tf_op jit(solution)/shard_map/prepare/pallas_call | solution.py:97
  20.0 0.4 collective-permute-done.2.rest_2_
  20.3 3.1 %collective-permute-done.3.rest_3_ = bf16[128,256]{1,0:T(8,128)(2,1)S(1)} collective-permute-done((bf16[128,256]{1,0:T(8,128)(2,1)S(1)}, bf16[128,256]{1,0:T(8,128)(2,1)S(1)}, u32[]{:S(2)}, u32[]{:S(2)}) %collective-permute-start.3) | collective-permute-done | bytes 65568 | tf_op jit(solution)/shard_map/ppermute | solution.py:44
  23.4 0.0 collective-permute-done.4.rest_4_.rest_0_
  23.5 1.7 %two_filters.2 = (bf16[512,128]{1,0:T(8,128)(2,1)S(1)}, bf16[512,256]{1,0:T(8,128)(2,1)S(1)}, f32[256,256]{1,0:T(8,128)S(1)}) custom-call(f32[2,128]{1,0:T(2,128)S(1)} %bitcast.18, f32[2,4,512,128]{3,2,1,0:T(8,128)S(1)} %get-tuple-element.83.spectra_ref, bf16[512,256]{1,0:T(8,128)(2,1)S(1)} %copy-done.2, bf16[256,512]{1,0:T(8,128)(2,1)S(1)} %copy-done.1, ...), custom_call_target="tpu_custom_call" | custom-call | flops 536870912 | bytes 1048576 | tf_op jit(solution)/shard_map/two_filters/pallas_call | solution.py:367
  25.1 1.9 %collective-permute-start.7 = (bf16[512,128]{1,0:T(8,128)(2,1)S(1)}, bf16[512,128]{1,0:T(8,128)(2,1)S(1)}, u32[]{:S(2)}, u32[]{:S(2)}) collective-permute-start(bf16[512,128]{1,0:T(8,128)(2,1)S(1)} %get-tuple-element.96), channel_id=1, source_target_pairs={{0,4},{1,5},{2,6},{3,7},{4,0},{5,1},{6,2},{7,3},{8,12},{9,13},{10,... | collective-permute-start | bytes 393224 | tf_op jit(solution)/shard_map/ppermute | solution.py:44
  27.0 0.2 own_half.2.keep_ref
  27.3 1.0 %collective-permute-start.11 = (bf16[128,1024]{1,0:T(8,128)(2,1)}, bf16[128,1024]{1,0:T(8,128)(2,1)S(1)}, u32[]{:S(2)}, u32[]{:S(2)}) collective-permute-start(bf16[128,1024]{1,0:T(8,128)(2,1)} %get-tuple-element.136.refs_4_), channel_id=1, source_target_pairs={{0,1},{1,0},{2,3},{3,2},{4,5},{5,4},{6,7},{7,6},{8,9},{9,8},{10,11... | collective-permute-start | bytes 786440 | tf_op jit(solution)/shard_map/ppermute | solution.py:44
  28.3 0.8 collective-permute-start.12
  29.0 3.1 %collective-permute-done.7.come_ref = bf16[512,128]{1,0:T(8,128)(2,1)S(1)} collective-permute-done((bf16[512,128]{1,0:T(8,128)(2,1)S(1)}, bf16[512,128]{1,0:T(8,128)(2,1)S(1)}, u32[]{:S(2)}, u32[]{:S(2)}) %collective-permute-start.7) | collective-permute-done | bytes 131104 | tf_op jit(solution)/shard_map/ppermute | solution.py:44
  32.1 0.8 second_gate.2
  32.9 2.0 %collective-permute-start.8 = (bf16[128,256]{1,0:T(8,128)(2,1)S(1)}, bf16[128,256]{1,0:T(8,128)(2,1)S(1)}, u32[]{:S(2)}, u32[]{:S(2)}) collective-permute-start(bf16[128,256]{1,0:T(8,128)(2,1)S(1)} %get-tuple-element.98), channel_id=1, source_target_pairs={{0,3},{1,2},{2,1},{3,0},{4,7},{5,6},{6,5},{7,4},{8,11},{9,10},{10,... | collective-permute-start | bytes 196616 | tf_op jit(solution)/shard_map/ppermute | solution.py:44
  34.9 1.2 %collective-permute-start.9 = (bf16[128,256]{1,0:T(8,128)(2,1)S(1)}, bf16[128,256]{1,0:T(8,128)(2,1)S(1)}, u32[]{:S(2)}, u32[]{:S(2)}) collective-permute-start(bf16[128,256]{1,0:T(8,128)(2,1)S(1)} %get-tuple-element.99), channel_id=1, source_target_pairs={{0,2},{1,3},{2,0},{3,1},{4,6},{5,7},{6,4},{7,5},{8,10},{9,11},{10,... | collective-permute-start | bytes 196616 | tf_op jit(solution)/shard_map/ppermute | solution.py:44
  36.1 0.4 collective-permute-start.10
  36.4 2.3 %collective-permute-done.8.rest_0_ = bf16[128,256]{1,0:T(8,128)(2,1)S(1)} collective-permute-done((bf16[128,256]{1,0:T(8,128)(2,1)S(1)}, bf16[128,256]{1,0:T(8,128)(2,1)S(1)}, u32[]{:S(2)}, u32[]{:S(2)}) %collective-permute-start.8) | collective-permute-done | bytes 65568 | tf_op jit(solution)/shard_map/ppermute | solution.py:44
  38.7 1.8 %collective-permute-start.14 = (bf16[128,1024]{1,0:T(8,128)(2,1)}, bf16[128,1024]{1,0:T(8,128)(2,1)}, u32[]{:S(2)}, u32[]{:S(2)}) collective-permute-start(bf16[128,1024]{1,0:T(8,128)(2,1)} %get-tuple-element.139.refs_7_), channel_id=1, source_target_pairs={{0,1},{1,0},{2,3},{3,2},{4,5},{5,4},{6,7},{7,6},{8,9},{9,8},{10,11... | collective-permute-start | bytes 786440 | tf_op jit(solution)/shard_map/ppermute | solution.py:44
  40.5 0.4 collective-permute-done.10.rest_2_
  41.0 0.0 collective-permute-done.11.refs_3_
  41.0 0.5 exit_projection.2
  41.5 1.3 %collective-permute-start.13 = (bf16[128,1024]{1,0:T(8,128)(2,1)S(1)}, bf16[128,1024]{1,0:T(8,128)(2,1)S(1)}, u32[]{:S(2)}, u32[]{:S(2)}) collective-permute-start(bf16[128,1024]{1,0:T(8,128)(2,1)S(1)} %exit_projection.2), channel_id=1, source_target_pairs={{0,8},{8,16},{16,24},{1,9},{9,17},{17,25},{2,10},{10,18},{18,26},{... | collective-permute-start | bytes 786440 | tf_op jit(solution)/shard_map/ppermute | solution.py:546
  42.9 1.0 %collective-permute-start.23 = (bf16[128,1024]{1,0:T(8,128)(2,1)}, bf16[128,1024]{1,0:T(8,128)(2,1)}, u32[]{:S(2)}, u32[]{:S(2)}) collective-permute-start(bf16[128,1024]{1,0:T(8,128)(2,1)} %get-tuple-element.136.refs_4_), channel_id=1, source_target_pairs={{0,2},{1,3},{2,0},{3,1},{4,6},{5,7},{6,4},{7,5},{8,10},{9,11},{10,... | collective-permute-start | bytes 786440 | tf_op jit(solution)/shard_map/ppermute | solution.py:44
  43.9 2.8 %hold_entry.1.weight_ref = bf16[1024,3072]{1,0:T(8,128)(2,1)S(1)} custom-call(bf16[1024,3072]{1,0:T(8,128)(2,1)} %bitcast.24), custom_call_target="tpu_custom_call" | custom-call | bytes 6291456 | tf_op jit(solution)/shard_map/hold_entry/pallas_call | solution.py:204
  46.7 0.6 far_pieces.1
  47.3 2.4 %collective-permute-start.15 = (bf16[128,256]{1,0:T(8,128)(2,1)S(1)}, bf16[128,256]{1,0:T(8,128)(2,1)S(1)}, u32[]{:S(2)}, u32[]{:S(2)}) collective-permute-start(bf16[128,256]{1,0:T(8,128)(2,1)S(1)} %get-tuple-element.116), channel_id=1, source_target_pairs={{0,4},{1,5},{2,6},{3,7},{4,0},{5,1},{6,2},{7,3},{8,12},{9,13},{10,... | collective-permute-start | bytes 196616 | tf_op jit(solution)/shard_map/ppermute | solution.py:44
  49.7 1.1 %collective-permute-start.16 = (bf16[128,256]{1,0:T(8,128)(2,1)S(1)}, bf16[128,256]{1,0:T(8,128)(2,1)S(1)}, u32[]{:S(2)}, u32[]{:S(2)}) collective-permute-start(bf16[128,256]{1,0:T(8,128)(2,1)S(1)} %get-tuple-element.117), channel_id=1, source_target_pairs={{0,6},{1,7},{2,4},{3,5},{4,2},{5,3},{6,0},{7,1},{8,14},{9,15},{10,... | collective-permute-start | bytes 196616 | tf_op jit(solution)/shard_map/ppermute | solution.py:44
  50.8 0.9 near_pieces.3
  51.8 0.1 collective-permute-start.19
  51.9 1.6 %collective-permute-start.20 = (bf16[128,512]{1,0:T(8,128)(2,1)S(1)}, bf16[128,512]{1,0:T(8,128)(2,1)S(1)}, u32[]{:S(2)}, u32[]{:S(2)}) collective-permute-start(bf16[128,512]{1,0:T(8,128)(2,1)S(1)} %get-tuple-element.122), channel_id=1, source_target_pairs={{0,2},{1,3},{2,0},{3,1},{4,6},{5,7},{6,4},{7,5},{8,10},{9,11},{10,... | collective-permute-start | bytes 393224 | tf_op jit(solution)/shard_map/ppermute | solution.py:44
  53.5 1.9 %collective-permute-start.21 = (bf16[128,512]{1,0:T(8,128)(2,1)S(1)}, bf16[128,512]{1,0:T(8,128)(2,1)S(1)}, u32[]{:S(2)}, u32[]{:S(2)}) collective-permute-start(bf16[128,512]{1,0:T(8,128)(2,1)S(1)} %get-tuple-element.123), channel_id=1, source_target_pairs={{0,1},{1,0},{2,3},{3,2},{4,5},{5,4},{6,7},{7,6},{8,9},{9,8},{10,11... | collective-permute-start | bytes 393224 | tf_op jit(solution)/shard_map/ppermute | solution.py:44
  55.3 1.3 %collective-permute-start.17 = (bf16[128,256]{1,0:T(8,128)(2,1)S(1)}, bf16[128,256]{1,0:T(8,128)(2,1)S(1)}, u32[]{:S(2)}, u32[]{:S(2)}) collective-permute-start(bf16[128,256]{1,0:T(8,128)(2,1)S(1)} %get-tuple-element.118), channel_id=1, source_target_pairs={{0,5},{1,4},{2,7},{3,6},{4,1},{5,0},{6,3},{7,2},{8,13},{9,12},{10,... | collective-permute-start | bytes 196616 | tf_op jit(solution)/shard_map/ppermute | solution.py:44
  56.6 2.0 %collective-permute-start.18 = (bf16[128,256]{1,0:T(8,128)(2,1)S(1)}, bf16[128,256]{1,0:T(8,128)(2,1)S(1)}, u32[]{:S(2)}, u32[]{:S(2)}) collective-permute-start(bf16[128,256]{1,0:T(8,128)(2,1)S(1)} %get-tuple-element.119), channel_id=1, source_target_pairs={{0,7},{1,6},{2,5},{3,4},{4,3},{5,2},{6,1},{7,0},{8,15},{9,14},{10,... | collective-permute-start | bytes 196616 | tf_op jit(solution)/shard_map/ppermute | solution.py:44
  58.6 3.4 %collective-permute-done.17.rest_2_ = bf16[128,256]{1,0:T(8,128)(2,1)S(1)} collective-permute-done((bf16[128,256]{1,0:T(8,128)(2,1)S(1)}, bf16[128,256]{1,0:T(8,128)(2,1)S(1)}, u32[]{:S(2)}, u32[]{:S(2)}) %collective-permute-start.17) | collective-permute-done | bytes 65568 | tf_op jit(solution)/shard_map/ppermute | solution.py:44
  62.1 2.7 %collective-permute-done.18.rest_3_ = bf16[128,256]{1,0:T(8,128)(2,1)S(1)} collective-permute-done((bf16[128,256]{1,0:T(8,128)(2,1)S(1)}, bf16[128,256]{1,0:T(8,128)(2,1)S(1)}, u32[]{:S(2)}, u32[]{:S(2)}) %collective-permute-start.18) | collective-permute-done | bytes 65568 | tf_op jit(solution)/shard_map/ppermute | solution.py:44
  64.8 1.5 %collective-permute-start.27 = (bf16[128,1024]{1,0:T(8,128)(2,1)}, bf16[128,1024]{1,0:T(8,128)(2,1)S(1)}, u32[]{:S(2)}, u32[]{:S(2)}) collective-permute-start(bf16[128,1024]{1,0:T(8,128)(2,1)} %collective-permute-done.23.refs_2_), channel_id=1, source_target_pairs={{0,1},{1,0},{2,3},{3,2},{4,5},{5,4},{6,7},{7,6},{8,9},{9,8},{10,11... | collective-permute-start | bytes 786440 | tf_op jit(solution)/shard_map/ppermute | solution.py:44
  66.2 1.6 %two_filters.3 = (bf16[512,128]{1,0:T(8,128)(2,1)S(1)}, bf16[512,256]{1,0:T(8,128)(2,1)S(1)}, f32[256,256]{1,0:T(8,128)S(1)}) custom-call(f32[2,128]{1,0:T(2,128)S(1)} %bitcast.20, f32[2,4,512,128]{3,2,1,0:T(8,128)S(1)} %get-tuple-element.83.spectra_ref, bf16[512,256]{1,0:T(8,128)(2,1)S(1)} %copy-done.2, bf16[256,512]{1,0:T(8,128)(2,1)S(1)} %copy-done.1, ...), custom_call_target="tpu_custom_call" | custom-call | flops 536870912 | bytes 1048576 | tf_op jit(solution)/shard_map/two_filters/pallas_call | solution.py:367
  67.9 2.3 %collective-permute-start.22 = (bf16[512,128]{1,0:T(8,128)(2,1)S(1)}, bf16[512,128]{1,0:T(8,128)(2,1)S(1)}, u32[]{:S(2)}, u32[]{:S(2)}) collective-permute-start(bf16[512,128]{1,0:T(8,128)(2,1)S(1)} %get-tuple-element.125), channel_id=1, source_target_pairs={{0,4},{1,5},{2,6},{3,7},{4,0},{5,1},{6,2},{7,3},{8,12},{9,13},{10,... | collective-permute-start | bytes 393224 | tf_op jit(solution)/shard_map/ppermute | solution.py:44
  70.2 0.2 own_half.3.keep_ref
  70.5 1.9 %hold_exit.1 = (bf16[1024,1024]{1,0:T(8,128)(2,1)S(1)}, bf16[4,128,256]{2,1,0:T(8,128)(2,1)S(1)}, bf16[128,1024]{1,0:T(8,128)(2,1)S(1)}, bf16[128,1024]{1,0:T(8,...) custom-call(bf16[1024,1024]{1,0:T(8,128)(2,1)} %bitcast.11, ...), custom_call_target="tpu_custom_call" | custom-call | bytes 3932160 | tf_op jit(solution)/shard_map/hold_exit/pallas_call | solution.py:204
  72.4 4.7 %collective-permute-done.22.come_ref = bf16[512,128]{1,0:T(8,128)(2,1)S(1)} collective-permute-done((bf16[512,128]{1,0:T(8,128)(2,1)S(1)}, bf16[512,128]{1,0:T(8,128)(2,1)S(1)}, u32[]{:S(2)}, u32[]{:S(2)}) %collective-permute-start.22) | collective-permute-done | bytes 131104 | tf_op jit(solution)/shard_map/ppermute | solution.py:44
  77.1 0.1 second_gate.3
  77.2 0.5 gradient_away.1
  77.6 2.1 %collective-permute-start.29 = (bf16[128,1024]{1,0:T(8,128)(2,1)S(1)}, bf16[128,1024]{1,0:T(8,128)(2,1)S(1)}, u32[]{:S(2)}, u32[]{:S(2)}) collective-permute-start(bf16[128,1024]{1,0:T(8,128)(2,1)S(1)} %gradient_away.1), channel_id=1, source_target_pairs={{0,4},{1,5},{2,6},{3,7},{4,0},{5,1},{6,2},{7,3},{8,12},{9,13},{10,... | collective-permute-start | bytes 786440 | tf_op jit(solution)/shard_map/ppermute | solution.py:44
  79.7 2.9 %collective-permute-start.24 = (bf16[128,256]{1,0:T(8,128)(2,1)S(1)}, bf16[128,256]{1,0:T(8,128)(2,1)S(1)}, u32[]{:S(2)}, u32[]{:S(2)}) collective-permute-start(bf16[128,256]{1,0:T(8,128)(2,1)S(1)} %get-tuple-element.150), channel_id=1, source_target_pairs={{0,3},{1,2},{2,1},{3,0},{4,7},{5,6},{6,5},{7,4},{8,11},{9,10},{10,... | collective-permute-start | bytes 196616 | tf_op jit(solution)/shard_map/ppermute | solution.py:44
  82.7 1.1 %collective-permute-start.26 = (bf16[128,256]{1,0:T(8,128)(2,1)S(1)}, bf16[128,256]{1,0:T(8,128)(2,1)S(1)}, u32[]{:S(2)}, u32[]{:S(2)}) collective-permute-start(bf16[128,256]{1,0:T(8,128)(2,1)S(1)} %get-tuple-element.152), channel_id=1, source_target_pairs={{0,1},{1,0},{2,3},{3,2},{4,5},{5,4},{6,7},{7,6},{8,9},{9,8},{10,11... | collective-permute-start | bytes 196616 | tf_op jit(solution)/shard_map/ppermute | solution.py:44
  83.7 3.9 %collective-permute-done.24.rest_0_ = bf16[128,256]{1,0:T(8,128)(2,1)S(1)} collective-permute-done((bf16[128,256]{1,0:T(8,128)(2,1)S(1)}, bf16[128,256]{1,0:T(8,128)(2,1)S(1)}, u32[]{:S(2)}, u32[]{:S(2)}) %collective-permute-start.24) | collective-permute-done | bytes 65568 | tf_op jit(solution)/shard_map/ppermute | solution.py:44
  87.7 0.7 collective-permute-done.25.rest_1_
  88.4 1.2 %exit_projection.3 = bf16[128,1024]{1,0:T(8,128)(2,1)} custom-call(s32[1]{0:T(128)} %bitcast.choice_ref, bf16[128,1024]{1,0:T(8,128)(2,1)S(1)} %collective-permute-done.13.x_ref, bf16[128,1024]{1,0:T(8,128)(2,1)S(1)} %get-tuple-element.114.other_ref, bf16[1024,1024]{1,0:T(8,128)(2,1)S(1)} %get-tuple-element.148.weight_ref, ...), custom_call_target="tpu_custom_call" | custom-call | flops 268435456 | bytes 2097152 | tf_op jit(solution)/shard_map/exit_projection/pallas_call | solution.py:439
  89.6 0.5 gradient_mine.1
  90.0 1.8 %collective-permute-done.29 = bf16[128,1024]{1,0:T(8,128)(2,1)S(1)} collective-permute-done((bf16[128,1024]{1,0:T(8,128)(2,1)S(1)}, bf16[128,1024]{1,0:T(8,128)(2,1)S(1)}, u32[]{:S(2)}, u32[]{:S(2)}) %collective-permute-start.29) | collective-permute-done | bytes 262176 | tf_op jit(solution)/shard_map/ppermute | solution.py:44
  91.9 0.9 add_bitcast_fusion
  (48 shorter events, 0.1 us)
Async XLA Ops:
  0.6 17.2 %copy-start.2 = (bf16[512,256]{1,0:T(8,128)(2,1)S(1)}, bf16[512,256]{1,0:T(8,128)(2,1)}, u32[]{:S(2)}) copy-start(bf16[512,256]{1,0:T(8,128)(2,1)} %constant.13.clone.forward_ref) | copy-start | bytes 786436
  0.6 17.2 %copy-start.5 = (bf16[1,2,128,1024]{3,2,1,0:T(8,128)(2,1)S(1)}, bf16[1,2,128,1024]{3,2,1,0:T(8,128)(2,1)}, u32[]{:S(2)}) copy-start(bf16[1,2,128,1024]{3,2,1,0:T(8,128)(2,1)} %param.23) | copy-start | bytes 1572868
  0.7 17.1 %copy-start.11 = (bf16[32,1024]{1,0:T(8,128)(2,1)S(1)}, bf16[32,1024]{1,0:T(8,128)(2,1)}, u32[]{:S(2)}) copy-start(bf16[32,1024]{1,0:T(8,128)(2,1)} %amino_ref.1) | copy-start | bytes 196612
  0.7 17.1 %copy-start.13 = (bf16[8,1024]{1,0:T(8,128)(2,1)S(1)}, bf16[8,1024]{1,0:T(8,128)(2,1)}, u32[]{:S(2)}) copy-start(bf16[8,1024]{1,0:T(8,128)(2,1)} %polymer_ref.1) | copy-start | bytes 49156
  0.7 17.1 %copy-start.15 = (s32[8]{0:T(128)S(1)}, s32[8]{0:T(128)}, u32[]{:S(2)}) copy-start(s32[8]{0:T(128)} %sizes_ref.1) | copy-start | bytes 100
  0.7 17.1 %copy-start.16 = (s32[128]{0:T(128)S(1)}, s32[128]{0:T(128)}, u32[]{:S(2)}) copy-start(s32[128]{0:T(128)} %param.14) | copy-start | bytes 1540
  3.8 14.0 %copy-start.4 = (f32[1,2,128,1024]{3,2,1,0:T(8,128)S(1)}, f32[1,2,128,1024]{3,2,1,0:T(8,128)}, u32[]{:S(2)}) copy-start(f32[1,2,128,1024]{3,2,1,0:T(8,128)} %param.20) | copy-start | bytes 3145732
  3.8 19.6 %copy-start.1 = (bf16[256,512]{1,0:T(8,128)(2,1)S(1)}, bf16[256,512]{1,0:T(8,128)(2,1)}, u32[]{:S(2)}) copy-start(bf16[256,512]{1,0:T(8,128)(2,1)} %constant.14.clone.backward_ref) | copy-start | bytes 786436
  3.9 19.6 %copy-start.12 = (f32[1,2,128]{2,1,0:T(2,128)S(1)}, f32[1,2,128]{2,1,0:T(2,128)}, u32[]{:S(2)}) copy-start(f32[1,2,128]{2,1,0:T(2,128)} %param.21) | copy-start | bytes 3076
  3.9 9.9 %collective-permute-start = (bf16[128,256]{1,0:T(8,128)(2,1)S(1)}, bf16[128,256]{1,0:T(8,128)(2,1)S(1)}, u32[]{:S(2)}, u32[]{:S(2)}) collective-permute-start(bf16[128,256]{1,0:T(8,128)(2,1)S(1)} %get-tuple-element.84), channel_id=1, source_target_pairs={{0,4},{1,5},{2,6},{3,7},{4,0},{5,1},{6,2},{7,3},{8,12},{9,13},{10,... | collective-permute-start | bytes 196616 | tf_op jit(solution)/shard_map/ppermute | solution.py:44
  8.0 8.5 %collective-permute-start.1 = (bf16[128,256]{1,0:T(8,128)(2,1)S(1)}, bf16[128,256]{1,0:T(8,128)(2,1)S(1)}, u32[]{:S(2)}, u32[]{:S(2)}) collective-permute-start(bf16[128,256]{1,0:T(8,128)(2,1)S(1)} %get-tuple-element.85), channel_id=1, source_target_pairs={{0,6},{1,7},{2,4},{3,5},{4,2},{5,3},{6,0},{7,1},{8,14},{9,15},{10,... | collective-permute-start | bytes 196616 | tf_op jit(solution)/shard_map/ppermute | solution.py:44
  10.3 13.2 %collective-permute-start.4 = (bf16[128,512]{1,0:T(8,128)(2,1)S(1)}, bf16[128,512]{1,0:T(8,128)(2,1)S(1)}, u32[]{:S(2)}, u32[]{:S(2)}) collective-permute-start(bf16[128,512]{1,0:T(8,128)(2,1)S(1)} %get-tuple-element.90), channel_id=1, source_target_pairs={{0,3},{1,2},{2,1},{3,0},{4,7},{5,6},{6,5},{7,4},{8,11},{9,10},{10,... | collective-permute-start | bytes 393224 | tf_op jit(solution)/shard_map/ppermute | solution.py:44
  11.5 12.0 %collective-permute-start.5 = (bf16[128,512]{1,0:T(8,128)(2,1)S(1)}, bf16[128,512]{1,0:T(8,128)(2,1)S(1)}, u32[]{:S(2)}, u32[]{:S(2)}) collective-permute-start(bf16[128,512]{1,0:T(8,128)(2,1)S(1)} %get-tuple-element.91), channel_id=1, source_target_pairs={{0,2},{1,3},{2,0},{3,1},{4,6},{5,7},{6,4},{7,5},{8,10},{9,11},{10,... | collective-permute-start | bytes 393224 | tf_op jit(solution)/shard_map/ppermute | solution.py:44
  13.3 10.2 %collective-permute-start.6 = (bf16[128,512]{1,0:T(8,128)(2,1)S(1)}, bf16[128,512]{1,0:T(8,128)(2,1)S(1)}, u32[]{:S(2)}, u32[]{:S(2)}) collective-permute-start(bf16[128,512]{1,0:T(8,128)(2,1)S(1)} %get-tuple-element.92), channel_id=1, source_target_pairs={{0,1},{1,0},{2,3},{3,2},{4,5},{5,4},{6,7},{7,6},{8,9},{9,8},{10,11... | collective-permute-start | bytes 393224 | tf_op jit(solution)/shard_map/ppermute | solution.py:44
  13.8 6.5 %collective-permute-start.2 = (bf16[128,256]{1,0:T(8,128)(2,1)S(1)}, bf16[128,256]{1,0:T(8,128)(2,1)S(1)}, u32[]{:S(2)}, u32[]{:S(2)}) collective-permute-start(bf16[128,256]{1,0:T(8,128)(2,1)S(1)} %get-tuple-element.86), channel_id=1, source_target_pairs={{0,5},{1,4},{2,7},{3,6},{4,1},{5,0},{6,3},{7,2},{8,13},{9,12},{10,... | collective-permute-start | bytes 196616 | tf_op jit(solution)/shard_map/ppermute | solution.py:44
  16.4 7.0 %collective-permute-start.3 = (bf16[128,256]{1,0:T(8,128)(2,1)S(1)}, bf16[128,256]{1,0:T(8,128)(2,1)S(1)}, u32[]{:S(2)}, u32[]{:S(2)}) collective-permute-start(bf16[128,256]{1,0:T(8,128)(2,1)S(1)} %get-tuple-element.87), channel_id=1, source_target_pairs={{0,7},{1,6},{2,5},{3,4},{4,3},{5,2},{6,1},{7,0},{8,15},{9,14},{10,... | collective-permute-start | bytes 196616 | tf_op jit(solution)/shard_map/ppermute | solution.py:44
  19.9 21.0 %copy-start = (bf16[1,1024,1024]{2,1,0:T(8,128)(2,1)S(1)}, bf16[1,1024,1024]{2,1,0:T(8,128)(2,1)}, u32[]{:S(2)}) copy-start(bf16[1,1024,1024]{2,1,0:T(8,128)(2,1)} %param.22) | copy-start | bytes 6291460
  20.0 21.1 %copy-start.3 = (bf16[1,128,1024]{2,1,0:T(8,128)(2,1)S(1)}, bf16[1,128,1024]{2,1,0:T(8,128)(2,1)}, u32[]{:S(2)}) copy-start(bf16[1,128,1024]{2,1,0:T(8,128)(2,1)} %param.13) | copy-start | bytes 786436
  25.1 7.0 %collective-permute-start.7 = (bf16[512,128]{1,0:T(8,128)(2,1)S(1)}, bf16[512,128]{1,0:T(8,128)(2,1)S(1)}, u32[]{:S(2)}, u32[]{:S(2)}) collective-permute-start(bf16[512,128]{1,0:T(8,128)(2,1)S(1)} %get-tuple-element.96), channel_id=1, source_target_pairs={{0,4},{1,5},{2,6},{3,7},{4,0},{5,1},{6,2},{7,3},{8,12},{9,13},{10,... | collective-permute-start | bytes 393224 | tf_op jit(solution)/shard_map/ppermute | solution.py:44
  27.3 13.7 %collective-permute-start.11 = (bf16[128,1024]{1,0:T(8,128)(2,1)}, bf16[128,1024]{1,0:T(8,128)(2,1)S(1)}, u32[]{:S(2)}, u32[]{:S(2)}) collective-permute-start(bf16[128,1024]{1,0:T(8,128)(2,1)} %get-tuple-element.136.refs_4_), channel_id=1, source_target_pairs={{0,1},{1,0},{2,3},{3,2},{4,5},{5,4},{6,7},{7,6},{8,9},{9,8},{10,11... | collective-permute-start | bytes 786440 | tf_op jit(solution)/shard_map/ppermute | solution.py:44
  28.3 12.7 %collective-permute-start.12 = (bf16[128,1024]{1,0:T(8,128)(2,1)}, bf16[128,1024]{1,0:T(8,128)(2,1)S(1)}, u32[]{:S(2)}, u32[]{:S(2)}) collective-permute-start(bf16[128,1024]{1,0:T(8,128)(2,1)} %get-tuple-element.139.refs_7_), channel_id=1, source_target_pairs={{0,2},{1,3},{2,0},{3,1},{4,6},{5,7},{6,4},{7,5},{8,10},{9,11},{10,... | collective-permute-start | bytes 786440 | tf_op jit(solution)/shard_map/ppermute | solution.py:44
  32.9 5.8 %collective-permute-start.8 = (bf16[128,256]{1,0:T(8,128)(2,1)S(1)}, bf16[128,256]{1,0:T(8,128)(2,1)S(1)}, u32[]{:S(2)}, u32[]{:S(2)}) collective-permute-start(bf16[128,256]{1,0:T(8,128)(2,1)S(1)} %get-tuple-element.98), channel_id=1, source_target_pairs={{0,3},{1,2},{2,1},{3,0},{4,7},{5,6},{6,5},{7,4},{8,11},{9,10},{10,... | collective-permute-start | bytes 196616 | tf_op jit(solution)/shard_map/ppermute | solution.py:44
  34.9 5.6 %collective-permute-start.9 = (bf16[128,256]{1,0:T(8,128)(2,1)S(1)}, bf16[128,256]{1,0:T(8,128)(2,1)S(1)}, u32[]{:S(2)}, u32[]{:S(2)}) collective-permute-start(bf16[128,256]{1,0:T(8,128)(2,1)S(1)} %get-tuple-element.99), channel_id=1, source_target_pairs={{0,2},{1,3},{2,0},{3,1},{4,6},{5,7},{6,4},{7,5},{8,10},{9,11},{10,... | collective-permute-start | bytes 196616 | tf_op jit(solution)/shard_map/ppermute | solution.py:44
  36.1 4.9 %collective-permute-start.10 = (bf16[128,256]{1,0:T(8,128)(2,1)S(1)}, bf16[128,256]{1,0:T(8,128)(2,1)S(1)}, u32[]{:S(2)}, u32[]{:S(2)}) collective-permute-start(bf16[128,256]{1,0:T(8,128)(2,1)S(1)} %get-tuple-element.100), channel_id=1, source_target_pairs={{0,1},{1,0},{2,3},{3,2},{4,5},{5,4},{6,7},{7,6},{8,9},{9,8},{10,11... | collective-permute-start | bytes 196616 | tf_op jit(solution)/shard_map/ppermute | solution.py:44
  38.7 7.9 %collective-permute-start.14 = (bf16[128,1024]{1,0:T(8,128)(2,1)}, bf16[128,1024]{1,0:T(8,128)(2,1)}, u32[]{:S(2)}, u32[]{:S(2)}) collective-permute-start(bf16[128,1024]{1,0:T(8,128)(2,1)} %get-tuple-element.139.refs_7_), channel_id=1, source_target_pairs={{0,1},{1,0},{2,3},{3,2},{4,5},{5,4},{6,7},{7,6},{8,9},{9,8},{10,11... | collective-permute-start | bytes 786440 | tf_op jit(solution)/shard_map/ppermute | solution.py:44
  41.0 2.9 %copy-start.8 = (bf16[128,1024]{1,0:T(8,128)(2,1)}, bf16[128,1024]{1,0:T(8,128)(2,1)S(1)}, u32[]{:S(2)}) copy-start(bf16[128,1024]{1,0:T(8,128)(2,1)S(1)} %collective-permute-done.11.refs_3_) | copy-start | bytes 786436
  41.0 1.9 %copy-start.6 = (bf16[128,1024]{1,0:T(8,128)(2,1)}, bf16[128,1024]{1,0:T(8,128)(2,1)S(1)}, u32[]{:S(2)}) copy-start(bf16[128,1024]{1,0:T(8,128)(2,1)S(1)} %collective-permute-done.12.refs_5_) | copy-start | bytes 786436
  41.5 5.1 %collective-permute-start.13 = (bf16[128,1024]{1,0:T(8,128)(2,1)S(1)}, bf16[128,1024]{1,0:T(8,128)(2,1)S(1)}, u32[]{:S(2)}, u32[]{:S(2)}) collective-permute-start(bf16[128,1024]{1,0:T(8,128)(2,1)S(1)} %exit_projection.2), channel_id=1, source_target_pairs={{0,8},{8,16},{16,24},{1,9},{9,17},{17,25},{2,10},{10,18},{18,26},{... | collective-permute-start | bytes 786440 | tf_op jit(solution)/shard_map/ppermute | solution.py:546
  42.9 10.6 %collective-permute-start.23 = (bf16[128,1024]{1,0:T(8,128)(2,1)}, bf16[128,1024]{1,0:T(8,128)(2,1)}, u32[]{:S(2)}, u32[]{:S(2)}) collective-permute-start(bf16[128,1024]{1,0:T(8,128)(2,1)} %get-tuple-element.136.refs_4_), channel_id=1, source_target_pairs={{0,2},{1,3},{2,0},{3,1},{4,6},{5,7},{6,4},{7,5},{8,10},{9,11},{10,... | collective-permute-start | bytes 786440 | tf_op jit(solution)/shard_map/ppermute | solution.py:44
  43.8 2.8 %copy-start.14 = (f32[1,1024]{1,0:T(1,128)S(1)}, f32[1,1024]{1,0:T(1,128)}, u32[]{:S(2)}) copy-start(f32[1,1024]{1,0:T(1,128)} %gain_ref.3) | copy-start | bytes 12292
  47.3 14.8 %copy-start.7 = (bf16[128,1024]{1,0:T(8,128)(2,1)S(1)}, bf16[128,1024]{1,0:T(8,128)(2,1)}, u32[]{:S(2)}) copy-start(bf16[128,1024]{1,0:T(8,128)(2,1)} %copy-done.6) | copy-start | bytes 786436
  47.3 8.0 %collective-permute-start.15 = (bf16[128,256]{1,0:T(8,128)(2,1)S(1)}, bf16[128,256]{1,0:T(8,128)(2,1)S(1)}, u32[]{:S(2)}, u32[]{:S(2)}) collective-permute-start(bf16[128,256]{1,0:T(8,128)(2,1)S(1)} %get-tuple-element.116), channel_id=1, source_target_pairs={{0,4},{1,5},{2,6},{3,7},{4,0},{5,1},{6,2},{7,3},{8,12},{9,13},{10,... | collective-permute-start | bytes 196616 | tf_op jit(solution)/shard_map/ppermute | solution.py:44
  49.7 7.0 %collective-permute-start.16 = (bf16[128,256]{1,0:T(8,128)(2,1)S(1)}, bf16[128,256]{1,0:T(8,128)(2,1)S(1)}, u32[]{:S(2)}, u32[]{:S(2)}) collective-permute-start(bf16[128,256]{1,0:T(8,128)(2,1)S(1)} %get-tuple-element.117), channel_id=1, source_target_pairs={{0,6},{1,7},{2,4},{3,5},{4,2},{5,3},{6,0},{7,1},{8,14},{9,15},{10,... | collective-permute-start | bytes 196616 | tf_op jit(solution)/shard_map/ppermute | solution.py:44
  50.8 19.6 %copy-start.9 = (bf16[128,1024]{1,0:T(8,128)(2,1)S(1)}, bf16[128,1024]{1,0:T(8,128)(2,1)}, u32[]{:S(2)}) copy-start(bf16[128,1024]{1,0:T(8,128)(2,1)} %copy-done.8) | copy-start | bytes 786436
  50.8 19.6 %copy-start.10 = (bf16[4,128,256]{2,1,0:T(8,128)(2,1)S(1)}, bf16[4,128,256]{2,1,0:T(8,128)(2,1)}, u32[]{:S(2)}) copy-start(bf16[4,128,256]{2,1,0:T(8,128)(2,1)} %get-tuple-element.133.refs_1_) | copy-start | bytes 786436
  51.8 13.0 %collective-permute-start.19 = (bf16[128,512]{1,0:T(8,128)(2,1)S(1)}, bf16[128,512]{1,0:T(8,128)(2,1)S(1)}, u32[]{:S(2)}, u32[]{:S(2)}) collective-permute-start(bf16[128,512]{1,0:T(8,128)(2,1)S(1)} %get-tuple-element.121), channel_id=1, source_target_pairs={{0,3},{1,2},{2,1},{3,0},{4,7},{5,6},{6,5},{7,4},{8,11},{9,10},{10,... | collective-permute-start | bytes 393224 | tf_op jit(solution)/shard_map/ppermute | solution.py:44
  51.9 12.9 %collective-permute-start.20 = (bf16[128,512]{1,0:T(8,128)(2,1)S(1)}, bf16[128,512]{1,0:T(8,128)(2,1)S(1)}, u32[]{:S(2)}, u32[]{:S(2)}) collective-permute-start(bf16[128,512]{1,0:T(8,128)(2,1)S(1)} %get-tuple-element.122), channel_id=1, source_target_pairs={{0,2},{1,3},{2,0},{3,1},{4,6},{5,7},{6,4},{7,5},{8,10},{9,11},{10,... | collective-permute-start | bytes 393224 | tf_op jit(solution)/shard_map/ppermute | solution.py:44
  53.5 11.3 %collective-permute-start.21 = (bf16[128,512]{1,0:T(8,128)(2,1)S(1)}, bf16[128,512]{1,0:T(8,128)(2,1)S(1)}, u32[]{:S(2)}, u32[]{:S(2)}) collective-permute-start(bf16[128,512]{1,0:T(8,128)(2,1)S(1)} %get-tuple-element.123), channel_id=1, source_target_pairs={{0,1},{1,0},{2,3},{3,2},{4,5},{5,4},{6,7},{7,6},{8,9},{9,8},{10,11... | collective-permute-start | bytes 393224 | tf_op jit(solution)/shard_map/ppermute | solution.py:44
  55.3 6.7 %collective-permute-start.17 = (bf16[128,256]{1,0:T(8,128)(2,1)S(1)}, bf16[128,256]{1,0:T(8,128)(2,1)S(1)}, u32[]{:S(2)}, u32[]{:S(2)}) collective-permute-start(bf16[128,256]{1,0:T(8,128)(2,1)S(1)} %get-tuple-element.118), channel_id=1, source_target_pairs={{0,5},{1,4},{2,7},{3,6},{4,1},{5,0},{6,3},{7,2},{8,13},{9,12},{10,... | collective-permute-start | bytes 196616 | tf_op jit(solution)/shard_map/ppermute | solution.py:44
  56.6 8.1 %collective-permute-start.18 = (bf16[128,256]{1,0:T(8,128)(2,1)S(1)}, bf16[128,256]{1,0:T(8,128)(2,1)S(1)}, u32[]{:S(2)}, u32[]{:S(2)}) collective-permute-start(bf16[128,256]{1,0:T(8,128)(2,1)S(1)} %get-tuple-element.119), channel_id=1, source_target_pairs={{0,7},{1,6},{2,5},{3,4},{4,3},{5,2},{6,1},{7,0},{8,15},{9,14},{10,... | collective-permute-start | bytes 196616 | tf_op jit(solution)/shard_map/ppermute | solution.py:44
  62.1 15.1 %collective-permute-start.28 = (bf16[128,1024]{1,0:T(8,128)(2,1)S(1)}, bf16[128,1024]{1,0:T(8,128)(2,1)S(1)}, u32[]{:S(2)}, u32[]{:S(2)}) collective-permute-start(bf16[128,1024]{1,0:T(8,128)(2,1)S(1)} %copy-done.7), channel_id=1, source_target_pairs={{0,1},{1,0},{2,3},{3,2},{4,5},{5,4},{6,7},{7,6},{8,9},{9,8},{10,11... | collective-permute-start | bytes 786440 | tf_op jit(solution)/shard_map/ppermute | solution.py:44
  64.8 12.4 %collective-permute-start.27 = (bf16[128,1024]{1,0:T(8,128)(2,1)}, bf16[128,1024]{1,0:T(8,128)(2,1)S(1)}, u32[]{:S(2)}, u32[]{:S(2)}) collective-permute-start(bf16[128,1024]{1,0:T(8,128)(2,1)} %collective-permute-done.23.refs_2_), channel_id=1, source_target_pairs={{0,1},{1,0},{2,3},{3,2},{4,5},{5,4},{6,7},{7,6},{8,9},{9,8},{10,11... | collective-permute-start | bytes 786440 | tf_op jit(solution)/shard_map/ppermute | solution.py:44
  67.9 9.2 %collective-permute-start.22 = (bf16[512,128]{1,0:T(8,128)(2,1)S(1)}, bf16[512,128]{1,0:T(8,128)(2,1)S(1)}, u32[]{:S(2)}, u32[]{:S(2)}) collective-permute-start(bf16[512,128]{1,0:T(8,128)(2,1)S(1)} %get-tuple-element.125), channel_id=1, source_target_pairs={{0,4},{1,5},{2,6},{3,7},{4,0},{5,1},{6,2},{7,3},{8,12},{9,13},{10,... | collective-permute-start | bytes 393224 | tf_op jit(solution)/shard_map/ppermute | solution.py:44
  77.6 14.2 %collective-permute-start.29 = (bf16[128,1024]{1,0:T(8,128)(2,1)S(1)}, bf16[128,1024]{1,0:T(8,128)(2,1)S(1)}, u32[]{:S(2)}, u32[]{:S(2)}) collective-permute-start(bf16[128,1024]{1,0:T(8,128)(2,1)S(1)} %gradient_away.1), channel_id=1, source_target_pairs={{0,4},{1,5},{2,6},{3,7},{4,0},{5,1},{6,2},{7,3},{8,12},{9,13},{10,... | collective-permute-start | bytes 786440 | tf_op jit(solution)/shard_map/ppermute | solution.py:44
  79.7 8.0 %collective-permute-start.24 = (bf16[128,256]{1,0:T(8,128)(2,1)S(1)}, bf16[128,256]{1,0:T(8,128)(2,1)S(1)}, u32[]{:S(2)}, u32[]{:S(2)}) collective-permute-start(bf16[128,256]{1,0:T(8,128)(2,1)S(1)} %get-tuple-element.150), channel_id=1, source_target_pairs={{0,3},{1,2},{2,1},{3,0},{4,7},{5,6},{6,5},{7,4},{8,11},{9,10},{10,... | collective-permute-start | bytes 196616 | tf_op jit(solution)/shard_map/ppermute | solution.py:44
  82.6 5.7 %collective-permute-start.25 = (bf16[128,256]{1,0:T(8,128)(2,1)S(1)}, bf16[128,256]{1,0:T(8,128)(2,1)S(1)}, u32[]{:S(2)}, u32[]{:S(2)}) collective-permute-start(bf16[128,256]{1,0:T(8,128)(2,1)S(1)} %get-tuple-element.151), channel_id=1, source_target_pairs={{0,2},{1,3},{2,0},{3,1},{4,6},{5,7},{6,4},{7,5},{8,10},{9,11},{10,... | collective-permute-start | bytes 196616 | tf_op jit(solution)/shard_map/ppermute | solution.py:44
  82.7 5.7 %collective-permute-start.26 = (bf16[128,256]{1,0:T(8,128)(2,1)S(1)}, bf16[128,256]{1,0:T(8,128)(2,1)S(1)}, u32[]{:S(2)}, u32[]{:S(2)}) collective-permute-start(bf16[128,256]{1,0:T(8,128)(2,1)S(1)} %get-tuple-element.152), channel_id=1, source_target_pairs={{0,1},{1,0},{2,3},{3,2},{4,5},{5,4},{6,7},{7,6},{8,9},{9,8},{10,11... | collective-permute-start | bytes 196616 | tf_op jit(solution)/shard_map/ppermute | solution.py:44

commit v5 on v4

--- a/solution.py
+++ b/solution.py
@@ -409,7 +409,7 @@
     rows, width = gates[0].shape
     out = jax.ShapeDtypeStruct((rows, width // 2), bf16)
     kept = (len(gates), rows, width // 2)
-    kept = pltpu.HBM(kept, bf16) if later else jax.ShapeDtypeStruct(kept, bf16)
+    kept = jax.ShapeDtypeStruct(kept, bf16)
     return pl.pallas_call(
         functools.partial(gate_kernel, order),
         out_shape=(out,) * len(gates) + (kept,),
@@ -551,7 +551,7 @@
     spread([(0, d) for d in lines] + [(1, d) for d in range(3, group, 2)], home)
 
     def second_beside(come):
-        spread([(0, d) for d in range(3, group, 2)], come)
+        spread([(0, d) for d in range(3, group, 2)], come[:2])
 
         def held(keep):
             early = [weight_out, first_hyenas] + [seeds[step, d] for step in range(2) for d in near if d % 2 == 0 or d == 1]
@@ -564,6 +564,7 @@
     seeds = [early.pop(0) if d % 2 == 0 or d == 1 else seeds[step, d] for step in range(2) for d in near]
     away = gradient(first_hyenas, second_hyenas, seeds, 1, bf16, "gradient_away")
     mine = gradient(first_hyenas, second_hyenas, seeds, 0, f32, "gradient_mine")
+    home, mine = lax.optimization_barrier((home, mine))
     passed = exit_projection(first_section, handed, embedded, weight_again, home, near)
     out_grad = mine + exchange(away, group).astype(f32)
     return (passed[None], out_grad[None])

time: 92.9 us -> 92.5 us (level)
  transfers between devices with their start and end apart: 30 -> 30, of which waited for: 11 -> 10; matrix products, arithmetic and copies ran while one was open for 0% -> 0% of each run, Pallas kernels for 16% -> 15%
where the time goes in v5:
time: 92.5 us; the launch traced here: 92.4 us
  starting transfers between devices  45 us (49%)
  waiting for transfers between devices  26.4 us (29%)
  Pallas kernels  19 us (21%)
  between operations  1.02 us (1%)
    ppermute x29, starting transfers between devices, exchange(): return lax.ppermute(value, 'seq', [(i, i ^ distance) for i in range(peers)])  43.7 us
    ppermute x29, waiting for transfers between devices, exchange(): return lax.ppermute(value, 'seq', [(i, i ^ distance) for i in range(peers)])  26.4 us
    pallas_call x2, Pallas kernels, hold(): pl.pallas_call(functools.partial(hold_kernel, count), out_shape=tuple((pl...  4.7 us
    pallas_call x2, Pallas kernels, filtered(): pl.pallas_call(functools.partial(filter_kernel, order), out_shape=(out, k...  3.3 us
    pallas_call x1, Pallas kernels, project(): pl.pallas_call(functools.partial(far_stream_kernel, far), out_shape=outs,...  3.13 us
    pallas_call x1, Pallas kernels, prepare(): pl.pallas_call(prepare_kernel, out_shape=(jax.ShapeDtypeStruct((2, chunks...  2.12 us
    pallas_call x2, Pallas kernels, project(): pl.pallas_call(functools.partial(near_kernel, near, other is None), out_s...  1.85 us
  transfers between devices with their start and end apart: 30, of which 10 were waited for; matrix products, arithmetic and copies ran while one was open for 0% of the time, Pallas kernels for 15%

profile of v5, /device:TPU:0, one launch (start us, length us, event | category | flops | bytes accessed | tf_op | source)
XLA Modules:
  0.0 92.4 jit_solution(15949912788199742869)
XLA Ops:
  0.6 0.0 copy-start.2
  0.7 3.1 %far_pieces_streamed.1 = (bf16[128,256]{1,0:T(8,128)(2,1)S(1)}, bf16[128,256]{1,0:T(8,128)(2,1)S(1)}, bf16[128,256]{1,0:T(8,128)(2,1)S(1)}, bf16[128,256]{1,0:T(...) custom-call(bf16[128,1024]{1,0:T(8,128)(2,1)} %bitcast.13, f32[1,1024]{1,0:T(1,128)} %gain_ref.3, ...), custom_call_target="tpu_custom_call" | custom-call | flops 268435456 | bytes 2097152 | tf_op jit(solution)/shard_map/far_pieces_streamed/pallas_call | solution.py:242
  3.8 0.0 copy-start.4
  3.8 0.0 copy-start.1
  3.9 0.0 copy-start.13
  3.9 4.1 %collective-permute-start = (bf16[128,256]{1,0:T(8,128)(2,1)S(1)}, bf16[128,256]{1,0:T(8,128)(2,1)S(1)}, u32[]{:S(2)}, u32[]{:S(2)}) collective-permute-start(bf16[128,256]{1,0:T(8,128)(2,1)S(1)} %get-tuple-element.89), channel_id=1, source_target_pairs={{0,4},{1,5},{2,6},{3,7},{4,0},{5,1},{6,2},{7,3},{8,12},{9,13},{10,... | collective-permute-start | bytes 196616 | tf_op jit(solution)/shard_map/ppermute | solution.py:44
  8.0 1.3 %collective-permute-start.1 = (bf16[128,256]{1,0:T(8,128)(2,1)S(1)}, bf16[128,256]{1,0:T(8,128)(2,1)S(1)}, u32[]{:S(2)}, u32[]{:S(2)}) collective-permute-start(bf16[128,256]{1,0:T(8,128)(2,1)S(1)} %get-tuple-element.90), channel_id=1, source_target_pairs={{0,6},{1,7},{2,4},{3,5},{4,2},{5,3},{6,0},{7,1},{8,14},{9,15},{10,... | collective-permute-start | bytes 196616 | tf_op jit(solution)/shard_map/ppermute | solution.py:44
  9.3 0.9 %near_pieces.2 = (bf16[128,512]{1,0:T(8,128)(2,1)S(1)}, bf16[128,512]{1,0:T(8,128)(2,1)S(1)}, bf16[128,512]{1,0:T(8,128)(2,1)S(1)}, bf16[128,512]{1,0:T(8,128)(2,1)S(1)}) custom-call(bf16[128,1024]{1,0:T(8,128)(2,1)S(1)} %get-tuple-element.93.normed_ref, bf16[1024,2048]{1,0:T(8,128)(2,1)S(1)} %get-tuple-element.94.weight_ref), custom_call_target="tpu_custom_call" | custom-call | flops 536870912 | bytes 4194304 | tf_op jit(solution)/shard_map/near_pieces/pallas_call | solution.py:271
  10.3 1.2 %collective-permute-start.4 = (bf16[128,512]{1,0:T(8,128)(2,1)S(1)}, bf16[128,512]{1,0:T(8,128)(2,1)S(1)}, u32[]{:S(2)}, u32[]{:S(2)}) collective-permute-start(bf16[128,512]{1,0:T(8,128)(2,1)S(1)} %get-tuple-element.95), channel_id=1, source_target_pairs={{0,3},{1,2},{2,1},{3,0},{4,7},{5,6},{6,5},{7,4},{8,11},{9,10},{10,... | collective-permute-start | bytes 393224 | tf_op jit(solution)/shard_map/ppermute | solution.py:44
  11.5 1.8 %collective-permute-start.5 = (bf16[128,512]{1,0:T(8,128)(2,1)S(1)}, bf16[128,512]{1,0:T(8,128)(2,1)S(1)}, u32[]{:S(2)}, u32[]{:S(2)}) collective-permute-start(bf16[128,512]{1,0:T(8,128)(2,1)S(1)} %get-tuple-element.96), channel_id=1, source_target_pairs={{0,2},{1,3},{2,0},{3,1},{4,6},{5,7},{6,4},{7,5},{8,10},{9,11},{10,... | collective-permute-start | bytes 393224 | tf_op jit(solution)/shard_map/ppermute | solution.py:44
  13.3 0.5 collective-permute-start.6
  13.8 2.6 %collective-permute-start.2 = (bf16[128,256]{1,0:T(8,128)(2,1)S(1)}, bf16[128,256]{1,0:T(8,128)(2,1)S(1)}, u32[]{:S(2)}, u32[]{:S(2)}) collective-permute-start(bf16[128,256]{1,0:T(8,128)(2,1)S(1)} %get-tuple-element.91), channel_id=1, source_target_pairs={{0,5},{1,4},{2,7},{3,6},{4,1},{5,0},{6,3},{7,2},{8,13},{9,12},{10,... | collective-permute-start | bytes 196616 | tf_op jit(solution)/shard_map/ppermute | solution.py:44
  16.4 0.0 collective-permute-done.1.rest_1_
  16.4 1.4 %collective-permute-start.3 = (bf16[128,256]{1,0:T(8,128)(2,1)S(1)}, bf16[128,256]{1,0:T(8,128)(2,1)S(1)}, u32[]{:S(2)}, u32[]{:S(2)}) collective-permute-start(bf16[128,256]{1,0:T(8,128)(2,1)S(1)} %get-tuple-element.92), channel_id=1, source_target_pairs={{0,7},{1,6},{2,5},{3,4},{4,3},{5,2},{6,1},{7,0},{8,15},{9,14},{10,... | collective-permute-start | bytes 196616 | tf_op jit(solution)/shard_map/ppermute | solution.py:44
  17.8 2.1 %prepare.1 = (f32[2,4,512,128]{3,2,1,0:T(8,128)S(1)}, bf16[128,1024]{1,0:T(8,128)(2,1)S(1)}, bf16[128,1024]{1,0:T(8,128)(2,1)}, bf16[128,1024]{1,0:T(8,128)(2,1)}) custom-call(s32[8]{0:T(128)S(1)} %copy-done.16, s32[1,128]{1,0:T(1,128)S(1)} %bitcast.22, bf16[32,1024]{1,0:T(8,128)(2,1)S(1)} %copy-done.12, bf16[8,1024]{1,0:T(8,128)(2,1)S(1)} %copy-done.14, ...), custom_call_target="tpu_custom_call" | custom-call | flops 268435456 | bytes 2097152 | tf_op jit(solution)/shard_map/prepare/pallas_call | solution.py:97
  20.0 0.4 collective-permute-done.2.rest_2_
  20.3 3.1 %collective-permute-done.3.rest_3_ = bf16[128,256]{1,0:T(8,128)(2,1)S(1)} collective-permute-done((bf16[128,256]{1,0:T(8,128)(2,1)S(1)}, bf16[128,256]{1,0:T(8,128)(2,1)S(1)}, u32[]{:S(2)}, u32[]{:S(2)}) %collective-permute-start.3) | collective-permute-done | bytes 65568 | tf_op jit(solution)/shard_map/ppermute | solution.py:44
  23.4 0.0 collective-permute-done.4.rest_4_.rest_0_
  23.4 0.0 collective-permute-done.5.rest_5_.rest_1_
  23.5 1.7 %two_filters.2 = (bf16[512,128]{1,0:T(8,128)(2,1)S(1)}, bf16[512,256]{1,0:T(8,128)(2,1)S(1)}, f32[256,256]{1,0:T(8,128)S(1)}) custom-call(f32[2,128]{1,0:T(2,128)S(1)} %bitcast.18, f32[2,4,512,128]{3,2,1,0:T(8,128)S(1)} %get-tuple-element.88.spectra_ref, bf16[512,256]{1,0:T(8,128)(2,1)S(1)} %copy-done.2, bf16[256,512]{1,0:T(8,128)(2,1)S(1)} %copy-done.1, ...), custom_call_target="tpu_custom_call" | custom-call | flops 536870912 | bytes 1048576 | tf_op jit(solution)/shard_map/two_filters/pallas_call | solution.py:367
  25.1 1.9 %collective-permute-start.7 = (bf16[512,128]{1,0:T(8,128)(2,1)S(1)}, bf16[512,128]{1,0:T(8,128)(2,1)S(1)}, u32[]{:S(2)}, u32[]{:S(2)}) collective-permute-start(bf16[512,128]{1,0:T(8,128)(2,1)S(1)} %get-tuple-element.101), channel_id=1, source_target_pairs={{0,4},{1,5},{2,6},{3,7},{4,0},{5,1},{6,2},{7,3},{8,12},{9,13},{10,... | collective-permute-start | bytes 393224 | tf_op jit(solution)/shard_map/ppermute | solution.py:44
  27.0 0.2 own_half.2.keep_ref
  27.3 1.0 %collective-permute-start.11 = (bf16[128,1024]{1,0:T(8,128)(2,1)}, bf16[128,1024]{1,0:T(8,128)(2,1)S(1)}, u32[]{:S(2)}, u32[]{:S(2)}) collective-permute-start(bf16[128,1024]{1,0:T(8,128)(2,1)} %get-tuple-element.141.refs_4_), channel_id=1, source_target_pairs={{0,1},{1,0},{2,3},{3,2},{4,5},{5,4},{6,7},{7,6},{8,9},{9,8},{10,11... | collective-permute-start | bytes 786440 | tf_op jit(solution)/shard_map/ppermute | solution.py:44
  28.3 0.8 collective-permute-start.12
  29.0 3.1 %collective-permute-done.7.come_ref = bf16[512,128]{1,0:T(8,128)(2,1)S(1)} collective-permute-done((bf16[512,128]{1,0:T(8,128)(2,1)S(1)}, bf16[512,128]{1,0:T(8,128)(2,1)S(1)}, u32[]{:S(2)}, u32[]{:S(2)}) %collective-permute-start.7) | collective-permute-done | bytes 131104 | tf_op jit(solution)/shard_map/ppermute | solution.py:44
  32.1 0.1 second_gate.2
  32.2 2.0 %collective-permute-start.8 = (bf16[128,256]{1,0:T(8,128)(2,1)S(1)}, bf16[128,256]{1,0:T(8,128)(2,1)S(1)}, u32[]{:S(2)}, u32[]{:S(2)}) collective-permute-start(bf16[128,256]{1,0:T(8,128)(2,1)S(1)} %get-tuple-element.103), channel_id=1, source_target_pairs={{0,3},{1,2},{2,1},{3,0},{4,7},{5,6},{6,5},{7,4},{8,11},{9,10},{10,... | collective-permute-start | bytes 196616 | tf_op jit(solution)/shard_map/ppermute | solution.py:44
  34.3 1.2 %collective-permute-start.9 = (bf16[128,256]{1,0:T(8,128)(2,1)S(1)}, bf16[128,256]{1,0:T(8,128)(2,1)S(1)}, u32[]{:S(2)}, u32[]{:S(2)}) collective-permute-start(bf16[128,256]{1,0:T(8,128)(2,1)S(1)} %get-tuple-element.104), channel_id=1, source_target_pairs={{0,2},{1,3},{2,0},{3,1},{4,6},{5,7},{6,4},{7,5},{8,10},{9,11},{10,... | collective-permute-start | bytes 196616 | tf_op jit(solution)/shard_map/ppermute | solution.py:44
  35.4 0.4 collective-permute-start.10
  35.8 2.9 %collective-permute-done.8.rest_0_ = bf16[128,256]{1,0:T(8,128)(2,1)S(1)} collective-permute-done((bf16[128,256]{1,0:T(8,128)(2,1)S(1)}, bf16[128,256]{1,0:T(8,128)(2,1)S(1)}, u32[]{:S(2)}, u32[]{:S(2)}) %collective-permute-start.8) | collective-permute-done | bytes 65568 | tf_op jit(solution)/shard_map/ppermute | solution.py:44
  38.7 1.8 %collective-permute-start.14 = (bf16[128,1024]{1,0:T(8,128)(2,1)}, bf16[128,1024]{1,0:T(8,128)(2,1)}, u32[]{:S(2)}, u32[]{:S(2)}) collective-permute-start(bf16[128,1024]{1,0:T(8,128)(2,1)} %get-tuple-element.144.refs_7_), channel_id=1, source_target_pairs={{0,1},{1,0},{2,3},{3,2},{4,5},{5,4},{6,7},{7,6},{8,9},{9,8},{10,11... | collective-permute-start | bytes 786440 | tf_op jit(solution)/shard_map/ppermute | solution.py:44
  40.6 0.5 exit_projection.2
  41.1 1.3 %collective-permute-start.13 = (bf16[128,1024]{1,0:T(8,128)(2,1)S(1)}, bf16[128,1024]{1,0:T(8,128)(2,1)S(1)}, u32[]{:S(2)}, u32[]{:S(2)}) collective-permute-start(bf16[128,1024]{1,0:T(8,128)(2,1)S(1)} %exit_projection.2), channel_id=1, source_target_pairs={{0,8},{8,16},{16,24},{1,9},{9,17},{17,25},{2,10},{10,18},{18,26},{... | collective-permute-start | bytes 786440 | tf_op jit(solution)/shard_map/ppermute | solution.py:546
  42.4 0.8 collective-permute-start.23
  43.2 2.8 %hold_entry.1.weight_ref = bf16[1024,3072]{1,0:T(8,128)(2,1)S(1)} custom-call(bf16[1024,3072]{1,0:T(8,128)(2,1)} %bitcast.24), custom_call_target="tpu_custom_call" | custom-call | bytes 6291456 | tf_op jit(solution)/shard_map/hold_entry/pallas_call | solution.py:204
  46.0 0.6 far_pieces.1
  46.6 2.1 %collective-permute-start.15 = (bf16[128,256]{1,0:T(8,128)(2,1)S(1)}, bf16[128,256]{1,0:T(8,128)(2,1)S(1)}, u32[]{:S(2)}, u32[]{:S(2)}) collective-permute-start(bf16[128,256]{1,0:T(8,128)(2,1)S(1)} %get-tuple-element.121), channel_id=1, source_target_pairs={{0,4},{1,5},{2,6},{3,7},{4,0},{5,1},{6,2},{7,3},{8,12},{9,13},{10,... | collective-permute-start | bytes 196616 | tf_op jit(solution)/shard_map/ppermute | solution.py:44
  48.7 1.7 %collective-permute-start.16 = (bf16[128,256]{1,0:T(8,128)(2,1)S(1)}, bf16[128,256]{1,0:T(8,128)(2,1)S(1)}, u32[]{:S(2)}, u32[]{:S(2)}) collective-permute-start(bf16[128,256]{1,0:T(8,128)(2,1)S(1)} %get-tuple-element.122), channel_id=1, source_target_pairs={{0,6},{1,7},{2,4},{3,5},{4,2},{5,3},{6,0},{7,1},{8,14},{9,15},{10,... | collective-permute-start | bytes 196616 | tf_op jit(solution)/shard_map/ppermute | solution.py:44
  50.4 0.9 %near_pieces.3 = (bf16[128,512]{1,0:T(8,128)(2,1)S(1)}, bf16[128,512]{1,0:T(8,128)(2,1)S(1)}, bf16[128,512]{1,0:T(8,128)(2,1)S(1)}, bf16[128,512]{1,0:T(8,128)(2,1)S(1)}) custom-call(bf16[128,1024]{1,0:T(8,128)(2,1)S(1)} %get-tuple-element.125.normed_ref, bf16[1024,3072]{1,0:T(8,128)(2,1)S(1)} %hold_entry.1.weight_ref), custom_call_target="tpu_custom_call" | custom-call | flops 536870912 | bytes 4194304 | tf_op jit(solution)/shard_map/near_pieces/pallas_call | solution.py:271
  51.3 0.5 collective-permute-start.19
  51.8 1.6 %collective-permute-start.20 = (bf16[128,512]{1,0:T(8,128)(2,1)S(1)}, bf16[128,512]{1,0:T(8,128)(2,1)S(1)}, u32[]{:S(2)}, u32[]{:S(2)}) collective-permute-start(bf16[128,512]{1,0:T(8,128)(2,1)S(1)} %get-tuple-element.127), channel_id=1, source_target_pairs={{0,2},{1,3},{2,0},{3,1},{4,6},{5,7},{6,4},{7,5},{8,10},{9,11},{10,... | collective-permute-start | bytes 393224 | tf_op jit(solution)/shard_map/ppermute | solution.py:44
  53.4 1.5 %collective-permute-start.21 = (bf16[128,512]{1,0:T(8,128)(2,1)S(1)}, bf16[128,512]{1,0:T(8,128)(2,1)S(1)}, u32[]{:S(2)}, u32[]{:S(2)}) collective-permute-start(bf16[128,512]{1,0:T(8,128)(2,1)S(1)} %get-tuple-element.128), channel_id=1, source_target_pairs={{0,1},{1,0},{2,3},{3,2},{4,5},{5,4},{6,7},{7,6},{8,9},{9,8},{10,11... | collective-permute-start | bytes 393224 | tf_op jit(solution)/shard_map/ppermute | solution.py:44
  54.9 1.5 %collective-permute-start.17 = (bf16[128,256]{1,0:T(8,128)(2,1)S(1)}, bf16[128,256]{1,0:T(8,128)(2,1)S(1)}, u32[]{:S(2)}, u32[]{:S(2)}) collective-permute-start(bf16[128,256]{1,0:T(8,128)(2,1)S(1)} %get-tuple-element.123), channel_id=1, source_target_pairs={{0,5},{1,4},{2,7},{3,6},{4,1},{5,0},{6,3},{7,2},{8,13},{9,12},{10,... | collective-permute-start | bytes 196616 | tf_op jit(solution)/shard_map/ppermute | solution.py:44
  56.4 1.8 %collective-permute-start.18 = (bf16[128,256]{1,0:T(8,128)(2,1)S(1)}, bf16[128,256]{1,0:T(8,128)(2,1)S(1)}, u32[]{:S(2)}, u32[]{:S(2)}) collective-permute-start(bf16[128,256]{1,0:T(8,128)(2,1)S(1)} %get-tuple-element.124), channel_id=1, source_target_pairs={{0,7},{1,6},{2,5},{3,4},{4,3},{5,2},{6,1},{7,0},{8,15},{9,14},{10,... | collective-permute-start | bytes 196616 | tf_op jit(solution)/shard_map/ppermute | solution.py:44
  58.2 3.4 %collective-permute-done.17.rest_2_ = bf16[128,256]{1,0:T(8,128)(2,1)S(1)} collective-permute-done((bf16[128,256]{1,0:T(8,128)(2,1)S(1)}, bf16[128,256]{1,0:T(8,128)(2,1)S(1)}, u32[]{:S(2)}, u32[]{:S(2)}) %collective-permute-start.17) | collective-permute-done | bytes 65568 | tf_op jit(solution)/shard_map/ppermute | solution.py:44
  61.5 0.2 collective-permute-start.28
  61.8 2.9 %collective-permute-done.18.rest_3_ = bf16[128,256]{1,0:T(8,128)(2,1)S(1)} collective-permute-done((bf16[128,256]{1,0:T(8,128)(2,1)S(1)}, bf16[128,256]{1,0:T(8,128)(2,1)S(1)}, u32[]{:S(2)}, u32[]{:S(2)}) %collective-permute-start.18) | collective-permute-done | bytes 65568 | tf_op jit(solution)/shard_map/ppermute | solution.py:44
  64.7 0.8 collective-permute-start.27
  65.5 1.7 %two_filters.3 = (bf16[512,128]{1,0:T(8,128)(2,1)S(1)}, bf16[512,256]{1,0:T(8,128)(2,1)S(1)}, f32[256,256]{1,0:T(8,128)S(1)}) custom-call(f32[2,128]{1,0:T(2,128)S(1)} %bitcast.20, f32[2,4,512,128]{3,2,1,0:T(8,128)S(1)} %get-tuple-element.88.spectra_ref, bf16[512,256]{1,0:T(8,128)(2,1)S(1)} %copy-done.2, bf16[256,512]{1,0:T(8,128)(2,1)S(1)} %copy-done.1, ...), custom_call_target="tpu_custom_call" | custom-call | flops 536870912 | bytes 1048576 | tf_op jit(solution)/shard_map/two_filters/pallas_call | solution.py:367
  67.2 2.9 %collective-permute-start.22 = (bf16[512,128]{1,0:T(8,128)(2,1)S(1)}, bf16[512,128]{1,0:T(8,128)(2,1)S(1)}, u32[]{:S(2)}, u32[]{:S(2)}) collective-permute-start(bf16[512,128]{1,0:T(8,128)(2,1)S(1)} %get-tuple-element.130), channel_id=1, source_target_pairs={{0,4},{1,5},{2,6},{3,7},{4,0},{5,1},{6,2},{7,3},{8,12},{9,13},{10,... | collective-permute-start | bytes 393224 | tf_op jit(solution)/shard_map/ppermute | solution.py:44
  70.0 0.2 own_half.3.keep_ref
  70.3 1.9 %hold_exit.1 = (bf16[1024,1024]{1,0:T(8,128)(2,1)S(1)}, bf16[4,128,256]{2,1,0:T(8,128)(2,1)S(1)}, bf16[128,1024]{1,0:T(8,128)(2,1)S(1)}, bf16[128,1024]{1,0:T(8,...) custom-call(bf16[1024,1024]{1,0:T(8,128)(2,1)} %bitcast.11, ...), custom_call_target="tpu_custom_call" | custom-call | bytes 3932160 | tf_op jit(solution)/shard_map/hold_exit/pallas_call | solution.py:204
  72.2 4.2 %collective-permute-done.22.come_ref = bf16[512,128]{1,0:T(8,128)(2,1)S(1)} collective-permute-done((bf16[512,128]{1,0:T(8,128)(2,1)S(1)}, bf16[512,128]{1,0:T(8,128)(2,1)S(1)}, u32[]{:S(2)}, u32[]{:S(2)}) %collective-permute-start.22) | collective-permute-done | bytes 131104 | tf_op jit(solution)/shard_map/ppermute | solution.py:44
  76.4 0.1 second_gate.3
  76.5 0.5 gradient_away.1
  76.9 2.4 %collective-permute-start.29 = (bf16[128,1024]{1,0:T(8,128)(2,1)S(1)}, bf16[128,1024]{1,0:T(8,128)(2,1)S(1)}, u32[]{:S(2)}, u32[]{:S(2)}) collective-permute-start(bf16[128,1024]{1,0:T(8,128)(2,1)S(1)} %gradient_away.1), channel_id=1, source_target_pairs={{0,4},{1,5},{2,6},{3,7},{4,0},{5,1},{6,2},{7,3},{8,12},{9,13},{10,... | collective-permute-start | bytes 786440 | tf_op jit(solution)/shard_map/ppermute | solution.py:44
  79.4 3.1 %collective-permute-start.24 = (bf16[128,256]{1,0:T(8,128)(2,1)S(1)}, bf16[128,256]{1,0:T(8,128)(2,1)S(1)}, u32[]{:S(2)}, u32[]{:S(2)}) collective-permute-start(bf16[128,256]{1,0:T(8,128)(2,1)S(1)} %get-tuple-element.155), channel_id=1, source_target_pairs={{0,3},{1,2},{2,1},{3,0},{4,7},{5,6},{6,5},{7,4},{8,11},{9,10},{10,... | collective-permute-start | bytes 196616 | tf_op jit(solution)/shard_map/ppermute | solution.py:44
  82.5 0.9 collective-permute-start.26
  83.4 0.5 gradient_mine.1
  83.9 3.4 %collective-permute-done.24.rest_0_ = bf16[128,256]{1,0:T(8,128)(2,1)S(1)} collective-permute-done((bf16[128,256]{1,0:T(8,128)(2,1)S(1)}, bf16[128,256]{1,0:T(8,128)(2,1)S(1)}, u32[]{:S(2)}, u32[]{:S(2)}) %collective-permute-start.24) | collective-permute-done | bytes 65568 | tf_op jit(solution)/shard_map/ppermute | solution.py:44
  87.3 0.7 collective-permute-done.25.rest_1_
  88.0 1.2 %exit_projection.3 = bf16[128,1024]{1,0:T(8,128)(2,1)} custom-call(s32[1]{0:T(128)} %bitcast.choice_ref, bf16[128,1024]{1,0:T(8,128)(2,1)S(1)} %collective-permute-done.13.x_ref, bf16[128,1024]{1,0:T(8,128)(2,1)S(1)} %get-tuple-element.119.other_ref, bf16[1024,1024]{1,0:T(8,128)(2,1)S(1)} %get-tuple-element.153.weight_ref, ...), custom_call_target="tpu_custom_call" | custom-call | flops 268435456 | bytes 2097152 | tf_op jit(solution)/shard_map/exit_projection/pallas_call | solution.py:439
  89.2 2.3 %collective-permute-done.29 = bf16[128,1024]{1,0:T(8,128)(2,1)S(1)} collective-permute-done((bf16[128,1024]{1,0:T(8,128)(2,1)S(1)}, bf16[128,1024]{1,0:T(8,128)(2,1)S(1)}, u32[]{:S(2)}, u32[]{:S(2)}) %collective-permute-start.29) | collective-permute-done | bytes 262176 | tf_op jit(solution)/shard_map/ppermute | solution.py:44
  91.5 0.9 add_bitcast_fusion
  (50 shorter events, 0.1 us)
Async XLA Ops:
  0.6 17.2 %copy-start.2 = (bf16[512,256]{1,0:T(8,128)(2,1)S(1)}, bf16[512,256]{1,0:T(8,128)(2,1)}, u32[]{:S(2)}) copy-start(bf16[512,256]{1,0:T(8,128)(2,1)} %constant.13.clone.forward_ref) | copy-start | bytes 786436
  0.6 17.2 %copy-start.5 = (bf16[1,2,128,1024]{3,2,1,0:T(8,128)(2,1)S(1)}, bf16[1,2,128,1024]{3,2,1,0:T(8,128)(2,1)}, u32[]{:S(2)}) copy-start(bf16[1,2,128,1024]{3,2,1,0:T(8,128)(2,1)} %param.23) | copy-start | bytes 1572868
  0.7 17.1 %copy-start.12 = (bf16[32,1024]{1,0:T(8,128)(2,1)S(1)}, bf16[32,1024]{1,0:T(8,128)(2,1)}, u32[]{:S(2)}) copy-start(bf16[32,1024]{1,0:T(8,128)(2,1)} %amino_ref.1) | copy-start | bytes 196612
  0.7 17.1 %copy-start.14 = (bf16[8,1024]{1,0:T(8,128)(2,1)S(1)}, bf16[8,1024]{1,0:T(8,128)(2,1)}, u32[]{:S(2)}) copy-start(bf16[8,1024]{1,0:T(8,128)(2,1)} %polymer_ref.1) | copy-start | bytes 49156
  0.7 17.1 %copy-start.16 = (s32[8]{0:T(128)S(1)}, s32[8]{0:T(128)}, u32[]{:S(2)}) copy-start(s32[8]{0:T(128)} %sizes_ref.1) | copy-start | bytes 100
  0.7 17.1 %copy-start.17 = (s32[128]{0:T(128)S(1)}, s32[128]{0:T(128)}, u32[]{:S(2)}) copy-start(s32[128]{0:T(128)} %param.14) | copy-start | bytes 1540
  3.8 14.0 %copy-start.4 = (f32[1,2,128,1024]{3,2,1,0:T(8,128)S(1)}, f32[1,2,128,1024]{3,2,1,0:T(8,128)}, u32[]{:S(2)}) copy-start(f32[1,2,128,1024]{3,2,1,0:T(8,128)} %param.20) | copy-start | bytes 3145732
  3.8 19.6 %copy-start.1 = (bf16[256,512]{1,0:T(8,128)(2,1)S(1)}, bf16[256,512]{1,0:T(8,128)(2,1)}, u32[]{:S(2)}) copy-start(bf16[256,512]{1,0:T(8,128)(2,1)} %constant.14.clone.backward_ref) | copy-start | bytes 786436
  3.9 19.6 %copy-start.13 = (f32[1,2,128]{2,1,0:T(2,128)S(1)}, f32[1,2,128]{2,1,0:T(2,128)}, u32[]{:S(2)}) copy-start(f32[1,2,128]{2,1,0:T(2,128)} %param.21) | copy-start | bytes 3076
  3.9 9.9 %collective-permute-start = (bf16[128,256]{1,0:T(8,128)(2,1)S(1)}, bf16[128,256]{1,0:T(8,128)(2,1)S(1)}, u32[]{:S(2)}, u32[]{:S(2)}) collective-permute-start(bf16[128,256]{1,0:T(8,128)(2,1)S(1)} %get-tuple-element.89), channel_id=1, source_target_pairs={{0,4},{1,5},{2,6},{3,7},{4,0},{5,1},{6,2},{7,3},{8,12},{9,13},{10,... | collective-permute-start | bytes 196616 | tf_op jit(solution)/shard_map/ppermute | solution.py:44
  8.0 8.5 %collective-permute-start.1 = (bf16[128,256]{1,0:T(8,128)(2,1)S(1)}, bf16[128,256]{1,0:T(8,128)(2,1)S(1)}, u32[]{:S(2)}, u32[]{:S(2)}) collective-permute-start(bf16[128,256]{1,0:T(8,128)(2,1)S(1)} %get-tuple-element.90), channel_id=1, source_target_pairs={{0,6},{1,7},{2,4},{3,5},{4,2},{5,3},{6,0},{7,1},{8,14},{9,15},{10,... | collective-permute-start | bytes 196616 | tf_op jit(solution)/shard_map/ppermute | solution.py:44
  10.3 13.2 %collective-permute-start.4 = (bf16[128,512]{1,0:T(8,128)(2,1)S(1)}, bf16[128,512]{1,0:T(8,128)(2,1)S(1)}, u32[]{:S(2)}, u32[]{:S(2)}) collective-permute-start(bf16[128,512]{1,0:T(8,128)(2,1)S(1)} %get-tuple-element.95), channel_id=1, source_target_pairs={{0,3},{1,2},{2,1},{3,0},{4,7},{5,6},{6,5},{7,4},{8,11},{9,10},{10,... | collective-permute-start | bytes 393224 | tf_op jit(solution)/shard_map/ppermute | solution.py:44
  11.5 12.0 %collective-permute-start.5 = (bf16[128,512]{1,0:T(8,128)(2,1)S(1)}, bf16[128,512]{1,0:T(8,128)(2,1)S(1)}, u32[]{:S(2)}, u32[]{:S(2)}) collective-permute-start(bf16[128,512]{1,0:T(8,128)(2,1)S(1)} %get-tuple-element.96), channel_id=1, source_target_pairs={{0,2},{1,3},{2,0},{3,1},{4,6},{5,7},{6,4},{7,5},{8,10},{9,11},{10,... | collective-permute-start | bytes 393224 | tf_op jit(solution)/shard_map/ppermute | solution.py:44
  13.3 10.2 %collective-permute-start.6 = (bf16[128,512]{1,0:T(8,128)(2,1)S(1)}, bf16[128,512]{1,0:T(8,128)(2,1)S(1)}, u32[]{:S(2)}, u32[]{:S(2)}) collective-permute-start(bf16[128,512]{1,0:T(8,128)(2,1)S(1)} %get-tuple-element.97), channel_id=1, source_target_pairs={{0,1},{1,0},{2,3},{3,2},{4,5},{5,4},{6,7},{7,6},{8,9},{9,8},{10,11... | collective-permute-start | bytes 393224 | tf_op jit(solution)/shard_map/ppermute | solution.py:44
  13.8 6.5 %collective-permute-start.2 = (bf16[128,256]{1,0:T(8,128)(2,1)S(1)}, bf16[128,256]{1,0:T(8,128)(2,1)S(1)}, u32[]{:S(2)}, u32[]{:S(2)}) collective-permute-start(bf16[128,256]{1,0:T(8,128)(2,1)S(1)} %get-tuple-element.91), channel_id=1, source_target_pairs={{0,5},{1,4},{2,7},{3,6},{4,1},{5,0},{6,3},{7,2},{8,13},{9,12},{10,... | collective-permute-start | bytes 196616 | tf_op jit(solution)/shard_map/ppermute | solution.py:44
  16.4 7.0 %collective-permute-start.3 = (bf16[128,256]{1,0:T(8,128)(2,1)S(1)}, bf16[128,256]{1,0:T(8,128)(2,1)S(1)}, u32[]{:S(2)}, u32[]{:S(2)}) collective-permute-start(bf16[128,256]{1,0:T(8,128)(2,1)S(1)} %get-tuple-element.92), channel_id=1, source_target_pairs={{0,7},{1,6},{2,5},{3,4},{4,3},{5,2},{6,1},{7,0},{8,15},{9,14},{10,... | collective-permute-start | bytes 196616 | tf_op jit(solution)/shard_map/ppermute | solution.py:44
  19.9 20.6 %copy-start = (bf16[1,1024,1024]{2,1,0:T(8,128)(2,1)S(1)}, bf16[1,1024,1024]{2,1,0:T(8,128)(2,1)}, u32[]{:S(2)}) copy-start(bf16[1,1024,1024]{2,1,0:T(8,128)(2,1)} %param.22) | copy-start | bytes 6291460
  20.0 20.6 %copy-start.3 = (bf16[1,128,1024]{2,1,0:T(8,128)(2,1)S(1)}, bf16[1,128,1024]{2,1,0:T(8,128)(2,1)}, u32[]{:S(2)}) copy-start(bf16[1,128,1024]{2,1,0:T(8,128)(2,1)} %param.13) | copy-start | bytes 786436
  25.1 7.0 %collective-permute-start.7 = (bf16[512,128]{1,0:T(8,128)(2,1)S(1)}, bf16[512,128]{1,0:T(8,128)(2,1)S(1)}, u32[]{:S(2)}, u32[]{:S(2)}) collective-permute-start(bf16[512,128]{1,0:T(8,128)(2,1)S(1)} %get-tuple-element.101), channel_id=1, source_target_pairs={{0,4},{1,5},{2,6},{3,7},{4,0},{5,1},{6,2},{7,3},{8,12},{9,13},{10,... | collective-permute-start | bytes 393224 | tf_op jit(solution)/shard_map/ppermute | solution.py:44
  27.3 13.3 %collective-permute-start.11 = (bf16[128,1024]{1,0:T(8,128)(2,1)}, bf16[128,1024]{1,0:T(8,128)(2,1)S(1)}, u32[]{:S(2)}, u32[]{:S(2)}) collective-permute-start(bf16[128,1024]{1,0:T(8,128)(2,1)} %get-tuple-element.141.refs_4_), channel_id=1, source_target_pairs={{0,1},{1,0},{2,3},{3,2},{4,5},{5,4},{6,7},{7,6},{8,9},{9,8},{10,11... | collective-permute-start | bytes 786440 | tf_op jit(solution)/shard_map/ppermute | solution.py:44
  28.3 12.3 %collective-permute-start.12 = (bf16[128,1024]{1,0:T(8,128)(2,1)}, bf16[128,1024]{1,0:T(8,128)(2,1)S(1)}, u32[]{:S(2)}, u32[]{:S(2)}) collective-permute-start(bf16[128,1024]{1,0:T(8,128)(2,1)} %get-tuple-element.144.refs_7_), channel_id=1, source_target_pairs={{0,2},{1,3},{2,0},{3,1},{4,6},{5,7},{6,4},{7,5},{8,10},{9,11},{10,... | collective-permute-start | bytes 786440 | tf_op jit(solution)/shard_map/ppermute | solution.py:44
  32.2 11.0 %copy-start.10 = (bf16[4,128,256]{2,1,0:T(8,128)(2,1)}, bf16[4,128,256]{2,1,0:T(8,128)(2,1)S(1)}, u32[]{:S(2)}) copy-start(bf16[4,128,256]{2,1,0:T(8,128)(2,1)S(1)} %get-tuple-element.138.refs_1_) | copy-start | bytes 786436
  32.2 6.5 %collective-permute-start.8 = (bf16[128,256]{1,0:T(8,128)(2,1)S(1)}, bf16[128,256]{1,0:T(8,128)(2,1)S(1)}, u32[]{:S(2)}, u32[]{:S(2)}) collective-permute-start(bf16[128,256]{1,0:T(8,128)(2,1)S(1)} %get-tuple-element.103), channel_id=1, source_target_pairs={{0,3},{1,2},{2,1},{3,0},{4,7},{5,6},{6,5},{7,4},{8,11},{9,10},{10,... | collective-permute-start | bytes 196616 | tf_op jit(solution)/shard_map/ppermute | solution.py:44
  34.3 6.2 %collective-permute-start.9 = (bf16[128,256]{1,0:T(8,128)(2,1)S(1)}, bf16[128,256]{1,0:T(8,128)(2,1)S(1)}, u32[]{:S(2)}, u32[]{:S(2)}) collective-permute-start(bf16[128,256]{1,0:T(8,128)(2,1)S(1)} %get-tuple-element.104), channel_id=1, source_target_pairs={{0,2},{1,3},{2,0},{3,1},{4,6},{5,7},{6,4},{7,5},{8,10},{9,11},{10,... | collective-permute-start | bytes 196616 | tf_op jit(solution)/shard_map/ppermute | solution.py:44
  35.4 5.1 %collective-permute-start.10 = (bf16[128,256]{1,0:T(8,128)(2,1)S(1)}, bf16[128,256]{1,0:T(8,128)(2,1)S(1)}, u32[]{:S(2)}, u32[]{:S(2)}) collective-permute-start(bf16[128,256]{1,0:T(8,128)(2,1)S(1)} %get-tuple-element.105), channel_id=1, source_target_pairs={{0,1},{1,0},{2,3},{3,2},{4,5},{5,4},{6,7},{7,6},{8,9},{9,8},{10,11... | collective-permute-start | bytes 196616 | tf_op jit(solution)/shard_map/ppermute | solution.py:44
  38.7 7.3 %collective-permute-start.14 = (bf16[128,1024]{1,0:T(8,128)(2,1)}, bf16[128,1024]{1,0:T(8,128)(2,1)}, u32[]{:S(2)}, u32[]{:S(2)}) collective-permute-start(bf16[128,1024]{1,0:T(8,128)(2,1)} %get-tuple-element.144.refs_7_), channel_id=1, source_target_pairs={{0,1},{1,0},{2,3},{3,2},{4,5},{5,4},{6,7},{7,6},{8,9},{9,8},{10,11... | collective-permute-start | bytes 786440 | tf_op jit(solution)/shard_map/ppermute | solution.py:44
  40.5 2.7 %copy-start.8 = (bf16[128,1024]{1,0:T(8,128)(2,1)}, bf16[128,1024]{1,0:T(8,128)(2,1)S(1)}, u32[]{:S(2)}) copy-start(bf16[128,1024]{1,0:T(8,128)(2,1)S(1)} %collective-permute-done.11.refs_3_) | copy-start | bytes 786436
  40.6 1.9 %copy-start.6 = (bf16[128,1024]{1,0:T(8,128)(2,1)}, bf16[128,1024]{1,0:T(8,128)(2,1)S(1)}, u32[]{:S(2)}) copy-start(bf16[128,1024]{1,0:T(8,128)(2,1)S(1)} %collective-permute-done.12.refs_5_) | copy-start | bytes 786436
  41.1 4.9 %collective-permute-start.13 = (bf16[128,1024]{1,0:T(8,128)(2,1)S(1)}, bf16[128,1024]{1,0:T(8,128)(2,1)S(1)}, u32[]{:S(2)}, u32[]{:S(2)}) collective-permute-start(bf16[128,1024]{1,0:T(8,128)(2,1)S(1)} %exit_projection.2), channel_id=1, source_target_pairs={{0,8},{8,16},{16,24},{1,9},{9,17},{17,25},{2,10},{10,18},{18,26},{... | collective-permute-start | bytes 786440 | tf_op jit(solution)/shard_map/ppermute | solution.py:546
  42.4 11.0 %collective-permute-start.23 = (bf16[128,1024]{1,0:T(8,128)(2,1)}, bf16[128,1024]{1,0:T(8,128)(2,1)}, u32[]{:S(2)}, u32[]{:S(2)}) collective-permute-start(bf16[128,1024]{1,0:T(8,128)(2,1)} %get-tuple-element.141.refs_4_), channel_id=1, source_target_pairs={{0,2},{1,3},{2,0},{3,1},{4,6},{5,7},{6,4},{7,5},{8,10},{9,11},{10,... | collective-permute-start | bytes 786440 | tf_op jit(solution)/shard_map/ppermute | solution.py:44
  43.2 2.8 %copy-start.15 = (f32[1,1024]{1,0:T(1,128)S(1)}, f32[1,1024]{1,0:T(1,128)}, u32[]{:S(2)}) copy-start(f32[1,1024]{1,0:T(1,128)} %gain_ref.3) | copy-start | bytes 12292
  46.6 14.9 %copy-start.7 = (bf16[128,1024]{1,0:T(8,128)(2,1)S(1)}, bf16[128,1024]{1,0:T(8,128)(2,1)}, u32[]{:S(2)}) copy-start(bf16[128,1024]{1,0:T(8,128)(2,1)} %copy-done.6) | copy-start | bytes 786436
  46.6 8.3 %collective-permute-start.15 = (bf16[128,256]{1,0:T(8,128)(2,1)S(1)}, bf16[128,256]{1,0:T(8,128)(2,1)S(1)}, u32[]{:S(2)}, u32[]{:S(2)}) collective-permute-start(bf16[128,256]{1,0:T(8,128)(2,1)S(1)} %get-tuple-element.121), channel_id=1, source_target_pairs={{0,4},{1,5},{2,6},{3,7},{4,0},{5,1},{6,2},{7,3},{8,12},{9,13},{10,... | collective-permute-start | bytes 196616 | tf_op jit(solution)/shard_map/ppermute | solution.py:44
  48.7 7.7 %collective-permute-start.16 = (bf16[128,256]{1,0:T(8,128)(2,1)S(1)}, bf16[128,256]{1,0:T(8,128)(2,1)S(1)}, u32[]{:S(2)}, u32[]{:S(2)}) collective-permute-start(bf16[128,256]{1,0:T(8,128)(2,1)S(1)} %get-tuple-element.122), channel_id=1, source_target_pairs={{0,6},{1,7},{2,4},{3,5},{4,2},{5,3},{6,0},{7,1},{8,14},{9,15},{10,... | collective-permute-start | bytes 196616 | tf_op jit(solution)/shard_map/ppermute | solution.py:44
  50.4 19.8 %copy-start.9 = (bf16[128,1024]{1,0:T(8,128)(2,1)S(1)}, bf16[128,1024]{1,0:T(8,128)(2,1)}, u32[]{:S(2)}) copy-start(bf16[128,1024]{1,0:T(8,128)(2,1)} %copy-done.8) | copy-start | bytes 786436
  50.4 19.9 %copy-start.11 = (bf16[4,128,256]{2,1,0:T(8,128)(2,1)S(1)}, bf16[4,128,256]{2,1,0:T(8,128)(2,1)}, u32[]{:S(2)}) copy-start(bf16[4,128,256]{2,1,0:T(8,128)(2,1)} %copy-done.10) | copy-start | bytes 786436
  51.3 14.1 %collective-permute-start.19 = (bf16[128,512]{1,0:T(8,128)(2,1)S(1)}, bf16[128,512]{1,0:T(8,128)(2,1)S(1)}, u32[]{:S(2)}, u32[]{:S(2)}) collective-permute-start(bf16[128,512]{1,0:T(8,128)(2,1)S(1)} %get-tuple-element.126), channel_id=1, source_target_pairs={{0,3},{1,2},{2,1},{3,0},{4,7},{5,6},{6,5},{7,4},{8,11},{9,10},{10,... | collective-permute-start | bytes 393224 | tf_op jit(solution)/shard_map/ppermute | solution.py:44
  51.8 13.7 %collective-permute-start.20 = (bf16[128,512]{1,0:T(8,128)(2,1)S(1)}, bf16[128,512]{1,0:T(8,128)(2,1)S(1)}, u32[]{:S(2)}, u32[]{:S(2)}) collective-permute-start(bf16[128,512]{1,0:T(8,128)(2,1)S(1)} %get-tuple-element.127), channel_id=1, source_target_pairs={{0,2},{1,3},{2,0},{3,1},{4,6},{5,7},{6,4},{7,5},{8,10},{9,11},{10,... | collective-permute-start | bytes 393224 | tf_op jit(solution)/shard_map/ppermute | solution.py:44
  53.4 12.1 %collective-permute-start.21 = (bf16[128,512]{1,0:T(8,128)(2,1)S(1)}, bf16[128,512]{1,0:T(8,128)(2,1)S(1)}, u32[]{:S(2)}, u32[]{:S(2)}) collective-permute-start(bf16[128,512]{1,0:T(8,128)(2,1)S(1)} %get-tuple-element.128), channel_id=1, source_target_pairs={{0,1},{1,0},{2,3},{3,2},{4,5},{5,4},{6,7},{7,6},{8,9},{9,8},{10,11... | collective-permute-start | bytes 393224 | tf_op jit(solution)/shard_map/ppermute | solution.py:44
  54.9 6.6 %collective-permute-start.17 = (bf16[128,256]{1,0:T(8,128)(2,1)S(1)}, bf16[128,256]{1,0:T(8,128)(2,1)S(1)}, u32[]{:S(2)}, u32[]{:S(2)}) collective-permute-start(bf16[128,256]{1,0:T(8,128)(2,1)S(1)} %get-tuple-element.123), channel_id=1, source_target_pairs={{0,5},{1,4},{2,7},{3,6},{4,1},{5,0},{6,3},{7,2},{8,13},{9,12},{10,... | collective-permute-start | bytes 196616 | tf_op jit(solution)/shard_map/ppermute | solution.py:44
  56.4 8.2 %collective-permute-start.18 = (bf16[128,256]{1,0:T(8,128)(2,1)S(1)}, bf16[128,256]{1,0:T(8,128)(2,1)S(1)}, u32[]{:S(2)}, u32[]{:S(2)}) collective-permute-start(bf16[128,256]{1,0:T(8,128)(2,1)S(1)} %get-tuple-element.124), channel_id=1, source_target_pairs={{0,7},{1,6},{2,5},{3,4},{4,3},{5,2},{6,1},{7,0},{8,15},{9,14},{10,... | collective-permute-start | bytes 196616 | tf_op jit(solution)/shard_map/ppermute | solution.py:44
  61.5 14.9 %collective-permute-start.28 = (bf16[128,1024]{1,0:T(8,128)(2,1)S(1)}, bf16[128,1024]{1,0:T(8,128)(2,1)S(1)}, u32[]{:S(2)}, u32[]{:S(2)}) collective-permute-start(bf16[128,1024]{1,0:T(8,128)(2,1)S(1)} %copy-done.7), channel_id=1, source_target_pairs={{0,1},{1,0},{2,3},{3,2},{4,5},{5,4},{6,7},{7,6},{8,9},{9,8},{10,11... | collective-permute-start | bytes 786440 | tf_op jit(solution)/shard_map/ppermute | solution.py:44
  64.7 11.8 %collective-permute-start.27 = (bf16[128,1024]{1,0:T(8,128)(2,1)}, bf16[128,1024]{1,0:T(8,128)(2,1)S(1)}, u32[]{:S(2)}, u32[]{:S(2)}) collective-permute-start(bf16[128,1024]{1,0:T(8,128)(2,1)} %collective-permute-done.23.refs_2_), channel_id=1, source_target_pairs={{0,1},{1,0},{2,3},{3,2},{4,5},{5,4},{6,7},{7,6},{8,9},{9,8},{10,11... | collective-permute-start | bytes 786440 | tf_op jit(solution)/shard_map/ppermute | solution.py:44
  67.2 9.2 %collective-permute-start.22 = (bf16[512,128]{1,0:T(8,128)(2,1)S(1)}, bf16[512,128]{1,0:T(8,128)(2,1)S(1)}, u32[]{:S(2)}, u32[]{:S(2)}) collective-permute-start(bf16[512,128]{1,0:T(8,128)(2,1)S(1)} %get-tuple-element.130), channel_id=1, source_target_pairs={{0,4},{1,5},{2,6},{3,7},{4,0},{5,1},{6,2},{7,3},{8,12},{9,13},{10,... | collective-permute-start | bytes 393224 | tf_op jit(solution)/shard_map/ppermute | solution.py:44
  76.9 14.6 %collective-permute-start.29 = (bf16[128,1024]{1,0:T(8,128)(2,1)S(1)}, bf16[128,1024]{1,0:T(8,128)(2,1)S(1)}, u32[]{:S(2)}, u32[]{:S(2)}) collective-permute-start(bf16[128,1024]{1,0:T(8,128)(2,1)S(1)} %gradient_away.1), channel_id=1, source_target_pairs={{0,4},{1,5},{2,6},{3,7},{4,0},{5,1},{6,2},{7,3},{8,12},{9,13},{10,... | collective-permute-start | bytes 786440 | tf_op jit(solution)/shard_map/ppermute | solution.py:44
  79.4 8.0 %collective-permute-start.24 = (bf16[128,256]{1,0:T(8,128)(2,1)S(1)}, bf16[128,256]{1,0:T(8,128)(2,1)S(1)}, u32[]{:S(2)}, u32[]{:S(2)}) collective-permute-start(bf16[128,256]{1,0:T(8,128)(2,1)S(1)} %get-tuple-element.155), channel_id=1, source_target_pairs={{0,3},{1,2},{2,1},{3,0},{4,7},{5,6},{6,5},{7,4},{8,11},{9,10},{10,... | collective-permute-start | bytes 196616 | tf_op jit(solution)/shard_map/ppermute | solution.py:44
  82.5 5.5 %collective-permute-start.25 = (bf16[128,256]{1,0:T(8,128)(2,1)S(1)}, bf16[128,256]{1,0:T(8,128)(2,1)S(1)}, u32[]{:S(2)}, u32[]{:S(2)}) collective-permute-start(bf16[128,256]{1,0:T(8,128)(2,1)S(1)} %get-tuple-element.156), channel_id=1, source_target_pairs={{0,2},{1,3},{2,0},{3,1},{4,6},{5,7},{6,4},{7,5},{8,10},{9,11},{10,... | collective-permute-start | bytes 196616 | tf_op jit(solution)/shard_map/ppermute | solution.py:44
  82.5 5.5 %collective-permute-start.26 = (bf16[128,256]{1,0:T(8,128)(2,1)S(1)}, bf16[128,256]{1,0:T(8,128)(2,1)S(1)}, u32[]{:S(2)}, u32[]{:S(2)}) collective-permute-start(bf16[128,256]{1,0:T(8,128)(2,1)S(1)} %get-tuple-element.157), channel_id=1, source_target_pairs={{0,1},{1,0},{2,3},{3,2},{4,5},{5,4},{6,7},{7,6},{8,9},{9,8},{10,11... | collective-permute-start | bytes 196616 | tf_op jit(solution)/shard_map/ppermute | solution.py:44

commit v6 on v5

--- a/solution.py
+++ b/solution.py
@@ -421,26 +421,41 @@
     )(keep, come, *gates)
 
 
-def exit_kernel(order, choice_ref, x_ref, other_ref, weight_ref, *rest):
-    hyenas, out_ref = rest[: len(order)], rest[len(order)]
+def exit_kernel(order, last, choice_ref, x_ref, other_ref, weight_ref, *rest):
+    hyenas, (out_ref, *rest) = rest[: len(order)], rest[len(order) :]
     me = lax.axis_index("seq")
     peers = 2 * len(order)
     block = weight_ref.shape[0] // peers
-    values = jnp.where(choice_ref[0] == 1, other_ref[...], x_ref[...])
-    total = values.astype(f32)
-    for distance, hyena in zip(order, hyenas):
-        near = pl.ds(pl.multiple_of((me ^ distance) * block, block), block)
-        far = pl.ds(pl.multiple_of((me ^ distance ^ len(order)) * block, block), block)
-        total += dot(hyena[...], jnp.concatenate([weight_ref[near, :], weight_ref[far, :]], axis=0))
-    out_ref[...] = total.astype(bf16)
-
-
-def exit_projection(choice, x, other, weight, hyenas, order):
+    width = x_ref.shape[1]
+    step = width // 2 if last else width
+    copies = []
+    for part in range(width // step):
+        columns = slice(part * step, (part + 1) * step)
+        total = jnp.where(choice_ref[0] == 1, other_ref[:, columns], x_ref[:, columns]).astype(f32)
+        for distance, hyena in zip(order, hyenas):
+            near = pl.ds(pl.multiple_of((me ^ distance) * block, block), block)
+            far = pl.ds(pl.multiple_of((me ^ distance ^ len(order)) * block, block), block)
+            total += dot(hyena[...], jnp.concatenate([weight_ref[near, columns], weight_ref[far, columns]], axis=0))
+        if last:
+            held_ref, sent = rest
+            held_ref[part] = total.astype(bf16)
+            copies.append(pltpu.make_async_copy(held_ref.at[part], out_ref.at[:, columns], sent.at[part]))
+            copies[-1].start()
+        else:
+            out_ref[...] = total.astype(bf16)
+    for copy in copies:
+        copy.wait()
+
+
+def exit_projection(choice, x, other, weight, hyenas, order, last=False):
+    rows, width = x.shape
+    scratch = [pltpu.VMEM((2, rows, width // 2), bf16), pltpu.SemaphoreType.DMA((2,))] if last else []
     return pl.pallas_call(
-        functools.partial(exit_kernel, order),
+        functools.partial(exit_kernel, order, last),
         out_shape=jax.ShapeDtypeStruct(x.shape, bf16),
         in_specs=[scalars()] + [whole()] * (3 + len(hyenas)),
-        out_specs=whole(),
+        out_specs=pl.BlockSpec(memory_space=pl.ANY) if last else whole(),
+        scratch_shapes=scratch,
         compiler_params=params(12),
         cost_estimate=cost(2 * x.size * weight.shape[0], 2 * weight.size),
         name="exit_projection",
@@ -565,7 +580,7 @@
     away = gradient(first_hyenas, second_hyenas, seeds, 1, bf16, "gradient_away")
     mine = gradient(first_hyenas, second_hyenas, seeds, 0, f32, "gradient_mine")
     home, mine = lax.optimization_barrier((home, mine))
-    passed = exit_projection(first_section, handed, embedded, weight_again, home, near)
+    passed = exit_projection(first_section, handed, embedded, weight_again, home, near, True)
     out_grad = mine + exchange(away, group).astype(f32)
     return (passed[None], out_grad[None])
 

time: 92.5 us -> 92.5 us (level)
  no operation moved by 1% of the time
where the time goes in v6:
time: 92.5 us; the launch traced here: 92.4 us
  starting transfers between devices  45 us (49%)
  waiting for transfers between devices  26.5 us (29%)
  Pallas kernels  18.9 us (20%)
  between operations  1.02 us (1%)
    ppermute x29, starting transfers between devices, exchange(): return lax.ppermute(value, 'seq', [(i, i ^ distance) for i in range(peers)])  43.7 us
    ppermute x29, waiting for transfers between devices, exchange(): return lax.ppermute(value, 'seq', [(i, i ^ distance) for i in range(peers)])  26.5 us
    pallas_call x2, Pallas kernels, hold(): pl.pallas_call(functools.partial(hold_kernel, count), out_shape=tuple((pl...  4.7 us
    pallas_call x2, Pallas kernels, filtered(): pl.pallas_call(functools.partial(filter_kernel, order), out_shape=(out, k...  3.3 us
    pallas_call x1, Pallas kernels, project(): pl.pallas_call(functools.partial(far_stream_kernel, far), out_shape=outs,...  3.13 us
    pallas_call x1, Pallas kernels, prepare(): pl.pallas_call(prepare_kernel, out_shape=(jax.ShapeDtypeStruct((2, chunks...  2.12 us
    pallas_call x2, Pallas kernels, project(): pl.pallas_call(functools.partial(near_kernel, near, other is None), out_s...  1.85 us
  transfers between devices with their start and end apart: 30, of which 10 were waited for; matrix products, arithmetic and copies ran while one was open for 0% of the time, Pallas kernels for 15%

profile of v6, /device:TPU:0, one launch (start us, length us, event | category | flops | bytes accessed | tf_op | source)
XLA Modules:
  0.0 92.4 jit_solution(14707080976438778430)
XLA Ops:
  0.6 0.0 copy-start.2
  0.7 3.1 %far_pieces_streamed.1 = (bf16[128,256]{1,0:T(8,128)(2,1)S(1)}, bf16[128,256]{1,0:T(8,128)(2,1)S(1)}, bf16[128,256]{1,0:T(8,128)(2,1)S(1)}, bf16[128,256]{1,0:T(...) custom-call(bf16[128,1024]{1,0:T(8,128)(2,1)} %bitcast.13, f32[1,1024]{1,0:T(1,128)} %gain_ref.3, ...), custom_call_target="tpu_custom_call" | custom-call | flops 268435456 | bytes 2097152 | tf_op jit(solution)/shard_map/far_pieces_streamed/pallas_call | solution.py:242
  3.8 0.0 copy-start.4
  3.8 0.0 copy-start.1
  3.9 0.0 copy-start.13
  3.9 4.1 %collective-permute-start = (bf16[128,256]{1,0:T(8,128)(2,1)S(1)}, bf16[128,256]{1,0:T(8,128)(2,1)S(1)}, u32[]{:S(2)}, u32[]{:S(2)}) collective-permute-start(bf16[128,256]{1,0:T(8,128)(2,1)S(1)} %get-tuple-element.89), channel_id=1, source_target_pairs={{0,4},{1,5},{2,6},{3,7},{4,0},{5,1},{6,2},{7,3},{8,12},{9,13},{10,... | collective-permute-start | bytes 196616 | tf_op jit(solution)/shard_map/ppermute | solution.py:44
  8.0 1.3 %collective-permute-start.1 = (bf16[128,256]{1,0:T(8,128)(2,1)S(1)}, bf16[128,256]{1,0:T(8,128)(2,1)S(1)}, u32[]{:S(2)}, u32[]{:S(2)}) collective-permute-start(bf16[128,256]{1,0:T(8,128)(2,1)S(1)} %get-tuple-element.90), channel_id=1, source_target_pairs={{0,6},{1,7},{2,4},{3,5},{4,2},{5,3},{6,0},{7,1},{8,14},{9,15},{10,... | collective-permute-start | bytes 196616 | tf_op jit(solution)/shard_map/ppermute | solution.py:44
  9.3 0.9 %near_pieces.2 = (bf16[128,512]{1,0:T(8,128)(2,1)S(1)}, bf16[128,512]{1,0:T(8,128)(2,1)S(1)}, bf16[128,512]{1,0:T(8,128)(2,1)S(1)}, bf16[128,512]{1,0:T(8,128)(2,1)S(1)}) custom-call(bf16[128,1024]{1,0:T(8,128)(2,1)S(1)} %get-tuple-element.93.normed_ref, bf16[1024,2048]{1,0:T(8,128)(2,1)S(1)} %get-tuple-element.94.weight_ref), custom_call_target="tpu_custom_call" | custom-call | flops 536870912 | bytes 4194304 | tf_op jit(solution)/shard_map/near_pieces/pallas_call | solution.py:271
  10.3 1.2 %collective-permute-start.4 = (bf16[128,512]{1,0:T(8,128)(2,1)S(1)}, bf16[128,512]{1,0:T(8,128)(2,1)S(1)}, u32[]{:S(2)}, u32[]{:S(2)}) collective-permute-start(bf16[128,512]{1,0:T(8,128)(2,1)S(1)} %get-tuple-element.95), channel_id=1, source_target_pairs={{0,3},{1,2},{2,1},{3,0},{4,7},{5,6},{6,5},{7,4},{8,11},{9,10},{10,... | collective-permute-start | bytes 393224 | tf_op jit(solution)/shard_map/ppermute | solution.py:44
  11.5 1.8 %collective-permute-start.5 = (bf16[128,512]{1,0:T(8,128)(2,1)S(1)}, bf16[128,512]{1,0:T(8,128)(2,1)S(1)}, u32[]{:S(2)}, u32[]{:S(2)}) collective-permute-start(bf16[128,512]{1,0:T(8,128)(2,1)S(1)} %get-tuple-element.96), channel_id=1, source_target_pairs={{0,2},{1,3},{2,0},{3,1},{4,6},{5,7},{6,4},{7,5},{8,10},{9,11},{10,... | collective-permute-start | bytes 393224 | tf_op jit(solution)/shard_map/ppermute | solution.py:44
  13.3 0.5 collective-permute-start.6
  13.8 2.6 %collective-permute-start.2 = (bf16[128,256]{1,0:T(8,128)(2,1)S(1)}, bf16[128,256]{1,0:T(8,128)(2,1)S(1)}, u32[]{:S(2)}, u32[]{:S(2)}) collective-permute-start(bf16[128,256]{1,0:T(8,128)(2,1)S(1)} %get-tuple-element.91), channel_id=1, source_target_pairs={{0,5},{1,4},{2,7},{3,6},{4,1},{5,0},{6,3},{7,2},{8,13},{9,12},{10,... | collective-permute-start | bytes 196616 | tf_op jit(solution)/shard_map/ppermute | solution.py:44
  16.4 0.0 collective-permute-done.1.rest_1_
  16.4 1.4 %collective-permute-start.3 = (bf16[128,256]{1,0:T(8,128)(2,1)S(1)}, bf16[128,256]{1,0:T(8,128)(2,1)S(1)}, u32[]{:S(2)}, u32[]{:S(2)}) collective-permute-start(bf16[128,256]{1,0:T(8,128)(2,1)S(1)} %get-tuple-element.92), channel_id=1, source_target_pairs={{0,7},{1,6},{2,5},{3,4},{4,3},{5,2},{6,1},{7,0},{8,15},{9,14},{10,... | collective-permute-start | bytes 196616 | tf_op jit(solution)/shard_map/ppermute | solution.py:44
  17.8 2.1 %prepare.1 = (f32[2,4,512,128]{3,2,1,0:T(8,128)S(1)}, bf16[128,1024]{1,0:T(8,128)(2,1)S(1)}, bf16[128,1024]{1,0:T(8,128)(2,1)}, bf16[128,1024]{1,0:T(8,128)(2,1)}) custom-call(s32[8]{0:T(128)S(1)} %copy-done.16, s32[1,128]{1,0:T(1,128)S(1)} %bitcast.22, bf16[32,1024]{1,0:T(8,128)(2,1)S(1)} %copy-done.12, bf16[8,1024]{1,0:T(8,128)(2,1)S(1)} %copy-done.14, ...), custom_call_target="tpu_custom_call" | custom-call | flops 268435456 | bytes 2097152 | tf_op jit(solution)/shard_map/prepare/pallas_call | solution.py:97
  20.0 0.4 collective-permute-done.2.rest_2_
  20.3 3.1 %collective-permute-done.3.rest_3_ = bf16[128,256]{1,0:T(8,128)(2,1)S(1)} collective-permute-done((bf16[128,256]{1,0:T(8,128)(2,1)S(1)}, bf16[128,256]{1,0:T(8,128)(2,1)S(1)}, u32[]{:S(2)}, u32[]{:S(2)}) %collective-permute-start.3) | collective-permute-done | bytes 65568 | tf_op jit(solution)/shard_map/ppermute | solution.py:44
  23.4 0.0 collective-permute-done.4.rest_4_.rest_0_
  23.4 0.0 collective-permute-done.5.rest_5_.rest_1_
  23.5 1.7 %two_filters.2 = (bf16[512,128]{1,0:T(8,128)(2,1)S(1)}, bf16[512,256]{1,0:T(8,128)(2,1)S(1)}, f32[256,256]{1,0:T(8,128)S(1)}) custom-call(f32[2,128]{1,0:T(2,128)S(1)} %bitcast.18, f32[2,4,512,128]{3,2,1,0:T(8,128)S(1)} %get-tuple-element.88.spectra_ref, bf16[512,256]{1,0:T(8,128)(2,1)S(1)} %copy-done.2, bf16[256,512]{1,0:T(8,128)(2,1)S(1)} %copy-done.1, ...), custom_call_target="tpu_custom_call" | custom-call | flops 536870912 | bytes 1048576 | tf_op jit(solution)/shard_map/two_filters/pallas_call | solution.py:367
  25.1 1.9 %collective-permute-start.7 = (bf16[512,128]{1,0:T(8,128)(2,1)S(1)}, bf16[512,128]{1,0:T(8,128)(2,1)S(1)}, u32[]{:S(2)}, u32[]{:S(2)}) collective-permute-start(bf16[512,128]{1,0:T(8,128)(2,1)S(1)} %get-tuple-element.101), channel_id=1, source_target_pairs={{0,4},{1,5},{2,6},{3,7},{4,0},{5,1},{6,2},{7,3},{8,12},{9,13},{10,... | collective-permute-start | bytes 393224 | tf_op jit(solution)/shard_map/ppermute | solution.py:44
  27.0 0.2 own_half.2.keep_ref
  27.3 1.0 %collective-permute-start.11 = (bf16[128,1024]{1,0:T(8,128)(2,1)}, bf16[128,1024]{1,0:T(8,128)(2,1)S(1)}, u32[]{:S(2)}, u32[]{:S(2)}) collective-permute-start(bf16[128,1024]{1,0:T(8,128)(2,1)} %get-tuple-element.141.refs_4_), channel_id=1, source_target_pairs={{0,1},{1,0},{2,3},{3,2},{4,5},{5,4},{6,7},{7,6},{8,9},{9,8},{10,11... | collective-permute-start | bytes 786440 | tf_op jit(solution)/shard_map/ppermute | solution.py:44
  28.3 0.8 collective-permute-start.12
  29.0 3.1 %collective-permute-done.7.come_ref = bf16[512,128]{1,0:T(8,128)(2,1)S(1)} collective-permute-done((bf16[512,128]{1,0:T(8,128)(2,1)S(1)}, bf16[512,128]{1,0:T(8,128)(2,1)S(1)}, u32[]{:S(2)}, u32[]{:S(2)}) %collective-permute-start.7) | collective-permute-done | bytes 131104 | tf_op jit(solution)/shard_map/ppermute | solution.py:44
  32.1 0.1 second_gate.2
  32.2 2.0 %collective-permute-start.8 = (bf16[128,256]{1,0:T(8,128)(2,1)S(1)}, bf16[128,256]{1,0:T(8,128)(2,1)S(1)}, u32[]{:S(2)}, u32[]{:S(2)}) collective-permute-start(bf16[128,256]{1,0:T(8,128)(2,1)S(1)} %get-tuple-element.103), channel_id=1, source_target_pairs={{0,3},{1,2},{2,1},{3,0},{4,7},{5,6},{6,5},{7,4},{8,11},{9,10},{10,... | collective-permute-start | bytes 196616 | tf_op jit(solution)/shard_map/ppermute | solution.py:44
  34.3 1.2 %collective-permute-start.9 = (bf16[128,256]{1,0:T(8,128)(2,1)S(1)}, bf16[128,256]{1,0:T(8,128)(2,1)S(1)}, u32[]{:S(2)}, u32[]{:S(2)}) collective-permute-start(bf16[128,256]{1,0:T(8,128)(2,1)S(1)} %get-tuple-element.104), channel_id=1, source_target_pairs={{0,2},{1,3},{2,0},{3,1},{4,6},{5,7},{6,4},{7,5},{8,10},{9,11},{10,... | collective-permute-start | bytes 196616 | tf_op jit(solution)/shard_map/ppermute | solution.py:44
  35.4 0.4 collective-permute-start.10
  35.8 2.9 %collective-permute-done.8.rest_0_ = bf16[128,256]{1,0:T(8,128)(2,1)S(1)} collective-permute-done((bf16[128,256]{1,0:T(8,128)(2,1)S(1)}, bf16[128,256]{1,0:T(8,128)(2,1)S(1)}, u32[]{:S(2)}, u32[]{:S(2)}) %collective-permute-start.8) | collective-permute-done | bytes 65568 | tf_op jit(solution)/shard_map/ppermute | solution.py:44
  38.7 1.8 %collective-permute-start.14 = (bf16[128,1024]{1,0:T(8,128)(2,1)}, bf16[128,1024]{1,0:T(8,128)(2,1)}, u32[]{:S(2)}, u32[]{:S(2)}) collective-permute-start(bf16[128,1024]{1,0:T(8,128)(2,1)} %get-tuple-element.144.refs_7_), channel_id=1, source_target_pairs={{0,1},{1,0},{2,3},{3,2},{4,5},{5,4},{6,7},{7,6},{8,9},{9,8},{10,11... | collective-permute-start | bytes 786440 | tf_op jit(solution)/shard_map/ppermute | solution.py:44
  40.6 0.5 exit_projection.2
  41.1 1.3 %collective-permute-start.13 = (bf16[128,1024]{1,0:T(8,128)(2,1)S(1)}, bf16[128,1024]{1,0:T(8,128)(2,1)S(1)}, u32[]{:S(2)}, u32[]{:S(2)}) collective-permute-start(bf16[128,1024]{1,0:T(8,128)(2,1)S(1)} %exit_projection.2), channel_id=1, source_target_pairs={{0,8},{8,16},{16,24},{1,9},{9,17},{17,25},{2,10},{10,18},{18,26},{... | collective-permute-start | bytes 786440 | tf_op jit(solution)/shard_map/ppermute | solution.py:561
  42.4 0.8 collective-permute-start.23
  43.2 2.8 %hold_entry.1.weight_ref = bf16[1024,3072]{1,0:T(8,128)(2,1)S(1)} custom-call(bf16[1024,3072]{1,0:T(8,128)(2,1)} %bitcast.24), custom_call_target="tpu_custom_call" | custom-call | bytes 6291456 | tf_op jit(solution)/shard_map/hold_entry/pallas_call | solution.py:204
  46.0 0.6 far_pieces.1
  46.6 2.1 %collective-permute-start.15 = (bf16[128,256]{1,0:T(8,128)(2,1)S(1)}, bf16[128,256]{1,0:T(8,128)(2,1)S(1)}, u32[]{:S(2)}, u32[]{:S(2)}) collective-permute-start(bf16[128,256]{1,0:T(8,128)(2,1)S(1)} %get-tuple-element.121), channel_id=1, source_target_pairs={{0,4},{1,5},{2,6},{3,7},{4,0},{5,1},{6,2},{7,3},{8,12},{9,13},{10,... | collective-permute-start | bytes 196616 | tf_op jit(solution)/shard_map/ppermute | solution.py:44
  48.7 1.7 %collective-permute-start.16 = (bf16[128,256]{1,0:T(8,128)(2,1)S(1)}, bf16[128,256]{1,0:T(8,128)(2,1)S(1)}, u32[]{:S(2)}, u32[]{:S(2)}) collective-permute-start(bf16[128,256]{1,0:T(8,128)(2,1)S(1)} %get-tuple-element.122), channel_id=1, source_target_pairs={{0,6},{1,7},{2,4},{3,5},{4,2},{5,3},{6,0},{7,1},{8,14},{9,15},{10,... | collective-permute-start | bytes 196616 | tf_op jit(solution)/shard_map/ppermute | solution.py:44
  50.4 0.9 %near_pieces.3 = (bf16[128,512]{1,0:T(8,128)(2,1)S(1)}, bf16[128,512]{1,0:T(8,128)(2,1)S(1)}, bf16[128,512]{1,0:T(8,128)(2,1)S(1)}, bf16[128,512]{1,0:T(8,128)(2,1)S(1)}) custom-call(bf16[128,1024]{1,0:T(8,128)(2,1)S(1)} %get-tuple-element.125.normed_ref, bf16[1024,3072]{1,0:T(8,128)(2,1)S(1)} %hold_entry.1.weight_ref), custom_call_target="tpu_custom_call" | custom-call | flops 536870912 | bytes 4194304 | tf_op jit(solution)/shard_map/near_pieces/pallas_call | solution.py:271
  51.3 0.5 collective-permute-start.19
  51.8 1.6 %collective-permute-start.20 = (bf16[128,512]{1,0:T(8,128)(2,1)S(1)}, bf16[128,512]{1,0:T(8,128)(2,1)S(1)}, u32[]{:S(2)}, u32[]{:S(2)}) collective-permute-start(bf16[128,512]{1,0:T(8,128)(2,1)S(1)} %get-tuple-element.127), channel_id=1, source_target_pairs={{0,2},{1,3},{2,0},{3,1},{4,6},{5,7},{6,4},{7,5},{8,10},{9,11},{10,... | collective-permute-start | bytes 393224 | tf_op jit(solution)/shard_map/ppermute | solution.py:44
  53.4 1.5 %collective-permute-start.21 = (bf16[128,512]{1,0:T(8,128)(2,1)S(1)}, bf16[128,512]{1,0:T(8,128)(2,1)S(1)}, u32[]{:S(2)}, u32[]{:S(2)}) collective-permute-start(bf16[128,512]{1,0:T(8,128)(2,1)S(1)} %get-tuple-element.128), channel_id=1, source_target_pairs={{0,1},{1,0},{2,3},{3,2},{4,5},{5,4},{6,7},{7,6},{8,9},{9,8},{10,11... | collective-permute-start | bytes 393224 | tf_op jit(solution)/shard_map/ppermute | solution.py:44
  54.9 1.5 %collective-permute-start.17 = (bf16[128,256]{1,0:T(8,128)(2,1)S(1)}, bf16[128,256]{1,0:T(8,128)(2,1)S(1)}, u32[]{:S(2)}, u32[]{:S(2)}) collective-permute-start(bf16[128,256]{1,0:T(8,128)(2,1)S(1)} %get-tuple-element.123), channel_id=1, source_target_pairs={{0,5},{1,4},{2,7},{3,6},{4,1},{5,0},{6,3},{7,2},{8,13},{9,12},{10,... | collective-permute-start | bytes 196616 | tf_op jit(solution)/shard_map/ppermute | solution.py:44
  56.4 1.8 %collective-permute-start.18 = (bf16[128,256]{1,0:T(8,128)(2,1)S(1)}, bf16[128,256]{1,0:T(8,128)(2,1)S(1)}, u32[]{:S(2)}, u32[]{:S(2)}) collective-permute-start(bf16[128,256]{1,0:T(8,128)(2,1)S(1)} %get-tuple-element.124), channel_id=1, source_target_pairs={{0,7},{1,6},{2,5},{3,4},{4,3},{5,2},{6,1},{7,0},{8,15},{9,14},{10,... | collective-permute-start | bytes 196616 | tf_op jit(solution)/shard_map/ppermute | solution.py:44
  58.2 3.4 %collective-permute-done.17.rest_2_ = bf16[128,256]{1,0:T(8,128)(2,1)S(1)} collective-permute-done((bf16[128,256]{1,0:T(8,128)(2,1)S(1)}, bf16[128,256]{1,0:T(8,128)(2,1)S(1)}, u32[]{:S(2)}, u32[]{:S(2)}) %collective-permute-start.17) | collective-permute-done | bytes 65568 | tf_op jit(solution)/shard_map/ppermute | solution.py:44
  61.5 0.2 collective-permute-start.28
  61.8 2.9 %collective-permute-done.18.rest_3_ = bf16[128,256]{1,0:T(8,128)(2,1)S(1)} collective-permute-done((bf16[128,256]{1,0:T(8,128)(2,1)S(1)}, bf16[128,256]{1,0:T(8,128)(2,1)S(1)}, u32[]{:S(2)}, u32[]{:S(2)}) %collective-permute-start.18) | collective-permute-done | bytes 65568 | tf_op jit(solution)/shard_map/ppermute | solution.py:44
  64.7 0.8 collective-permute-start.27
  65.5 1.7 %two_filters.3 = (bf16[512,128]{1,0:T(8,128)(2,1)S(1)}, bf16[512,256]{1,0:T(8,128)(2,1)S(1)}, f32[256,256]{1,0:T(8,128)S(1)}) custom-call(f32[2,128]{1,0:T(2,128)S(1)} %bitcast.20, f32[2,4,512,128]{3,2,1,0:T(8,128)S(1)} %get-tuple-element.88.spectra_ref, bf16[512,256]{1,0:T(8,128)(2,1)S(1)} %copy-done.2, bf16[256,512]{1,0:T(8,128)(2,1)S(1)} %copy-done.1, ...), custom_call_target="tpu_custom_call" | custom-call | flops 536870912 | bytes 1048576 | tf_op jit(solution)/shard_map/two_filters/pallas_call | solution.py:367
  67.2 2.9 %collective-permute-start.22 = (bf16[512,128]{1,0:T(8,128)(2,1)S(1)}, bf16[512,128]{1,0:T(8,128)(2,1)S(1)}, u32[]{:S(2)}, u32[]{:S(2)}) collective-permute-start(bf16[512,128]{1,0:T(8,128)(2,1)S(1)} %get-tuple-element.130), channel_id=1, source_target_pairs={{0,4},{1,5},{2,6},{3,7},{4,0},{5,1},{6,2},{7,3},{8,12},{9,13},{10,... | collective-permute-start | bytes 393224 | tf_op jit(solution)/shard_map/ppermute | solution.py:44
  70.0 0.2 own_half.3.keep_ref
  70.3 1.9 %hold_exit.1 = (bf16[1024,1024]{1,0:T(8,128)(2,1)S(1)}, bf16[4,128,256]{2,1,0:T(8,128)(2,1)S(1)}, bf16[128,1024]{1,0:T(8,128)(2,1)S(1)}, bf16[128,1024]{1,0:T(8,...) custom-call(bf16[1024,1024]{1,0:T(8,128)(2,1)} %bitcast.11, ...), custom_call_target="tpu_custom_call" | custom-call | bytes 3932160 | tf_op jit(solution)/shard_map/hold_exit/pallas_call | solution.py:204
  72.2 4.2 %collective-permute-done.22.come_ref = bf16[512,128]{1,0:T(8,128)(2,1)S(1)} collective-permute-done((bf16[512,128]{1,0:T(8,128)(2,1)S(1)}, bf16[512,128]{1,0:T(8,128)(2,1)S(1)}, u32[]{:S(2)}, u32[]{:S(2)}) %collective-permute-start.22) | collective-permute-done | bytes 131104 | tf_op jit(solution)/shard_map/ppermute | solution.py:44
  76.4 0.1 second_gate.3
  76.5 0.5 gradient_away.1
  76.9 2.4 %collective-permute-start.29 = (bf16[128,1024]{1,0:T(8,128)(2,1)S(1)}, bf16[128,1024]{1,0:T(8,128)(2,1)S(1)}, u32[]{:S(2)}, u32[]{:S(2)}) collective-permute-start(bf16[128,1024]{1,0:T(8,128)(2,1)S(1)} %gradient_away.1), channel_id=1, source_target_pairs={{0,4},{1,5},{2,6},{3,7},{4,0},{5,1},{6,2},{7,3},{8,12},{9,13},{10,... | collective-permute-start | bytes 786440 | tf_op jit(solution)/shard_map/ppermute | solution.py:44
  79.4 3.1 %collective-permute-start.24 = (bf16[128,256]{1,0:T(8,128)(2,1)S(1)}, bf16[128,256]{1,0:T(8,128)(2,1)S(1)}, u32[]{:S(2)}, u32[]{:S(2)}) collective-permute-start(bf16[128,256]{1,0:T(8,128)(2,1)S(1)} %get-tuple-element.155), channel_id=1, source_target_pairs={{0,3},{1,2},{2,1},{3,0},{4,7},{5,6},{6,5},{7,4},{8,11},{9,10},{10,... | collective-permute-start | bytes 196616 | tf_op jit(solution)/shard_map/ppermute | solution.py:44
  82.5 0.9 collective-permute-start.26
  83.4 0.5 gradient_mine.1
  83.9 3.4 %collective-permute-done.24.rest_0_ = bf16[128,256]{1,0:T(8,128)(2,1)S(1)} collective-permute-done((bf16[128,256]{1,0:T(8,128)(2,1)S(1)}, bf16[128,256]{1,0:T(8,128)(2,1)S(1)}, u32[]{:S(2)}, u32[]{:S(2)}) %collective-permute-start.24) | collective-permute-done | bytes 65568 | tf_op jit(solution)/shard_map/ppermute | solution.py:44
  87.3 0.7 collective-permute-done.25.rest_1_
  88.0 1.1 %exit_projection.3 = bf16[128,1024]{1,0:T(8,128)(2,1)} custom-call(s32[1]{0:T(128)} %bitcast.choice_ref, bf16[128,1024]{1,0:T(8,128)(2,1)S(1)} %collective-permute-done.13.x_ref, bf16[128,1024]{1,0:T(8,128)(2,1)S(1)} %get-tuple-element.119.other_ref, bf16[1024,1024]{1,0:T(8,128)(2,1)S(1)} %get-tuple-element.153.weight_ref, ...), custom_call_target="tpu_custom_call" | custom-call | flops 268435456 | bytes 2097152 | tf_op jit(solution)/shard_map/exit_projection/pallas_call | solution.py:453
  89.2 2.4 %collective-permute-done.29 = bf16[128,1024]{1,0:T(8,128)(2,1)S(1)} collective-permute-done((bf16[128,1024]{1,0:T(8,128)(2,1)S(1)}, bf16[128,1024]{1,0:T(8,128)(2,1)S(1)}, u32[]{:S(2)}, u32[]{:S(2)}) %collective-permute-start.29) | collective-permute-done | bytes 262176 | tf_op jit(solution)/shard_map/ppermute | solution.py:44
  91.5 0.9 add_bitcast_fusion
  (50 shorter events, 0.1 us)
Async XLA Ops:
  0.6 17.2 %copy-start.2 = (bf16[512,256]{1,0:T(8,128)(2,1)S(1)}, bf16[512,256]{1,0:T(8,128)(2,1)}, u32[]{:S(2)}) copy-start(bf16[512,256]{1,0:T(8,128)(2,1)} %constant.13.clone.forward_ref) | copy-start | bytes 786436
  0.6 17.2 %copy-start.5 = (bf16[1,2,128,1024]{3,2,1,0:T(8,128)(2,1)S(1)}, bf16[1,2,128,1024]{3,2,1,0:T(8,128)(2,1)}, u32[]{:S(2)}) copy-start(bf16[1,2,128,1024]{3,2,1,0:T(8,128)(2,1)} %param.23) | copy-start | bytes 1572868
  0.7 17.1 %copy-start.12 = (bf16[32,1024]{1,0:T(8,128)(2,1)S(1)}, bf16[32,1024]{1,0:T(8,128)(2,1)}, u32[]{:S(2)}) copy-start(bf16[32,1024]{1,0:T(8,128)(2,1)} %amino_ref.1) | copy-start | bytes 196612
  0.7 17.1 %copy-start.14 = (bf16[8,1024]{1,0:T(8,128)(2,1)S(1)}, bf16[8,1024]{1,0:T(8,128)(2,1)}, u32[]{:S(2)}) copy-start(bf16[8,1024]{1,0:T(8,128)(2,1)} %polymer_ref.1) | copy-start | bytes 49156
  0.7 17.1 %copy-start.16 = (s32[8]{0:T(128)S(1)}, s32[8]{0:T(128)}, u32[]{:S(2)}) copy-start(s32[8]{0:T(128)} %sizes_ref.1) | copy-start | bytes 100
  0.7 17.1 %copy-start.17 = (s32[128]{0:T(128)S(1)}, s32[128]{0:T(128)}, u32[]{:S(2)}) copy-start(s32[128]{0:T(128)} %param.14) | copy-start | bytes 1540
  3.8 14.0 %copy-start.4 = (f32[1,2,128,1024]{3,2,1,0:T(8,128)S(1)}, f32[1,2,128,1024]{3,2,1,0:T(8,128)}, u32[]{:S(2)}) copy-start(f32[1,2,128,1024]{3,2,1,0:T(8,128)} %param.20) | copy-start | bytes 3145732
  3.8 19.6 %copy-start.1 = (bf16[256,512]{1,0:T(8,128)(2,1)S(1)}, bf16[256,512]{1,0:T(8,128)(2,1)}, u32[]{:S(2)}) copy-start(bf16[256,512]{1,0:T(8,128)(2,1)} %constant.14.clone.backward_ref) | copy-start | bytes 786436
  3.9 19.6 %copy-start.13 = (f32[1,2,128]{2,1,0:T(2,128)S(1)}, f32[1,2,128]{2,1,0:T(2,128)}, u32[]{:S(2)}) copy-start(f32[1,2,128]{2,1,0:T(2,128)} %param.21) | copy-start | bytes 3076
  3.9 9.9 %collective-permute-start = (bf16[128,256]{1,0:T(8,128)(2,1)S(1)}, bf16[128,256]{1,0:T(8,128)(2,1)S(1)}, u32[]{:S(2)}, u32[]{:S(2)}) collective-permute-start(bf16[128,256]{1,0:T(8,128)(2,1)S(1)} %get-tuple-element.89), channel_id=1, source_target_pairs={{0,4},{1,5},{2,6},{3,7},{4,0},{5,1},{6,2},{7,3},{8,12},{9,13},{10,... | collective-permute-start | bytes 196616 | tf_op jit(solution)/shard_map/ppermute | solution.py:44
  8.0 8.5 %collective-permute-start.1 = (bf16[128,256]{1,0:T(8,128)(2,1)S(1)}, bf16[128,256]{1,0:T(8,128)(2,1)S(1)}, u32[]{:S(2)}, u32[]{:S(2)}) collective-permute-start(bf16[128,256]{1,0:T(8,128)(2,1)S(1)} %get-tuple-element.90), channel_id=1, source_target_pairs={{0,6},{1,7},{2,4},{3,5},{4,2},{5,3},{6,0},{7,1},{8,14},{9,15},{10,... | collective-permute-start | bytes 196616 | tf_op jit(solution)/shard_map/ppermute | solution.py:44
  10.3 13.2 %collective-permute-start.4 = (bf16[128,512]{1,0:T(8,128)(2,1)S(1)}, bf16[128,512]{1,0:T(8,128)(2,1)S(1)}, u32[]{:S(2)}, u32[]{:S(2)}) collective-permute-start(bf16[128,512]{1,0:T(8,128)(2,1)S(1)} %get-tuple-element.95), channel_id=1, source_target_pairs={{0,3},{1,2},{2,1},{3,0},{4,7},{5,6},{6,5},{7,4},{8,11},{9,10},{10,... | collective-permute-start | bytes 393224 | tf_op jit(solution)/shard_map/ppermute | solution.py:44
  11.5 12.0 %collective-permute-start.5 = (bf16[128,512]{1,0:T(8,128)(2,1)S(1)}, bf16[128,512]{1,0:T(8,128)(2,1)S(1)}, u32[]{:S(2)}, u32[]{:S(2)}) collective-permute-start(bf16[128,512]{1,0:T(8,128)(2,1)S(1)} %get-tuple-element.96), channel_id=1, source_target_pairs={{0,2},{1,3},{2,0},{3,1},{4,6},{5,7},{6,4},{7,5},{8,10},{9,11},{10,... | collective-permute-start | bytes 393224 | tf_op jit(solution)/shard_map/ppermute | solution.py:44
  13.3 10.2 %collective-permute-start.6 = (bf16[128,512]{1,0:T(8,128)(2,1)S(1)}, bf16[128,512]{1,0:T(8,128)(2,1)S(1)}, u32[]{:S(2)}, u32[]{:S(2)}) collective-permute-start(bf16[128,512]{1,0:T(8,128)(2,1)S(1)} %get-tuple-element.97), channel_id=1, source_target_pairs={{0,1},{1,0},{2,3},{3,2},{4,5},{5,4},{6,7},{7,6},{8,9},{9,8},{10,11... | collective-permute-start | bytes 393224 | tf_op jit(solution)/shard_map/ppermute | solution.py:44
  13.8 6.5 %collective-permute-start.2 = (bf16[128,256]{1,0:T(8,128)(2,1)S(1)}, bf16[128,256]{1,0:T(8,128)(2,1)S(1)}, u32[]{:S(2)}, u32[]{:S(2)}) collective-permute-start(bf16[128,256]{1,0:T(8,128)(2,1)S(1)} %get-tuple-element.91), channel_id=1, source_target_pairs={{0,5},{1,4},{2,7},{3,6},{4,1},{5,0},{6,3},{7,2},{8,13},{9,12},{10,... | collective-permute-start | bytes 196616 | tf_op jit(solution)/shard_map/ppermute | solution.py:44
  16.4 7.0 %collective-permute-start.3 = (bf16[128,256]{1,0:T(8,128)(2,1)S(1)}, bf16[128,256]{1,0:T(8,128)(2,1)S(1)}, u32[]{:S(2)}, u32[]{:S(2)}) collective-permute-start(bf16[128,256]{1,0:T(8,128)(2,1)S(1)} %get-tuple-element.92), channel_id=1, source_target_pairs={{0,7},{1,6},{2,5},{3,4},{4,3},{5,2},{6,1},{7,0},{8,15},{9,14},{10,... | collective-permute-start | bytes 196616 | tf_op jit(solution)/shard_map/ppermute | solution.py:44
  19.9 20.6 %copy-start = (bf16[1,1024,1024]{2,1,0:T(8,128)(2,1)S(1)}, bf16[1,1024,1024]{2,1,0:T(8,128)(2,1)}, u32[]{:S(2)}) copy-start(bf16[1,1024,1024]{2,1,0:T(8,128)(2,1)} %param.22) | copy-start | bytes 6291460
  20.0 20.6 %copy-start.3 = (bf16[1,128,1024]{2,1,0:T(8,128)(2,1)S(1)}, bf16[1,128,1024]{2,1,0:T(8,128)(2,1)}, u32[]{:S(2)}) copy-start(bf16[1,128,1024]{2,1,0:T(8,128)(2,1)} %param.13) | copy-start | bytes 786436
  25.1 7.0 %collective-permute-start.7 = (bf16[512,128]{1,0:T(8,128)(2,1)S(1)}, bf16[512,128]{1,0:T(8,128)(2,1)S(1)}, u32[]{:S(2)}, u32[]{:S(2)}) collective-permute-start(bf16[512,128]{1,0:T(8,128)(2,1)S(1)} %get-tuple-element.101), channel_id=1, source_target_pairs={{0,4},{1,5},{2,6},{3,7},{4,0},{5,1},{6,2},{7,3},{8,12},{9,13},{10,... | collective-permute-start | bytes 393224 | tf_op jit(solution)/shard_map/ppermute | solution.py:44
  27.3 13.3 %collective-permute-start.11 = (bf16[128,1024]{1,0:T(8,128)(2,1)}, bf16[128,1024]{1,0:T(8,128)(2,1)S(1)}, u32[]{:S(2)}, u32[]{:S(2)}) collective-permute-start(bf16[128,1024]{1,0:T(8,128)(2,1)} %get-tuple-element.141.refs_4_), channel_id=1, source_target_pairs={{0,1},{1,0},{2,3},{3,2},{4,5},{5,4},{6,7},{7,6},{8,9},{9,8},{10,11... | collective-permute-start | bytes 786440 | tf_op jit(solution)/shard_map/ppermute | solution.py:44
  28.3 12.3 %collective-permute-start.12 = (bf16[128,1024]{1,0:T(8,128)(2,1)}, bf16[128,1024]{1,0:T(8,128)(2,1)S(1)}, u32[]{:S(2)}, u32[]{:S(2)}) collective-permute-start(bf16[128,1024]{1,0:T(8,128)(2,1)} %get-tuple-element.144.refs_7_), channel_id=1, source_target_pairs={{0,2},{1,3},{2,0},{3,1},{4,6},{5,7},{6,4},{7,5},{8,10},{9,11},{10,... | collective-permute-start | bytes 786440 | tf_op jit(solution)/shard_map/ppermute | solution.py:44
  32.2 11.0 %copy-start.10 = (bf16[4,128,256]{2,1,0:T(8,128)(2,1)}, bf16[4,128,256]{2,1,0:T(8,128)(2,1)S(1)}, u32[]{:S(2)}) copy-start(bf16[4,128,256]{2,1,0:T(8,128)(2,1)S(1)} %get-tuple-element.138.refs_1_) | copy-start | bytes 786436
  32.2 6.5 %collective-permute-start.8 = (bf16[128,256]{1,0:T(8,128)(2,1)S(1)}, bf16[128,256]{1,0:T(8,128)(2,1)S(1)}, u32[]{:S(2)}, u32[]{:S(2)}) collective-permute-start(bf16[128,256]{1,0:T(8,128)(2,1)S(1)} %get-tuple-element.103), channel_id=1, source_target_pairs={{0,3},{1,2},{2,1},{3,0},{4,7},{5,6},{6,5},{7,4},{8,11},{9,10},{10,... | collective-permute-start | bytes 196616 | tf_op jit(solution)/shard_map/ppermute | solution.py:44
  34.3 6.2 %collective-permute-start.9 = (bf16[128,256]{1,0:T(8,128)(2,1)S(1)}, bf16[128,256]{1,0:T(8,128)(2,1)S(1)}, u32[]{:S(2)}, u32[]{:S(2)}) collective-permute-start(bf16[128,256]{1,0:T(8,128)(2,1)S(1)} %get-tuple-element.104), channel_id=1, source_target_pairs={{0,2},{1,3},{2,0},{3,1},{4,6},{5,7},{6,4},{7,5},{8,10},{9,11},{10,... | collective-permute-start | bytes 196616 | tf_op jit(solution)/shard_map/ppermute | solution.py:44
  35.4 5.1 %collective-permute-start.10 = (bf16[128,256]{1,0:T(8,128)(2,1)S(1)}, bf16[128,256]{1,0:T(8,128)(2,1)S(1)}, u32[]{:S(2)}, u32[]{:S(2)}) collective-permute-start(bf16[128,256]{1,0:T(8,128)(2,1)S(1)} %get-tuple-element.105), channel_id=1, source_target_pairs={{0,1},{1,0},{2,3},{3,2},{4,5},{5,4},{6,7},{7,6},{8,9},{9,8},{10,11... | collective-permute-start | bytes 196616 | tf_op jit(solution)/shard_map/ppermute | solution.py:44
  38.7 7.3 %collective-permute-start.14 = (bf16[128,1024]{1,0:T(8,128)(2,1)}, bf16[128,1024]{1,0:T(8,128)(2,1)}, u32[]{:S(2)}, u32[]{:S(2)}) collective-permute-start(bf16[128,1024]{1,0:T(8,128)(2,1)} %get-tuple-element.144.refs_7_), channel_id=1, source_target_pairs={{0,1},{1,0},{2,3},{3,2},{4,5},{5,4},{6,7},{7,6},{8,9},{9,8},{10,11... | collective-permute-start | bytes 786440 | tf_op jit(solution)/shard_map/ppermute | solution.py:44
  40.5 2.7 %copy-start.8 = (bf16[128,1024]{1,0:T(8,128)(2,1)}, bf16[128,1024]{1,0:T(8,128)(2,1)S(1)}, u32[]{:S(2)}) copy-start(bf16[128,1024]{1,0:T(8,128)(2,1)S(1)} %collective-permute-done.11.refs_3_) | copy-start | bytes 786436
  40.6 1.9 %copy-start.6 = (bf16[128,1024]{1,0:T(8,128)(2,1)}, bf16[128,1024]{1,0:T(8,128)(2,1)S(1)}, u32[]{:S(2)}) copy-start(bf16[128,1024]{1,0:T(8,128)(2,1)S(1)} %collective-permute-done.12.refs_5_) | copy-start | bytes 786436
  41.1 4.9 %collective-permute-start.13 = (bf16[128,1024]{1,0:T(8,128)(2,1)S(1)}, bf16[128,1024]{1,0:T(8,128)(2,1)S(1)}, u32[]{:S(2)}, u32[]{:S(2)}) collective-permute-start(bf16[128,1024]{1,0:T(8,128)(2,1)S(1)} %exit_projection.2), channel_id=1, source_target_pairs={{0,8},{8,16},{16,24},{1,9},{9,17},{17,25},{2,10},{10,18},{18,26},{... | collective-permute-start | bytes 786440 | tf_op jit(solution)/shard_map/ppermute | solution.py:561
  42.4 11.0 %collective-permute-start.23 = (bf16[128,1024]{1,0:T(8,128)(2,1)}, bf16[128,1024]{1,0:T(8,128)(2,1)}, u32[]{:S(2)}, u32[]{:S(2)}) collective-permute-start(bf16[128,1024]{1,0:T(8,128)(2,1)} %get-tuple-element.141.refs_4_), channel_id=1, source_target_pairs={{0,2},{1,3},{2,0},{3,1},{4,6},{5,7},{6,4},{7,5},{8,10},{9,11},{10,... | collective-permute-start | bytes 786440 | tf_op jit(solution)/shard_map/ppermute | solution.py:44
  43.2 2.8 %copy-start.15 = (f32[1,1024]{1,0:T(1,128)S(1)}, f32[1,1024]{1,0:T(1,128)}, u32[]{:S(2)}) copy-start(f32[1,1024]{1,0:T(1,128)} %gain_ref.3) | copy-start | bytes 12292
  46.6 14.9 %copy-start.7 = (bf16[128,1024]{1,0:T(8,128)(2,1)S(1)}, bf16[128,1024]{1,0:T(8,128)(2,1)}, u32[]{:S(2)}) copy-start(bf16[128,1024]{1,0:T(8,128)(2,1)} %copy-done.6) | copy-start | bytes 786436
  46.6 8.3 %collective-permute-start.15 = (bf16[128,256]{1,0:T(8,128)(2,1)S(1)}, bf16[128,256]{1,0:T(8,128)(2,1)S(1)}, u32[]{:S(2)}, u32[]{:S(2)}) collective-permute-start(bf16[128,256]{1,0:T(8,128)(2,1)S(1)} %get-tuple-element.121), channel_id=1, source_target_pairs={{0,4},{1,5},{2,6},{3,7},{4,0},{5,1},{6,2},{7,3},{8,12},{9,13},{10,... | collective-permute-start | bytes 196616 | tf_op jit(solution)/shard_map/ppermute | solution.py:44
  48.7 7.7 %collective-permute-start.16 = (bf16[128,256]{1,0:T(8,128)(2,1)S(1)}, bf16[128,256]{1,0:T(8,128)(2,1)S(1)}, u32[]{:S(2)}, u32[]{:S(2)}) collective-permute-start(bf16[128,256]{1,0:T(8,128)(2,1)S(1)} %get-tuple-element.122), channel_id=1, source_target_pairs={{0,6},{1,7},{2,4},{3,5},{4,2},{5,3},{6,0},{7,1},{8,14},{9,15},{10,... | collective-permute-start | bytes 196616 | tf_op jit(solution)/shard_map/ppermute | solution.py:44
  50.4 19.8 %copy-start.9 = (bf16[128,1024]{1,0:T(8,128)(2,1)S(1)}, bf16[128,1024]{1,0:T(8,128)(2,1)}, u32[]{:S(2)}) copy-start(bf16[128,1024]{1,0:T(8,128)(2,1)} %copy-done.8) | copy-start | bytes 786436
  50.4 19.9 %copy-start.11 = (bf16[4,128,256]{2,1,0:T(8,128)(2,1)S(1)}, bf16[4,128,256]{2,1,0:T(8,128)(2,1)}, u32[]{:S(2)}) copy-start(bf16[4,128,256]{2,1,0:T(8,128)(2,1)} %copy-done.10) | copy-start | bytes 786436
  51.3 14.1 %collective-permute-start.19 = (bf16[128,512]{1,0:T(8,128)(2,1)S(1)}, bf16[128,512]{1,0:T(8,128)(2,1)S(1)}, u32[]{:S(2)}, u32[]{:S(2)}) collective-permute-start(bf16[128,512]{1,0:T(8,128)(2,1)S(1)} %get-tuple-element.126), channel_id=1, source_target_pairs={{0,3},{1,2},{2,1},{3,0},{4,7},{5,6},{6,5},{7,4},{8,11},{9,10},{10,... | collective-permute-start | bytes 393224 | tf_op jit(solution)/shard_map/ppermute | solution.py:44
  51.8 13.7 %collective-permute-start.20 = (bf16[128,512]{1,0:T(8,128)(2,1)S(1)}, bf16[128,512]{1,0:T(8,128)(2,1)S(1)}, u32[]{:S(2)}, u32[]{:S(2)}) collective-permute-start(bf16[128,512]{1,0:T(8,128)(2,1)S(1)} %get-tuple-element.127), channel_id=1, source_target_pairs={{0,2},{1,3},{2,0},{3,1},{4,6},{5,7},{6,4},{7,5},{8,10},{9,11},{10,... | collective-permute-start | bytes 393224 | tf_op jit(solution)/shard_map/ppermute | solution.py:44
  53.4 12.1 %collective-permute-start.21 = (bf16[128,512]{1,0:T(8,128)(2,1)S(1)}, bf16[128,512]{1,0:T(8,128)(2,1)S(1)}, u32[]{:S(2)}, u32[]{:S(2)}) collective-permute-start(bf16[128,512]{1,0:T(8,128)(2,1)S(1)} %get-tuple-element.128), channel_id=1, source_target_pairs={{0,1},{1,0},{2,3},{3,2},{4,5},{5,4},{6,7},{7,6},{8,9},{9,8},{10,11... | collective-permute-start | bytes 393224 | tf_op jit(solution)/shard_map/ppermute | solution.py:44
  54.9 6.6 %collective-permute-start.17 = (bf16[128,256]{1,0:T(8,128)(2,1)S(1)}, bf16[128,256]{1,0:T(8,128)(2,1)S(1)}, u32[]{:S(2)}, u32[]{:S(2)}) collective-permute-start(bf16[128,256]{1,0:T(8,128)(2,1)S(1)} %get-tuple-element.123), channel_id=1, source_target_pairs={{0,5},{1,4},{2,7},{3,6},{4,1},{5,0},{6,3},{7,2},{8,13},{9,12},{10,... | collective-permute-start | bytes 196616 | tf_op jit(solution)/shard_map/ppermute | solution.py:44
  56.4 8.2 %collective-permute-start.18 = (bf16[128,256]{1,0:T(8,128)(2,1)S(1)}, bf16[128,256]{1,0:T(8,128)(2,1)S(1)}, u32[]{:S(2)}, u32[]{:S(2)}) collective-permute-start(bf16[128,256]{1,0:T(8,128)(2,1)S(1)} %get-tuple-element.124), channel_id=1, source_target_pairs={{0,7},{1,6},{2,5},{3,4},{4,3},{5,2},{6,1},{7,0},{8,15},{9,14},{10,... | collective-permute-start | bytes 196616 | tf_op jit(solution)/shard_map/ppermute | solution.py:44
  61.5 14.9 %collective-permute-start.28 = (bf16[128,1024]{1,0:T(8,128)(2,1)S(1)}, bf16[128,1024]{1,0:T(8,128)(2,1)S(1)}, u32[]{:S(2)}, u32[]{:S(2)}) collective-permute-start(bf16[128,1024]{1,0:T(8,128)(2,1)S(1)} %copy-done.7), channel_id=1, source_target_pairs={{0,1},{1,0},{2,3},{3,2},{4,5},{5,4},{6,7},{7,6},{8,9},{9,8},{10,11... | collective-permute-start | bytes 786440 | tf_op jit(solution)/shard_map/ppermute | solution.py:44
  64.7 11.8 %collective-permute-start.27 = (bf16[128,1024]{1,0:T(8,128)(2,1)}, bf16[128,1024]{1,0:T(8,128)(2,1)S(1)}, u32[]{:S(2)}, u32[]{:S(2)}) collective-permute-start(bf16[128,1024]{1,0:T(8,128)(2,1)} %collective-permute-done.23.refs_2_), channel_id=1, source_target_pairs={{0,1},{1,0},{2,3},{3,2},{4,5},{5,4},{6,7},{7,6},{8,9},{9,8},{10,11... | collective-permute-start | bytes 786440 | tf_op jit(solution)/shard_map/ppermute | solution.py:44
  67.2 9.2 %collective-permute-start.22 = (bf16[512,128]{1,0:T(8,128)(2,1)S(1)}, bf16[512,128]{1,0:T(8,128)(2,1)S(1)}, u32[]{:S(2)}, u32[]{:S(2)}) collective-permute-start(bf16[512,128]{1,0:T(8,128)(2,1)S(1)} %get-tuple-element.130), channel_id=1, source_target_pairs={{0,4},{1,5},{2,6},{3,7},{4,0},{5,1},{6,2},{7,3},{8,12},{9,13},{10,... | collective-permute-start | bytes 393224 | tf_op jit(solution)/shard_map/ppermute | solution.py:44
  76.9 14.6 %collective-permute-start.29 = (bf16[128,1024]{1,0:T(8,128)(2,1)S(1)}, bf16[128,1024]{1,0:T(8,128)(2,1)S(1)}, u32[]{:S(2)}, u32[]{:S(2)}) collective-permute-start(bf16[128,1024]{1,0:T(8,128)(2,1)S(1)} %gradient_away.1), channel_id=1, source_target_pairs={{0,4},{1,5},{2,6},{3,7},{4,0},{5,1},{6,2},{7,3},{8,12},{9,13},{10,... | collective-permute-start | bytes 786440 | tf_op jit(solution)/shard_map/ppermute | solution.py:44
  79.4 8.0 %collective-permute-start.24 = (bf16[128,256]{1,0:T(8,128)(2,1)S(1)}, bf16[128,256]{1,0:T(8,128)(2,1)S(1)}, u32[]{:S(2)}, u32[]{:S(2)}) collective-permute-start(bf16[128,256]{1,0:T(8,128)(2,1)S(1)} %get-tuple-element.155), channel_id=1, source_target_pairs={{0,3},{1,2},{2,1},{3,0},{4,7},{5,6},{6,5},{7,4},{8,11},{9,10},{10,... | collective-permute-start | bytes 196616 | tf_op jit(solution)/shard_map/ppermute | solution.py:44
  82.5 5.5 %collective-permute-start.25 = (bf16[128,256]{1,0:T(8,128)(2,1)S(1)}, bf16[128,256]{1,0:T(8,128)(2,1)S(1)}, u32[]{:S(2)}, u32[]{:S(2)}) collective-permute-start(bf16[128,256]{1,0:T(8,128)(2,1)S(1)} %get-tuple-element.156), channel_id=1, source_target_pairs={{0,2},{1,3},{2,0},{3,1},{4,6},{5,7},{6,4},{7,5},{8,10},{9,11},{10,... | collective-permute-start | bytes 196616 | tf_op jit(solution)/shard_map/ppermute | solution.py:44
  82.5 5.5 %collective-permute-start.26 = (bf16[128,256]{1,0:T(8,128)(2,1)S(1)}, bf16[128,256]{1,0:T(8,128)(2,1)S(1)}, u32[]{:S(2)}, u32[]{:S(2)}) collective-permute-start(bf16[128,256]{1,0:T(8,128)(2,1)S(1)} %get-tuple-element.157), channel_id=1, source_target_pairs={{0,1},{1,0},{2,3},{3,2},{4,5},{5,4},{6,7},{7,6},{8,9},{9,8},{10,11... | collective-permute-start | bytes 196616 | tf_op jit(solution)/shard_map/ppermute | solution.py:44
